TPU v7x, 128 devices: a whole 4x4x4 slice. The times are simulated.
128 devices in a mesh: dp: 16 (over y, z_lo, core), mp: 8 (over z_hi, x).
Axes of the slice: x: 4, y: 4, z: 4 (z_hi: 2, z_lo: 2; z = z_hi * 2 + z_lo), core: 2. Of those that a mesh axis runs over, the one named last changes fastest.
Arguments:
- tokens: bfloat16 [16384, 2048], P(('dp', 'mp')), may hold values from -6 to 6
- cotangent: bfloat16 [16384, 2048], P(('dp', 'mp')), may hold values from -6 to 6
- attention_norm_scale: bfloat16 [2048], replicated, may hold values from 0.099609375 to 1.8984375
- attention_norm_bias: bfloat16 [2048], replicated, may hold values from -3 to 3
- query_projection: bfloat16 [2048, 2048], P('dp', 'mp'), may hold values from -0.125 to 0.125
- query_projection_bias: bfloat16 [2048], P('mp'), may hold values from -3 to 3
- keyvalue_projection: bfloat16 [2048, 256], P('dp'), may hold values from -0.125 to 0.125
- value_projection_bias: bfloat16 [128], replicated, may hold values from -3 to 3
- attention_output_weight: bfloat16 [2048, 2048], P('mp', 'dp'), may hold values from -0.5 to 0.5
- attention_output_bias: bfloat16 [2048], replicated, may hold values from -3 to 3
- feedforward_norm_scale: bfloat16 [2048], replicated, may hold values from 0.099609375 to 1.8984375
- feedforward_norm_bias: bfloat16 [2048], replicated, may hold values from -3 to 3
- up_projection_weight: bfloat16 [2048, 8192], P('dp', 'mp'), may hold values from -0.125 to 0.125
- up_projection_bias: bfloat16 [8192], P('mp'), may hold values from -3 to 3
- down_projection_weight: bfloat16 [8192, 2048], P('mp', 'dp'), may hold values from -0.0625 to 0.0625
- down_projection_bias: bfloat16 [2048], replicated, may hold values from -3 to 3
- sequence_adapter: int32 [16, 1], P('dp'), may hold values from 0 to 7
- query_adapter_input: bfloat16 [8, 2048, 16], replicated, may hold values from -0.125 to 0.125
- query_adapter_output: bfloat16 [8, 16, 2048], P(None, None, 'mp'), may hold values from -0.75 to 0.75
- keyvalue_adapter_input: bfloat16 [8, 2048, 16], replicated, may hold values from -0.125 to 0.125
- keyvalue_adapter_output: bfloat16 [8, 16, 256], replicated, may hold values from -0.75 to 0.75
- output_adapter_input: bfloat16 [8, 2048, 16], P(None, 'mp'), may hold values from -0.5 to 0.5
- output_adapter_output: bfloat16 [8, 16, 2048], replicated, may hold values from -0.75 to 0.75
- up_adapter_input: bfloat16 [8, 2048, 16], replicated, may hold values from -0.125 to 0.125
- up_adapter_output: bfloat16 [8, 16, 8192], P(None, None, 'mp'), may hold values from -0.75 to 0.75
- down_adapter_input: bfloat16 [8, 8192, 16], P(None, 'mp'), may hold values from -0.0625 to 0.0625
- down_adapter_output: bfloat16 [8, 16, 2048], replicated, may hold values from -0.75 to 0.75
Outputs:
- layer_output: bfloat16 [16384, 2048], P(('dp', 'mp'))
- grad_tokens: bfloat16 [16384, 2048], P(('dp', 'mp'))
- grad_query_lora_a: float32 [8, 2048, 16], replicated
- grad_query_lora_b: float32 [8, 16, 2048], replicated
- grad_keyval_lora_a: float32 [8, 2048, 16], replicated
- grad_keyval_lora_b: float32 [8, 16, 256], replicated
- grad_output_lora_a: float32 [8, 2048, 16], replicated
- grad_output_lora_b: float32 [8, 16, 2048], replicated
- grad_up_lora_a: float32 [8, 2048, 16], replicated
- grad_up_lora_b: float32 [8, 16, 8192], replicated
- grad_down_lora_a: float32 [8, 8192, 16], replicated
- grad_down_lora_b: float32 [8, 16, 2048], replicated
Inputs may be any that keep to these rules, and one draw needn't show every extreme that they name: `sequence_adapter`: each of the 8 adapters is chosen by at least one sequence.
All inputs are finite; a program needn't handle non-finite values.
Results may differ from a plain program's by a relative error of at most 0.024.
Values may be sent and summed in bfloat16 or wider, within the bound.
No kernel may reach another device: no remote copies, remote signals or barrier semaphores. Data moves between devices by JAX's collectives and lax.ppermute only.
A program may use at most 192 MiB of HBM per device.

v0:
```python
import math

import jax
import jax.numpy as jnp
from jax import lax
from jax.sharding import PartitionSpec as P

MODEL_WIDTH = 2048
H = 16
HEAD_WIDTH = 128
FEED_HIDDEN = 8192
ADAPTER_RANK = 16
ADAPTER_COUNT = 8
BLOCK = 256
QROWS = 512


def rows_first(arrays, axis, dims):
    turned = [jnp.moveaxis(a, dim, 0) for a, dim in zip(arrays, dims)]
    widths = [t[0].size for t in turned]
    both = jnp.concatenate([t.reshape(-1, w) for t, w in zip(turned, widths)], axis=1)
    filled = lax.all_gather(both, axis, axis=0, tiled=True)
    blocks = jnp.split(filled, [sum(widths[:k]) for k in range(1, len(widths))], axis=1)
    return tuple(
        (
            jnp.moveaxis(b.reshape(-1, *t.shape[1:]), 0, dim)
            for b, t, dim in zip(blocks, turned, dims)
        )
    )


def side_by_side(arrays, axis, dim, along):
    ends, at = ([], 0)
    for a in arrays[:-1]:
        at += a.shape[along]
        ends.append(at)
    both = jnp.concatenate(arrays, axis=along)
    return tuple(jnp.split(lax.all_gather(both, axis, axis=dim, tiled=True), ends, axis=along))


def in_one_piece(arrays, axis, dim, along):
    ends, at = ([], 0)
    for a in arrays[:-1]:
        at += a.shape[along]
        ends.append(at)
    both = jnp.concatenate(arrays, axis=along)
    return tuple(
        jnp.split(lax.psum_scatter(both, axis, scatter_dimension=dim, tiled=True), ends, axis=along)
    )


def layer_norm(values, gain, shift):
    mean_value = jnp.mean(values, axis=-1, keepdims=True)
    centred = values - mean_value
    variance = jnp.mean(centred * centred, axis=-1, keepdims=True)
    return centred * lax.rsqrt(variance + 1e-05) * gain + shift


def gelu_tanh(values):
    inner_product = math.sqrt(2.0 / math.pi) * (values + 0.044715 * values * values * values)
    return 0.5 * values * (1.0 + jnp.tanh(inner_product))


def select_adapter(adapter_stack, adapter_position):
    return lax.dynamic_index_in_dim(adapter_stack, adapter_position, 0, keepdims=False)


def mixed_dot(left, right):
    return jnp.dot(left, right, preferred_element_type=jnp.float32)


def mixed_dot_t(left, right):
    return lax.dot_general(
        left, right, (((1,), (1,)), ((), ())), preferred_element_type=jnp.float32
    )


def mixed_tdot(left, right):
    return lax.dot_general(
        left, right, (((0,), (0,)), ((), ())), preferred_element_type=jnp.float32
    )


def spread(piece, along, offset, full_shape):
    return lax.dynamic_update_slice_in_dim(jnp.zeros(full_shape, jnp.float32), piece, offset, along)


def stacked(whole, adapter_position):
    chosen = (jnp.arange(ADAPTER_COUNT, dtype=jnp.int32) == adapter_position).astype(jnp.float32)
    return chosen[:, None, None] * whole[None]


def shards(
    tokens,
    cotangent,
    attention_norm_scale,
    attention_norm_bias,
    query_projection,
    query_projection_bias,
    keyvalue_projection,
    value_projection_bias,
    attention_output_weight,
    attention_output_bias,
    feedforward_norm_scale,
    feedforward_norm_bias,
    up_projection_weight,
    up_projection_bias,
    down_projection_weight,
    down_projection_bias,
    sequence_adapter,
    query_adapter_input,
    query_adapter_output,
    keyvalue_adapter_input,
    keyvalue_adapter_output,
    output_adapter_input,
    output_adapter_output,
    up_adapter_input,
    up_adapter_output,
    down_adapter_input,
    down_adapter_output,
):
    adapter_position = sequence_adapter[0, 0]
    local_rows = tokens.shape[0]
    parts = lax.axis_size("mp")
    position = lax.axis_index("mp")
    length = local_rows * parts
    heads_here = H // parts
    scale = HEAD_WIDTH ** (-0.5)
    gain_one = attention_norm_scale.astype(jnp.float32)
    shift_one = attention_norm_bias.astype(jnp.float32)
    gain_two = feedforward_norm_scale.astype(jnp.float32)
    shift_two = feedforward_norm_bias.astype(jnp.float32)
    input_rows = tokens.astype(jnp.float32)
    query_input_side = select_adapter(query_adapter_input, adapter_position)
    query_output_side = select_adapter(query_adapter_output, adapter_position)
    keyvalue_input_side = select_adapter(keyvalue_adapter_input, adapter_position)
    keyvalue_output_side = select_adapter(keyvalue_adapter_output, adapter_position)
    output_input_side = select_adapter(output_adapter_input, adapter_position)
    output_output_side = select_adapter(output_adapter_output, adapter_position)
    up_input_side = select_adapter(up_adapter_input, adapter_position)
    up_output_side = select_adapter(up_adapter_output, adapter_position)
    down_input_side = select_adapter(down_adapter_input, adapter_position)
    down_output_side = select_adapter(down_adapter_output, adapter_position)
    w_query, w_keyval, w_output = rows_first(
        (query_projection, keyvalue_projection, attention_output_weight), "dp", (0, 0, 1)
    )
    normed = layer_norm(input_rows, gain_one, shift_one).astype(jnp.bfloat16)
    keyval_inner = mixed_dot(normed, keyvalue_input_side).astype(jnp.bfloat16)
    keyval_bias = jnp.concatenate(
        [jnp.zeros((HEAD_WIDTH,), jnp.float32), value_projection_bias.astype(jnp.float32)]
    )
    keyval_local = (
        mixed_dot(normed, w_keyval) + keyval_bias + mixed_dot(keyval_inner, keyvalue_output_side)
    ).astype(jnp.bfloat16)
    normed_all, keyval = side_by_side((normed, keyval_local), "mp", 0, 1)
    query_inner = mixed_dot(normed_all, query_input_side).astype(jnp.bfloat16)
    query = (
        mixed_dot(normed_all, w_query)
        + query_projection_bias.astype(jnp.float32)
        + mixed_dot(query_inner, query_output_side)
    ).astype(jnp.bfloat16)
    keys = keyval[:, :HEAD_WIDTH]
    values = keyval[:, HEAD_WIDTH:]
    count = length // QROWS
    key_block = jnp.arange(length, dtype=jnp.int32) // BLOCK
    starts = jnp.arange(count, dtype=jnp.int32) * QROWS
    query_blocks = query.reshape(count, QROWS, heads_here, HEAD_WIDTH)

    def masked_scores(rows_query, start):
        scores = (
            jnp.einsum("qhd,kd->qhk", rows_query, keys, preferred_element_type=jnp.float32) * scale
        )
        query_block = (start + jnp.arange(QROWS, dtype=jnp.int32)) // BLOCK
        allowed = key_block[None, None, :] <= query_block[:, None, None]
        return jnp.where(allowed, scores, -1e30)

    def forward_block(element_item):
        rows_query, start = element_item
        scores = masked_scores(rows_query, start)
        top = jnp.max(scores, axis=-1, keepdims=True)
        expo = jnp.exp(scores - top)
        total = jnp.sum(expo, axis=-1, keepdims=True)
        probs = (expo / total).astype(jnp.bfloat16)
        result = jnp.einsum("qhk,kd->qhd", probs, values, preferred_element_type=jnp.float32)
        return (result, (top + jnp.log(total))[..., 0])

    attended_blocks, log_totals = lax.map(forward_block, (query_blocks, starts))
    attended = attended_blocks.reshape(length, heads_here * HEAD_WIDTH).astype(jnp.bfloat16)
    output_inner = mixed_dot(attended, output_input_side).astype(jnp.bfloat16)
    output_part = mixed_dot(attended, w_output) + mixed_dot(output_inner, output_output_side)
    middle = input_rows + (
        lax.psum_scatter(
            output_part.astype(jnp.bfloat16), "mp", scatter_dimension=0, tiled=True
        ).astype(jnp.float32)
        + attention_output_bias.astype(jnp.float32)
    )
    w_up, w_down = rows_first((up_projection_weight, down_projection_weight), "dp", (0, 1))
    normed_two = layer_norm(middle, gain_two, shift_two).astype(jnp.bfloat16)
    normed_two_all = lax.all_gather(normed_two, "mp", axis=0, tiled=True)
    up_inner = mixed_dot(normed_two_all, up_input_side).astype(jnp.bfloat16)
    pre = (
        mixed_dot(normed_two_all, w_up)
        + up_projection_bias.astype(jnp.float32)
        + mixed_dot(up_inner, up_output_side)
    )
    act = gelu_tanh(pre).astype(jnp.bfloat16)
    down_inner = mixed_dot(act, down_input_side).astype(jnp.bfloat16)
    down_part = mixed_dot(act, w_down) + mixed_dot(down_inner, down_output_side)
    layer_output = (
        middle
        + (
            lax.psum_scatter(
                down_part.astype(jnp.bfloat16), "mp", scatter_dimension=0, tiled=True
            ).astype(jnp.float32)
            + down_projection_bias.astype(jnp.float32)
        )
    ).astype(jnp.bfloat16)
    w_query, w_keyval, w_output, w_up, w_down = (w_query, w_keyval, w_output, w_up, w_down)
    grad_out_all = lax.all_gather(cotangent, "mp", axis=0, tiled=True)
    grad_down_b = mixed_tdot(down_inner, grad_out_all)
    down_back = mixed_dot_t(grad_out_all, down_output_side).astype(jnp.bfloat16)
    grad_down_a = mixed_tdot(act, down_back)
    grad_act = mixed_dot_t(grad_out_all, w_down) + mixed_dot_t(down_back, down_input_side)
    _, gelu_back = jax.vjp(gelu_tanh, pre)
    grad_pre = gelu_back(grad_act)[0].astype(jnp.bfloat16)
    grad_up_b = mixed_tdot(up_inner, grad_pre)
    up_back = mixed_dot_t(grad_pre, up_output_side).astype(jnp.bfloat16)
    grad_up_a = mixed_tdot(normed_two_all, up_back)
    grad_normed_two_part = mixed_dot_t(grad_pre, w_up) + mixed_dot_t(up_back, up_input_side)
    grad_normed_two = lax.psum_scatter(
        grad_normed_two_part.astype(jnp.bfloat16), "mp", scatter_dimension=0, tiled=True
    ).astype(jnp.float32)
    _, norm_two_back = jax.vjp(lambda values_in: layer_norm(values_in, gain_two, shift_two), middle)
    grad_middle = cotangent.astype(jnp.float32) + norm_two_back(grad_normed_two)[0]
    grad_branch_all = lax.all_gather(grad_middle.astype(jnp.bfloat16), "mp", axis=0, tiled=True)
    grad_output_b = mixed_tdot(output_inner, grad_branch_all)
    output_back = mixed_dot_t(grad_branch_all, output_output_side).astype(jnp.bfloat16)
    grad_output_a = mixed_tdot(attended, output_back)
    grad_attended = (
        mixed_dot_t(grad_branch_all, w_output) + mixed_dot_t(output_back, output_input_side)
    ).astype(jnp.bfloat16)
    grad_blocks = grad_attended.reshape(count, QROWS, heads_here, HEAD_WIDTH)

    def backward_block(loop_carry, element_item):
        grad_keys, grad_values = loop_carry
        rows_query, rows_grad, rows_total, start = element_item
        scores = masked_scores(rows_query, start)
        probs = jnp.exp(scores - rows_total[..., None])
        grad_probs = jnp.einsum(
            "qhd,kd->qhk", rows_grad, values, preferred_element_type=jnp.float32
        )
        grad_scores = (
            probs * (grad_probs - jnp.sum(probs * grad_probs, axis=-1, keepdims=True))
        ).astype(jnp.bfloat16)
        grad_rows = (
            jnp.einsum("qhk,kd->qhd", grad_scores, keys, preferred_element_type=jnp.float32) * scale
        )
        grad_keys = (
            grad_keys
            + jnp.einsum("qhk,qhd->kd", grad_scores, rows_query, preferred_element_type=jnp.float32)
            * scale
        )
        grad_values = grad_values + jnp.einsum(
            "qhk,qhd->kd", probs.astype(jnp.bfloat16), rows_grad, preferred_element_type=jnp.float32
        )
        return ((grad_keys, grad_values), grad_rows.astype(jnp.bfloat16))

    empty = jnp.zeros((length, HEAD_WIDTH), jnp.float32)
    (grad_keys, grad_values), grad_query_blocks = lax.scan(
        backward_block, (empty, empty), (query_blocks, grad_blocks, log_totals, starts)
    )
    grad_query = grad_query_blocks.reshape(length, heads_here * HEAD_WIDTH)
    grad_query_b = mixed_tdot(query_inner, grad_query)
    query_back = mixed_dot_t(grad_query, query_output_side).astype(jnp.bfloat16)
    grad_query_a = mixed_tdot(normed_all, query_back)
    grad_normed_part = mixed_dot_t(grad_query, w_query) + mixed_dot_t(query_back, query_input_side)
    grad_normed, grad_keyval = tuple(
        (
            part.astype(jnp.float32)
            for part in in_one_piece(
                (
                    grad_normed_part.astype(jnp.bfloat16),
                    jnp.concatenate([grad_keys, grad_values], axis=1).astype(jnp.bfloat16),
                ),
                "mp",
                0,
                1,
            )
        )
    )
    grad_keyval = grad_keyval.astype(jnp.bfloat16)
    grad_keyval_b = mixed_tdot(keyval_inner, grad_keyval)
    keyval_back = mixed_dot_t(grad_keyval, keyvalue_output_side).astype(jnp.bfloat16)
    grad_keyval_a = mixed_tdot(normed, keyval_back)
    grad_normed = (
        grad_normed
        + mixed_dot_t(grad_keyval, w_keyval)
        + mixed_dot_t(keyval_back, keyvalue_input_side)
    )
    _, norm_one_back = jax.vjp(
        lambda values_in: layer_norm(values_in, gain_one, shift_one), input_rows
    )
    grad_tokens = (grad_middle + norm_one_back(grad_normed)[0]).astype(jnp.bfloat16)
    model_slice = MODEL_WIDTH // parts
    hidden_slice = FEED_HIDDEN // parts
    pieces = (
        spread(grad_query_a, 0, 0, (MODEL_WIDTH, ADAPTER_RANK)),
        spread(grad_query_b, 1, position * model_slice, (ADAPTER_RANK, MODEL_WIDTH)),
        spread(grad_keyval_a, 0, 0, (MODEL_WIDTH, ADAPTER_RANK)),
        spread(grad_keyval_b, 0, 0, (ADAPTER_RANK, 2 * HEAD_WIDTH)),
        spread(grad_output_a, 0, position * model_slice, (MODEL_WIDTH, ADAPTER_RANK)),
        spread(grad_output_b, 0, 0, (ADAPTER_RANK, MODEL_WIDTH)),
        spread(grad_up_a, 0, 0, (MODEL_WIDTH, ADAPTER_RANK)),
        spread(grad_up_b, 1, position * hidden_slice, (ADAPTER_RANK, FEED_HIDDEN)),
        spread(grad_down_a, 0, position * hidden_slice, (FEED_HIDDEN, ADAPTER_RANK)),
        spread(grad_down_b, 0, 0, (ADAPTER_RANK, MODEL_WIDTH)),
    )
    spreads = [stacked(whole, adapter_position) for whole in pieces]
    summed = lax.psum(
        (
            spreads[0],
            spreads[1],
            spreads[2],
            spreads[3],
            spreads[4],
            spreads[5],
            spreads[6],
            spreads[7],
            spreads[8],
            spreads[9],
        ),
        ("dp", "mp"),
    )
    return (
        layer_output,
        grad_tokens,
        summed[0],
        summed[1],
        summed[2],
        summed[3],
        summed[4],
        summed[5],
        summed[6],
        summed[7],
        summed[8],
        summed[9],
    )


def solution(mesh):
    in_specs = (
        P(("dp", "mp"), None),
        P(("dp", "mp"), None),
        P(),
        P(),
        P("dp", "mp"),
        P("mp"),
        P("dp", None),
        P(),
        P("mp", "dp"),
        P(),
        P(),
        P(),
        P("dp", "mp"),
        P("mp"),
        P("mp", "dp"),
        P(),
        P("dp", None),
        P(),
        P(None, None, "mp"),
        P(),
        P(),
        P(None, "mp", None),
        P(),
        P(),
        P(None, None, "mp"),
        P(None, "mp", None),
        P(),
    )
    out_specs = (
        P(("dp", "mp"), None),
        P(("dp", "mp"), None),
        P(),
        P(),
        P(),
        P(),
        P(),
        P(),
        P(),
        P(),
        P(),
        P(),
    )
    return jax.shard_map(shards, mesh=mesh, in_specs=in_specs, out_specs=out_specs, check_vma=False)
```

profile of v0, /device:TPU:1, one launch (start us, length us, event | category | flops | bytes accessed | tf_op | source)
XLA Modules:
  0.0 1120.0 jit_solution(17072962652177014390)
XLA Ops:
  20.7 34.9 %all-gather.7.cloned.1.call-done = bf16[2048,768]{0,1:T(8,128)(2,1)} async-done(((bf16[128,768]{0,1:T(8,128)(2,1)}), bf16[2048,768]{0,1:T(8,128)(2,1)}) %all-gather.7.cloned.1.call-update) | async-done | bytes 3145744 | tf_op jit(solution)/shard_map/all_gather | solution.py:22
  58.3 75.7 %all-gather.9.cloned.1.call-done = bf16[1024,2304]{1,0:T(8,128)(2,1)} async-done(((bf16[128,2304]{1,0:T(8,128)(2,1)}), bf16[1024,2304]{1,0:T(8,128)(2,1)}) %all-gather.9.cloned.1.call-update) | async-done | bytes 4718608 | tf_op jit(solution)/shard_map/all_gather | solution.py:38
  134.0 3.5 fusion.92
  142.5 11.3 %while.32 = (s32[]{:T(128)}, bf16[2,512,2,128]{3,1,2,0:T(8,128)(2,1)S(1)}, f32[2,512,2]{1,2,0:T(2,128)S(1)}, s32[2]{0:T(128)S(1)}, bf16[2,512,2,128]{3,1,2,0:T(8...) while((s32[]{:T(128)}, ...), condition=%wide.region_5.6_spmd.clone, body=%wide.region_2.5_spmd.clone.sunk | while | flops 549993472 | bytes 16035953 | solution.py:187
  157.9 4.1 add_convert_fusion.3
  164.1 80.0 %reduce-scatter.5.cloned.1.call-done = bf16[128,2048]{1,0:T(8,128)(2,1)} async-done(((bf16[1024,2048]{1,0:T(8,128)(2,1)}), bf16[128,2048]{1,0:T(8,128)(2,1)}) %reduce-scatter.5.cloned.1.call-update) | async-done | bytes 524304 | tf_op jit(solution)/shard_map/reduce_scatter | solution.py:192
  249.6 67.8 %all-gather.15.cloned.1.call-done = bf16[1024,2048]{1,0:T(8,128)(2,1)} async-done(((bf16[128,2048]{1,0:T(8,128)(2,1)}), bf16[1024,2048]{1,0:T(8,128)(2,1)}) %all-gather.15.cloned.1.call-update) | async-done | bytes 4194320 | tf_op jit(solution)/shard_map/all_gather | solution.py:219
  320.7 3.5 fusion.147
  324.3 54.4 %all-gather.13.cloned.1.call-done = bf16[2048,2048]{0,1:T(8,128)(2,1)} async-done(((bf16[128,2048]{0,1:T(8,128)(2,1)}), bf16[2048,2048]{0,1:T(8,128)(2,1)}) %all-gather.13.cloned.1.call-update) | async-done | bytes 8388624 | tf_op jit(solution)/shard_map/all_gather | solution.py:22
  378.7 73.6 %all-gather.11.cloned.1.call-done = bf16[1024,2048]{1,0:T(8,128)(2,1)} async-done(((bf16[128,2048]{1,0:T(8,128)(2,1)}), bf16[1024,2048]{1,0:T(8,128)(2,1)}) %all-gather.11.cloned.1.call-update) | async-done | bytes 4194320 | tf_op jit(solution)/shard_map/all_gather | solution.py:199
  452.2 7.9 fusion.70
  461.4 4.4 fusion.63
  467.0 7.9 fusion.60
  476.4 4.5 fusion.68
  486.6 6.9 fusion.66
  493.5 4.1 add_convert_fusion.2
  498.3 67.9 %reduce-scatter.9.cloned.1.call-done = bf16[128,2048]{1,0:T(8,128)(2,1)} async-done(((bf16[1024,2048]{1,0:T(8,128)(2,1)}), bf16[128,2048]{1,0:T(8,128)(2,1)}) %reduce-scatter.9.cloned.1.call-update) | async-done | bytes 524304 | tf_op jit(solution)/shard_map/reduce_scatter | solution.py:230
  567.7 86.6 %reduce-scatter.7.cloned.1.call-done = bf16[128,2048]{1,0:T(8,128)(2,1)} async-done(((bf16[1024,2048]{1,0:T(8,128)(2,1)}), bf16[128,2048]{1,0:T(8,128)(2,1)}) %reduce-scatter.7.cloned.1.call-update) | async-done | bytes 524304 | tf_op jit(solution)/shard_map/reduce_scatter | solution.py:212
  658.9 71.2 %all-gather.17.cloned.1.call-done = bf16[1024,2048]{1,0:T(8,128)(2,1)} async-done(((bf16[128,2048]{1,0:T(8,128)(2,1)}), bf16[1024,2048]{1,0:T(8,128)(2,1)}) %all-gather.17.cloned.1.call-update) | async-done | bytes 4194320 | tf_op jit(solution)/shard_map/all_gather | solution.py:235
  730.1 3.9 fusion.100
  737.2 26.8 %while.33 = (s32[]{:T(128)}, f32[1024,128]{1,0:T(8,128)}, f32[1024,128]{1,0:T(8,128)}, bf16[2,512,2,128]{3,2,1,0:T(2,128)(2,1)}, s32[2]{0:T(128)S(1)}, /*index=5...) while((s32[]{:T(128)}, f32[1024,128]{1,0:T(8,128)}, ...), condition=%wide.region_15.16_spmd.clone, body=%wide.region_13.15_spmd.clone.sunk | while | flops 1359363072 | bytes 84977200 | solution.py:269
  760.6 3.5 fusion.266
  792.4 67.8 %reduce-scatter.11.cloned.1.call-done = bf16[128,2304]{1,0:T(8,128)(2,1)} async-done(((bf16[1024,2304]{1,0:T(8,128)(2,1)}), bf16[128,2304]{1,0:T(8,128)(2,1)}) %reduce-scatter.11.cloned.1.call-update) | async-done | bytes 589840 | tf_op jit(solution)/shard_map/reduce_scatter | solution.py:48
  870.3 226.6 %all-reduce.4.cloned.1.call-done = (f32[8,2048,16]{1,2,0:T(8,128)}, f32[8,16,2048]{2,1,0:T(8,128)}, f32[8,2048,16]{1,2,0:T(8,128)}, f32[8,16,256]{2,1,0:T(8,128)...) async-done(((f32[8,2048,16]{1,2,0:T(8,128)}, ...) | async-done | bytes 15859728 | tf_op jit(solution)/shard_map/psum | solution.py:319
  (319 shorter events, 142.7 us)
Async XLA Ops:
  7.2 453.0 %copy-start = (bf16[8,2048,16]{1,2,0:T(8,128)(2,1)S(1)}, bf16[8,2048,16]{1,2,0:T(8,128)(2,1)}, u32[]{:S(2)}) copy-start(bf16[8,2048,16]{1,2,0:T(8,128)(2,1)} %param.54) | copy-start | bytes 1572868
  7.2 51.1 %copy-start.64 = (bf16[256]{0:T(256)(128)(2,1)S(1)}, bf16[256]{0:T(256)(128)(2,1)}, u32[]{:S(2)}) copy-start(bf16[256]{0:T(256)(128)(2,1)} %param.36) | copy-start | bytes 1540
  7.2 48.4 %all-gather.7.cloned.1.call-start = ((), (), s32[]{:S(2)}) async-start(), calls=%async_computation.4 | async-start | bytes 3342336 | tf_op jit(solution)/shard_map/all_gather | solution.py:22
  10.8 123.3 %all-gather.9.cloned.1.call-start = ((), (), s32[]{:S(2)}) async-start(), calls=%async_computation.5 | async-start | bytes 5308416 | tf_op jit(solution)/shard_map/all_gather | solution.py:38
  18.0 119.5 %copy-start.20 = (bf16[128,2048]{1,0:T(8,128)(2,1)}, bf16[128,2048]{1,0:T(8,128)(2,1)S(1)}, u32[]{:S(2)}) copy-start(bf16[128,2048]{1,0:T(8,128)(2,1)S(1)} %fusion.98) | copy-start | bytes 1572868
  58.2 185.9 %reduce-scatter.5.cloned.1.call-start = ((), (), s32[]{:S(2)}) async-start(), calls=%async_computation.6 | async-start | bytes 4718592 | tf_op jit(solution)/shard_map/reduce_scatter | solution.py:192
  162.0 82.1 %copy-start.4 = (bf16[128,2048]{1,0:T(8,128)(2,1)S(1)}, bf16[128,2048]{1,0:T(8,128)(2,1)}, u32[]{:S(2)}) copy-start(bf16[128,2048]{1,0:T(8,128)(2,1)} %param.31) | copy-start | bytes 1572868
  162.1 87.5 %copy-start.60 = (bf16[1024]{0:T(1024)(128)(2,1)S(1)}, bf16[1024]{0:T(1024)(128)(2,1)}, u32[]{:S(2)}) copy-start(bf16[1024]{0:T(1024)(128)(2,1)} %param.44) | copy-start | bytes 6148
  162.1 155.2 %all-gather.15.cloned.1.call-start = ((), (), s32[]{:S(2)}) async-start(), calls=%async_computation.10 | async-start | bytes 4718592 | tf_op jit(solution)/shard_map/all_gather | solution.py:219
  162.7 216.0 %all-gather.13.cloned.1.call-start = ((), (), s32[]{:S(2)}) async-start(), calls=%async_computation.8 | async-start | bytes 8912896 | tf_op jit(solution)/shard_map/all_gather | solution.py:22
  164.0 288.2 %all-gather.11.cloned.1.call-start = ((), (), s32[]{:S(2)}) async-start(), calls=%async_computation.7 | async-start | bytes 4718592 | tf_op jit(solution)/shard_map/all_gather | solution.py:199
  249.0 317.2 %reduce-scatter.9.cloned.1.call-start = ((), (), s32[]{:S(2)}) async-start(), calls=%async_computation.11 | async-start | bytes 4718592 | tf_op jit(solution)/shard_map/reduce_scatter | solution.py:230
  452.2 8.0 copy-start.7
  484.3 170.0 %reduce-scatter.7.cloned.1.call-start = ((), (), s32[]{:S(2)}) async-start(), calls=%async_computation.9 | async-start | bytes 4718592 | tf_op jit(solution)/shard_map/reduce_scatter | solution.py:212
  497.6 68.6 %copy-start.15 = (bf16[128,2048]{1,0:T(8,128)(2,1)S(1)}, bf16[128,2048]{1,0:T(8,128)(2,1)}, u32[]{:S(2)}) copy-start(bf16[128,2048]{1,0:T(8,128)(2,1)} %reduce-scatter.5.cloned.1.call-done) | copy-start | bytes 1572868
  497.6 160.2 %copy-start.28 = (bf16[128,2048]{1,0:T(8,128)(2,1)S(1)}, bf16[128,2048]{1,0:T(8,128)(2,1)}, u32[]{:S(2)}) copy-start(bf16[128,2048]{1,0:T(8,128)(2,1)} %param.32) | copy-start | bytes 1572868
  497.7 232.4 %all-gather.17.cloned.1.call-start = ((), (), s32[]{:S(2)}) async-start(), calls=%async_computation.12 | async-start | bytes 4718592 | tf_op jit(solution)/shard_map/all_gather | solution.py:235
  658.8 201.5 %reduce-scatter.11.cloned.1.call-start = ((), (), s32[]{:S(2)}) async-start(), calls=%async_computation.13 | async-start | bytes 5308416 | tf_op jit(solution)/shard_map/reduce_scatter | solution.py:48
  774.8 322.1 %all-reduce.4.cloned.1.call-start = ((), (), s32[]{:S(2)}) async-start(), calls=%async_computation.14 | async-start | bytes 31719424 | tf_op jit(solution)/shard_map/psum | solution.py:319
  780.3 6.5 copy-start.27
  787.7 73.6 %copy-start.21 = (bf16[128,2048]{1,0:T(8,128)(2,1)S(1)}, bf16[128,2048]{1,0:T(8,128)(2,1)}, u32[]{:S(2)}) copy-start(bf16[128,2048]{1,0:T(8,128)(2,1)} %copy-done.20) | copy-start | bytes 1572868
  787.7 73.8 %copy-start.51 = (bf16[128,16]{0,1:T(8,128)(2,1)S(1)}, bf16[128,16]{0,1:T(8,128)(2,1)}, u32[]{:S(2)}) copy-start(bf16[128,16]{0,1:T(8,128)(2,1)} %copy-done.50) | copy-start | bytes 12292
  1096.9 7.4 copy-start.36
  1106.3 6.7 copy-start.1
  (66 other events, 223.5 us)
Sparse Core Ops, SparseCore 0:
  10.9 44.7 all-gather.6
  58.5 75.4 all-gather.8
  162.2 81.8 reduce-scatter.4
  246.3 70.9 all-gather.14
  319.4 59.2 all-gather.12
  381.4 70.7 all-gather.10
  484.4 81.7 reduce-scatter.8
  570.7 83.5 reduce-scatter.6
  658.9 71.0 all-gather.16
  774.9 85.3 reduce-scatter.10
  869.0 227.8 all-reduce.3
where the time goes:
time: 1130 us; the launch traced here: 1120 us
  waiting for transfers between devices  907 us (80%)
  matrix products  120 us (11%)
  other arithmetic  44.6 us (4%)
  local copies, waits for them, and re-layouts  30.6 us (3%)
  between operations  15.7 us (1%)
    psum x1, waiting for transfers between devices, shards(): lax.psum((spreads[0], spreads[1], spreads[2], spreads[3], spreads[4], spr...  227 us
    all_gather x2, waiting for transfers between devices, rows_first(): filled = lax.all_gather(both, axis, axis=0, tiled=True)  89.3 us
    reduce_scatter x1, waiting for transfers between devices, shards(): lax.psum_scatter(down_part.astype(jnp.bfloat16), 'mp', scatter_dimension=...  86.6 us
    reduce_scatter x1, waiting for transfers between devices, shards(): lax.psum_scatter(output_part.astype(jnp.bfloat16), 'mp', scatter_dimensio...  80 us
    all_gather x1, waiting for transfers between devices, side_by_side(): lax.all_gather(both, axis, axis=dim, tiled=True)  75.7 us
    all_gather x1, waiting for transfers between devices, shards(): normed_two_all = lax.all_gather(normed_two, 'mp', axis=0, tiled=True)  73.6 us
    all_gather x1, waiting for transfers between devices, shards(): lax.all_gather(grad_middle.astype(jnp.bfloat16), 'mp', axis=0, tiled=True)  71.2 us
    reduce_scatter x1, waiting for transfers between devices, shards(): lax.psum_scatter(grad_normed_two_part.astype(jnp.bfloat16), 'mp', scatter...  67.9 us
  transfers between devices with their start and end apart: 11, of which 11 were waited for; matrix products, arithmetic and copies ran while one was open for 5% of the time, Pallas kernels for 0%

commit v1 on v0

v1 whole, which is shorter than its diff:
```python
import math

import jax
import jax.numpy as jnp
from jax import lax
from jax.sharding import Mesh
from jax.sharding import PartitionSpec as P

MODEL_WIDTH = 2048
H = 16
HEAD_WIDTH = 128
FEED_HIDDEN = 8192
ADAPTER_RANK = 16
ADAPTER_COUNT = 8
BLOCK = 256

AXES = ("y", "zl", "core", "zh", "x")
SIZES = (4, 2, 2, 2, 4)
DP = ("y", "zl", "core")
MP = ("zh", "x")
PLACES = (0, 3, 1, 2)
Z_RING = (0, 2, 1, 3)
ROWS = 128
RIDE = 128

f32 = jnp.float32
bf16 = jnp.bfloat16


def ring_x(a, step):
    return lax.ppermute(a, "x", [(i, (i + step) % 4) for i in range(4)])


def ring_y(a, step):
    return lax.ppermute(a, "y", [(i, (i + step) % 4) for i in range(4)])


def ring_z(a, step):
    return lax.ppermute(a, ("zl", "zh"), [(Z_RING[i], Z_RING[(i + step) % 4]) for i in range(4)])


def other_core(a):
    return lax.ppermute(a, "core", [(0, 1), (1, 0)])


def other_half(a):
    return lax.ppermute(a, "zh", [(0, 1), (1, 0)])


def turn(a):
    return lax.ppermute(a, ("core", "zh"), [(0, 0), (1, 2), (2, 1), (3, 3)])


def gather_row(a):
    half = a.shape[0] // 2
    left, right = ring_x(a, 1), ring_x(a, -1)
    near = other_core(a)
    far = jnp.concatenate([ring_x(left[:half], 1), ring_x(right[half:], -1)], axis=0)
    sides = other_core(jnp.concatenate([left, right], axis=0))
    far_other = other_core(far)
    n = a.shape[0]
    return jnp.stack(
        [
            jnp.stack([a, near]),
            jnp.stack([left, sides[:n]]),
            jnp.stack([right, sides[n:]]),
            jnp.stack([far, far_other]),
        ]
    )


def scatter_row(parts):
    parts = parts.astype(bf16)
    mine, theirs = parts[:, 0], parts[:, 1]
    half = parts.shape[2] // 2
    far = (mine[3].astype(f32) + other_core(theirs[3]).astype(f32)).astype(bf16)
    up, down = ring_x(far[:half], 1), ring_x(far[half:], -1)
    rest = mine[:3].astype(f32) + other_core(theirs[:3]).astype(f32)
    to_right = jnp.concatenate([rest[2, :half] + up.astype(f32), rest[2, half:]]).astype(bf16)
    to_left = jnp.concatenate([rest[1, :half], rest[1, half:] + down.astype(f32)]).astype(bf16)
    return rest[0] + ring_x(to_right, 1).astype(f32) + ring_x(to_left, -1).astype(f32)


def rolled(blocks, me):
    both = jnp.concatenate([blocks, blocks], axis=0)
    return lax.dynamic_slice_in_dim(both, lax.rem(4 - me, 4), 4, 0)


def gather_ring(a, ring, me):
    half = a.shape[-2] // 2
    left, right = ring(a, 1), ring(a, -1)
    far = jnp.concatenate(
        [ring(left[..., :half, :], 1), ring(right[..., half:, :], -1)], axis=-2
    )
    return rolled(jnp.stack([a, right, far, left]), me)


def gather_plane(a, y, z):
    half = a.shape[0] // 2
    first = gather_ring(gather_ring(a[:half], ring_y, y), ring_z, z)
    second = gather_ring(gather_ring(a[half:], ring_z, z), ring_y, y)
    return jnp.concatenate([jnp.moveaxis(first, 0, 1), second], axis=2)


def layer_norm(values, gain, shift):
    mean_value = jnp.mean(values, axis=-1, keepdims=True)
    centred = values - mean_value
    variance = jnp.mean(centred * centred, axis=-1, keepdims=True)
    return centred * lax.rsqrt(variance + 1e-05) * gain + shift


def gelu_tanh(values):
    inner_product = math.sqrt(2.0 / math.pi) * (values + 0.044715 * values * values * values)
    return 0.5 * values * (1.0 + jnp.tanh(inner_product))


def pick(adapter_stack, position):
    return lax.dynamic_index_in_dim(adapter_stack, position, 0, keepdims=False)


def dot(left, right):
    return jnp.dot(left, right, preferred_element_type=f32)


def dot_t(left, right):
    return lax.dot_general(left, right, (((1,), (1,)), ((), ())), preferred_element_type=f32)


def tdot(left, right):
    return lax.dot_general(left, right, (((0,), (0,)), ((), ())), preferred_element_type=f32)


def shards(
    tokens,
    cotangent,
    attention_norm_scale,
    attention_norm_bias,
    query_projection,
    query_projection_bias,
    keyvalue_projection,
    value_projection_bias,
    attention_output_weight,
    attention_output_bias,
    feedforward_norm_scale,
    feedforward_norm_bias,
    up_projection_weight,
    up_projection_bias,
    down_projection_weight,
    down_projection_bias,
    sequence_adapter,
    query_adapter_input,
    query_adapter_output,
    keyvalue_adapter_input,
    keyvalue_adapter_output,
    output_adapter_input,
    output_adapter_output,
    up_adapter_input,
    up_adapter_output,
    down_adapter_input,
    down_adapter_output,
):
    y, core, zl, zh, x = (lax.axis_index(n) for n in ("y", "core", "zl", "zh", "x"))
    z = zh * 2 + zl
    scale = HEAD_WIDTH ** (-0.5)
    local = (ROWS, MODEL_WIDTH)
    gain_one, shift_one = attention_norm_scale.astype(f32), attention_norm_bias.astype(f32)
    gain_two, shift_two = feedforward_norm_scale.astype(f32), feedforward_norm_bias.astype(f32)

    mine = sequence_adapter[0, 0]
    theirs = other_core(sequence_adapter)[0, 0]
    picks = (mine, theirs)
    low = jnp.where(core == 0, mine, theirs)
    high = jnp.where(core == 0, theirs, mine)

    def ordered(stack):
        return jnp.concatenate([pick(stack, low), pick(stack, high)], axis=0)

    small = jnp.concatenate(
        [
            ordered(query_adapter_output),
            ordered(jnp.swapaxes(output_adapter_input, 1, 2)),
            ordered(up_adapter_output),
            ordered(jnp.swapaxes(down_adapter_input, 1, 2)),
        ],
        axis=1,
    )
    biases = jnp.concatenate(
        [
            query_projection_bias,
            jnp.zeros((256,), bf16),
            up_projection_bias,
            jnp.zeros((1024,), bf16),
        ]
    )
    small = turn(
        jnp.concatenate([small, biases[None], jnp.zeros((15, 2560), bf16)], axis=0)
    )
    by_core = small[:32].reshape(2, ADAPTER_RANK, 2560)
    by_core = jnp.where(core == 0, by_core, by_core[::-1])
    q_out, o_in, u_out, d_in = (
        by_core[:, :, :256],
        by_core[:, :, 256:512],
        by_core[:, :, 512:1536],
        by_core[:, :, 1536:],
    )
    q_bias, u_bias = small[32, :256].astype(f32), small[32, 512:1536].astype(f32)

    def both(stack):
        return jnp.stack([pick(stack, p) for p in picks])

    attention_shard = turn(
        jnp.concatenate(
            [query_projection, keyvalue_projection, attention_output_weight.T], axis=1
        )
    )
    plane = gather_plane(attention_shard, y, z)
    plane = plane.reshape(4, 2, 2, ROWS, 768)
    plane = jnp.swapaxes(plane, 1, 2).reshape(MODEL_WIDTH, 768)
    w_query, w_keyval, w_output = plane[:, :256], plane[:, 256:512], plane[:, 512:]

    feed_shard = jnp.concatenate([up_projection_weight, down_projection_weight.T], axis=1)
    feed = lax.all_gather(feed_shard, DP + ("zh",), axis=0, tiled=True)
    feed = feed.reshape(16, 2, ROWS, 2048)
    feed = lax.dynamic_index_in_dim(feed, core, 1, keepdims=False).reshape(MODEL_WIDTH, 2048)
    w_up, w_down = feed[:, :1024], feed[:, 1024:]

    cot_all = lax.all_gather(cotangent, ("core", "x"), axis=0, tiled=True)
    cot_all = cot_all.reshape(2, 4, *local)
    cot_all = jnp.where(core == 0, cot_all, cot_all[::-1])
    cot_all = rolled(jnp.swapaxes(cot_all, 0, 1), lax.rem(4 - x, 4))
    cot_all = jnp.stack([cot_all[p] for p in PLACES])

    input_rows = tokens.astype(f32)
    normed = layer_norm(input_rows, gain_one, shift_one).astype(bf16)
    normed_all = gather_row(normed)

    kv_in, kv_out = pick(keyvalue_adapter_input, mine), pick(keyvalue_adapter_output, mine)
    keyval_inner = dot(normed, kv_in).astype(bf16)
    keyval_bias = jnp.concatenate(
        [jnp.zeros((HEAD_WIDTH,), f32), value_projection_bias.astype(f32)]
    )
    keyval = (dot(normed, w_keyval) + keyval_bias + dot(keyval_inner, kv_out)).astype(bf16)
    keyval_all = gather_row(jnp.concatenate([keyval, other_half(keyval)], axis=1))
    keyval_all = keyval_all.reshape(4, 2, ROWS, 2, 256).transpose(1, 3, 0, 2, 4)
    keyval_all = keyval_all.reshape(2, 1024, 256)
    keys, values = keyval_all[..., :HEAD_WIDTH], keyval_all[..., HEAD_WIDTH:]

    def per_sequence(a):
        return jnp.swapaxes(a, 0, 1).reshape(2, 4 * ROWS, a.shape[-1])

    def per_place(a):
        return jnp.swapaxes(a.reshape(2, 4, ROWS, a.shape[-1]), 0, 1)

    def low_in(a, sides):
        return jnp.einsum("stw,swr->str", a, sides, preferred_element_type=f32)

    def low_in_t(a, sides):
        return jnp.einsum("stw,srw->str", a, sides, preferred_element_type=f32)

    normed_seq = per_sequence(normed_all)
    query_inner = low_in(normed_seq, both(query_adapter_input)).astype(bf16)
    query = (
        jnp.einsum("stw,wn->stn", normed_seq, w_query, preferred_element_type=f32)
        + q_bias
        + jnp.einsum("str,srn->stn", query_inner, q_out, preferred_element_type=f32)
    ).astype(bf16)

    place_x = jnp.stack([lax.rem(x + p, 4) for p in PLACES])
    own_block = jnp.repeat(place_x // 2, ROWS)
    allowed = jnp.concatenate(
        [
            own_block[None, :] <= own_block[:, None],
            jnp.broadcast_to(zh == 1, (4 * ROWS, 4 * ROWS)),
        ],
        axis=1,
    )
    heads = query.reshape(2, 4 * ROWS, 2, HEAD_WIDTH)

    def scores_of():
        raw = jnp.einsum("sqhd,skd->shqk", heads, keys, preferred_element_type=f32) * scale
        return jnp.where(allowed, raw, -1e30)

    scores = scores_of()
    top = jnp.max(scores, axis=-1, keepdims=True)
    expo = jnp.exp(scores - top)
    total = jnp.sum(expo, axis=-1, keepdims=True)
    probs_low = (expo / total).astype(bf16)
    log_total = top + jnp.log(total)
    attended = jnp.einsum("shqk,skd->sqhd", probs_low, values, preferred_element_type=f32)
    attended = attended.reshape(2, 4 * ROWS, 256).astype(bf16)

    def ride(main, *extra):
        width = sum(e.shape[-1] for e in extra)
        pad = jnp.zeros((*main.shape[:-1], -width % RIDE), f32)
        return per_place(jnp.concatenate([main, *extra, pad], axis=-1))

    out_part = ride(
        jnp.einsum("stw,nw->stn", attended, w_output, preferred_element_type=f32),
        low_in_t(attended, o_in),
    )
    out_sum = scatter_row(out_part)
    output_inner = out_sum[:, 2048:2064].astype(bf16)
    middle = (
        input_rows
        + out_sum[:, :2048]
        + attention_output_bias.astype(f32)
        + dot(output_inner, pick(output_adapter_output, mine))
    )
    normed_two = layer_norm(middle, gain_two, shift_two).astype(bf16)
    normed_two_seq = per_sequence(gather_row(normed_two))
    up_inner = low_in(normed_two_seq, both(up_adapter_input)).astype(bf16)
    pre = (
        jnp.einsum("stw,wn->stn", normed_two_seq, w_up, preferred_element_type=f32)
        + u_bias
        + jnp.einsum("str,srn->stn", up_inner, u_out, preferred_element_type=f32)
    )
    act = gelu_tanh(pre).astype(bf16)
    down_sum = scatter_row(
        ride(
            jnp.einsum("stw,nw->stn", act, w_down, preferred_element_type=f32),
            low_in_t(act, d_in),
        )
    )
    down_inner = down_sum[:, 2048:2064].astype(bf16)
    layer_output = (
        middle
        + down_sum[:, :2048]
        + down_projection_bias.astype(f32)
        + dot(down_inner, pick(down_adapter_output, mine))
    ).astype(bf16)

    cot_seq = per_sequence(cot_all)
    grad_down_b = tdot(down_inner, cotangent)
    down_back = low_in_t(cot_seq, both(down_adapter_output)).astype(bf16)
    grad_down_a = jnp.einsum("stw,str->srw", act, down_back, preferred_element_type=f32)
    grad_act = jnp.einsum(
        "stn,nw->stw", cot_seq, w_down, preferred_element_type=f32
    ) + jnp.einsum("str,srw->stw", down_back, d_in, preferred_element_type=f32)
    _, gelu_back = jax.vjp(gelu_tanh, pre)
    grad_pre = gelu_back(grad_act)[0].astype(bf16)
    grad_up_b = jnp.einsum("str,stw->srw", up_inner, grad_pre, preferred_element_type=f32)
    up_sum = scatter_row(
        ride(
            jnp.einsum("stw,nw->stn", grad_pre, w_up, preferred_element_type=f32),
            low_in_t(grad_pre, u_out),
        )
    )
    up_back = up_sum[:, 2048:2064].astype(bf16)
    grad_up_a = tdot(up_back, normed_two)
    grad_normed_two = up_sum[:, :2048] + dot_t(up_back, pick(up_adapter_input, mine))
    _, norm_two_back = jax.vjp(lambda v: layer_norm(v, gain_two, shift_two), middle)
    grad_middle = cotangent.astype(f32) + norm_two_back(grad_normed_two)[0]
    grad_branch = grad_middle.astype(bf16)

    branch_seq = per_sequence(gather_row(grad_branch))
    grad_output_b = tdot(output_inner, grad_branch)
    output_back = low_in_t(branch_seq, both(output_adapter_output)).astype(bf16)
    grad_output_a = jnp.einsum("stw,str->srw", attended, output_back, preferred_element_type=f32)
    grad_attended = (
        jnp.einsum("stn,nw->stw", branch_seq, w_output, preferred_element_type=f32)
        + jnp.einsum("str,srw->stw", output_back, o_in, preferred_element_type=f32)
    ).astype(bf16)
    grad_heads = grad_attended.reshape(2, 4 * ROWS, 2, HEAD_WIDTH)
    probs = jnp.exp(scores_of() - log_total)
    grad_probs = jnp.einsum("sqhd,skd->shqk", grad_heads, values, preferred_element_type=f32)
    grad_scores = (
        probs * (grad_probs - jnp.sum(probs * grad_probs, axis=-1, keepdims=True))
    ).astype(bf16)
    grad_query = (
        jnp.einsum("shqk,skd->sqhd", grad_scores, keys, preferred_element_type=f32) * scale
    )
    grad_query = grad_query.reshape(2, 4 * ROWS, 256).astype(bf16)
    grad_keys = jnp.einsum("shqk,sqhd->skd", grad_scores, heads, preferred_element_type=f32) * scale
    grad_values = jnp.einsum(
        "shqk,sqhd->skd", probs.astype(bf16), grad_heads, preferred_element_type=f32
    )
    grad_query_b = jnp.einsum("str,stw->srw", query_inner, grad_query, preferred_element_type=f32)
    grad_kv = jnp.concatenate([grad_keys, grad_values], axis=-1).reshape(2, 2, 4 * ROWS, 256)
    query_sum = scatter_row(
        ride(
            jnp.einsum("stw,nw->stn", grad_query, w_query, preferred_element_type=f32),
            grad_kv[:, 0],
            grad_kv[:, 1],
            low_in_t(grad_query, q_out),
        )
    )
    grad_keyval = (
        query_sum[:, 2048:2304] + other_half(query_sum[:, 2304:2560].astype(bf16)).astype(f32)
    ).astype(bf16)
    query_back = query_sum[:, 2560:2576].astype(bf16)
    grad_query_a = tdot(query_back, normed)
    grad_keyval_b = tdot(keyval_inner, grad_keyval)
    keyval_back = dot_t(grad_keyval, kv_out).astype(bf16)
    grad_keyval_a = tdot(keyval_back, normed)
    grad_normed = (
        query_sum[:, :2048]
        + dot_t(query_back, pick(query_adapter_input, mine))
        + dot_t(grad_keyval, w_keyval)
        + dot_t(keyval_back, kv_in)
    )
    _, norm_one_back = jax.vjp(lambda v: layer_norm(v, gain_one, shift_one), input_rows)
    grad_tokens = (grad_middle + norm_one_back(grad_normed)[0]).astype(bf16)

    ids = jnp.arange(ADAPTER_COUNT, dtype=jnp.int32)
    hot_mine = (ids == mine).astype(f32)[:, None, None]
    hot_theirs = (ids == theirs).astype(f32)[:, None, None]

    def whole(piece):
        return (hot_mine * piece[None]).astype(bf16)

    def placed(pair, width):
        stacked = (hot_mine * pair[0][None] + hot_theirs * pair[1][None]).astype(bf16)
        here = (core * 4 + x) * pair.shape[-1]
        return lax.dynamic_update_slice_in_dim(
            jnp.zeros((ADAPTER_COUNT, ADAPTER_RANK, width), bf16), stacked, here, 2
        )

    feed_grads = jnp.concatenate(
        [
            whole(grad_up_a),
            placed(grad_up_b, FEED_HIDDEN),
            placed(grad_down_a, FEED_HIDDEN),
            whole(grad_down_b),
        ],
        axis=2,
    )
    feed_grads = lax.psum(feed_grads, AXES).astype(f32)
    up_a, up_b, down_a, down_b = jnp.split(feed_grads, (2048, 10240, 18432), axis=2)
    rest_grads = jnp.concatenate(
        [
            whole(grad_query_a),
            placed(grad_query_b, MODEL_WIDTH),
            whole(grad_keyval_a),
            whole(grad_keyval_b),
            placed(grad_output_a, MODEL_WIDTH),
            whole(grad_output_b),
        ],
        axis=2,
    )
    rest_grads = lax.psum(rest_grads, AXES).astype(f32)
    query_a, query_b, keyval_a, keyval_b, output_a, output_b = jnp.split(
        rest_grads, (2048, 4096, 6144, 6400, 8448), axis=2
    )

    def side_in(a):
        return jnp.swapaxes(a, 1, 2)

    return (
        layer_output,
        grad_tokens,
        side_in(query_a),
        query_b,
        side_in(keyval_a),
        keyval_b,
        side_in(output_a),
        output_b,
        side_in(up_a),
        up_b,
        side_in(down_a),
        down_b,
    )


def solution(mesh):
    fine = Mesh(mesh.devices.reshape(SIZES), AXES)
    in_specs = (
        P(AXES, None),
        P(AXES, None),
        P(),
        P(),
        P(DP, MP),
        P(MP),
        P(DP, None),
        P(),
        P(MP, DP),
        P(),
        P(),
        P(),
        P(DP, MP),
        P(MP),
        P(MP, DP),
        P(),
        P(DP, None),
        P(),
        P(None, None, MP),
        P(),
        P(),
        P(None, MP, None),
        P(),
        P(),
        P(None, None, MP),
        P(None, MP, None),
        P(),
    )
    out_specs = (P(AXES, None), P(AXES, None)) + (P(),) * 10
    return jax.shard_map(shards, mesh=fine, in_specs=in_specs, out_specs=out_specs, check_vma=False)
```

time: 1130 us -> 771 us (0.68)
  waiting for transfers between devices: 907 us -> 262 us
  local copies, waits for them, and re-layouts: 30.6 us -> 220 us
  starting transfers between devices: 1.17 us -> 119 us
  matrix products: 120 us -> 75.7 us
  other arithmetic: 44.6 us -> 60.1 us
    all_gather x6 -> x2, waiting for transfers between devices: 378 us -> 0.01 us  [the longest x1 0.01 us: shards(): cot_all = lax.all_gather(cotangent, ('core', 'x'), axis=0, tiled=True)]
    reduce_scatter x4 -> x0, waiting for transfers between devices: 302 us -> none  [the longest x1 86.6 us: shards(): lax.psum_scatter(down_part.astype(jnp.bfloat16), 'mp', scatter_dimension=...]
    ppermute x0 -> x73, starting transfers between devices: none -> 119 us  [the longest x32 57.9 us: ring_x(): return lax.ppermute(a, 'x', [(i, (i + step) % 4) for i in range(4)])]
    ppermute x0 -> x73, waiting for transfers between devices: none -> 109 us  [the longest x32 76.2 us: ring_x(): return lax.ppermute(a, 'x', [(i, (i + step) % 4) for i in range(4)])]
    psum x1, waiting for transfers between devices: 227 us -> 153 us  [shards(): rest_grads = lax.psum(rest_grads, AXES).astype(f32)]
    dot_general x54 -> x46, matrix products: 120 us -> 75.7 us  [the longest x1 8.06 us: shards(): jnp.einsum('stn,nw->stw', cot_seq, w_down, preferred_element_type=f32)]
    reshape x2 -> x3, local copies, waits for them, and re-layouts: 0.25 us -> 42.4 us  [the longest x1 27.4 us: shards(): feed = feed.reshape(16, 2, ROWS, 2048)]
    concatenate x0 -> x15, local copies, waits for them, and re-layouts: none -> 36.7 us  [the longest x5 33 us: ride(): return per_place(jnp.concatenate([main, *extra, pad], axis=-1))]
  transfers between devices with their start and end apart: 11 -> 76, of which waited for: 11 -> 32; matrix products, arithmetic and copies ran while one was open for 5% -> 18% of each run, Pallas kernels for 0% -> 0%
where the time goes in v1:
time: 771 us; the launch traced here: 757 us
  waiting for transfers between devices  262 us (34%)
  local copies, waits for them, and re-layouts  220 us (29%)
  starting transfers between devices  119 us (15%)
  matrix products  75.7 us (10%)
  other arithmetic  60.1 us (8%)
  between operations  20.5 us (3%)
    psum x1, waiting for transfers between devices, shards(): rest_grads = lax.psum(rest_grads, AXES).astype(f32)  153 us
    ppermute x32, waiting for transfers between devices, ring_x(): return lax.ppermute(a, 'x', [(i, (i + step) % 4) for i in range(4)])  76.2 us
    unnamed x174, local copies, waits for them, and re-layouts  58.8 us
    ppermute x32, starting transfers between devices, ring_x(): return lax.ppermute(a, 'x', [(i, (i + step) % 4) for i in range(4)])  57.9 us
    concatenate x5, local copies, waits for them, and re-layouts, ride(): return per_place(jnp.concatenate([main, *extra, pad], axis=-1))  33 us
    ppermute x21, starting transfers between devices, other_core(): return lax.ppermute(a, 'core', [(0, 1), (1, 0)])  32.5 us
    reshape x1, local copies, waits for them, and re-layouts, shards(): feed = feed.reshape(16, 2, ROWS, 2048)  27.4 us
    dynamic_slice x1, local copies, waits for them, and re-layouts, shards(): lax.dynamic_index_in_dim(feed, core, 1, keepdims=False)  20 us
  transfers between devices with their start and end apart: 76, of which 32 were waited for; matrix products, arithmetic and copies ran while one was open for 18% of the time, Pallas kernels for 0%

profile of v1, /device:TPU:1, one launch (start us, length us, event | category | flops | bytes accessed | tf_op | source)
XLA Modules:
  0.0 757.5 jit_solution(3256454645133415630)
XLA Ops:
  20.3 5.4 collective-permute-start
  71.6 7.5 collective-permute-done.5
  105.1 8.8 %copy.150 = bf16[4,2,2,128,768]{3,1,2,0,4:T(2,128)(2,1)} copy(bf16[4,2,2,128,768]{4,3,0,2,1:T(8,128)(2,1)} %bitcast.567) | data formatting | bytes 6291456 | tf_op jit(solution)/shard_map/reshape | solution.py:217
  113.9 6.3 reshape.255
  178.2 7.8 %concatenate.192 = bf16[2,512,2176]{2,1,0:T(8,128)(2,1)} concatenate(bf16[2,512,2048]{2,1,0:T(8,128)(2,1)} %convolution_convert_fusion.1, bf16[2,512,16]{2,1,0:T(8,128)(2,1)S(1)} %copy.159, bf16[2,512,112]{2,1,0:T(8,128)(2,1)S(1)} %broadcast.164), dimensions={2} | concatenate | bytes 8912896 | tf_op jit(solution)/shard_map/concatenate | solution.py:295
  191.9 12.3 %collective-permute-start.38 = (bf16[64,2176]{1,0:T(8,128)(2,1)S(1)}, bf16[64,2176]{1,0:T(8,128)(2,1)S(1)}, u32[]{:S(2)}, u32[]{:S(2)}) collective-permute-start(bf16[64,2176]{1,0:T(8,128)(2,1)S(1)} %get-tuple-element.68), channel_id=1, source_target_pairs={{0,3},{1,0},{2,1},{3,2},{4,7},{5,4},{6,5},{7,6},{8,11},{9,8},{10,9... | collective-permute-start | bytes 835592 | tf_op jit(solution)/shard_map/ppermute | solution.py:31
  215.1 8.4 %collective-permute-done.39 = bf16[128,2176]{1,0:T(8,128)(2,1)S(1)} collective-permute-done((bf16[128,2176]{1,0:T(8,128)(2,1)S(1)}, bf16[128,2176]{1,0:T(8,128)(2,1)S(1)}, u32[]{:S(2)}, u32[]{:S(2)}) %collective-permute-start.39) | collective-permute-done | bytes 557088 | tf_op jit(solution)/shard_map/ppermute | solution.py:31
  233.4 6.8 collective-permute-done.41
  260.0 5.4 fusion.12
  271.1 27.4 %reshape.261 = bf16[16,2,128,2048]{2,1,0,3:T(2,128)(2,1)} reshape(bf16[4096,2048]{0,1:T(8,128)(2,1)} %all-gather.3.cloned.1.call-done) | data formatting | bytes 33554432 | tf_op jit(solution)/shard_map/reshape | solution.py:223
  298.5 20.0 %constant_dynamic-slice_fusion.5 = bf16[16,1,128,2048]{2,1,0,3:T(2,128)(2,1)} fusion(bf16[16,2,128,2048]{2,1,0,3:T(2,128)(2,1)} %reshape.261, s32[]{:T(128)S(6)} %select_n.102), kind=kLoop, calls=%fused_computation.366 | loop fusion | bytes 16777220 | tf_op jit(solution)/shard_map/jit(dynamic_index_in_dim)/dynamic_slice | solution.py:224
  318.5 39.1 %copy.209 = bf16[16,1,128,2048]{3,2,0,1:T(8,128)(2,1)} copy(bf16[16,1,128,2048]{2,1,0,3:T(2,128)(2,1)} %constant_dynamic-slice_fusion.5) | data formatting | bytes 16777216
  357.5 8.1 %fusion.20 = f32[2,512,1024]{2,1,0:T(8,128)S(1)} fusion(bf16[2,512,2048]{2,1,0:T(8,128)(2,1)} %bitcast.562, bf16[2048,2048]{1,0:T(8,128)(2,1)} %bitcast.569), kind=kOutput, calls=%fused_computation.49 | convolution fusion | flops 4294967296 | bytes 12582912 | tf_op jit(solution)/shard_map/stn,nw->stw/dot_general | solution.py:336
  378.3 6.1 convolution_convert_fusion.2
  384.4 6.3 convolution_convert_fusion.3
  390.9 7.8 %concatenate.198 = bf16[2,512,2176]{2,1,0:T(8,128)(2,1)} concatenate(bf16[2,512,2048]{2,1,0:T(8,128)(2,1)} %convolution_convert_fusion.3, bf16[2,512,16]{2,1,0:T(8,128)(2,1)S(1)} %copy.164, bf16[2,512,112]{2,1,0:T(8,128)(2,1)S(1)} %broadcast.164), dimensions={2} | concatenate | bytes 8912896 | tf_op jit(solution)/shard_map/concatenate | solution.py:295
  402.6 7.8 %concatenate.202 = bf16[2,512,2176]{2,1,0:T(8,128)(2,1)} concatenate(bf16[2,512,2048]{2,1,0:T(8,128)(2,1)} %convolution_convert_fusion.2, bf16[2,512,16]{2,1,0:T(8,128)(2,1)S(1)} %copy.166, bf16[2,512,112]{2,1,0:T(8,128)(2,1)S(1)} %broadcast.164), dimensions={2} | concatenate | bytes 8912896 | tf_op jit(solution)/shard_map/concatenate | solution.py:295
  434.6 8.2 %collective-permute-done.58 = bf16[128,2176]{1,0:T(8,128)(2,1)S(1)} collective-permute-done((bf16[128,2176]{1,0:T(8,128)(2,1)S(1)}, bf16[128,2176]{1,0:T(8,128)(2,1)S(1)}, u32[]{:S(2)}, u32[]{:S(2)}) %collective-permute-start.58) | collective-permute-done | bytes 557088 | tf_op jit(solution)/shard_map/ppermute | solution.py:31
  455.4 9.5 %collective-permute-done.60 = bf16[128,2048]{1,0:T(8,128)(2,1)S(1)} collective-permute-done((bf16[128,2048]{1,0:T(8,128)(2,1)S(1)}, bf16[128,2048]{1,0:T(8,128)(2,1)S(1)}, u32[]{:S(2)}, u32[]{:S(2)}) %collective-permute-start.60) | collective-permute-done | bytes 524320 | tf_op jit(solution)/shard_map/ppermute | solution.py:31
  476.1 5.7 pad_maximum_fusion
  517.0 8.9 %concatenate.212 = bf16[2,4,128,2688]{3,2,1,0:T(8,128)(2,1)} concatenate(bf16[2,4,128,2048]{3,2,1,0:T(8,128)(2,1)} %convolution_convert_fusion, bf16[2,4,128,256]{3,2,1,0:T(8,128)(2,1)} %bitcast.594, bf16[2,4,128,256]{3,2,1,0:T(8,128)(2,1)S(1)} %bitcast.593, bf16[2,4,128,16]{3,2,1,0:T(8,128)(2,1)S(1)} %bitcast.600, bf16[2,4,128,112]{3,2,1,0:T(8,128)(2,1)} %concatenate.211), dimensions={3} | concatenate | bytes 11010048 | tf_op jit(solution)/shard_map/concatenate | solution.py:295
  536.3 7.7 %collective-permute-done.68 = bf16[64,2688]{1,0:T(8,128)(2,1)S(1)} collective-permute-done((bf16[64,2688]{1,0:T(8,128)(2,1)S(1)}, bf16[64,2688]{1,0:T(8,128)(2,1)S(1)}, u32[]{:S(2)}, u32[]{:S(2)}) %collective-permute-start.68) | collective-permute-done | bytes 344096 | tf_op jit(solution)/shard_map/ppermute | solution.py:31
  547.3 13.2 %collective-permute-done.71 = bf16[128,2688]{1,0:T(8,128)(2,1)S(1)} collective-permute-done((bf16[128,2688]{1,0:T(8,128)(2,1)S(1)}, bf16[128,2688]{1,0:T(8,128)(2,1)S(1)}, u32[]{:S(2)}, u32[]{:S(2)}) %collective-permute-start.71) | collective-permute-done | bytes 688160 | tf_op jit(solution)/shard_map/ppermute | solution.py:31
  581.9 153.1 %all-reduce.5.cloned.1.call-done = (bf16[8,16,10496]{2,1,0:T(8,128)(2,1)}, bf16[8,16,20480]{2,1,0:T(8,128)(2,1)}) async-done(((bf16[8,16,10496]{2,1,0:T(8,128)(2,1)}, bf16[8,16,20480]{2,1,0:T(8,128)(2,1)}), (bf16[8,16,10496]{2,1,0:T(8,128)(2,1)}, bf16[8,16,20480]{2,1,0:T(8,128)(2,1)})) %all-reduce.5.cloned.1.call-update) | async-done | bytes 7929872 | tf_op jit(solution)/shard_map/psum | solution.py:440
  (574 shorter events, 339.6 us)
Async XLA Ops:
  7.2 252.8 %all-gather.5.cloned.1.call-start = ((), (), s32[]{:S(2)}) async-start(), calls=%async_computation.1 | async-start | bytes 4718592 | tf_op jit(solution)/shard_map/all_gather | solution.py:227
  8.0 263.2 %all-gather.3.cloned.1.call-start = ((), (), s32[]{:S(2)}) async-start(), calls=%async_computation | async-start | bytes 17301504 | tf_op jit(solution)/shard_map/all_gather | solution.py:222
  13.4 54.2 %collective-permute-start.27 = (bf16[128,2048]{1,0:T(8,128)(2,1)S(1)}, bf16[128,2048]{1,0:T(8,128)(2,1)S(1)}, u32[]{:S(2)}, u32[]{:S(2)}) collective-permute-start(bf16[128,2048]{1,0:T(8,128)(2,1)S(1)} %fusion.49), channel_id=1, source_target_pairs={{0,3},{1,0},{2,1},{3,2},{4,7},{5,4},{6,5},{7,6},{8,11},{9,8},{10,9... | collective-permute-start | bytes 1572872 | tf_op jit(solution)/shard_map/ppermute | solution.py:31
  16.8 51.5 %collective-permute-start.26 = (bf16[128,2048]{1,0:T(8,128)(2,1)S(1)}, bf16[128,2048]{1,0:T(8,128)(2,1)S(1)}, u32[]{:S(2)}, u32[]{:S(2)}) collective-permute-start(bf16[128,2048]{1,0:T(8,128)(2,1)S(1)} %fusion.49), channel_id=1, source_target_pairs={{0,1},{1,2},{2,3},{3,0},{4,5},{5,6},{6,7},{7,4},{8,9},{9,10},{10,1... | collective-permute-start | bytes 1572872 | tf_op jit(solution)/shard_map/ppermute | solution.py:31
  16.8 16.9 %collective-permute-start.32 = (s32[1,1]{1,0:T(1,128)}, s32[1,1]{1,0:T(1,128)}, u32[]{:S(2)}, u32[]{:S(2)}) collective-permute-start(s32[1,1]{1,0:T(1,128)} %param.43), channel_id=1, source_target_pairs={{0,8},{8,0},{1,9},{9,1},{2,10},{10,2},{3,11},{11,3},{4,12},{12,4},... | collective-permute-start | bytes 20 | tf_op jit(solution)/shard_map/ppermute | solution.py:43
  20.3 23.5 %collective-permute-start = (bf16[128,768]{1,0:T(8,128)(2,1)}, bf16[128,768]{1,0:T(8,128)(2,1)S(1)}, u32[]{:S(2)}, u32[]{:S(2)}) collective-permute-start(bf16[128,768]{1,0:T(8,128)(2,1)} %pad_maximum_fusion.16), channel_id=1, source_target_pairs={{0,0},{4,8},{8,4},{12,12},{1,1},{5,9},{9,5},{13,13},{2,2},{6,10},{... | collective-permute-start | bytes 589832 | tf_op jit(solution)/shard_map/ppermute | solution.py:51
  27.7 707.4 %all-reduce.5.cloned.1.call-start = ((), (), s32[]{:S(2)}) async-start(), calls=%async_computation.2 | async-start | bytes 15859712 | tf_op jit(solution)/shard_map/psum | solution.py:440
  56.6 72.9 %collective-permute-start.25 = (bf16[128,2048]{1,0:T(8,128)(2,1)S(1)}, bf16[128,2048]{1,0:T(8,128)(2,1)}, u32[]{:S(2)}, u32[]{:S(2)}) collective-permute-start(bf16[128,2048]{1,0:T(8,128)(2,1)S(1)} %fusion.49), channel_id=1, source_target_pairs={{0,8},{8,0},{1,9},{9,1},{2,10},{10,2},{3,11},{11,3},{4,12},{12,4},... | collective-permute-start | bytes 1572872 | tf_op jit(solution)/shard_map/ppermute | solution.py:43
  64.8 14.6 %collective-permute-start.6 = (bf16[4,64,768]{2,1,0:T(8,128)(2,1)S(1)}, bf16[4,64,768]{2,1,0:T(8,128)(2,1)S(1)}, u32[]{:S(2)}, u32[]{:S(2)}) collective-permute-start(bf16[4,64,768]{2,1,0:T(8,128)(2,1)S(1)} %get-tuple-element.19), channel_id=1, source_target_pairs={{0,16},{16,4},{4,20},{20,0},{1,17},{17,5},{5,21},{21,1},{2,18},{18... | collective-permute-start | bytes 1179656 | tf_op jit(solution)/shard_map/ppermute | solution.py:39
  68.4 16.4 %collective-permute-start.13 = (bf16[4,64,768]{2,1,0:T(8,128)(2,1)S(1)}, bf16[4,64,768]{2,1,0:T(8,128)(2,1)S(1)}, u32[]{:S(2)}, u32[]{:S(2)}) collective-permute-start(bf16[4,64,768]{2,1,0:T(8,128)(2,1)S(1)} %get-tuple-element.21), channel_id=1, source_target_pairs={{0,96},{32,0},{64,32},{96,64},{1,97},{33,1},{65,33},{97,65},{2,98}... | collective-permute-start | bytes 1179656 | tf_op jit(solution)/shard_map/ppermute | solution.py:35
  79.5 44.4 %collective-permute-start.30 = (bf16[64,2048]{1,0:T(8,128)(2,1)S(1)}, bf16[64,2048]{1,0:T(8,128)(2,1)}, u32[]{:S(2)}, u32[]{:S(2)}) collective-permute-start(bf16[64,2048]{1,0:T(8,128)(2,1)S(1)} %slice.517), channel_id=1, source_target_pairs={{0,3},{1,0},{2,1},{3,2},{4,7},{5,4},{6,5},{7,6},{8,11},{9,8},{10,9... | collective-permute-start | bytes 786440 | tf_op jit(solution)/shard_map/ppermute | solution.py:31
  81.9 77.4 %collective-permute-start.28 = (bf16[256,2048]{1,0:T(8,128)(2,1)}, bf16[256,2048]{1,0:T(8,128)(2,1)}, u32[]{:S(2)}, u32[]{:S(2)}) collective-permute-start(bf16[256,2048]{1,0:T(8,128)(2,1)} %pad_maximum_fusion.3), channel_id=1, source_target_pairs={{0,8},{8,0},{1,9},{9,1},{2,10},{10,2},{3,11},{11,3},{4,12},{12,4},... | collective-permute-start | bytes 3145736 | tf_op jit(solution)/shard_map/ppermute | solution.py:43
  124.9 23.1 %collective-permute-start.31 = (bf16[128,2048]{1,0:T(8,128)(2,1)S(1)}, bf16[128,2048]{1,0:T(8,128)(2,1)}, u32[]{:S(2)}, u32[]{:S(2)}) collective-permute-start(bf16[128,2048]{1,0:T(8,128)(2,1)S(1)} %constant_dynamic-update-slice_fusion.6), channel_id=1, source_target_pairs={{0,8},{8,0},{1,9},{9,1},{2,10},{10,2},{3,11},{11,3},{4,12},{12,4},... | collective-permute-start | bytes 1572872 | tf_op jit(solution)/shard_map/ppermute | solution.py:43
  191.8 14.9 %collective-permute-start.36 = (bf16[64,2176]{1,0:T(8,128)(2,1)S(1)}, bf16[64,2176]{1,0:T(8,128)(2,1)S(1)}, u32[]{:S(2)}, u32[]{:S(2)}) collective-permute-start(bf16[64,2176]{1,0:T(8,128)(2,1)S(1)} %get-tuple-element.67), channel_id=1, source_target_pairs={{0,1},{1,2},{2,3},{3,0},{4,5},{5,6},{6,7},{7,4},{8,9},{9,10},{10,1... | collective-permute-start | bytes 835592 | tf_op jit(solution)/shard_map/ppermute | solution.py:31
  191.9 17.8 %collective-permute-start.38 = (bf16[64,2176]{1,0:T(8,128)(2,1)S(1)}, bf16[64,2176]{1,0:T(8,128)(2,1)S(1)}, u32[]{:S(2)}, u32[]{:S(2)}) collective-permute-start(bf16[64,2176]{1,0:T(8,128)(2,1)S(1)} %get-tuple-element.68), channel_id=1, source_target_pairs={{0,3},{1,0},{2,1},{3,2},{4,7},{5,4},{6,5},{7,6},{8,11},{9,8},{10,9... | collective-permute-start | bytes 835592 | tf_op jit(solution)/shard_map/ppermute | solution.py:31
  229.3 14.8 %collective-permute-start.42 = (bf16[128,2048]{1,0:T(8,128)(2,1)S(1)}, bf16[128,2048]{1,0:T(8,128)(2,1)S(1)}, u32[]{:S(2)}, u32[]{:S(2)}) collective-permute-start(bf16[128,2048]{1,0:T(8,128)(2,1)S(1)} %add_convert_fusion.1), channel_id=1, source_target_pairs={{0,3},{1,0},{2,1},{3,2},{4,7},{5,4},{6,5},{7,6},{8,11},{9,8},{10,9... | collective-permute-start | bytes 1572872 | tf_op jit(solution)/shard_map/ppermute | solution.py:31
  426.1 16.8 %collective-permute-start.58 = (bf16[128,2176]{1,0:T(8,128)(2,1)S(1)}, bf16[128,2176]{1,0:T(8,128)(2,1)S(1)}, u32[]{:S(2)}, u32[]{:S(2)}) collective-permute-start(bf16[128,2176]{1,0:T(8,128)(2,1)S(1)} %pad_maximum_fusion.13), channel_id=1, source_target_pairs={{0,3},{1,0},{2,1},{3,2},{4,7},{5,4},{6,5},{7,6},{8,11},{9,8},{10,9... | collective-permute-start | bytes 1671176 | tf_op jit(solution)/shard_map/ppermute | solution.py:31
  432.0 22.7 %collective-permute-start.52 = (bf16[128,2176]{1,0:T(8,128)(2,1)S(1)}, bf16[128,2176]{1,0:T(8,128)(2,1)S(1)}, u32[]{:S(2)}, u32[]{:S(2)}) collective-permute-start(bf16[128,2176]{1,0:T(8,128)(2,1)S(1)} %pad_maximum_fusion.11), channel_id=1, source_target_pairs={{0,3},{1,0},{2,1},{3,2},{4,7},{5,4},{6,5},{7,6},{8,11},{9,8},{10,9... | collective-permute-start | bytes 1671176 | tf_op jit(solution)/shard_map/ppermute | solution.py:31
  434.6 20.2 %collective-permute-start.50 = (bf16[128,2176]{1,0:T(8,128)(2,1)S(1)}, bf16[128,2176]{1,0:T(8,128)(2,1)S(1)}, u32[]{:S(2)}, u32[]{:S(2)}) collective-permute-start(bf16[128,2176]{1,0:T(8,128)(2,1)S(1)} %pad_maximum_fusion.10), channel_id=1, source_target_pairs={{0,1},{1,2},{2,3},{3,0},{4,5},{5,6},{6,7},{7,4},{8,9},{9,10},{10,1... | collective-permute-start | bytes 1671176 | tf_op jit(solution)/shard_map/ppermute | solution.py:31
  444.2 21.8 %collective-permute-start.61 = (bf16[128,2048]{1,0:T(8,128)(2,1)S(1)}, bf16[128,2048]{1,0:T(8,128)(2,1)S(1)}, u32[]{:S(2)}, u32[]{:S(2)}) collective-permute-start(bf16[128,2048]{1,0:T(8,128)(2,1)S(1)} %fusion.75), channel_id=1, source_target_pairs={{0,3},{1,0},{2,1},{3,2},{4,7},{5,4},{6,5},{7,6},{8,11},{9,8},{10,9... | collective-permute-start | bytes 1572872 | tf_op jit(solution)/shard_map/ppermute | solution.py:31
  447.7 17.2 %collective-permute-start.60 = (bf16[128,2048]{1,0:T(8,128)(2,1)S(1)}, bf16[128,2048]{1,0:T(8,128)(2,1)S(1)}, u32[]{:S(2)}, u32[]{:S(2)}) collective-permute-start(bf16[128,2048]{1,0:T(8,128)(2,1)S(1)} %fusion.75), channel_id=1, source_target_pairs={{0,1},{1,2},{2,3},{3,0},{4,5},{5,6},{6,7},{7,4},{8,9},{9,10},{10,1... | collective-permute-start | bytes 1572872 | tf_op jit(solution)/shard_map/ppermute | solution.py:31
  447.7 34.1 %collective-permute-start.59 = (bf16[128,2048]{1,0:T(8,128)(2,1)S(1)}, bf16[128,2048]{1,0:T(8,128)(2,1)S(1)}, u32[]{:S(2)}, u32[]{:S(2)}) collective-permute-start(bf16[128,2048]{1,0:T(8,128)(2,1)S(1)} %fusion.75), channel_id=1, source_target_pairs={{0,8},{8,0},{1,9},{9,1},{2,10},{10,2},{3,11},{11,3},{4,12},{12,4},... | collective-permute-start | bytes 1572872 | tf_op jit(solution)/shard_map/ppermute | solution.py:43
  544.1 16.4 %collective-permute-start.71 = (bf16[128,2688]{1,0:T(8,128)(2,1)S(1)}, bf16[128,2688]{1,0:T(8,128)(2,1)S(1)}, u32[]{:S(2)}, u32[]{:S(2)}) collective-permute-start(bf16[128,2688]{1,0:T(8,128)(2,1)S(1)} %pad_maximum_fusion.7), channel_id=1, source_target_pairs={{0,3},{1,0},{2,1},{3,2},{4,7},{5,4},{6,5},{7,6},{8,11},{9,8},{10,9... | collective-permute-start | bytes 2064392 | tf_op jit(solution)/shard_map/ppermute | solution.py:31
  546.8 17.0 %collective-permute-start.69 = (bf16[128,2688]{1,0:T(8,128)(2,1)S(1)}, bf16[128,2688]{1,0:T(8,128)(2,1)S(1)}, u32[]{:S(2)}, u32[]{:S(2)}) collective-permute-start(bf16[128,2688]{1,0:T(8,128)(2,1)S(1)} %pad_maximum_fusion.6), channel_id=1, source_target_pairs={{0,1},{1,2},{2,3},{3,0},{4,5},{5,6},{6,7},{7,4},{8,9},{9,10},{10,1... | collective-permute-start | bytes 2064392 | tf_op jit(solution)/shard_map/ppermute | solution.py:31
  (125 other events, 1373.0 us)
Sparse Core Ops, SparseCore 0:
  9.8 40.7 all-gather.4
  52.8 137.3 all-gather.2
  573.7 161.2 all-reduce.4

commit v2 on v1

v2 whole, which is shorter than its diff:
```python
import functools
import math

import jax
import jax.numpy as jnp
from jax import lax
from jax.experimental import pallas as pl
from jax.experimental.pallas import tpu as pltpu
from jax.sharding import Mesh
from jax.sharding import PartitionSpec as P

MODEL_WIDTH = 2048
H = 16
HEAD_WIDTH = 128
FEED_HIDDEN = 8192
ADAPTER_RANK = 16
ADAPTER_COUNT = 8
BLOCK = 256

AXES = ("y", "zl", "core", "zh", "x")
SIZES = (4, 2, 2, 2, 4)
DP = ("y", "zl", "core")
MP = ("zh", "x")
PLACES = (0, 3, 1, 2)
Z_RING = (0, 2, 1, 3)
ROWS = 128
RIDE = 128

f32 = jnp.float32
bf16 = jnp.bfloat16


def ring_x(a, step):
    return lax.ppermute(a, "x", [(i, (i + step) % 4) for i in range(4)])


def ring_y(a, step):
    return lax.ppermute(a, "y", [(i, (i + step) % 4) for i in range(4)])


def ring_z(a, step):
    return lax.ppermute(a, ("zl", "zh"), [(Z_RING[i], Z_RING[(i + step) % 4]) for i in range(4)])


def other_core(a):
    return lax.ppermute(a, "core", [(0, 1), (1, 0)])


def other_half(a):
    return lax.ppermute(a, "zh", [(0, 1), (1, 0)])


def turn(a):
    return lax.ppermute(a, ("core", "zh"), [(0, 0), (1, 2), (2, 1), (3, 3)])


def gather_row(a):
    half = a.shape[0] // 2
    left, right = ring_x(a, 1), ring_x(a, -1)
    near = other_core(a)
    top, bottom = ring_x(left[:half], 1), ring_x(right[half:], -1)
    left_other, right_other = other_core(left), other_core(right)
    return (
        (a, near),
        (left, left_other),
        (right, right_other),
        (top, bottom, other_core(top), other_core(bottom)),
    )


def scatter_row(mine, theirs):
    half = mine[0].shape[0] // 2
    far = mine[3].astype(f32) + other_core(theirs[3]).astype(f32)
    up = ring_x(far[:half].astype(bf16), 1)
    down = ring_x(far[half:].astype(bf16), -1)
    right = mine[2].astype(f32) + other_core(theirs[2]).astype(f32)
    left = mine[1].astype(f32) + other_core(theirs[1]).astype(f32)
    near = mine[0].astype(f32) + other_core(theirs[0]).astype(f32)
    right = jnp.concatenate([right[:half] + up.astype(f32), right[half:]]).astype(bf16)
    left = jnp.concatenate([left[:half], left[half:] + down.astype(f32)]).astype(bf16)
    return near + ring_x(right, 1).astype(f32) + ring_x(left, -1).astype(f32)


def gather_ring(a, ring):
    half = a.shape[-2] // 2
    left, right = ring(a, 1), ring(a, -1)
    return a, left, right, ring(left[..., :half, :], 1), ring(right[..., half:, :], -1)


def stacked_ring(pieces):
    own, left, right, top, bottom = pieces
    return jnp.stack([own, right, jnp.concatenate([top, bottom], axis=-2), left])


def rolled(blocks, me):
    both = jnp.concatenate([blocks, blocks], axis=0)
    return lax.dynamic_slice_in_dim(both, lax.rem(4 - me, 4), 4, 0)


def own_slice(pair, zh):
    kept = jnp.where(zh == 0, pair[:16], pair[16:])
    sent = jnp.where(zh == 0, pair[16:], pair[:16])
    total = kept + other_half(sent.astype(bf16)).astype(f32)
    return turn(total.astype(bf16))


def scatter_sequence(slices, zh, x):
    kept = lax.dynamic_index_in_dim(slices, zh, 0, keepdims=False)
    sent = lax.dynamic_index_in_dim(slices, 1 - zh, 0, keepdims=False)
    total = kept + other_half(sent.astype(bf16)).astype(f32)
    both = jnp.concatenate([total, total], axis=0)
    near = lax.dynamic_slice_in_dim(both, x, 4, 0)
    low = near.astype(bf16)
    return (
        near[0]
        + ring_x(low[1], 1).astype(f32)
        + ring_x(low[3], -1).astype(f32)
        + ring_x(low[2], 2).astype(f32)
    )


def gather_sequences(piece, zh, x):
    other = other_half(piece)
    pair = jnp.where(zh == 0, jnp.stack([piece, other]), jnp.stack([other, piece]))
    row = rolled(jnp.stack([pair, ring_x(pair, -1), ring_x(pair, 2), ring_x(pair, 1)]), x)
    return lax.all_gather(row, DP, axis=0)


def layer_norm(values, gain, shift):
    mean_value = jnp.mean(values, axis=-1, keepdims=True)
    centred = values - mean_value
    variance = jnp.mean(centred * centred, axis=-1, keepdims=True)
    return centred * lax.rsqrt(variance + 1e-05) * gain + shift


def gelu_tanh(values):
    inner_product = math.sqrt(2.0 / math.pi) * (values + 0.044715 * values * values * values)
    return 0.5 * values * (1.0 + jnp.tanh(inner_product))


def pick(adapter_stack, position):
    return lax.dynamic_index_in_dim(adapter_stack, position, 0, keepdims=False)


def dot(left, right):
    return jnp.dot(left, right, preferred_element_type=f32)


def dot_t(left, right):
    return lax.dot_general(left, right, (((1,), (1,)), ((), ())), preferred_element_type=f32)


def tdot(left, right):
    return lax.dot_general(left, right, (((0,), (0,)), ((), ())), preferred_element_type=f32)


def lane_owner(rows, row_core):
    lane = lax.broadcasted_iota(jnp.int32, (rows, RIDE), 1)
    return (lane // ADAPTER_RANK) == row_core


def place_mask(core):
    row = lax.broadcasted_iota(jnp.int32, (2 * ROWS, RIDE), 0)
    return lane_owner(2 * ROWS, jnp.where(row < ROWS, core, 1 - core))


def copy(source, target, sem):
    pltpu.make_async_copy(source, target, sem).start()


def wait(target, sem):
    pltpu.make_async_copy(target, target, sem).wait()


def copy_place(pieces, target_mine, target_theirs, sem):
    half = ROWS // 2
    if len(pieces) == 2:
        copy(pieces[0], target_mine, sem)
        copy(pieces[1], target_theirs, sem)
    else:
        copy(pieces[0], target_mine.at[pl.ds(0, half)], sem)
        copy(pieces[1], target_mine.at[pl.ds(half, half)], sem)
        copy(pieces[2], target_theirs.at[pl.ds(0, half)], sem)
        copy(pieces[3], target_theirs.at[pl.ds(half, half)], sem)


def split_pieces(refs):
    return (refs[0:2], refs[2:4], refs[4:6], refs[6:10])


def assemble_kernel(at, *refs):
    pieces, (out, sem) = refs[:10], refs[10:]
    y, z = at[3], at[4]
    half = ROWS // 2
    for which in range(2):
        group = pieces[5 * which : 5 * which + 5]
        for piece, step, first, count in (
            (group[0], 0, 0, half),
            (group[1], 3, 0, half),
            (group[2], 1, 0, half),
            (group[3], 2, 0, half // 2),
            (group[4], 2, half // 2, half // 2),
        ):
            for k in range(4):
                if which == 0:
                    to_y, to_z = lax.rem(y + k, 4), lax.rem(z + step, 4)
                else:
                    to_y, to_z = lax.rem(y + step, 4), lax.rem(z + k, 4)
                shard = (to_y * 2 + lax.rem(to_z, 2)) * 2 + to_z // 2
                row = pl.multiple_of(shard * ROWS + which * half + first, 32)
                copy(piece.at[k], out.at[pl.ds(row, count)], sem)
    wait(out, sem)


def pack_kernel(at, query, keyval, output, up, down, attention_out, feed_out):
    attention_out[:, :256] = query[...]
    attention_out[:, 256:512] = keyval[...]
    attention_out[:, 512:] = output[...].astype(f32).T.astype(bf16)
    feed_out[:, :1024] = up[...]
    feed_out[:, 1024:] = down[...].astype(f32).T.astype(bf16)


def finish_kernel(widths, ids, gathered, *outs):
    first = 0
    for out, width in zip(outs, widths):
        out[...] = jnp.zeros_like(out)
        for s in range(16):
            out[ids[s]] += gathered[s, 0, 0, :, first : first + width].astype(f32)
        first += width


def attention_kernel(at, *refs):
    rows_in = split_pieces(refs[:10])
    kv_in = refs[10:14]
    w, q_in, q_out, o_in, q_bias, bias = refs[14:20]
    inner_out, query_out, kv_all, lse_out, att_out = refs[20:25]
    parts = (refs[25:29], refs[29:33])
    rows, kvs, ws, sems = refs[33:]
    s = pl.program_id(0)
    core = at[0]

    @pl.when(s == 0)
    def _():
        copy(w, ws, sems.at[2])
        for p in range(4):
            here = pl.ds(p * ROWS, ROWS)
            copy_place(rows_in[p], rows.at[0, here], rows.at[1, here], sems.at[0])
            for q in range(2):
                for half in range(2):
                    copy(
                        kv_in[p].at[pl.ds(q * ROWS, ROWS), pl.ds(half * 256, 256)],
                        kvs.at[q, half * 4 + p],
                        sems.at[1],
                    )
        wait(rows, sems.at[0])
        wait(ws, sems.at[2])
        wait(kvs, sems.at[1])

    owner = lane_owner(4 * ROWS, jnp.where(s == 0, core, 1 - core))
    x = rows[s]
    inner = jnp.where(owner, dot_t(x, q_in[...]), 0.0).astype(bf16)
    inner_out[0] = inner
    query = (dot(x, ws[:, :256]) + q_bias[...] + dot(inner, q_out[...])).astype(bf16)
    query_out[0] = query
    kv = kvs[s]
    kv_all[0] = kv
    keys = kv[:, :, :HEAD_WIDTH].reshape(8 * ROWS, HEAD_WIDTH)
    values_t = kv[:, :, HEAD_WIDTH:].reshape(8 * ROWS, HEAD_WIDTH).astype(f32).T.astype(bf16)
    columns = []
    for h in range(2):
        chunks = []
        for c in range(2):
            lanes = slice(c * 256, c * 256 + 256)
            q = query[lanes, h * HEAD_WIDTH : (h + 1) * HEAD_WIDTH]
            scores = dot_t(keys, q) * (HEAD_WIDTH**-0.5)
            scores = scores.reshape(8, ROWS, 256) + bias[:, lanes][:, None, :]
            scores = scores.reshape(8 * ROWS, 256)
            top = jnp.max(scores, axis=0, keepdims=True)
            expo = jnp.exp(scores - top)
            total = jnp.sum(expo, axis=0, keepdims=True)
            probs = (expo * (1.0 / total)).astype(bf16)
            lse_out[0, h : h + 1, lanes] = top + jnp.log(total)
            chunks.append(dot(values_t, probs).T)
        columns.append(jnp.concatenate(chunks, axis=0))
    attended = jnp.concatenate(columns, axis=1).astype(bf16)
    att_out[0] = attended
    low = jnp.where(owner, dot_t(attended, o_in[...]), 0.0).astype(bf16)
    for which in range(2):

        @pl.when(s == which)
        def _(which=which):
            for p in range(4):
                here = slice(p * ROWS, (p + 1) * ROWS)
                parts[which][p][:, :MODEL_WIDTH] = dot_t(attended[here], ws[:, 512:]).astype(bf16)
                parts[which][p][:, MODEL_WIDTH:] = low[here]


def feed_kernel(at, *refs):
    rows_in = split_pieces(refs[:10])
    feed, u_in, u_out, d_in, u_bias = refs[10:15]
    inner_out, pre_out, act_out = refs[15:18]
    parts = (refs[18:22], refs[22:26])
    rows, up, down, sems = refs[26:]
    p = pl.program_id(0)
    core = at[0]

    @pl.when(p == 0)
    def _():
        copy(feed.at[:, core, :, pl.ds(0, 1024)], up, sems.at[4])
        for k in range(4):
            copy_place(
                rows_in[k], rows.at[k, pl.ds(0, ROWS)], rows.at[k, pl.ds(ROWS, ROWS)], sems.at[k]
            )
        copy(feed.at[:, core, :, pl.ds(1024, 1024)], down, sems.at[5])
        wait(up, sems.at[4])

    wait(rows.at[p], sems.at[p])
    mask = place_mask(core)
    x = rows[p]
    inner = jnp.where(mask, dot_t(x, u_in[...]), 0.0).astype(bf16)
    inner_out[0] = inner
    pre = dot(x, up[...].reshape(MODEL_WIDTH, 1024)) + u_bias[...] + dot(inner, u_out[...])
    pre_out[0] = pre
    act = gelu_tanh(pre).astype(bf16)
    act_out[0] = act

    @pl.when(p == 0)
    def _():
        wait(down, sems.at[5])

    low = jnp.where(mask, dot_t(act, d_in[...]), 0.0).astype(bf16)
    out = dot_t(act, down[...].reshape(MODEL_WIDTH, 1024)).astype(bf16)
    for k in range(4):

        @pl.when(p == k)
        def _(k=k):
            for which in range(2):
                here = slice(which * ROWS, (which + 1) * ROWS)
                parts[which][k][:, :MODEL_WIDTH] = out[here]
                parts[which][k][:, MODEL_WIDTH:] = low[here]


def feed_back_kernel(at, *refs):
    cot, feed, pre_in, act_in, inner_in, d_out, d_in, u_out = refs[:8]
    up_b, down_a = refs[8:10]
    parts = (refs[10:14], refs[14:18])
    rows, up, down, sems = refs[18:]
    p = pl.program_id(0)
    core, x = at[0], at[1]

    @pl.when(p == 0)
    def _():
        copy(feed.at[:, core, :, pl.ds(1024, 1024)], down, sems.at[5])
        for k in range(4):
            there = lax.rem(x + PLACES[k], 4)
            copy(cot.at[core, there], rows.at[k, pl.ds(0, ROWS)], sems.at[k])
            copy(cot.at[1 - core, there], rows.at[k, pl.ds(ROWS, ROWS)], sems.at[k])
        copy(feed.at[:, core, :, pl.ds(0, 1024)], up, sems.at[4])
        up_b[...] = jnp.zeros_like(up_b)
        down_a[...] = jnp.zeros_like(down_a)
        wait(down, sems.at[5])

    wait(rows.at[p], sems.at[p])
    mask = place_mask(core)
    grad = rows[p]
    back = jnp.where(mask, dot_t(grad, d_out[...]), 0.0)
    back_t = back.T[:32].astype(bf16)
    act = act_in[0]
    down_a[...] += dot(back_t, act)
    grad_act = dot(grad, down[...].reshape(MODEL_WIDTH, 1024)) + dot(back.astype(bf16), d_in[...])
    pre = pre_in[0]
    k0 = math.sqrt(2.0 / math.pi)
    square = pre * pre
    bend = jnp.tanh(k0 * (pre + 0.044715 * square * pre))
    slope = 0.5 * (1.0 + bend) + 0.5 * pre * (1.0 - bend * bend) * (
        k0 * (1.0 + 3.0 * 0.044715 * square)
    )
    grad_pre = (grad_act * slope).astype(bf16)
    inner_t = inner_in[0].astype(f32).T[:32].astype(bf16)
    up_b[...] += dot(inner_t, grad_pre)
    low = jnp.where(mask, dot_t(grad_pre, u_out[...]), 0.0).astype(bf16)

    @pl.when(p == 0)
    def _():
        wait(up, sems.at[4])

    out = dot_t(grad_pre, up[...].reshape(MODEL_WIDTH, 1024)).astype(bf16)
    for k in range(4):

        @pl.when(p == k)
        def _(k=k):
            for which in range(2):
                here = slice(which * ROWS, (which + 1) * ROWS)
                parts[which][k][:, :MODEL_WIDTH] = out[here]
                parts[which][k][:, MODEL_WIDTH:] = low[here]


def attention_back_kernel(at, *refs):
    rows_in = split_pieces(refs[:10])
    w, inner_in, query_in, kv_in, lse_in, att_in, o_out, o_in, q_out, bias = refs[10:20]
    query_b, output_a = refs[20:22]
    parts = (refs[22:26], refs[26:30])
    rows, ws, grad_k, grad_v, sems = refs[30:]
    s = pl.program_id(0)
    core = at[0]

    @pl.when(s == 0)
    def _():
        copy(w, ws, sems.at[1])
        for p in range(4):
            here = pl.ds(p * ROWS, ROWS)
            copy_place(rows_in[p], rows.at[0, here], rows.at[1, here], sems.at[0])
        query_b[...] = jnp.zeros_like(query_b)
        output_a[...] = jnp.zeros_like(output_a)
        wait(rows, sems.at[0])
        wait(ws, sems.at[1])

    owner = lane_owner(4 * ROWS, jnp.where(s == 0, core, 1 - core))
    scale = HEAD_WIDTH**-0.5
    x = rows[s]
    back = jnp.where(owner, dot_t(x, o_out[...]), 0.0)
    output_a[...] += dot(back.T[:32].astype(bf16), att_in[0])
    grad_att = (dot(x, ws[:, 512:]) + dot(back.astype(bf16), o_in[...])).astype(bf16)
    query = query_in[0]
    kv = kv_in[0]
    keys = kv[:, :, :HEAD_WIDTH].reshape(8 * ROWS, HEAD_WIDTH)
    values = kv[:, :, HEAD_WIDTH:].reshape(8 * ROWS, HEAD_WIDTH)
    keys_t = keys.astype(f32).T.astype(bf16)
    columns = []
    for h in range(2):
        chunks = []
        for c in range(2):
            lanes = slice(c * 256, c * 256 + 256)
            head = slice(h * HEAD_WIDTH, (h + 1) * HEAD_WIDTH)
            q, g = query[lanes, head], grad_att[lanes, head]
            scores = dot_t(keys, q) * scale
            scores = scores.reshape(8, ROWS, 256) + bias[:, lanes][:, None, :]
            probs = jnp.exp(scores.reshape(8 * ROWS, 256) - lse_in[0, h : h + 1, lanes])
            grad_probs = dot_t(values, g)
            delta = jnp.sum(probs * grad_probs, axis=0, keepdims=True)
            grad_scores = (probs * (grad_probs - delta)).astype(bf16)
            chunks.append((dot(keys_t, grad_scores) * scale).T)
            more_k = dot(grad_scores, q) * scale
            more_v = dot(probs.astype(bf16), g)
            if h == 0 and c == 0:
                grad_k[...] = more_k
                grad_v[...] = more_v
            else:
                grad_k[...] += more_k
                grad_v[...] += more_v
        columns.append(jnp.concatenate(chunks, axis=0))
    grad_query = jnp.concatenate(columns, axis=1).astype(bf16)
    query_b[...] += dot(inner_in[0].astype(f32).T[:32].astype(bf16), grad_query)
    low = jnp.where(owner, dot_t(grad_query, q_out[...]), 0.0).astype(bf16)
    for which in range(2):

        @pl.when(s == which)
        def _(which=which):
            for p in range(4):
                here = slice(p * ROWS, (p + 1) * ROWS)
                part = parts[which][p]
                part[:, :2048] = dot_t(grad_query[here], ws[:, :256]).astype(bf16)
                part[:, 2048:2176] = grad_k[here].astype(bf16)
                part[:, 2176:2304] = grad_v[here].astype(bf16)
                after = slice((p + 4) * ROWS, (p + 5) * ROWS)
                part[:, 2304:2432] = grad_k[after].astype(bf16)
                part[:, 2432:2560] = grad_v[after].astype(bf16)
                part[:, 2560:] = low[here]


VMEM_LIMIT = 56 * 1024 * 1024
ANY = pl.BlockSpec(memory_space=pl.ANY)


def whole_block(shape):
    return pl.BlockSpec(shape, lambda i, at: (0,) * len(shape))


def step_block(shape):
    return pl.BlockSpec((1, *shape), lambda i, at: (i,) + (0,) * len(shape))


def call(kernel, steps, at, ins, outs, scratch, name, flops=0):
    arrays = [a for a, _ in ins]
    in_specs = [whole_block(a.shape) if b is None else b for a, b in ins]
    out_specs = [whole_block(s) if b is None else b for s, _, b in outs]
    return pl.pallas_call(
        kernel,
        out_shape=[jax.ShapeDtypeStruct(s, d) for s, d, _ in outs],
        grid_spec=pltpu.PrefetchScalarGridSpec(
            num_scalar_prefetch=1,
            grid=(steps,),
            in_specs=in_specs,
            out_specs=out_specs,
            scratch_shapes=scratch,
        ),
        compiler_params=pltpu.CompilerParams(vmem_limit_bytes=VMEM_LIMIT),
        cost_estimate=pl.CostEstimate(
            flops=flops,
            bytes_accessed=sum(a.size * a.dtype.itemsize for a in arrays)
            + sum(math.prod(s) * 4 for s, _, _ in outs),
            transcendentals=0,
        ),
        name=name,
    )(at, *arrays)


def flat(places):
    return [(piece, ANY) for place in places for piece in place]


def part_outs(width):
    return [((ROWS, width), bf16, None)] * 8


def dma(n):
    return pltpu.SemaphoreType.DMA((n,))


def finish(gathered, ids, widths):
    total = gathered.shape[-1]
    return pl.pallas_call(
        functools.partial(finish_kernel, widths),
        out_shape=[
            jax.ShapeDtypeStruct((ADAPTER_COUNT, ADAPTER_RANK, 8 * w), f32) for w in widths
        ],
        grid_spec=pltpu.PrefetchScalarGridSpec(
            num_scalar_prefetch=1,
            grid=(4, 2),
            in_specs=[
                pl.BlockSpec((16, 1, 1, ADAPTER_RANK, total), lambda i, j, ids: (0, i, j, 0, 0))
            ],
            out_specs=[
                pl.BlockSpec((ADAPTER_COUNT, ADAPTER_RANK, w), lambda i, j, ids: (0, 0, j * 4 + i))
                for w in widths
            ],
        ),
        compiler_params=pltpu.CompilerParams(vmem_limit_bytes=VMEM_LIMIT),
        name="finish",
    )(ids, gathered)


def shards(
    tokens,
    cotangent,
    attention_norm_scale,
    attention_norm_bias,
    query_projection,
    query_projection_bias,
    keyvalue_projection,
    value_projection_bias,
    attention_output_weight,
    attention_output_bias,
    feedforward_norm_scale,
    feedforward_norm_bias,
    up_projection_weight,
    up_projection_bias,
    down_projection_weight,
    down_projection_bias,
    sequence_adapter,
    query_adapter_input,
    query_adapter_output,
    keyvalue_adapter_input,
    keyvalue_adapter_output,
    output_adapter_input,
    output_adapter_output,
    up_adapter_input,
    up_adapter_output,
    down_adapter_input,
    down_adapter_output,
):
    y, core, zl, zh, x = (lax.axis_index(n) for n in ("y", "core", "zl", "zh", "x"))
    z = zh * 2 + zl
    at = jnp.stack([core, x, zh, y, z]).astype(jnp.int32)
    gain_one, shift_one = attention_norm_scale.astype(f32), attention_norm_bias.astype(f32)
    gain_two, shift_two = feedforward_norm_scale.astype(f32), feedforward_norm_bias.astype(f32)

    attention_shard, feed_shard = call(
        pack_kernel,
        1,
        at,
        [
            (query_projection, None),
            (keyvalue_projection, None),
            (attention_output_weight, None),
            (up_projection_weight, None),
            (down_projection_weight, None),
        ],
        [((ROWS, 768), bf16, None), ((ROWS, 2048), bf16, None)],
        [],
        "pack",
    )
    feed = lax.all_gather(feed_shard, DP + ("zh",), axis=0, tiled=True)
    feed = feed.reshape(16, 2, ROWS, 2048)
    late_cotangent, late_ids, _ = lax.optimization_barrier((cotangent, sequence_adapter, feed))
    cot_all = lax.all_gather(late_cotangent, ("core", "x"), axis=0, tiled=True)
    cot_all = cot_all.reshape(2, 4, ROWS, MODEL_WIDTH)
    all_ids = lax.all_gather(late_ids, DP, axis=0, tiled=True)[:, 0]

    attention_shard = turn(attention_shard)
    half = ROWS // 2
    along_y = stacked_ring(gather_ring(attention_shard[:half], ring_y))
    along_z = stacked_ring(gather_ring(attention_shard[half:], ring_z))
    pieces = (*gather_ring(along_y, ring_z), *gather_ring(along_z, ring_y))
    (w,) = call(
        assemble_kernel,
        1,
        at,
        [(piece, ANY) for piece in pieces],
        [((MODEL_WIDTH, 768), bf16, None)],
        [pltpu.SemaphoreType.DMA],
        "assemble",
    )

    mine = sequence_adapter[0, 0]
    theirs = other_core(sequence_adapter)[0, 0]
    low = jnp.where(core == 0, mine, theirs)
    high = jnp.where(core == 0, theirs, mine)

    def ordered(stack):
        return jnp.concatenate([pick(stack, low), pick(stack, high)], axis=0)

    def ordered_t(stack):
        return ordered(jnp.swapaxes(stack, 1, 2))

    def padded(pair):
        return jnp.concatenate([pair, jnp.zeros((RIDE - 32, pair.shape[1]), bf16)], axis=0)

    small = jnp.concatenate(
        [
            ordered(query_adapter_output),
            ordered_t(output_adapter_input),
            ordered(up_adapter_output),
            ordered_t(down_adapter_input),
        ],
        axis=1,
    )
    biases = jnp.concatenate(
        [
            query_projection_bias,
            jnp.zeros((256,), bf16),
            up_projection_bias,
            jnp.zeros((1024,), bf16),
        ]
    )
    small = turn(jnp.concatenate([small, biases[None], jnp.zeros((15, 2560), bf16)], axis=0))
    q_bias, u_bias = small[32:33, :256].astype(f32), small[32:33, 512:1536].astype(f32)
    small = padded(small[:32])
    q_out, o_in, u_out, d_in = (
        small[:, :256],
        small[:, 256:512],
        small[:, 512:1536],
        small[:, 1536:],
    )
    q_in, u_in = padded(ordered_t(query_adapter_input)), padded(ordered_t(up_adapter_input))
    o_out, d_out = padded(ordered(output_adapter_output)), padded(ordered(down_adapter_output))

    input_rows = tokens.astype(f32)
    normed = layer_norm(input_rows, gain_one, shift_one).astype(bf16)
    normed_places = gather_row(normed)

    kv_in, kv_out = pick(keyvalue_adapter_input, mine), pick(keyvalue_adapter_output, mine)
    keyval_inner = dot(normed, kv_in).astype(bf16)
    keyval_bias = jnp.concatenate(
        [jnp.zeros((HEAD_WIDTH,), f32), value_projection_bias.astype(f32)]
    )
    keyval = (dot(normed, w[:, 256:512]) + keyval_bias + dot(keyval_inner, kv_out)).astype(bf16)
    keyval = jnp.concatenate([keyval, other_half(keyval)], axis=1)
    keyval = jnp.concatenate([keyval, other_core(keyval)], axis=0)
    keyval_places = (keyval, ring_x(keyval, 1), ring_x(keyval, -1), ring_x(keyval, 2))

    place_block = jnp.stack([lax.rem(x + p, 4) for p in PLACES]) // 2
    own = place_block[:, None] <= place_block[None, :]
    bias = jnp.concatenate([own, jnp.broadcast_to(zh == 1, (4, 4))], axis=0)
    bias = jnp.repeat(jnp.where(bias, 0.0, -1e30).astype(f32), ROWS, axis=1)

    group = (2, 4 * ROWS)
    row_scratch = pltpu.VMEM((2, 4 * ROWS, MODEL_WIDTH), bf16)
    w_scratch = pltpu.VMEM((MODEL_WIDTH, 768), bf16)
    inner_one, query, keyval_all, log_total, attended, *out_parts = call(
        attention_kernel,
        2,
        at,
        [
            *flat(normed_places),
            *[(piece, ANY) for piece in keyval_places],
            (w, ANY),
            (q_in, None),
            (q_out, None),
            (o_in, None),
            (q_bias, None),
            (bias, None),
        ],
        [
            ((*group, RIDE), bf16, step_block((4 * ROWS, RIDE))),
            ((*group, 256), bf16, step_block((4 * ROWS, 256))),
            ((2, 8, ROWS, 256), bf16, step_block((8, ROWS, 256))),
            ((2, 2, 4 * ROWS), f32, step_block((2, 4 * ROWS))),
            ((*group, 256), bf16, step_block((4 * ROWS, 256))),
            *part_outs(MODEL_WIDTH + RIDE),
        ],
        [row_scratch, pltpu.VMEM((2, 8, ROWS, 256), bf16), w_scratch, dma(3)],
        "attention",
        9000000000,
    )
    out_sum = scatter_row(out_parts[:4], out_parts[4:])
    output_inner = out_sum[:, MODEL_WIDTH:].astype(bf16)
    middle = (
        input_rows
        + out_sum[:, :MODEL_WIDTH]
        + attention_output_bias.astype(f32)
        + dot(output_inner, o_out)
    )
    normed_two = layer_norm(middle, gain_two, shift_two).astype(bf16)
    place_scratch = pltpu.VMEM((4, 2 * ROWS, MODEL_WIDTH), bf16)
    feed_scratch = pltpu.VMEM((16, ROWS, 1024), bf16)
    inner_two, pre, act, *down_parts = call(
        feed_kernel,
        4,
        at,
        [
            *flat(gather_row(normed_two)),
            (feed, ANY),
            (u_in, None),
            (u_out, None),
            (d_in, None),
            (u_bias, None),
        ],
        [
            ((4, 2 * ROWS, RIDE), bf16, step_block((2 * ROWS, RIDE))),
            ((4, 2 * ROWS, 1024), f32, step_block((2 * ROWS, 1024))),
            ((4, 2 * ROWS, 1024), bf16, step_block((2 * ROWS, 1024))),
            *part_outs(MODEL_WIDTH + RIDE),
        ],
        [place_scratch, feed_scratch, feed_scratch, dma(6)],
        "feed",
        9500000000,
    )
    down_sum = scatter_row(down_parts[:4], down_parts[4:])
    down_inner = down_sum[:, MODEL_WIDTH:].astype(bf16)
    layer_output = (
        middle
        + down_sum[:, :MODEL_WIDTH]
        + down_projection_bias.astype(f32)
        + dot(down_inner, d_out)
    ).astype(bf16)

    up_b, down_a, *up_parts = call(
        feed_back_kernel,
        4,
        at,
        [
            (cot_all, ANY),
            (feed, ANY),
            (pre, step_block((2 * ROWS, 1024))),
            (act, step_block((2 * ROWS, 1024))),
            (inner_two, step_block((2 * ROWS, RIDE))),
            (d_out, None),
            (d_in, None),
            (u_out, None),
        ],
        [((32, 1024), f32, None), ((32, 1024), f32, None), *part_outs(MODEL_WIDTH + RIDE)],
        [place_scratch, feed_scratch, feed_scratch, dma(6)],
        "feed_back",
        9500000000,
    )
    up_sum = scatter_row(up_parts[:4], up_parts[4:])
    up_back = up_sum[:, MODEL_WIDTH:].astype(bf16)
    grad_normed_two = up_sum[:, :MODEL_WIDTH] + dot(up_back, u_in)
    _, norm_two_back = jax.vjp(lambda v: layer_norm(v, gain_two, shift_two), middle)
    grad_middle = cotangent.astype(f32) + norm_two_back(grad_normed_two)[0]
    grad_branch = grad_middle.astype(bf16)

    query_b, output_a, *query_parts = call(
        attention_back_kernel,
        2,
        at,
        [
            *flat(gather_row(grad_branch)),
            (w, ANY),
            (inner_one, step_block((4 * ROWS, RIDE))),
            (query, step_block((4 * ROWS, 256))),
            (keyval_all, step_block((8, ROWS, 256))),
            (log_total, step_block((2, 4 * ROWS))),
            (attended, step_block((4 * ROWS, 256))),
            (o_out, None),
            (o_in, None),
            (q_out, None),
            (bias, None),
        ],
        [((32, 256), f32, None), ((32, 256), f32, None), *part_outs(2688)],
        [
            row_scratch,
            w_scratch,
            pltpu.VMEM((8 * ROWS, HEAD_WIDTH), f32),
            pltpu.VMEM((8 * ROWS, HEAD_WIDTH), f32),
            dma(2),
        ],
        "attention_back",
        8000000000,
    )
    query_sum = scatter_row(query_parts[:4], query_parts[4:])
    grad_keyval = (
        query_sum[:, 2048:2304] + other_half(query_sum[:, 2304:2560].astype(bf16)).astype(f32)
    ).astype(bf16)
    query_back = query_sum[:, 2560:].astype(bf16)
    keyval_back = dot_t(grad_keyval, kv_out).astype(bf16)
    grad_normed = (
        query_sum[:, :MODEL_WIDTH]
        + dot(query_back, q_in)
        + dot_t(grad_keyval, w[:, 256:512])
        + dot_t(keyval_back, kv_in)
    )
    _, norm_one_back = jax.vjp(lambda v: layer_norm(v, gain_one, shift_one), input_rows)
    grad_tokens = (grad_middle + norm_one_back(grad_normed)[0]).astype(bf16)

    def ridden(back, rows):
        piece = tdot(back, rows)
        return piece[:16] + piece[16:32]

    def sliced(piece):
        return piece.reshape(16, 2, 4, -1).transpose(1, 2, 0, 3)

    def joined(*pieces):
        return jnp.concatenate([p.astype(bf16) for p in pieces], axis=-1)

    early = gather_sequences(own_slice(jnp.concatenate([up_b, down_a], axis=1), zh), zh, x)
    up_b, down_a = finish(early, all_ids, (1024, 1024))
    middle_set = joined(
        scatter_sequence(
            jnp.concatenate(
                [
                    sliced(ridden(up_back, normed_two)),
                    sliced(ridden(down_inner, cotangent)),
                    sliced(ridden(output_inner, grad_branch)),
                ],
                axis=-1,
            ),
            zh,
            x,
        ),
        own_slice(output_a, zh),
    )
    up_a, down_b, output_b, output_a = finish(
        gather_sequences(middle_set, zh, x), all_ids, (256, 256, 256, 256)
    )
    keyval_b = tdot(keyval_inner, grad_keyval).reshape(2, 4, 16, 32)
    late_set = joined(
        scatter_sequence(
            jnp.concatenate(
                [
                    sliced(ridden(query_back, normed)),
                    sliced(tdot(keyval_back, normed)),
                    jnp.pad(keyval_b, ((0, 0), (0, 0), (0, 0), (0, 96))),
                ],
                axis=-1,
            ),
            zh,
            x,
        ),
        own_slice(query_b, zh),
    )
    query_a, keyval_a, keyval_b, query_b = finish(
        gather_sequences(late_set, zh, x), all_ids, (256, 256, 128, 256)
    )
    keyval_b = keyval_b.reshape(8, 16, 8, 128)[..., :32].transpose(0, 2, 1, 3).reshape(8, 16, 256)

    def side_in(a):
        return jnp.swapaxes(a, 1, 2)

    return (
        layer_output,
        grad_tokens,
        side_in(query_a),
        query_b,
        side_in(keyval_a),
        keyval_b,
        side_in(output_a),
        output_b,
        side_in(up_a),
        up_b,
        side_in(down_a),
        down_b,
    )

def solution(mesh):
    fine = Mesh(mesh.devices.reshape(SIZES), AXES)
    in_specs = (
        P(AXES, None),
        P(AXES, None),
        P(),
        P(),
        P(DP, MP),
        P(MP),
        P(DP, None),
        P(),
        P(MP, DP),
        P(),
        P(),
        P(),
        P(DP, MP),
        P(MP),
        P(MP, DP),
        P(),
        P(DP, None),
        P(),
        P(None, None, MP),
        P(),
        P(),
        P(None, MP, None),
        P(),
        P(),
        P(None, None, MP),
        P(None, MP, None),
        P(),
    )
    out_specs = (P(AXES, None), P(AXES, None)) + (P(),) * 10
    return jax.shard_map(shards, mesh=fine, in_specs=in_specs, out_specs=out_specs, check_vma=False)
```

time: 771 us -> 584 us (0.76)
  local copies, waits for them, and re-layouts: 220 us -> 33.9 us
  Pallas kernels: 0 us -> 130 us
  waiting for transfers between devices: 262 us -> 167 us
  matrix products: 75.7 us -> 15.2 us
  starting transfers between devices: 119 us -> 171 us
  other arithmetic: 60.1 us -> 32 us
    psum x1 -> x0, waiting for transfers between devices: 153 us -> none  [shards(): rest_grads = lax.psum(rest_grads, AXES).astype(f32)]
    pallas_call x0 -> x9, Pallas kernels: none -> 130 us  [the longest x6 104 us: call(): pl.pallas_call(kernel, out_shape=[jax.ShapeDtypeStruct(s, d) for s, d, _...]
    dot_general x30 -> x0, matrix products: 62.9 us -> none  [the longest x1 8.06 us: shards(): jnp.einsum('stn,nw->stw', cot_seq, w_down, preferred_element_type=f32)]
    unnamed x174 -> x228, local copies, waits for them, and re-layouts: 58.8 us -> 13.2 us
    reshape x3 -> x13, local copies, waits for them, and re-layouts: 42.4 us -> 5.15 us  [the longest x10 3.56 us: sliced(): return piece.reshape(16, 2, 4, -1).transpose(1, 2, 0, 3)]
    concatenate x10 -> x2, local copies, waits for them, and re-layouts: 36.5 us -> 0.09 us  [the longest x1 0.08 us: padded(): jnp.concatenate([pair, jnp.zeros((RIDE - 32, pair.shape[1]), bf16)], axis=0)]
    ppermute x2 -> x5, starting transfers between devices: 7.31 us -> 42.1 us  [turn(): return lax.ppermute(a, ('core', 'zh'), [(0, 0), (1, 2), (2, 1), (3, 3)])]
    ppermute x32 -> x46, waiting for transfers between devices: 76.2 us -> 104 us  [ring_x(): return lax.ppermute(a, 'x', [(i, (i + step) % 4) for i in range(4)])]
  transfers between devices with their start and end apart: 76 -> 115, of which waited for: 32 -> 49; matrix products, arithmetic and copies ran while one was open for 18% -> 11% of each run, Pallas kernels for 0% -> 16%
where the time goes in v2:
time: 584 us; the launch traced here: 574 us
  starting transfers between devices  171 us (29%)
  waiting for transfers between devices  167 us (29%)
  Pallas kernels  130 us (22%)
  local copies, waits for them, and re-layouts  33.9 us (6%)
  other arithmetic  32 us (5%)
  between operations  18.6 us (3%)
  matrix products  15.2 us (3%)
  blocking collectives  6 us (1%)
    pallas_call x6, Pallas kernels, call(): pl.pallas_call(kernel, out_shape=[jax.ShapeDtypeStruct(s, d) for s, d, _...  104 us
    ppermute x46, waiting for transfers between devices, ring_x(): return lax.ppermute(a, 'x', [(i, (i + step) % 4) for i in range(4)])  104 us
    ppermute x46, starting transfers between devices, ring_x(): return lax.ppermute(a, 'x', [(i, (i + step) % 4) for i in range(4)])  63 us
    ppermute x5, starting transfers between devices, turn(): return lax.ppermute(a, ('core', 'zh'), [(0, 0), (1, 2), (2, 1), (3, 3)])  42.1 us
    ppermute x33, starting transfers between devices, other_core(): return lax.ppermute(a, 'core', [(0, 1), (1, 0)])  41 us
    pallas_call x3, Pallas kernels, finish(): pl.pallas_call(functools.partial(finish_kernel, widths), out_shape=[jax.S...  25.2 us
    all_gather x3, waiting for transfers between devices, gather_sequences(): return lax.all_gather(row, DP, axis=0)  24.6 us
    ppermute x10, waiting for transfers between devices, other_half(): return lax.ppermute(a, 'zh', [(0, 1), (1, 0)])  21.3 us
  transfers between devices with their start and end apart: 115, of which 49 were waited for; matrix products, arithmetic and copies ran while one was open for 11% of the time, Pallas kernels for 16%

profile of v2, /device:TPU:1, one launch (start us, length us, event | category | flops | bytes accessed | tf_op | source)
XLA Modules:
  0.0 573.7 jit_solution(10919434711979758193)
XLA Ops:
  14.6 5.7 collective-permute-start.9
  45.6 6.1 %collective-permute-done.14.refs_1_ = bf16[4,64,768]{2,1,0:T(8,128)(2,1)S(1)} collective-permute-done((bf16[4,64,768]{2,1,0:T(8,128)(2,1)S(1)}, bf16[4,64,768]{2,1,0:T(8,128)(2,1)S(1)}, u32[]{:S(2)}, u32[]{:S(2)}) %collective-permute-start.14) | collective-permute-done | bytes 393248 | tf_op jit(solution)/shard_map/ppermute | solution.py:42
  63.9 6.8 %collective-permute-start.32 = (bf16[48,2560]{1,0:T(8,128)(2,1)S(1)}, bf16[48,2560]{1,0:T(8,128)(2,1)S(1)}, u32[]{:S(2)}, u32[]{:S(2)}) collective-permute-start(bf16[48,2560]{1,0:T(8,128)(2,1)S(1)} %maximum_maximum_fusion.4), channel_id=1, source_target_pairs={{0,0},{4,8},{8,4},{12,12},{1,1},{5,9},{9,5},{13,13},{2,2},{6,10},{... | collective-permute-start | bytes 737288 | tf_op jit(solution)/shard_map/ppermute | solution.py:54
  104.8 19.9 %attention.1 = (bf16[2,512,128]{2,1,0:T(8,128)(2,1)}, bf16[2,512,256]{2,1,0:T(8,128)(2,1)}, bf16[2,8,128,256]{3,2,1,0:T(8,128)(2,1)}, f32[2,2,512]{2,1,0:T(2,128...) custom-call(s32[5]{0:T(128)} %stack.167.at, ...), custom_call_target="tpu_custom_call" | custom-call | flops 8999999488 | bytes 22701056 | tf_op jit(solution)/shard_map/attention/pallas_call | solution.py:487
  132.3 4.9 collective-permute-done.39
  141.5 9.4 %collective-permute-done.40 = bf16[128,2176]{1,0:T(8,128)(2,1)S(1)} collective-permute-done((bf16[128,2176]{1,0:T(8,128)(2,1)S(1)}, bf16[128,2176]{1,0:T(8,128)(2,1)S(1)}, u32[]{:S(2)}, u32[]{:S(2)}) %collective-permute-start.40) | collective-permute-done | bytes 557088 | tf_op jit(solution)/shard_map/ppermute | solution.py:34
  161.0 9.5 %collective-permute-done.42.refs_2_ = bf16[128,2048]{1,0:T(8,128)(2,1)S(1)} collective-permute-done((bf16[128,2048]{1,0:T(8,128)(2,1)S(1)}, bf16[128,2048]{1,0:T(8,128)(2,1)S(1)}, u32[]{:S(2)}, u32[]{:S(2)}) %collective-permute-start.42) | collective-permute-done | bytes 524320 | tf_op jit(solution)/shard_map/ppermute | solution.py:34
  174.3 9.0 %collective-permute-start.41 = (bf16[128,2048]{1,0:T(8,128)(2,1)S(1)}, bf16[128,2048]{1,0:T(8,128)(2,1)S(1)}, u32[]{:S(2)}, u32[]{:S(2)}) collective-permute-start(bf16[128,2048]{1,0:T(8,128)(2,1)S(1)} %add_convert_fusion.5.refs_0_), channel_id=1, source_target_pairs={{0,8},{8,0},{1,9},{9,1},{2,10},{10,2},{3,11},{11,3},{4,12},{12,4},... | collective-permute-start | bytes 1572872 | tf_op jit(solution)/shard_map/ppermute | solution.py:46
  196.3 21.7 %feed.1 = (bf16[4,256,128]{2,1,0:T(8,128)(2,1)}, f32[4,256,1024]{2,1,0:T(8,128)}, bf16[4,256,1024]{2,1,0:T(8,128)(2,1)}, bf16[128,2176]{1,0:T(8,128)(2,1)}, bf16...) custom-call(s32[5]{0:T(128)} %stack.167.at, ...), custom_call_target="tpu_custom_call" | custom-call | flops 9500000256 | bytes 39849984 | tf_op jit(solution)/shard_map/feed/pallas_call | solution.py:487
  236.8 31.9 %feed_back.1 = (f32[32,1024]{1,0:T(8,128)}, f32[32,1024]{1,0:T(8,128)}, bf16[128,2176]{1,0:T(8,128)(2,1)}, bf16[128,2176]{1,0:T(8,128)(2,1)}, bf16[128,2176]{1,0...) custom-call(s32[5]{0:T(128)} %stack.167.at, ...), custom_call_target="tpu_custom_call" | custom-call | flops 9500000256 | bytes 37748736 | tf_op jit(solution)/shard_map/feed_back/pallas_call | solution.py:487
  287.4 8.8 %collective-permute-done.65 = bf16[128,2176]{1,0:T(8,128)(2,1)} collective-permute-done((bf16[128,2176]{1,0:T(8,128)(2,1)}, bf16[128,2176]{1,0:T(8,128)(2,1)}, u32[]{:S(2)}, u32[]{:S(2)}) %collective-permute-start.65) | collective-permute-done | bytes 557088 | tf_op jit(solution)/shard_map/ppermute | solution.py:34
  333.5 23.9 %attention_back.1 = (f32[32,256]{1,0:T(8,128)}, f32[32,256]{1,0:T(8,128)}, bf16[128,2688]{1,0:T(8,128)(2,1)}, bf16[128,2688]{1,0:T(8,128)(2,1)}, bf16[128,2688]{...) custom-call(s32[5]{0:T(128)} %stack.167.at, ...), custom_call_target="tpu_custom_call" | custom-call | flops 8000000000 | bytes 21454848 | tf_op jit(solution)/shard_map/attention_back/pallas_call | solution.py:487
  363.0 5.9 %collective-permute-start.99 = (bf16[16,256]{1,0:T(8,128)(2,1)S(1)}, bf16[16,256]{1,0:T(8,128)(2,1)S(1)}, u32[]{:S(2)}, u32[]{:S(2)}) collective-permute-start(bf16[16,256]{1,0:T(8,128)(2,1)S(1)} %add_convert_fusion.7), channel_id=1, source_target_pairs={{0,0},{4,8},{8,4},{12,12},{1,1},{5,9},{9,5},{13,13},{2,2},{6,10},{... | collective-permute-start | bytes 24584 | tf_op jit(solution)/shard_map/ppermute | solution.py:54
  402.8 8.4 %collective-permute-done.82 = bf16[128,2688]{1,0:T(8,128)(2,1)S(1)} collective-permute-done((bf16[128,2688]{1,0:T(8,128)(2,1)S(1)}, bf16[128,2688]{1,0:T(8,128)(2,1)S(1)}, u32[]{:S(2)}, u32[]{:S(2)}) %collective-permute-start.82) | collective-permute-done | bytes 688160 | tf_op jit(solution)/shard_map/ppermute | solution.py:34
  411.1 5.3 collective-permute-done.79
  436.7 14.8 %collective-permute-start.89 = (bf16[16,256]{1,0:T(8,128)(2,1)S(1)}, bf16[16,256]{1,0:T(8,128)(2,1)S(1)}, u32[]{:S(2)}, u32[]{:S(2)}) collective-permute-start(bf16[16,256]{1,0:T(8,128)(2,1)S(1)} %add_convert_fusion.8), channel_id=1, source_target_pairs={{0,0},{4,8},{8,4},{12,12},{1,1},{5,9},{9,5},{13,13},{2,2},{6,10},{... | collective-permute-start | bytes 24584 | tf_op jit(solution)/shard_map/ppermute | solution.py:54
  465.8 4.6 collective-permute-done.104
  470.4 8.9 %collective-permute-start.105 = (bf16[16,2048]{1,0:T(8,128)(2,1)S(1)}, bf16[16,2048]{1,0:T(8,128)(2,1)S(1)}, u32[]{:S(2)}, u32[]{:S(2)}) collective-permute-start(bf16[16,2048]{1,0:T(8,128)(2,1)S(1)} %add_convert_fusion.6), channel_id=1, source_target_pairs={{0,0},{4,8},{8,4},{12,12},{1,1},{5,9},{9,5},{13,13},{2,2},{6,10},{... | collective-permute-start | bytes 196616 | tf_op jit(solution)/shard_map/ppermute | solution.py:54
  481.7 5.0 collective-permute-done.106
  500.5 6.0 %all-reduce.4.ids = s32[16]{0:T(128)} all-reduce(s32[16]{0:T(128)S(1)} %bitcast_dynamic-update-slice_fusion.18), channel_id=1, replica_groups=mesh['y'=4,'zl'=2,'core'=2,'zh'=2,'x'=4] {'y','zl','core'}, use_global_device_ids=true, to_apply=%add.4 | all-reduce | flops 16 | bytes 128 | tf_op jit(solution)/shard_map/squeeze | solution.py:598
  514.8 7.7 %finish.4 = (f32[8,16,2048]{2,1,0:T(8,128)}, f32[8,16,2048]{2,1,0:T(8,128)}, f32[8,16,2048]{2,1,0:T(8,128)}, f32[8,16,2048]{2,1,0:T(8,128)}) custom-call(s32[16]{0:T(128)} %all-reduce.4.ids, bf16[16,4,2,16,1024]{4,3,2,1,0:T(8,128)(2,1)} %bitcast.222), custom_call_target="tpu_custom_call" | custom-call | tf_op jit(solution)/shard_map/finish/pallas_call | solution.py:522
  522.4 7.4 %finish.3 = (f32[8,16,2048]{2,1,0:T(8,128)}, f32[8,16,2048]{2,1,0:T(8,128)}, f32[8,16,1024]{2,1,0:T(8,128)}, f32[8,16,2048]{2,1,0:T(8,128)}) custom-call(s32[16]{0:T(128)} %all-reduce.4.ids, bf16[16,4,2,16,896]{4,3,2,1,0:T(8,128)(2,1)} %bitcast.223), custom_call_target="tpu_custom_call" | custom-call | tf_op jit(solution)/shard_map/finish/pallas_call | solution.py:522
  532.0 24.6 %all-gather.17.cloned.1.call-done = bf16[64,2,16,2048]{3,2,1,0:T(8,128)(2,1)} async-done(((bf16[4,2,16,2048]{3,2,1,0:T(8,128)(2,1)}), bf16[64,2,16,2048]{3,2,1,0:T(8,128)(2,1)}) %all-gather.17.cloned.1.call-update) | async-done | bytes 8388624 | tf_op jit(solution)/shard_map/all_gather | solution.py:126
  556.6 10.1 %finish.5 = (f32[8,16,8192]{2,1,0:T(8,128)}, f32[8,16,8192]{2,1,0:T(8,128)}) custom-call(s32[16]{0:T(128)} %all-reduce.4.ids, bf16[16,4,2,16,2048]{4,3,2,1,0:T(8,128)(2,1)} %bitcast.221), custom_call_target="tpu_custom_call" | custom-call | tf_op jit(solution)/shard_map/finish/pallas_call | solution.py:522
  (637 shorter events, 288.9 us)
Async XLA Ops:
  7.2 153.7 %all-gather.9.cloned.1.call-start = ((), (), s32[]{:S(2)}) async-start(), calls=%async_computation | async-start | bytes 17301504 | tf_op jit(solution)/shard_map/all_gather | solution.py:593
  10.7 226.0 %all-gather.11.cloned.1.call-start = ((), (), s32[]{:S(2)}) async-start(), calls=%async_computation.1 | async-start | bytes 4718592 | tf_op jit(solution)/shard_map/all_gather | solution.py:596
  13.2 43.8 %collective-permute-start.1 = (bf16[128,2048]{1,0:T(8,128)(2,1)S(1)}, bf16[128,2048]{1,0:T(8,128)(2,1)S(1)}, u32[]{:S(2)}, u32[]{:S(2)}) collective-permute-start(bf16[128,2048]{1,0:T(8,128)(2,1)S(1)} %fusion.9.refs_0_), channel_id=1, source_target_pairs={{0,1},{1,2},{2,3},{3,0},{4,5},{5,6},{6,7},{7,4},{8,9},{9,10},{10,1... | collective-permute-start | bytes 1572872 | tf_op jit(solution)/shard_map/ppermute | solution.py:34
  41.9 15.0 %collective-permute-start.23 = (bf16[4,64,768]{2,1,0:T(8,128)(2,1)S(1)}, bf16[4,64,768]{2,1,0:T(8,128)(2,1)S(1)}, u32[]{:S(2)}, u32[]{:S(2)}) collective-permute-start(bf16[4,64,768]{2,1,0:T(8,128)(2,1)S(1)} %pad_maximum_fusion.9.refs_5_), channel_id=1, source_target_pairs={{0,96},{32,0},{64,32},{96,64},{1,97},{33,1},{65,33},{97,65},{2,98}... | collective-permute-start | bytes 1179656 | tf_op jit(solution)/shard_map/ppermute | solution.py:38
  51.7 27.3 %collective-permute-start.3 = (bf16[128,2048]{1,0:T(8,128)(2,1)S(1)}, bf16[128,2048]{1,0:T(8,128)(2,1)S(1)}, u32[]{:S(2)}, u32[]{:S(2)}) collective-permute-start(bf16[128,2048]{1,0:T(8,128)(2,1)S(1)} %fusion.9.refs_0_), channel_id=1, source_target_pairs={{0,3},{1,0},{2,1},{3,2},{4,7},{5,4},{6,5},{7,6},{8,11},{9,8},{10,9... | collective-permute-start | bytes 1572872 | tf_op jit(solution)/shard_map/ppermute | solution.py:34
  61.3 26.6 %collective-permute-start = (bf16[128,2048]{1,0:T(8,128)(2,1)S(1)}, bf16[128,2048]{1,0:T(8,128)(2,1)S(1)}, u32[]{:S(2)}, u32[]{:S(2)}) collective-permute-start(bf16[128,2048]{1,0:T(8,128)(2,1)S(1)} %fusion.9.refs_0_), channel_id=1, source_target_pairs={{0,8},{8,0},{1,9},{9,1},{2,10},{10,2},{3,11},{11,3},{4,12},{12,4},... | collective-permute-start | bytes 1572872 | tf_op jit(solution)/shard_map/ppermute | solution.py:46
  63.9 19.4 %collective-permute-start.32 = (bf16[48,2560]{1,0:T(8,128)(2,1)S(1)}, bf16[48,2560]{1,0:T(8,128)(2,1)S(1)}, u32[]{:S(2)}, u32[]{:S(2)}) collective-permute-start(bf16[48,2560]{1,0:T(8,128)(2,1)S(1)} %maximum_maximum_fusion.4), channel_id=1, source_target_pairs={{0,0},{4,8},{8,4},{12,12},{1,1},{5,9},{9,5},{13,13},{2,2},{6,10},{... | collective-permute-start | bytes 737288 | tf_op jit(solution)/shard_map/ppermute | solution.py:54
  161.0 353.8 %all-gather.15.cloned.1.call-start = ((), (), s32[]{:S(2)}) async-start(), calls=%async_computation.3 | async-start | bytes 4456448 | tf_op jit(solution)/shard_map/all_gather | solution.py:126
  171.7 16.9 %collective-permute-start.47 = (bf16[64,2048]{1,0:T(8,128)(2,1)S(1)}, bf16[64,2048]{1,0:T(8,128)(2,1)S(1)}, u32[]{:S(2)}, u32[]{:S(2)}) collective-permute-start(bf16[64,2048]{1,0:T(8,128)(2,1)S(1)} %slice.376), channel_id=1, source_target_pairs={{0,3},{1,0},{2,1},{3,2},{4,7},{5,4},{6,5},{7,6},{8,11},{9,8},{10,9... | collective-permute-start | bytes 786440 | tf_op jit(solution)/shard_map/ppermute | solution.py:34
  174.3 20.7 %collective-permute-start.41 = (bf16[128,2048]{1,0:T(8,128)(2,1)S(1)}, bf16[128,2048]{1,0:T(8,128)(2,1)S(1)}, u32[]{:S(2)}, u32[]{:S(2)}) collective-permute-start(bf16[128,2048]{1,0:T(8,128)(2,1)S(1)} %add_convert_fusion.5.refs_0_), channel_id=1, source_target_pairs={{0,8},{8,0},{1,9},{9,1},{2,10},{10,2},{3,11},{11,3},{4,12},{12,4},... | collective-permute-start | bytes 1572872 | tf_op jit(solution)/shard_map/ppermute | solution.py:46
  218.7 51.3 %collective-permute-start.50 = (bf16[128,2176]{1,0:T(8,128)(2,1)}, bf16[128,2176]{1,0:T(8,128)(2,1)S(1)}, u32[]{:S(2)}, u32[]{:S(2)}) collective-permute-start(bf16[128,2176]{1,0:T(8,128)(2,1)} %get-tuple-element.81), channel_id=1, source_target_pairs={{0,8},{8,0},{1,9},{9,1},{2,10},{10,2},{3,11},{11,3},{4,12},{12,4},... | collective-permute-start | bytes 1671176 | tf_op jit(solution)/shard_map/ppermute | solution.py:46
  231.9 38.1 %collective-permute-start.57 = (bf16[128,2176]{1,0:T(8,128)(2,1)}, bf16[128,2176]{1,0:T(8,128)(2,1)S(1)}, u32[]{:S(2)}, u32[]{:S(2)}) collective-permute-start(bf16[128,2176]{1,0:T(8,128)(2,1)} %pad_maximum_fusion.5), channel_id=1, source_target_pairs={{0,3},{1,0},{2,1},{3,2},{4,7},{5,4},{6,5},{7,6},{8,11},{9,8},{10,9... | collective-permute-start | bytes 1671176 | tf_op jit(solution)/shard_map/ppermute | solution.py:34
  236.3 33.7 %collective-permute-start.54 = (bf16[128,2176]{1,0:T(8,128)(2,1)}, bf16[128,2176]{1,0:T(8,128)(2,1)}, u32[]{:S(2)}, u32[]{:S(2)}) collective-permute-start(bf16[128,2176]{1,0:T(8,128)(2,1)} %pad_maximum_fusion.4), channel_id=1, source_target_pairs={{0,1},{1,2},{2,3},{3,0},{4,5},{5,6},{6,7},{7,4},{8,9},{9,10},{10,1... | collective-permute-start | bytes 1671176 | tf_op jit(solution)/shard_map/ppermute | solution.py:34
  272.1 15.4 %collective-permute-start.58 = (bf16[128,2176]{1,0:T(8,128)(2,1)}, bf16[128,2176]{1,0:T(8,128)(2,1)S(1)}, u32[]{:S(2)}, u32[]{:S(2)}) collective-permute-start(bf16[128,2176]{1,0:T(8,128)(2,1)} %get-tuple-element.93), channel_id=1, source_target_pairs={{0,8},{8,0},{1,9},{9,1},{2,10},{10,2},{3,11},{11,3},{4,12},{12,4},... | collective-permute-start | bytes 1671176 | tf_op jit(solution)/shard_map/ppermute | solution.py:46
  370.3 22.1 %collective-permute-start.80 = (bf16[128,2688]{1,0:T(8,128)(2,1)}, bf16[128,2688]{1,0:T(8,128)(2,1)}, u32[]{:S(2)}, u32[]{:S(2)}) collective-permute-start(bf16[128,2688]{1,0:T(8,128)(2,1)} %get-tuple-element.112), channel_id=1, source_target_pairs={{0,8},{8,0},{1,9},{9,1},{2,10},{10,2},{3,11},{11,3},{4,12},{12,4},... | collective-permute-start | bytes 2064392 | tf_op jit(solution)/shard_map/ppermute | solution.py:46
  374.0 15.5 %collective-permute-start.77 = (bf16[128,2688]{1,0:T(8,128)(2,1)}, bf16[128,2688]{1,0:T(8,128)(2,1)}, u32[]{:S(2)}, u32[]{:S(2)}) collective-permute-start(bf16[128,2688]{1,0:T(8,128)(2,1)} %get-tuple-element.110), channel_id=1, source_target_pairs={{0,8},{8,0},{1,9},{9,1},{2,10},{10,2},{3,11},{11,3},{4,12},{12,4},... | collective-permute-start | bytes 2064392 | tf_op jit(solution)/shard_map/ppermute | solution.py:46
  374.0 19.8 %collective-permute-start.76 = (bf16[128,2688]{1,0:T(8,128)(2,1)}, bf16[128,2688]{1,0:T(8,128)(2,1)}, u32[]{:S(2)}, u32[]{:S(2)}) collective-permute-start(bf16[128,2688]{1,0:T(8,128)(2,1)} %get-tuple-element.108), channel_id=1, source_target_pairs={{0,8},{8,0},{1,9},{9,1},{2,10},{10,2},{3,11},{11,3},{4,12},{12,4},... | collective-permute-start | bytes 2064392 | tf_op jit(solution)/shard_map/ppermute | solution.py:46
  374.5 28.3 %collective-permute-start.75 = (bf16[128,2688]{1,0:T(8,128)(2,1)}, bf16[128,2688]{1,0:T(8,128)(2,1)}, u32[]{:S(2)}, u32[]{:S(2)}) collective-permute-start(bf16[128,2688]{1,0:T(8,128)(2,1)} %get-tuple-element.106), channel_id=1, source_target_pairs={{0,8},{8,0},{1,9},{9,1},{2,10},{10,2},{3,11},{11,3},{4,12},{12,4},... | collective-permute-start | bytes 2064392 | tf_op jit(solution)/shard_map/ppermute | solution.py:46
  389.4 133.1 %all-gather.13.cloned.1.call-start = ((), (), s32[]{:S(2)}) async-start(), calls=%async_computation.2 | async-start | bytes 3899392 | tf_op jit(solution)/shard_map/all_gather | solution.py:126
  435.1 16.5 %collective-permute-start.87 = (bf16[16,640]{1,0:T(8,128)(2,1)S(1)}, bf16[16,640]{1,0:T(8,128)(2,1)S(1)}, u32[]{:S(2)}, u32[]{:S(2)}) collective-permute-start(bf16[16,640]{1,0:T(8,128)(2,1)S(1)} %get-tuple-element.168), channel_id=1, source_target_pairs={{0,2},{1,3},{2,0},{3,1},{4,6},{5,7},{6,4},{7,5},{8,10},{9,11},{10,... | collective-permute-start | bytes 61448 | tf_op jit(solution)/shard_map/ppermute | solution.py:34
  435.2 16.4 %collective-permute-start.86 = (bf16[16,640]{1,0:T(8,128)(2,1)S(1)}, bf16[16,640]{1,0:T(8,128)(2,1)S(1)}, u32[]{:S(2)}, u32[]{:S(2)}) collective-permute-start(bf16[16,640]{1,0:T(8,128)(2,1)S(1)} %get-tuple-element.169), channel_id=1, source_target_pairs={{0,3},{1,0},{2,1},{3,2},{4,7},{5,4},{6,5},{7,6},{8,11},{9,8},{10,9... | collective-permute-start | bytes 61448 | tf_op jit(solution)/shard_map/ppermute | solution.py:34
  436.2 15.4 %collective-permute-start.85 = (bf16[16,640]{1,0:T(8,128)(2,1)S(1)}, bf16[16,640]{1,0:T(8,128)(2,1)S(1)}, u32[]{:S(2)}, u32[]{:S(2)}) collective-permute-start(bf16[16,640]{1,0:T(8,128)(2,1)S(1)} %get-tuple-element.167), channel_id=1, source_target_pairs={{0,1},{1,2},{2,3},{3,0},{4,5},{5,6},{6,7},{7,4},{8,9},{9,10},{10,1... | collective-permute-start | bytes 61448 | tf_op jit(solution)/shard_map/ppermute | solution.py:34
  436.7 16.1 %collective-permute-start.89 = (bf16[16,256]{1,0:T(8,128)(2,1)S(1)}, bf16[16,256]{1,0:T(8,128)(2,1)S(1)}, u32[]{:S(2)}, u32[]{:S(2)}) collective-permute-start(bf16[16,256]{1,0:T(8,128)(2,1)S(1)} %add_convert_fusion.8), channel_id=1, source_target_pairs={{0,0},{4,8},{8,4},{12,12},{1,1},{5,9},{9,5},{13,13},{2,2},{6,10},{... | collective-permute-start | bytes 24584 | tf_op jit(solution)/shard_map/ppermute | solution.py:54
  465.6 91.0 %all-gather.17.cloned.1.call-start = ((), (), s32[]{:S(2)}) async-start(), calls=%async_computation.4 | async-start | bytes 8912896 | tf_op jit(solution)/shard_map/all_gather | solution.py:126
  (195 other events, 1758.5 us)
Sparse Core Ops, SparseCore 0:
  10.8 125.8 all-gather.8
  161.1 36.5 all-gather.10
  389.5 40.0 all-gather.14
  465.7 37.3 all-gather.12
  504.6 51.9 all-gather.16

commit v3 on v2

--- a/solution.py
+++ b/solution.py
@@ -54,76 +54,103 @@
     return lax.ppermute(a, ("core", "zh"), [(0, 0), (1, 2), (2, 1), (3, 3)])
 
 
-def gather_row(a):
+def plane_pairs(step, swapped):
+    def index(y, z, core):
+        return ((y * 2 + z % 2) * 2 + core) * 2 + z // 2
+
+    pairs = []
+    for y in range(4):
+        for z in range(4):
+            for core in range(2):
+                if (core == 0) != swapped:
+                    to = index((y + step) % 4, z, core)
+                else:
+                    to = index(y, (z + step) % 4, core)
+                pairs.append((index(y, z, core), to))
+    return pairs
+
+
+def gather_cross(a, swapped):
+    return [a] + [
+        lax.ppermute(a, ("y", "zl", "core", "zh"), plane_pairs(-step, swapped))
+        for step in (1, 2, 3)
+    ]
+
+
+def gather_sides(a):
+    return a, other_core(a), ring_x(a, 1), ring_x(a, -1)
+
+
+def gather_rest(a, near, left, right):
     half = a.shape[0] // 2
-    left, right = ring_x(a, 1), ring_x(a, -1)
-    near = other_core(a)
     top, bottom = ring_x(left[:half], 1), ring_x(right[half:], -1)
-    left_other, right_other = other_core(left), other_core(right)
     return (
         (a, near),
-        (left, left_other),
-        (right, right_other),
+        (left, other_core(left)),
+        (right, other_core(right)),
         (top, bottom, other_core(top), other_core(bottom)),
     )
 
 
-def scatter_row(mine, theirs):
-    half = mine[0].shape[0] // 2
-    far = mine[3].astype(f32) + other_core(theirs[3]).astype(f32)
-    up = ring_x(far[:half].astype(bf16), 1)
-    down = ring_x(far[half:].astype(bf16), -1)
-    right = mine[2].astype(f32) + other_core(theirs[2]).astype(f32)
-    left = mine[1].astype(f32) + other_core(theirs[1]).astype(f32)
-    near = mine[0].astype(f32) + other_core(theirs[0]).astype(f32)
-    right = jnp.concatenate([right[:half] + up.astype(f32), right[half:]]).astype(bf16)
-    left = jnp.concatenate([left[:half], left[half:] + down.astype(f32)]).astype(bf16)
-    return near + ring_x(right, 1).astype(f32) + ring_x(left, -1).astype(f32)
-
-
-def gather_ring(a, ring):
-    half = a.shape[-2] // 2
-    left, right = ring(a, 1), ring(a, -1)
-    return a, left, right, ring(left[..., :half, :], 1), ring(right[..., half:, :], -1)
-
-
-def stacked_ring(pieces):
-    own, left, right, top, bottom = pieces
-    return jnp.stack([own, right, jnp.concatenate([top, bottom], axis=-2), left])
-
-
-def rolled(blocks, me):
+def gather_row(a):
+    return gather_rest(*gather_sides(a))
+
+
+def add_cores(mine, theirs):
+    return mine.astype(f32) + other_core(theirs).astype(f32)
+
+
+def scatter_row(mine, theirs, far_mine, far_theirs):
+    half = far_mine.shape[0] // 2
+    far = add_cores(far_mine, far_theirs).astype(bf16)
+    up, down = ring_x(far[:half], 1), ring_x(far[half:], -1)
+    near = add_cores(mine, theirs)
+    right = jnp.concatenate([near[2, :half] + up.astype(f32), near[2, half:]]).astype(bf16)
+    left = jnp.concatenate([near[1, :half], near[1, half:] + down.astype(f32)]).astype(bf16)
+    return near[0] + ring_x(right, 1).astype(f32) + ring_x(left, -1).astype(f32)
+
+
+def scatter_start(mine, theirs, far_mine, far_theirs):
+    far = add_cores(far_mine, far_theirs).astype(bf16)
+    near = add_cores(mine, theirs)
+    return near[0], near[1].astype(bf16), near[2].astype(bf16), far
+
+
+def scatter_last(near, left, right, far):
+    parts = (ring_x(left, -1), ring_x(right, 1), ring_x(far, 2))
+    return near + sum(part.astype(f32) for part in parts)
+
+
+def rolled(blocks, me, step=0):
     both = jnp.concatenate([blocks, blocks], axis=0)
-    return lax.dynamic_slice_in_dim(both, lax.rem(4 - me, 4), 4, 0)
-
-
-def own_slice(pair, zh):
-    kept = jnp.where(zh == 0, pair[:16], pair[16:])
-    sent = jnp.where(zh == 0, pair[16:], pair[:16])
-    total = kept + other_half(sent.astype(bf16)).astype(f32)
-    return turn(total.astype(bf16))
-
-
-def scatter_sequence(slices, zh, x):
-    kept = lax.dynamic_index_in_dim(slices, zh, 0, keepdims=False)
-    sent = lax.dynamic_index_in_dim(slices, 1 - zh, 0, keepdims=False)
-    total = kept + other_half(sent.astype(bf16)).astype(f32)
-    both = jnp.concatenate([total, total], axis=0)
-    near = lax.dynamic_slice_in_dim(both, x, 4, 0)
-    low = near.astype(bf16)
+    return lax.dynamic_slice_in_dim(both, lax.rem(me + step, 4), 4, 0)
+
+
+def ring_by_core(a):
+    pairs = [(i, (i + 1) % 4) for i in range(4)] + [(4 + i, 4 + (i + 3) % 4) for i in range(4)]
+    return lax.ppermute(a, ("core", "x"), pairs)
+
+
+def by_core(core, own, other):
+    return jnp.where(
+        core == 0, jnp.concatenate([own, other], -1), jnp.concatenate([other, own], -1)
+    )
+
+
+def row_slice(pair, core):
+    own = jnp.where(core == 0, pair[:16], pair[16:]).astype(bf16)
+    other = jnp.where(core == 0, pair[16:], pair[:16]).astype(bf16)
+    return by_core(core, own, other_core(other))
+
+
+def scatter_sequence(slices):
+    low = slices
     return (
-        near[0]
+        low[0].astype(f32)
         + ring_x(low[1], 1).astype(f32)
         + ring_x(low[3], -1).astype(f32)
         + ring_x(low[2], 2).astype(f32)
-    )
-
-
-def gather_sequences(piece, zh, x):
-    other = other_half(piece)
-    pair = jnp.where(zh == 0, jnp.stack([piece, other]), jnp.stack([other, piece]))
-    row = rolled(jnp.stack([pair, ring_x(pair, -1), ring_x(pair, 2), ring_x(pair, 1)]), x)
-    return lax.all_gather(row, DP, axis=0)
+    ).astype(bf16)
 
 
 def layer_norm(values, gain, shift):
@@ -156,7 +183,8 @@
 
 def lane_owner(rows, row_core):
     lane = lax.broadcasted_iota(jnp.int32, (rows, RIDE), 1)
-    return (lane // ADAPTER_RANK) == row_core
+    owner = lax.rem(lane // ADAPTER_RANK, 2)
+    return jnp.logical_and(owner == row_core, lane < 4 * ADAPTER_RANK)
 
 
 def place_mask(core):
@@ -188,27 +216,23 @@
     return (refs[0:2], refs[2:4], refs[4:6], refs[6:10])
 
 
+def copy_row(gathered, at, target_of, sem_of):
+    core, x = at[0], at[1]
+    for p in range(4):
+        there = lax.rem(x + PLACES[p], 4)
+        copy(gathered.at[core, there], target_of(p, 0), sem_of(p))
+        copy(gathered.at[1 - core, there], target_of(p, 1), sem_of(p))
+
+
 def assemble_kernel(at, *refs):
-    pieces, (out, sem) = refs[:10], refs[10:]
-    y, z = at[3], at[4]
-    half = ROWS // 2
-    for which in range(2):
-        group = pieces[5 * which : 5 * which + 5]
-        for piece, step, first, count in (
-            (group[0], 0, 0, half),
-            (group[1], 3, 0, half),
-            (group[2], 1, 0, half),
-            (group[3], 2, 0, half // 2),
-            (group[4], 2, half // 2, half // 2),
-        ):
-            for k in range(4):
-                if which == 0:
-                    to_y, to_z = lax.rem(y + k, 4), lax.rem(z + step, 4)
-                else:
-                    to_y, to_z = lax.rem(y + step, 4), lax.rem(z + k, 4)
-                shard = (to_y * 2 + lax.rem(to_z, 2)) * 2 + to_z // 2
-                row = pl.multiple_of(shard * ROWS + which * half + first, 32)
-                copy(piece.at[k], out.at[pl.ds(row, count)], sem)
+    pieces, (out, sem) = refs[:4], refs[4:]
+    core, y, z = at[0], at[3], at[4]
+    for far, piece in enumerate(pieces):
+        for near in range(4):
+            to_y = lax.rem(y + jnp.where(core == 0, near, far), 4)
+            to_z = lax.rem(z + jnp.where(core == 0, far, near), 4)
+            shard = (to_y * 2 + lax.rem(to_z, 2)) * 2 + to_z // 2
+            copy(piece.at[near], out.at[pl.ds(pl.multiple_of(shard * ROWS, ROWS), ROWS)], sem)
     wait(out, sem)
 
 
@@ -220,22 +244,93 @@
     feed_out[:, 1024:] = down[...].astype(f32).T.astype(bf16)
 
 
-def finish_kernel(widths, ids, gathered, *outs):
+def sum_kernel(at, *refs):
+    pieces, (out, total) = refs[:-2], refs[-2:]
+    total[...] = jnp.zeros_like(total)
+    count = out.shape[0]
+    row = 1
+    for piece in pieces:
+        for k in range(piece.shape[0]):
+            place = at[row] - at[0]
+            place = jnp.where(jnp.logical_and(place >= 0, place < count), place, count)
+            total[place] += piece[k].astype(f32)
+            row += 1
+    out[...] = total[:count].astype(bf16)
+
+
+def slices_kernel(count, at, *refs):
+    ins, out = refs[: 2 * count], refs[2 * count]
+    x = at[1]
+    for n in range(count):
+        back, rows = ins[2 * n], ins[2 * n + 1]
+        turned = back[...].astype(f32).T
+        turned = (turned[:16] + turned[16:32]).astype(bf16)
+        product = dot(turned, rows[...]).astype(bf16)
+        for to in range(4):
+            place = lax.rem(to + 4 - x, 4)
+            for c in range(2):
+                first = (c * 4 + to) * 256
+                lanes = slice(n * 512 + c * 256, n * 512 + (c + 1) * 256)
+                out[place, :, lanes] = product[:, first : first + 256]
+
+
+def spread(scratch, outs, widths):
+    x, c = pl.program_id(0), pl.program_id(1)
     first = 0
     for out, width in zip(outs, widths):
-        out[...] = jnp.zeros_like(out)
-        for s in range(16):
-            out[ids[s]] += gathered[s, 0, 0, :, first : first + width].astype(f32)
-        first += width
+        if width < 128:
+            out[...] = scratch[x, :, :, first : first + 128].astype(f32)
+            first += 128
+        else:
+            here = pl.ds(pl.multiple_of(first + c * width, 128), width)
+            out[...] = scratch[x, :, :, here].astype(f32)
+            first += 2 * width
+
+
+def feed_spread_kernel(widths, at, *refs):
+    gathered, (scratch, sem) = refs[0], refs[-2:]
+
+    @pl.when((pl.program_id(0) == 0) & (pl.program_id(1) == 0))
+    def _():
+        for c in range(2):
+            for x in range(4):
+                copy(gathered.at[c, x], scratch.at[x, pl.ds(4 * c, 4)], sem)
+        wait(scratch, sem)
+
+    spread(scratch, refs[1:-2], widths)
+
+
+def late_spread_kernel(widths, at, *refs):
+    own, other, near, near_other, far, far_other = refs[:6]
+    scratch, sem = refs[-2:]
+    core, x = at[0], at[1]
+
+    @pl.when((pl.program_id(0) == 0) & (pl.program_id(1) == 0))
+    def _():
+        mine, theirs = pl.ds(4 * core, 4), pl.ds(4 * (1 - core), 4)
+        side = lax.rem(x + jnp.where(core == 0, 3, 1), 4)
+        other_side = lax.rem(x + jnp.where(core == 0, 1, 3), 4)
+        across = lax.rem(x + 2, 4)
+        copy(own, scratch.at[x, mine], sem)
+        copy(other, scratch.at[x, theirs], sem)
+        for part, where in ((0, mine), (1, theirs)):
+            copy(near.at[pl.ds(4 * part, 4)], scratch.at[side, where], sem)
+        for part, where in ((0, theirs), (1, mine)):
+            copy(near_other.at[pl.ds(4 * part, 4)], scratch.at[other_side, where], sem)
+        copy(far, scratch.at[across, mine], sem)
+        copy(far_other, scratch.at[across, theirs], sem)
+        wait(scratch, sem)
+
+    spread(scratch, refs[6:-2], widths)
 
 
 def attention_kernel(at, *refs):
     rows_in = split_pieces(refs[:10])
     kv_in = refs[10:14]
-    w, q_in, q_out, o_in, q_bias, bias = refs[14:20]
-    inner_out, query_out, kv_all, lse_out, att_out = refs[20:25]
-    parts = (refs[25:29], refs[29:33])
-    rows, kvs, ws, sems = refs[33:]
+    w, q_in, q_out, kv_out, o_in, q_bias, kv_bias, bias = refs[14:22]
+    inner_out, query_out, kv_all, lse_out, att_out = refs[22:27]
+    parts, far_parts = refs[27:29], refs[29:31]
+    rows, kvs, ws, sems = refs[31:]
     s = pl.program_id(0)
     core = at[0]
 
@@ -246,12 +341,7 @@
             here = pl.ds(p * ROWS, ROWS)
             copy_place(rows_in[p], rows.at[0, here], rows.at[1, here], sems.at[0])
             for q in range(2):
-                for half in range(2):
-                    copy(
-                        kv_in[p].at[pl.ds(q * ROWS, ROWS), pl.ds(half * 256, 256)],
-                        kvs.at[q, half * 4 + p],
-                        sems.at[1],
-                    )
+                copy(kv_in[p].at[pl.ds(q * ROWS, ROWS)], kvs.at[q, p], sems.at[1])
         wait(rows, sems.at[0])
         wait(ws, sems.at[2])
         wait(kvs, sems.at[1])
@@ -262,7 +352,8 @@
     inner_out[0] = inner
     query = (dot(x, ws[:, :256]) + q_bias[...] + dot(inner, q_out[...])).astype(bf16)
     query_out[0] = query
-    kv = kvs[s]
+    kv_own = (dot(x, ws[:, 256:512]) + kv_bias[...] + dot(inner, kv_out[...])).astype(bf16)
+    kv = jnp.concatenate([kv_own.reshape(4, ROWS, 256), kvs[s]], axis=0)
     kv_all[0] = kv
     keys = kv[:, :, :HEAD_WIDTH].reshape(8 * ROWS, HEAD_WIDTH)
     values_t = kv[:, :, HEAD_WIDTH:].reshape(8 * ROWS, HEAD_WIDTH).astype(f32).T.astype(bf16)
@@ -291,16 +382,32 @@
         def _(which=which):
             for p in range(4):
                 here = slice(p * ROWS, (p + 1) * ROWS)
-                parts[which][p][:, :MODEL_WIDTH] = dot_t(attended[here], ws[:, 512:]).astype(bf16)
-                parts[which][p][:, MODEL_WIDTH:] = low[here]
+                part = parts[which].at[p] if p < 3 else far_parts[which]
+                part[:, :MODEL_WIDTH] = dot_t(attended[here], ws[:, 512:]).astype(bf16)
+                part[:, MODEL_WIDTH:] = low[here]
+
+
+def store_parts(p, parts, far_parts, out, low):
+    for which in range(2):
+        here = slice(which * ROWS, (which + 1) * ROWS)
+
+        @pl.when(p < 3)
+        def _(which=which, here=here):
+            parts[which][0, :, :MODEL_WIDTH] = out[here]
+            parts[which][0, :, MODEL_WIDTH:] = low[here]
+
+        @pl.when(p == 3)
+        def _(which=which, here=here):
+            far_parts[which][:, :MODEL_WIDTH] = out[here]
+            far_parts[which][:, MODEL_WIDTH:] = low[here]
 
 
 def feed_kernel(at, *refs):
     rows_in = split_pieces(refs[:10])
     feed, u_in, u_out, d_in, u_bias = refs[10:15]
     inner_out, pre_out, act_out = refs[15:18]
-    parts = (refs[18:22], refs[22:26])
-    rows, up, down, sems = refs[26:]
+    parts, far_parts = refs[18:20], refs[20:22]
+    rows, up, down, sems = refs[22:]
     p = pl.program_id(0)
     core = at[0]
 
@@ -330,31 +437,23 @@
 
     low = jnp.where(mask, dot_t(act, d_in[...]), 0.0).astype(bf16)
     out = dot_t(act, down[...].reshape(MODEL_WIDTH, 1024)).astype(bf16)
-    for k in range(4):
-
-        @pl.when(p == k)
-        def _(k=k):
-            for which in range(2):
-                here = slice(which * ROWS, (which + 1) * ROWS)
-                parts[which][k][:, :MODEL_WIDTH] = out[here]
-                parts[which][k][:, MODEL_WIDTH:] = low[here]
+    store_parts(p, parts, far_parts, out, low)
 
 
 def feed_back_kernel(at, *refs):
     cot, feed, pre_in, act_in, inner_in, d_out, d_in, u_out = refs[:8]
     up_b, down_a = refs[8:10]
-    parts = (refs[10:14], refs[14:18])
-    rows, up, down, sems = refs[18:]
+    parts, far_parts = refs[10:12], refs[12:14]
+    rows, up, down, sems = refs[14:]
     p = pl.program_id(0)
-    core, x = at[0], at[1]
+    core = at[0]
 
     @pl.when(p == 0)
     def _():
         copy(feed.at[:, core, :, pl.ds(1024, 1024)], down, sems.at[5])
-        for k in range(4):
-            there = lax.rem(x + PLACES[k], 4)
-            copy(cot.at[core, there], rows.at[k, pl.ds(0, ROWS)], sems.at[k])
-            copy(cot.at[1 - core, there], rows.at[k, pl.ds(ROWS, ROWS)], sems.at[k])
+        copy_row(
+            cot, at, lambda k, which: rows.at[k, pl.ds(which * ROWS, ROWS)], lambda k: sems.at[k]
+        )
         copy(feed.at[:, core, :, pl.ds(0, 1024)], up, sems.at[4])
         up_b[...] = jnp.zeros_like(up_b)
         down_a[...] = jnp.zeros_like(down_a)
@@ -385,31 +484,23 @@
         wait(up, sems.at[4])
 
     out = dot_t(grad_pre, up[...].reshape(MODEL_WIDTH, 1024)).astype(bf16)
-    for k in range(4):
-
-        @pl.when(p == k)
-        def _(k=k):
-            for which in range(2):
-                here = slice(which * ROWS, (which + 1) * ROWS)
-                parts[which][k][:, :MODEL_WIDTH] = out[here]
-                parts[which][k][:, MODEL_WIDTH:] = low[here]
+    store_parts(p, parts, far_parts, out, low)
 
 
 def attention_back_kernel(at, *refs):
-    rows_in = split_pieces(refs[:10])
-    w, inner_in, query_in, kv_in, lse_in, att_in, o_out, o_in, q_out, bias = refs[10:20]
-    query_b, output_a = refs[20:22]
-    parts = (refs[22:26], refs[26:30])
-    rows, ws, grad_k, grad_v, sems = refs[30:]
+    branch, w, inner_in, query_in, kv_in, lse_in, att_in, o_out, o_in, q_out, bias = refs[:11]
+    query_b, output_a = refs[11:13]
+    parts, far_parts = refs[13:15], refs[15:17]
+    rows, ws, grad_k, grad_v, sems = refs[17:]
     s = pl.program_id(0)
     core = at[0]
 
     @pl.when(s == 0)
     def _():
         copy(w, ws, sems.at[1])
-        for p in range(4):
-            here = pl.ds(p * ROWS, ROWS)
-            copy_place(rows_in[p], rows.at[0, here], rows.at[1, here], sems.at[0])
+        copy_row(
+            branch, at, lambda p, which: rows.at[which, pl.ds(p * ROWS, ROWS)], lambda p: sems.at[0]
+        )
         query_b[...] = jnp.zeros_like(query_b)
         output_a[...] = jnp.zeros_like(output_a)
         wait(rows, sems.at[0])
@@ -458,7 +549,7 @@
         def _(which=which):
             for p in range(4):
                 here = slice(p * ROWS, (p + 1) * ROWS)
-                part = parts[which][p]
+                part = parts[which].at[p] if p < 3 else far_parts[which]
                 part[:, :2048] = dot_t(grad_query[here], ws[:, :256]).astype(bf16)
                 part[:, 2048:2176] = grad_k[here].astype(bf16)
                 part[:, 2176:2304] = grad_v[here].astype(bf16)
@@ -509,35 +600,67 @@
     return [(piece, ANY) for place in places for piece in place]
 
 
-def part_outs(width):
-    return [((ROWS, width), bf16, None)] * 8
+def part_outs(width, steps=False):
+    block = pl.BlockSpec((1, ROWS, width), lambda i, at: (jnp.minimum(i, 2), 0, 0))
+    near = ((3, ROWS, width), bf16, block if steps else None)
+    return [near, near, ((ROWS, width), bf16, None), ((ROWS, width), bf16, None)]
 
 
 def dma(n):
     return pltpu.SemaphoreType.DMA((n,))
 
 
-def finish(gathered, ids, widths):
-    total = gathered.shape[-1]
+def sum_by_adapter(pieces, first, ids, count):
+    width = pieces[0].shape[-1]
+    block = max(w for w in range(128, 2305, 128) if width % w == 0)
     return pl.pallas_call(
-        functools.partial(finish_kernel, widths),
+        sum_kernel,
+        out_shape=jax.ShapeDtypeStruct((count, ADAPTER_RANK, width), bf16),
+        grid_spec=pltpu.PrefetchScalarGridSpec(
+            num_scalar_prefetch=1,
+            grid=(width // block,),
+            in_specs=[
+                pl.BlockSpec((p.shape[0], ADAPTER_RANK, block), lambda i, at: (0, 0, i))
+                for p in pieces
+            ],
+            out_specs=pl.BlockSpec((count, ADAPTER_RANK, block), lambda i, at: (0, 0, i)),
+            scratch_shapes=[pltpu.VMEM((count + 1, ADAPTER_RANK, block), f32)],
+        ),
+        compiler_params=pltpu.CompilerParams(vmem_limit_bytes=VMEM_LIMIT),
+        name="sum_by_adapter",
+    )(jnp.concatenate([jnp.reshape(first, (1,)), ids]).astype(jnp.int32), *pieces)
+
+
+def spread_out(kernel, at, pieces, widths, name):
+    total = pieces[0].shape[-1]
+    wide = [(w, lambda i, j, at: (0, 0, j * 4 + i)) for w in widths]
+    blocks = [b if b[0] >= 128 else (128, lambda i, j, at: (0, 0, i)) for b in wide]
+    return pl.pallas_call(
+        functools.partial(kernel, widths),
         out_shape=[
-            jax.ShapeDtypeStruct((ADAPTER_COUNT, ADAPTER_RANK, 8 * w), f32) for w in widths
+            jax.ShapeDtypeStruct((ADAPTER_COUNT, ADAPTER_RANK, 8 * w if w >= 128 else 512), f32)
+            for w in widths
         ],
         grid_spec=pltpu.PrefetchScalarGridSpec(
             num_scalar_prefetch=1,
             grid=(4, 2),
-            in_specs=[
-                pl.BlockSpec((16, 1, 1, ADAPTER_RANK, total), lambda i, j, ids: (0, i, j, 0, 0))
-            ],
-            out_specs=[
-                pl.BlockSpec((ADAPTER_COUNT, ADAPTER_RANK, w), lambda i, j, ids: (0, 0, j * 4 + i))
-                for w in widths
+            in_specs=[ANY] * len(pieces),
+            out_specs=[pl.BlockSpec((ADAPTER_COUNT, ADAPTER_RANK, w), m) for w, m in blocks],
+            scratch_shapes=[
+                pltpu.VMEM((4, ADAPTER_COUNT, ADAPTER_RANK, total), bf16),
+                pltpu.SemaphoreType.DMA,
             ],
         ),
         compiler_params=pltpu.CompilerParams(vmem_limit_bytes=VMEM_LIMIT),
-        name="finish",
-    )(ids, gathered)
+        name=name,
+    )(at, *pieces)
+
+
+def slices_of(at, pairs, name):
+    shape = (4, ADAPTER_RANK, 512 * len(pairs))
+    ins = [(a, None) for pair in pairs for a in pair]
+    kernel = functools.partial(slices_kernel, len(pairs))
+    return call(kernel, 1, at, ins, [(shape, bf16, None)], [], name)[0]
 
 
 def shards(
@@ -575,6 +698,8 @@
     gain_one, shift_one = attention_norm_scale.astype(f32), attention_norm_bias.astype(f32)
     gain_two, shift_two = feedforward_norm_scale.astype(f32), feedforward_norm_bias.astype(f32)
 
+    cot_all = lax.all_gather(cotangent, ("core", "x"), axis=0, tiled=True)
+    cot_all = cot_all.reshape(2, 4, ROWS, MODEL_WIDTH)
     attention_shard, feed_shard = call(
         pack_kernel,
         1,
@@ -590,27 +715,26 @@
         [],
         "pack",
     )
-    feed = lax.all_gather(feed_shard, DP + ("zh",), axis=0, tiled=True)
-    feed = feed.reshape(16, 2, ROWS, 2048)
-    late_cotangent, late_ids, _ = lax.optimization_barrier((cotangent, sequence_adapter, feed))
-    cot_all = lax.all_gather(late_cotangent, ("core", "x"), axis=0, tiled=True)
-    cot_all = cot_all.reshape(2, 4, ROWS, MODEL_WIDTH)
-    all_ids = lax.all_gather(late_ids, DP, axis=0, tiled=True)[:, 0]
-
     attention_shard = turn(attention_shard)
-    half = ROWS // 2
-    along_y = stacked_ring(gather_ring(attention_shard[:half], ring_y))
-    along_z = stacked_ring(gather_ring(attention_shard[half:], ring_z))
-    pieces = (*gather_ring(along_y, ring_z), *gather_ring(along_z, ring_y))
+    input_rows = tokens.astype(f32)
+    normed = layer_norm(input_rows, gain_one, shift_one).astype(bf16)
+    column = jnp.stack(gather_cross(attention_shard, False))
+    column, normed = lax.optimization_barrier((column, normed))
+    plane = gather_cross(column, True)
+    plane, normed_sides = lax.optimization_barrier((plane, gather_sides(normed)))
+    normed_places = gather_rest(*normed_sides)
     (w,) = call(
         assemble_kernel,
         1,
         at,
-        [(piece, ANY) for piece in pieces],
+        [(piece, ANY) for piece in plane],
         [((MODEL_WIDTH, 768), bf16, None)],
         [pltpu.SemaphoreType.DMA],
         "assemble",
     )
+    feed_shard, w, cot_all = lax.optimization_barrier((feed_shard, w, cot_all))
+    feed = lax.all_gather(feed_shard, DP + ("zh",), axis=0, tiled=True)
+    feed = feed.reshape(16, 2, ROWS, 2048)
 
     mine = sequence_adapter[0, 0]
     theirs = other_core(sequence_adapter)[0, 0]
@@ -623,8 +747,9 @@
     def ordered_t(stack):
         return ordered(jnp.swapaxes(stack, 1, 2))
 
-    def padded(pair):
-        return jnp.concatenate([pair, jnp.zeros((RIDE - 32, pair.shape[1]), bf16)], axis=0)
+    def padded(*pairs):
+        rest = jnp.zeros((RIDE - 32 * len(pairs), pairs[0].shape[1]), bf16)
+        return jnp.concatenate([*pairs, rest], axis=0)
 
     small = jnp.concatenate(
         [
@@ -652,12 +777,11 @@
         small[:, 512:1536],
         small[:, 1536:],
     )
-    q_in, u_in = padded(ordered_t(query_adapter_input)), padded(ordered_t(up_adapter_input))
+    q_in = padded(ordered_t(query_adapter_input), ordered_t(keyvalue_adapter_input))
+    u_in = padded(ordered_t(up_adapter_input))
+    kv_out_pair = ordered(keyvalue_adapter_output)
+    kv_out_both = padded(jnp.zeros_like(kv_out_pair), kv_out_pair)
     o_out, d_out = padded(ordered(output_adapter_output)), padded(ordered(down_adapter_output))
-
-    input_rows = tokens.astype(f32)
-    normed = layer_norm(input_rows, gain_one, shift_one).astype(bf16)
-    normed_places = gather_row(normed)
 
     kv_in, kv_out = pick(keyvalue_adapter_input, mine), pick(keyvalue_adapter_output, mine)
     keyval_inner = dot(normed, kv_in).astype(bf16)
@@ -665,7 +789,7 @@
         [jnp.zeros((HEAD_WIDTH,), f32), value_projection_bias.astype(f32)]
     )
     keyval = (dot(normed, w[:, 256:512]) + keyval_bias + dot(keyval_inner, kv_out)).astype(bf16)
-    keyval = jnp.concatenate([keyval, other_half(keyval)], axis=1)
+    keyval = other_half(keyval)
     keyval = jnp.concatenate([keyval, other_core(keyval)], axis=0)
     keyval_places = (keyval, ring_x(keyval, 1), ring_x(keyval, -1), ring_x(keyval, 2))
 
@@ -687,8 +811,10 @@
             (w, ANY),
             (q_in, None),
             (q_out, None),
+            (kv_out_both, None),
             (o_in, None),
             (q_bias, None),
+            (keyval_bias[None], None),
             (bias, None),
         ],
         [
@@ -699,11 +825,11 @@
             ((*group, 256), bf16, step_block((4 * ROWS, 256))),
             *part_outs(MODEL_WIDTH + RIDE),
         ],
-        [row_scratch, pltpu.VMEM((2, 8, ROWS, 256), bf16), w_scratch, dma(3)],
+        [row_scratch, pltpu.VMEM((2, 4, ROWS, 256), bf16), w_scratch, dma(3)],
         "attention",
         9000000000,
     )
-    out_sum = scatter_row(out_parts[:4], out_parts[4:])
+    out_sum = scatter_row(*out_parts)
     output_inner = out_sum[:, MODEL_WIDTH:].astype(bf16)
     middle = (
         input_rows
@@ -730,20 +856,15 @@
             ((4, 2 * ROWS, RIDE), bf16, step_block((2 * ROWS, RIDE))),
             ((4, 2 * ROWS, 1024), f32, step_block((2 * ROWS, 1024))),
             ((4, 2 * ROWS, 1024), bf16, step_block((2 * ROWS, 1024))),
-            *part_outs(MODEL_WIDTH + RIDE),
+            *part_outs(MODEL_WIDTH + RIDE, True),
         ],
         [place_scratch, feed_scratch, feed_scratch, dma(6)],
         "feed",
         9500000000,
     )
-    down_sum = scatter_row(down_parts[:4], down_parts[4:])
-    down_inner = down_sum[:, MODEL_WIDTH:].astype(bf16)
-    layer_output = (
-        middle
-        + down_sum[:, :MODEL_WIDTH]
-        + down_projection_bias.astype(f32)
-        + dot(down_inner, d_out)
-    ).astype(bf16)
+    down_low = scatter_start(*down_parts)
+    down_low, act = lax.optimization_barrier((down_low, act))
+    down_moved = (ring_x(down_low[1], -1), ring_x(down_low[2], 1), ring_x(down_low[3], 2))
 
     up_b, down_a, *up_parts = call(
         feed_back_kernel,
@@ -759,24 +880,52 @@
             (d_in, None),
             (u_out, None),
         ],
-        [((32, 1024), f32, None), ((32, 1024), f32, None), *part_outs(MODEL_WIDTH + RIDE)],
+        [((32, 1024), f32, None), ((32, 1024), f32, None), *part_outs(MODEL_WIDTH + RIDE, True)],
         [place_scratch, feed_scratch, feed_scratch, dma(6)],
         "feed_back",
         9500000000,
     )
-    up_sum = scatter_row(up_parts[:4], up_parts[4:])
+    up_parts, down_moved = lax.optimization_barrier((up_parts, down_moved))
+    down_sum = down_low[0] + sum(part.astype(f32) for part in down_moved)
+    up_sum = scatter_row(*up_parts)
     up_back = up_sum[:, MODEL_WIDTH:].astype(bf16)
     grad_normed_two = up_sum[:, :MODEL_WIDTH] + dot(up_back, u_in)
     _, norm_two_back = jax.vjp(lambda v: layer_norm(v, gain_two, shift_two), middle)
     grad_middle = cotangent.astype(f32) + norm_two_back(grad_normed_two)[0]
     grad_branch = grad_middle.astype(bf16)
 
+    down_inner = down_sum[:, MODEL_WIDTH:].astype(bf16)
+    layer_output = (
+        middle
+        + down_sum[:, :MODEL_WIDTH]
+        + down_projection_bias.astype(f32)
+        + dot(down_inner, d_out)
+    ).astype(bf16)
+
+    branch_all = lax.all_gather(grad_branch, ("core", "x"), axis=0, tiled=True)
+    branch_all = branch_all.reshape(2, 4, ROWS, MODEL_WIDTH)
+    feed_set = jnp.concatenate(
+        [
+            row_slice(up_b, core),
+            row_slice(down_a, core),
+            scatter_sequence(
+                slices_of(
+                    at,
+                    [(up_back, normed_two), (output_inner, grad_branch), (down_inner, cotangent)],
+                    "slices",
+                )
+            ),
+            jnp.full((16, RIDE), mine, jnp.int32).astype(bf16),
+        ],
+        axis=-1,
+    )
+    feed_all = lax.all_gather(feed_set, DP + ("zh",), axis=0)
     query_b, output_a, *query_parts = call(
         attention_back_kernel,
         2,
         at,
         [
-            *flat(gather_row(grad_branch)),
+            (branch_all, ANY),
             (w, ANY),
             (inner_one, step_block((4 * ROWS, RIDE))),
             (query, step_block((4 * ROWS, 256))),
@@ -799,12 +948,13 @@
         "attention_back",
         8000000000,
     )
-    query_sum = scatter_row(query_parts[:4], query_parts[4:])
+    query_sum = scatter_row(*query_parts)
     grad_keyval = (
         query_sum[:, 2048:2304] + other_half(query_sum[:, 2304:2560].astype(bf16)).astype(f32)
     ).astype(bf16)
     query_back = query_sum[:, 2560:].astype(bf16)
     keyval_back = dot_t(grad_keyval, kv_out).astype(bf16)
+    keyval_ride = jnp.pad(keyval_back, ((0, 0), (0, RIDE - 16)))
     grad_normed = (
         query_sum[:, :MODEL_WIDTH]
         + dot(query_back, q_in)
@@ -814,56 +964,65 @@
     _, norm_one_back = jax.vjp(lambda v: layer_norm(v, gain_one, shift_one), input_rows)
     grad_tokens = (grad_middle + norm_one_back(grad_normed)[0]).astype(bf16)
 
-    def ridden(back, rows):
-        piece = tdot(back, rows)
-        return piece[:16] + piece[16:32]
-
-    def sliced(piece):
-        return piece.reshape(16, 2, 4, -1).transpose(1, 2, 0, 3)
-
-    def joined(*pieces):
-        return jnp.concatenate([p.astype(bf16) for p in pieces], axis=-1)
-
-    early = gather_sequences(own_slice(jnp.concatenate([up_b, down_a], axis=1), zh), zh, x)
-    up_b, down_a = finish(early, all_ids, (1024, 1024))
-    middle_set = joined(
-        scatter_sequence(
-            jnp.concatenate(
-                [
-                    sliced(ridden(up_back, normed_two)),
-                    sliced(ridden(down_inner, cotangent)),
-                    sliced(ridden(output_inner, grad_branch)),
-                ],
-                axis=-1,
+    late_set = jnp.concatenate(
+        [
+            scatter_sequence(
+                jnp.concatenate(
+                    [
+                        slices_of(
+                            at,
+                            [(query_back, normed), (keyval_ride, normed)],
+                            "late_slices",
+                        ),
+                        jnp.pad(
+                            rolled(
+                                tdot(keyval_inner, grad_keyval)
+                                .astype(bf16)
+                                .reshape(16, 4, 64)
+                                .transpose(1, 0, 2),
+                                x,
+                            ),
+                            ((0, 0), (0, 0), (0, 64)),
+                        ),
+                    ],
+                    axis=-1,
+                )
             ),
-            zh,
-            x,
-        ),
-        own_slice(output_a, zh),
-    )
-    up_a, down_b, output_b, output_a = finish(
-        gather_sequences(middle_set, zh, x), all_ids, (256, 256, 256, 256)
-    )
-    keyval_b = tdot(keyval_inner, grad_keyval).reshape(2, 4, 16, 32)
-    late_set = joined(
-        scatter_sequence(
-            jnp.concatenate(
-                [
-                    sliced(ridden(query_back, normed)),
-                    sliced(tdot(keyval_back, normed)),
-                    jnp.pad(keyval_b, ((0, 0), (0, 0), (0, 0), (0, 96))),
-                ],
-                axis=-1,
-            ),
-            zh,
-            x,
-        ),
-        own_slice(query_b, zh),
-    )
-    query_a, keyval_a, keyval_b, query_b = finish(
-        gather_sequences(late_set, zh, x), all_ids, (256, 256, 128, 256)
-    )
-    keyval_b = keyval_b.reshape(8, 16, 8, 128)[..., :32].transpose(0, 2, 1, 3).reshape(8, 16, 256)
+            row_slice(query_b, core),
+            row_slice(output_a, core),
+        ],
+        axis=-1,
+    )
+    column = jnp.stack(
+        [late_set, ring_y(late_set, -1), ring_y(late_set, 2), ring_y(late_set, 1)]
+    )
+    feed_all, column = lax.optimization_barrier((feed_all, column))
+    all_ids = feed_all[:, 0, 5632].astype(jnp.int32)
+    feed_sum = sum_by_adapter([feed_all], 4 * core, all_ids, 4)
+    feed_sum = lax.all_gather(feed_sum, ("core", "x"), axis=0).reshape(2, 4, 4, 16, 5760)
+    late_pieces = [column, ring_z(column, -1), ring_z(column, 2), ring_z(column, 1)]
+    plane_ids = all_ids.reshape(4, 2, 2, 2)
+    plane_ids = jnp.where(core == 0, plane_ids[:, :, 0], plane_ids[:, :, 1])
+    plane_ids = rolled(jnp.swapaxes(plane_ids, 1, 2).reshape(4, 4), y)
+    plane_ids = rolled(plane_ids.T, z)
+    late_sum = sum_by_adapter(late_pieces, 0, plane_ids.reshape(16), ADAPTER_COUNT)
+    kept = jnp.where(core == 0, late_sum[:4], late_sum[4:])
+    sent = jnp.where(core == 0, late_sum[4:], late_sum[:4])
+    own_half = (kept.astype(f32) + other_core(sent).astype(f32)).astype(bf16)
+    other_part = other_core(own_half)
+    near = ring_by_core(jnp.concatenate([own_half, other_part], axis=0))
+    far = ring_x(own_half, 2)
+    query_a, keyval_a, keyval_b, query_b, output_a = spread_out(
+        late_spread_kernel,
+        at,
+        [own_half, other_part, near, other_core(near), far, other_core(far)],
+        (256, 256, 64, 256, 256),
+        "late_spread",
+    )
+    keyval_b = keyval_b.reshape(8, 16, 4, 128)[..., :64].reshape(8, 16, 256)
+    up_b, down_a, up_a, output_b, down_b = spread_out(
+        feed_spread_kernel, at, [feed_sum], (1024, 1024, 256, 256, 256), "feed_spread"
+    )
 
     def side_in(a):
         return jnp.swapaxes(a, 1, 2)

time: 584 us -> 495 us (0.85)
  starting transfers between devices: 171 us -> 94.7 us
  blocking collectives: 6 us -> 0 us
    ppermute x5 -> x2, starting transfers between devices: 42.1 us -> 10.1 us  [turn(): return lax.ppermute(a, ('core', 'zh'), [(0, 0), (1, 2), (2, 1), (3, 3)])]
    ppermute x46 -> x33, starting transfers between devices: 63 us -> 33.5 us  [ring_x(): return lax.ppermute(a, 'x', [(i, (i + step) % 4) for i in range(4)])]
    ppermute x10 -> x2, waiting for transfers between devices: 21.3 us -> 2.52 us  [other_half(): return lax.ppermute(a, 'zh', [(0, 1), (1, 0)])]
    ppermute x0 -> x7, waiting for transfers between devices: none -> 18.8 us  [the longest x1 13.7 us: ring_by_core(): return lax.ppermute(a, ('core', 'x'), pairs)]
    ppermute x33 -> x28, starting transfers between devices: 41 us -> 30.1 us  [other_core(): return lax.ppermute(a, 'core', [(0, 1), (1, 0)])]
    ppermute x0 -> x7, starting transfers between devices: none -> 10.1 us  [the longest x6 8.29 us: gather_cross(): lax.ppermute(a, ('y', 'zl', 'core', 'zh'), plane_pairs(-step, swapped))]
    ppermute x33 -> x28, waiting for transfers between devices: 2.85 us -> 12.1 us  [other_core(): return lax.ppermute(a, 'core', [(0, 1), (1, 0)])]
    ppermute x8 -> x3, starting transfers between devices: 10 us -> 3.34 us  [ring_y(): return lax.ppermute(a, 'y', [(i, (i + step) % 4) for i in range(4)])]
  transfers between devices with their start and end apart: 115 -> 83, of which waited for: 49 -> 41; matrix products, arithmetic and copies ran while one was open for 11% -> 13% of each run, Pallas kernels for 16% -> 20%
where the time goes in v3:
time: 495 us; the launch traced here: 486 us
  waiting for transfers between devices  163 us (33%)
  Pallas kernels  133 us (27%)
  starting transfers between devices  94.7 us (19%)
  local copies, waits for them, and re-layouts  33.9 us (7%)
  other arithmetic  32 us (6%)
  between operations  17.3 us (3%)
  matrix products  10.9 us (2%)
    pallas_call x8, Pallas kernels, call(): pl.pallas_call(kernel, out_shape=[jax.ShapeDtypeStruct(s, d) for s, d, _...  111 us
    ppermute x33, waiting for transfers between devices, ring_x(): return lax.ppermute(a, 'x', [(i, (i + step) % 4) for i in range(4)])  98.6 us
    ppermute x33, starting transfers between devices, ring_x(): return lax.ppermute(a, 'x', [(i, (i + step) % 4) for i in range(4)])  33.5 us
    ppermute x28, starting transfers between devices, other_core(): return lax.ppermute(a, 'core', [(0, 1), (1, 0)])  30.1 us
    pallas_call x2, Pallas kernels, spread_out(): pl.pallas_call(functools.partial(kernel, widths), out_shape=[jax.ShapeDty...  14 us
    ppermute x1, waiting for transfers between devices, ring_by_core(): return lax.ppermute(a, ('core', 'x'), pairs)  13.7 us
    ppermute x28, waiting for transfers between devices, other_core(): return lax.ppermute(a, 'core', [(0, 1), (1, 0)])  12.1 us
    unnamed x173, local copies, waits for them, and re-layouts  11.9 us
  transfers between devices with their start and end apart: 83, of which 41 were waited for; matrix products, arithmetic and copies ran while one was open for 13% of the time, Pallas kernels for 20%

profile of v3, /device:TPU:1, one launch (start us, length us, event | category | flops | bytes accessed | tf_op | source)
XLA Modules:
  0.0 485.6 jit_solution(7517884338806663745)
XLA Ops:
  11.3 6.9 %collective-permute-start = (bf16[128,768]{1,0:T(8,128)(2,1)}, bf16[128,768]{1,0:T(8,128)(2,1)S(1)}, u32[]{:S(2)}, u32[]{:S(2)}) collective-permute-start(bf16[128,768]{1,0:T(8,128)(2,1)} %get-tuple-element.79), channel_id=1, source_target_pairs={{0,0},{4,8},{8,4},{12,12},{1,1},{5,9},{9,5},{13,13},{2,2},{6,10},{... | collective-permute-start | bytes 589832 | tf_op jit(solution)/shard_map/ppermute | solution.py:54
  25.6 4.5 collective-permute-done.3
  38.5 15.5 %collective-permute-done.9.refs_4_ = bf16[128,2048]{1,0:T(8,128)(2,1)S(1)} collective-permute-done((bf16[128,2048]{1,0:T(8,128)(2,1)S(1)}, bf16[128,2048]{1,0:T(8,128)(2,1)S(1)}, u32[]{:S(2)}, u32[]{:S(2)}) %collective-permute-start.9) | collective-permute-done | bytes 524320 | tf_op jit(solution)/shard_map/ppermute | solution.py:34
  58.1 4.3 assemble.1.refs_14_.refs_1_
  99.8 21.5 %attention.1 = (bf16[2,512,128]{2,1,0:T(8,128)(2,1)}, bf16[2,512,256]{2,1,0:T(8,128)(2,1)}, bf16[2,8,128,256]{3,2,1,0:T(8,128)(2,1)}, f32[2,2,512]{2,1,0:T(2,128...) custom-call(s32[5]{0:T(128)} %stack.68.at, ...), custom_call_target="tpu_custom_call" | custom-call | flops 8999999488 | bytes 22243328 | tf_op jit(solution)/shard_map/attention/pallas_call | solution.py:578
  129.0 5.9 %collective-permute-done.25 = bf16[64,2176]{1,0:T(8,128)(2,1)S(1)} collective-permute-done((bf16[64,2176]{1,0:T(8,128)(2,1)S(1)}, bf16[64,2176]{1,0:T(8,128)(2,1)S(1)}, u32[]{:S(2)}, u32[]{:S(2)}) %collective-permute-start.25) | collective-permute-done | bytes 278560 | tf_op jit(solution)/shard_map/ppermute | solution.py:34
  138.7 9.5 %collective-permute-done.28 = bf16[128,2176]{1,0:T(8,128)(2,1)S(1)} collective-permute-done((bf16[128,2176]{1,0:T(8,128)(2,1)S(1)}, bf16[128,2176]{1,0:T(8,128)(2,1)S(1)}, u32[]{:S(2)}, u32[]{:S(2)}) %collective-permute-start.28) | collective-permute-done | bytes 557088 | tf_op jit(solution)/shard_map/ppermute | solution.py:34
  159.3 4.2 collective-permute-done.32.refs_4_
  165.4 4.2 collective-permute-start.33
  179.9 21.1 %feed.1 = (bf16[4,256,128]{2,1,0:T(8,128)(2,1)}, f32[4,256,1024]{2,1,0:T(8,128)}, bf16[4,256,1024]{2,1,0:T(8,128)(2,1)}, bf16[3,128,2176]{2,1,0:T(8,128)(2,1)}, ...) custom-call(s32[5]{0:T(128)} %stack.68.at, bf16[128,2048]{1,0:T(8,128)(2,1)} %copy-done.11, ...), custom_call_target="tpu_custom_call" | custom-call | flops 9500000256 | bytes 39849984 | tf_op jit(solution)/shard_map/feed/pallas_call | solution.py:578
  209.9 31.0 %feed_back.1 = (f32[32,1024]{1,0:T(8,128)}, f32[32,1024]{1,0:T(8,128)}, bf16[3,128,2176]{2,1,0:T(8,128)(2,1)}, bf16[3,128,2176]{2,1,0:T(8,128)(2,1)}, bf16[128,2...) custom-call(s32[5]{0:T(128)} %stack.68.at, bf16[2,4,128,2048]{3,2,1,0:T(8,128)(2,1)} %bitcast.240, ...), custom_call_target="tpu_custom_call" | custom-call | flops 9500000256 | bytes 37748736 | tf_op jit(solution)/shard_map/feed_back/pallas_call | solution.py:578
  248.0 5.9 %collective-permute-done.45 = bf16[64,2176]{1,0:T(8,128)(2,1)S(1)} collective-permute-done((bf16[64,2176]{1,0:T(8,128)(2,1)S(1)}, bf16[64,2176]{1,0:T(8,128)(2,1)S(1)}, u32[]{:S(2)}, u32[]{:S(2)}) %collective-permute-start.45) | collective-permute-done | bytes 278560 | tf_op jit(solution)/shard_map/ppermute | solution.py:34
  256.6 10.5 %collective-permute-done.48 = bf16[128,2176]{1,0:T(8,128)(2,1)S(1)} collective-permute-done((bf16[128,2176]{1,0:T(8,128)(2,1)S(1)}, bf16[128,2176]{1,0:T(8,128)(2,1)S(1)}, u32[]{:S(2)}, u32[]{:S(2)}) %collective-permute-start.48) | collective-permute-done | bytes 557088 | tf_op jit(solution)/shard_map/ppermute | solution.py:34
  289.9 4.1 collective-permute-done.58
  297.6 10.0 %all-gather.12.cloned.1.call-done = bf16[1024,2048]{1,0:T(8,128)(2,1)} async-done(((bf16[128,2048]{1,0:T(8,128)(2,1)}), bf16[1024,2048]{1,0:T(8,128)(2,1)}) %all-gather.12.cloned.1.call-update) | async-done | bytes 4194320 | tf_op jit(solution)/shard_map/all_gather | solution.py:905
  307.6 23.9 %attention_back.1 = (f32[32,256]{1,0:T(8,128)}, f32[32,256]{1,0:T(8,128)}, bf16[3,128,2688]{2,1,0:T(8,128)(2,1)}, bf16[3,128,2688]{2,1,0:T(8,128)(2,1)}, bf16[12...) custom-call(s32[5]{0:T(128)} %stack.68.at, bf16[2,4,128,2048]{3,2,1,0:T(8,128)(2,1)} %bitcast.241, ...), custom_call_target="tpu_custom_call" | custom-call | flops 8000000000 | bytes 21454848 | tf_op jit(solution)/shard_map/attention_back/pallas_call | solution.py:578
  338.8 7.4 %collective-permute-done.51 = bf16[64,2688]{1,0:T(8,128)(2,1)S(1)} collective-permute-done((bf16[64,2688]{1,0:T(8,128)(2,1)S(1)}, bf16[64,2688]{1,0:T(8,128)(2,1)S(1)}, u32[]{:S(2)}, u32[]{:S(2)}) %collective-permute-start.51) | collective-permute-done | bytes 344096 | tf_op jit(solution)/shard_map/ppermute | solution.py:34
  352.4 11.0 %collective-permute-done.54 = bf16[128,2688]{1,0:T(8,128)(2,1)S(1)} collective-permute-done((bf16[128,2688]{1,0:T(8,128)(2,1)}, bf16[128,2688]{1,0:T(8,128)(2,1)S(1)}, u32[]{:S(2)}, u32[]{:S(2)}) %collective-permute-start.54) | collective-permute-done | bytes 688160 | tf_op jit(solution)/shard_map/ppermute | solution.py:34
  392.6 9.4 %all-gather.14.cloned.1.call-done = bf16[512,5760]{1,0:T(8,128)(2,1)} async-done(((bf16[16,5760]{1,0:T(8,128)(2,1)}), bf16[512,5760]{1,0:T(8,128)(2,1)}) %all-gather.14.cloned.1.call-update) | async-done | bytes 5898256 | tf_op jit(solution)/shard_map/all_gather | solution.py:922
  404.1 5.6 %sum_by_adapter.3 = bf16[4,16,5760]{2,1,0:T(8,128)(2,1)} custom-call(s32[33]{0:T(128)} %pad_add_fusion.4.at, bf16[32,16,5760]{2,1,0:T(8,128)(2,1)} %bitcast.226), custom_call_target="tpu_custom_call" | custom-call | tf_op jit(solution)/shard_map/sum_by_adapter/pallas_call | solution.py:616
  421.1 5.0 %collective-permute-done.70.refs_2_ = bf16[4,16,2176]{2,1,0:T(8,128)(2,1)S(1)} collective-permute-done((bf16[4,16,2176]{2,1,0:T(8,128)(2,1)S(1)}, bf16[4,16,2176]{2,1,0:T(8,128)(2,1)S(1)}, u32[]{:S(2)}, u32[]{:S(2)}) %collective-permute-start.70) | collective-permute-done | bytes 278560 | tf_op jit(solution)/shard_map/ppermute | solution.py:42
  442.0 13.7 %collective-permute-done.74.refs_2_ = bf16[8,16,2176]{2,1,0:T(8,128)(2,1)S(1)} collective-permute-done((bf16[8,16,2176]{2,1,0:T(8,128)(2,1)S(1)}, bf16[8,16,2176]{2,1,0:T(8,128)(2,1)S(1)}, u32[]{:S(2)}, u32[]{:S(2)}) %collective-permute-start.74) | collective-permute-done | bytes 557088 | tf_op jit(solution)/shard_map/ppermute | solution.py:131
  462.9 5.7 %late_spread.1 = (f32[8,16,2048]{2,1,0:T(8,128)}, f32[8,16,2048]{2,1,0:T(8,128)}, f32[8,16,512]{2,1,0:T(8,128)}, f32[8,16,2048]{2,1,0:T(8,128)}, f32[8,16,2048]{2,1,0:T(8,128)}) custom-call(s32[5]{0:T(128)} %stack.68.at, bf16[4,16,2176]{2,1,0:T(8,128)(2,1)} %copy-done.10, bf16[4,16,2176]{2,1,0:T(8,128)(2,1)} %copy-done.18, bf16[8,16,2176]{2,1,0:T(8,128)(2,1)} %copy-done.26, ...), custom_call_target="tpu_custom_call" | custom-call | tf_op jit(solution)/shard_map/late_spread/pallas_call | solution.py:638
  470.5 8.3 %feed_spread.1 = (f32[8,16,8192]{2,1,0:T(8,128)}, f32[8,16,8192]{2,1,0:T(8,128)}, f32[8,16,2048]{2,1,0:T(8,128)}, f32[8,16,2048]{2,1,0:T(8,128)}, f32[8,16,2048]{2,1,0:T(8,128)}) custom-call(s32[5]{0:T(128)} %stack.68.at, bf16[2,4,4,16,5760]{4,3,2,1,0:T(8,128)(2,1)} %bitcast.227), custom_call_target="tpu_custom_call" | custom-call | tf_op jit(solution)/shard_map/feed_spread/pallas_call | solution.py:638
  (480 shorter events, 219.2 us)
Async XLA Ops:
  7.2 55.3 %all-gather.8.cloned.1.call-start = ((), (), s32[]{:S(2)}) async-start(), calls=%async_computation | async-start | bytes 4718592 | tf_op jit(solution)/shard_map/all_gather | solution.py:701
  7.9 172.0 %all-gather.10.cloned.1.call-start = ((), (), s32[]{:S(2)}) async-start(), calls=%async_computation.1 | async-start | bytes 17301504 | tf_op jit(solution)/shard_map/all_gather | solution.py:736
  30.9 23.1 %collective-permute-start.9 = (bf16[128,2048]{1,0:T(8,128)(2,1)S(1)}, bf16[128,2048]{1,0:T(8,128)(2,1)S(1)}, u32[]{:S(2)}, u32[]{:S(2)}) collective-permute-start(bf16[128,2048]{1,0:T(8,128)(2,1)S(1)} %fusion.16.refs_0_.refs_1_.refs_3_), channel_id=1, source_target_pairs={{0,3},{1,0},{2,1},{3,2},{4,7},{5,4},{6,5},{7,6},{8,11},{9,8},{10,9... | collective-permute-start | bytes 1572872 | tf_op jit(solution)/shard_map/ppermute | solution.py:34
  33.5 22.5 %collective-permute-start.6 = (bf16[4,128,768]{2,1,0:T(8,128)(2,1)S(1)}, bf16[4,128,768]{2,1,0:T(8,128)(2,1)S(1)}, u32[]{:S(2)}, u32[]{:S(2)}) collective-permute-start(bf16[4,128,768]{2,1,0:T(8,128)(2,1)S(1)} %pad_maximum_fusion.refs_0_), channel_id=1, source_target_pairs={{0,16},{8,40},{16,4},{24,56},{4,20},{12,44},{20,0},{28,60},{32,48}... | collective-permute-start | bytes 2359304 | tf_op jit(solution)/shard_map/ppermute | solution.py:75
  34.8 21.2 %collective-permute-start.5 = (bf16[4,128,768]{2,1,0:T(8,128)(2,1)S(1)}, bf16[4,128,768]{2,1,0:T(8,128)(2,1)S(1)}, u32[]{:S(2)}, u32[]{:S(2)}) collective-permute-start(bf16[4,128,768]{2,1,0:T(8,128)(2,1)S(1)} %pad_maximum_fusion.refs_0_), channel_id=1, source_target_pairs={{0,4},{8,72},{16,20},{24,88},{4,0},{12,76},{20,16},{28,92},{32,36}... | collective-permute-start | bytes 2359304 | tf_op jit(solution)/shard_map/ppermute | solution.py:75
  37.7 18.3 %collective-permute-start.4 = (bf16[4,128,768]{2,1,0:T(8,128)(2,1)S(1)}, bf16[4,128,768]{2,1,0:T(8,128)(2,1)S(1)}, u32[]{:S(2)}, u32[]{:S(2)}) collective-permute-start(bf16[4,128,768]{2,1,0:T(8,128)(2,1)S(1)} %pad_maximum_fusion.refs_0_), channel_id=1, source_target_pairs={{0,20},{8,104},{16,0},{24,120},{4,16},{12,108},{20,4},{28,124},{32... | collective-permute-start | bytes 2359304 | tf_op jit(solution)/shard_map/ppermute | solution.py:75
  38.5 15.5 %collective-permute-start.8 = (bf16[128,2048]{1,0:T(8,128)(2,1)S(1)}, bf16[128,2048]{1,0:T(8,128)(2,1)S(1)}, u32[]{:S(2)}, u32[]{:S(2)}) collective-permute-start(bf16[128,2048]{1,0:T(8,128)(2,1)S(1)} %fusion.16.refs_0_.refs_1_.refs_3_), channel_id=1, source_target_pairs={{0,1},{1,2},{2,3},{3,0},{4,5},{5,6},{6,7},{7,4},{8,9},{9,10},{10,1... | collective-permute-start | bytes 1572872 | tf_op jit(solution)/shard_map/ppermute | solution.py:34
  62.5 245.1 %all-gather.12.cloned.1.call-start = ((), (), s32[]{:S(2)}) async-start(), calls=%async_computation.2 | async-start | bytes 4718592 | tf_op jit(solution)/shard_map/all_gather | solution.py:905
  71.0 19.1 %collective-permute-start.22 = (bf16[48,2560]{1,0:T(8,128)(2,1)S(1)}, bf16[48,2560]{1,0:T(8,128)(2,1)S(1)}, u32[]{:S(2)}, u32[]{:S(2)}) collective-permute-start(bf16[48,2560]{1,0:T(8,128)(2,1)S(1)} %maximum_maximum_fusion.3), channel_id=1, source_target_pairs={{0,0},{4,8},{8,4},{12,12},{1,1},{5,9},{9,5},{13,13},{2,2},{6,10},{... | collective-permute-start | bytes 737288 | tf_op jit(solution)/shard_map/ppermute | solution.py:54
  137.6 13.6 %collective-permute-start.26 = (bf16[128,2176]{1,0:T(8,128)(2,1)S(1)}, bf16[128,2176]{1,0:T(8,128)(2,1)S(1)}, u32[]{:S(2)}, u32[]{:S(2)}) collective-permute-start(bf16[128,2176]{1,0:T(8,128)(2,1)S(1)} %pad_maximum_fusion.3), channel_id=1, source_target_pairs={{0,1},{1,2},{2,3},{3,0},{4,5},{5,6},{6,7},{7,4},{8,9},{9,10},{10,1... | collective-permute-start | bytes 1671176 | tf_op jit(solution)/shard_map/ppermute | solution.py:34
  156.0 22.1 %collective-permute-start.29 = (bf16[128,2048]{1,0:T(8,128)(2,1)S(1)}, bf16[128,2048]{1,0:T(8,128)(2,1)S(1)}, u32[]{:S(2)}, u32[]{:S(2)}) collective-permute-start(bf16[128,2048]{1,0:T(8,128)(2,1)S(1)} %add_convert_fusion.5.refs_0_.refs_1_), channel_id=1, source_target_pairs={{0,8},{8,0},{1,9},{9,1},{2,10},{10,2},{3,11},{11,3},{4,12},{12,4},... | collective-permute-start | bytes 1572872 | tf_op jit(solution)/shard_map/ppermute | solution.py:46
  208.4 32.5 %collective-permute-start.40 = (bf16[128,2176]{1,0:T(8,128)(2,1)S(1)}, bf16[128,2176]{1,0:T(8,128)(2,1)S(1)}, u32[]{:S(2)}, u32[]{:S(2)}) collective-permute-start(bf16[128,2176]{1,0:T(8,128)(2,1)S(1)} %get-tuple-element.111), channel_id=1, source_target_pairs={{0,3},{1,0},{2,1},{3,2},{4,7},{5,4},{6,5},{7,6},{8,11},{9,8},{10,9... | collective-permute-start | bytes 1671176 | tf_op jit(solution)/shard_map/ppermute | solution.py:34
  208.4 32.5 %collective-permute-start.41 = (bf16[128,2176]{1,0:T(8,128)(2,1)S(1)}, bf16[128,2176]{1,0:T(8,128)(2,1)S(1)}, u32[]{:S(2)}, u32[]{:S(2)}) collective-permute-start(bf16[128,2176]{1,0:T(8,128)(2,1)S(1)} %get-tuple-element.112), channel_id=1, source_target_pairs={{0,1},{1,2},{2,3},{3,0},{4,5},{5,6},{6,7},{7,4},{8,9},{9,10},{10,1... | collective-permute-start | bytes 1671176 | tf_op jit(solution)/shard_map/ppermute | solution.py:34
  209.9 31.0 %collective-permute-start.42 = (bf16[128,2176]{1,0:T(8,128)(2,1)S(1)}, bf16[128,2176]{1,0:T(8,128)(2,1)S(1)}, u32[]{:S(2)}, u32[]{:S(2)}) collective-permute-start(bf16[128,2176]{1,0:T(8,128)(2,1)S(1)} %add_convert_fusion.2), channel_id=1, source_target_pairs={{0,2},{1,3},{2,0},{3,1},{4,6},{5,7},{6,4},{7,5},{8,10},{9,11},{10,... | collective-permute-start | bytes 1671176 | tf_op jit(solution)/shard_map/ppermute | solution.py:34
  256.5 13.6 %collective-permute-start.46 = (bf16[128,2176]{1,0:T(8,128)(2,1)S(1)}, bf16[128,2176]{1,0:T(8,128)(2,1)S(1)}, u32[]{:S(2)}, u32[]{:S(2)}) collective-permute-start(bf16[128,2176]{1,0:T(8,128)(2,1)S(1)} %pad_maximum_fusion.5), channel_id=1, source_target_pairs={{0,1},{1,2},{2,3},{3,0},{4,5},{5,6},{6,7},{7,4},{8,9},{9,10},{10,1... | collective-permute-start | bytes 1671176 | tf_op jit(solution)/shard_map/ppermute | solution.py:34
  272.9 129.1 %all-gather.14.cloned.1.call-start = ((), (), s32[]{:S(2)}) async-start(), calls=%async_computation.3 | async-start | bytes 6082560 | tf_op jit(solution)/shard_map/all_gather | solution.py:922
  297.1 173.4 %all-gather.16.cloned.1.call-start = ((), (), s32[]{:S(2)}) async-start(), calls=%async_computation.4 | async-start | bytes 6635520 | tf_op jit(solution)/shard_map/all_gather | solution.py:1002
  347.2 16.2 %collective-permute-start.54 = (bf16[128,2688]{1,0:T(8,128)(2,1)}, bf16[128,2688]{1,0:T(8,128)(2,1)S(1)}, u32[]{:S(2)}, u32[]{:S(2)}) collective-permute-start(bf16[128,2688]{1,0:T(8,128)(2,1)} %pad_maximum_fusion.2), channel_id=1, source_target_pairs={{0,3},{1,0},{2,1},{3,2},{4,7},{5,4},{6,5},{7,6},{8,11},{9,8},{10,9... | collective-permute-start | bytes 2064392 | tf_op jit(solution)/shard_map/ppermute | solution.py:34
  350.5 16.8 %collective-permute-start.52 = (bf16[128,2688]{1,0:T(8,128)(2,1)}, bf16[128,2688]{1,0:T(8,128)(2,1)}, u32[]{:S(2)}, u32[]{:S(2)}) collective-permute-start(bf16[128,2688]{1,0:T(8,128)(2,1)} %pad_maximum_fusion.1), channel_id=1, source_target_pairs={{0,1},{1,2},{2,3},{3,0},{4,5},{5,6},{6,7},{7,4},{8,9},{9,10},{10,1... | collective-permute-start | bytes 2064392 | tf_op jit(solution)/shard_map/ppermute | solution.py:34
  350.5 21.6 %collective-permute-start.65 = (bf16[16,256]{1,0:T(8,128)(2,1)S(1)}, bf16[16,256]{1,0:T(8,128)(2,1)S(1)}, u32[]{:S(2)}, u32[]{:S(2)}) collective-permute-start(bf16[16,256]{1,0:T(8,128)(2,1)S(1)} %get-tuple-element.213), channel_id=1, source_target_pairs={{0,8},{8,0},{1,9},{9,1},{2,10},{10,2},{3,11},{11,3},{4,12},{12,4},... | collective-permute-start | bytes 24584 | tf_op jit(solution)/shard_map/ppermute | solution.py:46
  352.2 29.9 %collective-permute-start.64 = (bf16[16,256]{1,0:T(8,128)(2,1)S(1)}, bf16[16,256]{1,0:T(8,128)(2,1)S(1)}, u32[]{:S(2)}, u32[]{:S(2)}) collective-permute-start(bf16[16,256]{1,0:T(8,128)(2,1)S(1)} %get-tuple-element.211), channel_id=1, source_target_pairs={{0,8},{8,0},{1,9},{9,1},{2,10},{10,2},{3,11},{11,3},{4,12},{12,4},... | collective-permute-start | bytes 24584 | tf_op jit(solution)/shard_map/ppermute | solution.py:46
  411.1 15.0 %collective-permute-start.70 = (bf16[4,16,2176]{2,1,0:T(8,128)(2,1)S(1)}, bf16[4,16,2176]{2,1,0:T(8,128)(2,1)S(1)}, u32[]{:S(2)}, u32[]{:S(2)}) collective-permute-start(bf16[4,16,2176]{2,1,0:T(8,128)(2,1)S(1)} %pad_maximum_fusion.8.refs_0_), channel_id=1, source_target_pairs={{0,4},{16,20},{4,0},{20,16},{1,5},{17,21},{5,1},{21,17},{2,6},{18,... | collective-permute-start | bytes 835592 | tf_op jit(solution)/shard_map/ppermute | solution.py:42
  437.1 18.5 %collective-permute-start.74 = (bf16[8,16,2176]{2,1,0:T(8,128)(2,1)S(1)}, bf16[8,16,2176]{2,1,0:T(8,128)(2,1)S(1)}, u32[]{:S(2)}, u32[]{:S(2)}) collective-permute-start(bf16[8,16,2176]{2,1,0:T(8,128)(2,1)S(1)} %pad_maximum_fusion.7), channel_id=1, source_target_pairs={{0,1},{1,2},{2,3},{3,0},{8,11},{9,8},{10,9},{11,10},{4,5},{5,6},{6... | collective-permute-start | bytes 1671176 | tf_op jit(solution)/shard_map/ppermute | solution.py:131
  440.9 15.9 %collective-permute-start.76 = (bf16[4,16,2176]{2,1,0:T(8,128)(2,1)S(1)}, bf16[4,16,2176]{2,1,0:T(8,128)(2,1)S(1)}, u32[]{:S(2)}, u32[]{:S(2)}) collective-permute-start(bf16[4,16,2176]{2,1,0:T(8,128)(2,1)S(1)} %add_convert_fusion.6.refs_0_), channel_id=1, source_target_pairs={{0,2},{1,3},{2,0},{3,1},{4,6},{5,7},{6,4},{7,5},{8,10},{9,11},{10,... | collective-permute-start | bytes 835592 | tf_op jit(solution)/shard_map/ppermute | solution.py:34
  (143 other events, 1401.6 us)
Sparse Core Ops, SparseCore 0:
  9.7 45.6 all-gather.7
  62.7 109.2 all-gather.9
  273.0 34.5 all-gather.11
  309.7 92.2 all-gather.13
  409.8 44.1 all-gather.15

commit v4 on v3

--- a/solution.py
+++ b/solution.py
@@ -28,6 +28,9 @@
 
 f32 = jnp.float32
 bf16 = jnp.bfloat16
+
+
+together = lax.optimization_barrier
 
 
 def ring_x(a, step):
@@ -100,14 +103,30 @@
     return mine.astype(f32) + other_core(theirs).astype(f32)
 
 
-def scatter_row(mine, theirs, far_mine, far_theirs):
-    half = far_mine.shape[0] // 2
-    far = add_cores(far_mine, far_theirs).astype(bf16)
-    up, down = ring_x(far[:half], 1), ring_x(far[half:], -1)
-    near = add_cores(mine, theirs)
+def scatter_far(far_mine, far_theirs):
+    return add_cores(far_mine, far_theirs).astype(bf16)
+
+
+def scatter_sides(far):
+    half = far.shape[0] // 2
+    return ring_x(far[:half], 1), ring_x(far[half:], -1)
+
+
+def scatter_joined(near, up, down):
+    half = up.shape[0]
     right = jnp.concatenate([near[2, :half] + up.astype(f32), near[2, half:]]).astype(bf16)
     left = jnp.concatenate([near[1, :half], near[1, half:] + down.astype(f32)]).astype(bf16)
+    return right, left
+
+
+def scatter_last(near, up, down):
+    right, left = scatter_joined(near, up, down)
     return near[0] + ring_x(right, 1).astype(f32) + ring_x(left, -1).astype(f32)
+
+
+def scatter_row(mine, theirs, far_mine, far_theirs):
+    up, down = scatter_sides(scatter_far(far_mine, far_theirs))
+    return scatter_last(add_cores(mine, theirs), up, down)
 
 
 def scatter_start(mine, theirs, far_mine, far_theirs):
@@ -116,14 +135,16 @@
     return near[0], near[1].astype(bf16), near[2].astype(bf16), far
 
 
-def scatter_last(near, left, right, far):
-    parts = (ring_x(left, -1), ring_x(right, 1), ring_x(far, 2))
-    return near + sum(part.astype(f32) for part in parts)
-
-
-def rolled(blocks, me, step=0):
-    both = jnp.concatenate([blocks, blocks], axis=0)
-    return lax.dynamic_slice_in_dim(both, lax.rem(me + step, 4), 4, 0)
+def gather_y(a):
+    return [a, ring_y(a, -1), ring_y(a, 2), ring_y(a, 1)]
+
+
+def gather_z(a):
+    return [a, ring_z(a, -1), ring_z(a, 2), ring_z(a, 1)]
+
+
+def halves_of(sums, core):
+    return jnp.where(core == 0, sums[:4], sums[4:]), jnp.where(core == 0, sums[4:], sums[:4])
 
 
 def ring_by_core(a):
@@ -137,20 +158,20 @@
     )
 
 
-def row_slice(pair, core):
+def row_slice(pair, core, widths):
     own = jnp.where(core == 0, pair[:16], pair[16:]).astype(bf16)
-    other = jnp.where(core == 0, pair[16:], pair[:16]).astype(bf16)
-    return by_core(core, own, other_core(other))
+    other = other_core(jnp.where(core == 0, pair[16:], pair[:16]).astype(bf16))
+    ends = [sum(widths[:k]) for k in range(1, len(widths))]
+    pieces = zip(jnp.split(own, ends, axis=1), jnp.split(other, ends, axis=1))
+    return jnp.concatenate([by_core(core, a, b) for a, b in pieces], axis=1)
 
 
 def scatter_sequence(slices):
-    low = slices
-    return (
-        low[0].astype(f32)
-        + ring_x(low[1], 1).astype(f32)
-        + ring_x(low[3], -1).astype(f32)
-        + ring_x(low[2], 2).astype(f32)
-    ).astype(bf16)
+    return slices[0], ring_x(slices[1], 1), ring_x(slices[3], -1), ring_x(slices[2], 2)
+
+
+def total(parts):
+    return sum(part.astype(f32) for part in parts).astype(bf16)
 
 
 def layer_norm(values, gain, shift):
@@ -244,18 +265,15 @@
     feed_out[:, 1024:] = down[...].astype(f32).T.astype(bf16)
 
 
-def sum_kernel(at, *refs):
+def sum_kernel(ids, *refs):
     pieces, (out, total) = refs[:-2], refs[-2:]
     total[...] = jnp.zeros_like(total)
-    count = out.shape[0]
-    row = 1
+    row = 0
     for piece in pieces:
         for k in range(piece.shape[0]):
-            place = at[row] - at[0]
-            place = jnp.where(jnp.logical_and(place >= 0, place < count), place, count)
-            total[place] += piece[k].astype(f32)
+            total[ids[row]] += piece[k].astype(f32)
             row += 1
-    out[...] = total[:count].astype(bf16)
+    out[...] = total[...].astype(bf16)
 
 
 def slices_kernel(count, at, *refs):
@@ -324,27 +342,40 @@
     spread(scratch, refs[6:-2], widths)
 
 
+def copy_rows(rows_in, rows, sems):
+    half = ROWS // 2
+    for s in range(2):
+        for p in range(4):
+            pieces = rows_in[p]
+            if len(pieces) == 2:
+                copy(pieces[s], rows.at[s, pl.ds(p * ROWS, ROWS)], sems.at[s])
+            else:
+                for n in range(2):
+                    here = pl.ds(p * ROWS + n * half, half)
+                    copy(pieces[2 * s + n], rows.at[s, here], sems.at[s])
+
+
 def attention_kernel(at, *refs):
     rows_in = split_pieces(refs[:10])
     kv_in = refs[10:14]
     w, q_in, q_out, kv_out, o_in, q_bias, kv_bias, bias = refs[14:22]
-    inner_out, query_out, kv_all, lse_out, att_out = refs[22:27]
-    parts, far_parts = refs[27:29], refs[29:31]
-    rows, kvs, ws, sems = refs[31:]
+    inner_out, inner_far, query_out, kv_all, lse_out, att_out = refs[22:28]
+    parts, far_parts = refs[28:30], refs[30:32]
+    rows, kvs, ws, sems = refs[32:]
     s = pl.program_id(0)
     core = at[0]
 
     @pl.when(s == 0)
     def _():
         copy(w, ws, sems.at[2])
+        copy_rows(rows_in, rows, sems)
         for p in range(4):
-            here = pl.ds(p * ROWS, ROWS)
-            copy_place(rows_in[p], rows.at[0, here], rows.at[1, here], sems.at[0])
             for q in range(2):
-                copy(kv_in[p].at[pl.ds(q * ROWS, ROWS)], kvs.at[q, p], sems.at[1])
-        wait(rows, sems.at[0])
+                copy(kv_in[p].at[pl.ds(q * ROWS, ROWS)], kvs.at[q, p], sems.at[3])
         wait(ws, sems.at[2])
-        wait(kvs, sems.at[1])
+        wait(kvs, sems.at[3])
+
+    wait(rows.at[s], sems.at[s])
 
     owner = lane_owner(4 * ROWS, jnp.where(s == 0, core, 1 - core))
     x = rows[s]
@@ -353,7 +384,8 @@
     query = (dot(x, ws[:, :256]) + q_bias[...] + dot(inner, q_out[...])).astype(bf16)
     query_out[0] = query
     kv_own = (dot(x, ws[:, 256:512]) + kv_bias[...] + dot(inner, kv_out[...])).astype(bf16)
-    kv = jnp.concatenate([kv_own.reshape(4, ROWS, 256), kvs[s]], axis=0)
+    inner_far[0] = kvs[s, :, :, 256:].reshape(4 * ROWS, RIDE)
+    kv = jnp.concatenate([kv_own.reshape(4, ROWS, 256), kvs[s, :, :, :256]], axis=0)
     kv_all[0] = kv
     keys = kv[:, :, :HEAD_WIDTH].reshape(8 * ROWS, HEAD_WIDTH)
     values_t = kv[:, :, HEAD_WIDTH:].reshape(8 * ROWS, HEAD_WIDTH).astype(f32).T.astype(bf16)
@@ -441,10 +473,10 @@
 
 
 def feed_back_kernel(at, *refs):
-    cot, feed, pre_in, act_in, inner_in, d_out, d_in, u_out = refs[:8]
-    up_b, down_a = refs[8:10]
-    parts, far_parts = refs[10:12], refs[12:14]
-    rows, up, down, sems = refs[14:]
+    cot, feed, pre_in, act_in, inner_in, d_in, u_out = refs[:7]
+    up_b, down_a = refs[7:9]
+    parts, far_parts = refs[9:11], refs[11:13]
+    rows, up, down, sems = refs[13:]
     p = pl.program_id(0)
     core = at[0]
 
@@ -461,12 +493,11 @@
 
     wait(rows.at[p], sems.at[p])
     mask = place_mask(core)
-    grad = rows[p]
-    back = jnp.where(mask, dot_t(grad, d_out[...]), 0.0)
-    back_t = back.T[:32].astype(bf16)
+    grad, back = rows[p, :, :MODEL_WIDTH], rows[p, :, MODEL_WIDTH:]
+    back_t = back.astype(f32).T[:32].astype(bf16)
     act = act_in[0]
     down_a[...] += dot(back_t, act)
-    grad_act = dot(grad, down[...].reshape(MODEL_WIDTH, 1024)) + dot(back.astype(bf16), d_in[...])
+    grad_act = dot(grad, down[...].reshape(MODEL_WIDTH, 1024)) + dot(back, d_in[...])
     pre = pre_in[0]
     k0 = math.sqrt(2.0 / math.pi)
     square = pre * pre
@@ -487,24 +518,59 @@
     store_parts(p, parts, far_parts, out, low)
 
 
+def late_kernel(at, *refs):
+    rows_in = split_pieces(refs[:10])
+    backs, backs_far, keyval_b = refs[10:13]
+    outs, (rows, sems) = refs[13:15], refs[15:]
+    core, x = at[0], at[1]
+    copy_rows(rows_in, rows, sems)
+    product = jnp.zeros((64, MODEL_WIDTH), f32)
+    for s in range(2):
+        wait(rows.at[s], sems.at[s])
+        back = backs[s].astype(f32).T
+        back = jnp.concatenate([back[:32], back[32:64] + backs_far[s].astype(f32)], axis=0)
+        product += dot(back.astype(bf16), rows[s])
+    first, second = keyval_b[:16], keyval_b[16:]
+    lane = lax.broadcasted_iota(jnp.int32, (ADAPTER_RANK, RIDE), 1) // 64
+    for which in range(2):
+        out = outs[which]
+        is_first = (core == 0) if which == 0 else (core != 0)
+        for n in range(2):
+            both = product[32 * n : 32 * n + 32]
+            picked = jnp.where(is_first, both[:16], both[16:]).astype(bf16)
+            for to in range(4):
+                place = lax.rem(to + 4 - x, 4)
+                for c in range(2):
+                    begin = (c * 4 + to) * 256
+                    lanes = slice(n * 512 + c * 256, n * 512 + (c + 1) * 256)
+                    out[place, :, lanes] = picked[:, begin : begin + 256]
+        picked = jnp.where(is_first, first, second).astype(bf16)
+        for to in range(4):
+            place = lax.rem(to + 4 - x, 4)
+            part = picked[:, (to // 2) * 128 : (to // 2) * 128 + 128]
+            out[place, :, 1024:1152] = jnp.where(lane == to % 2, part, jnp.zeros_like(part))
+
+
 def attention_back_kernel(at, *refs):
-    branch, w, inner_in, query_in, kv_in, lse_in, att_in, o_out, o_in, q_out, bias = refs[:11]
-    query_b, output_a = refs[11:13]
-    parts, far_parts = refs[13:15], refs[15:17]
-    rows, ws, grad_k, grad_v, sems = refs[17:]
+    rows_in = split_pieces(refs[:10])
+    w, inner_in, inner_far, query_in, kv_in, lse_in, att_in = refs[10:17]
+    o_out, o_in, q_out, kv_out, bias = refs[17:22]
+    query_b, output_a, keyval_b, backs, backs_far = refs[22:27]
+    parts, far_parts = refs[27:29], refs[29:31]
+    rows, ws, grad_k, grad_v, sems = refs[31:]
     s = pl.program_id(0)
     core = at[0]
 
     @pl.when(s == 0)
     def _():
-        copy(w, ws, sems.at[1])
-        copy_row(
-            branch, at, lambda p, which: rows.at[which, pl.ds(p * ROWS, ROWS)], lambda p: sems.at[0]
-        )
+        copy(w, ws, sems.at[2])
+        copy_rows(rows_in, rows, sems)
         query_b[...] = jnp.zeros_like(query_b)
         output_a[...] = jnp.zeros_like(output_a)
-        wait(rows, sems.at[0])
-        wait(ws, sems.at[1])
+        keyval_b[...] = jnp.zeros_like(keyval_b)
+        wait(ws, sems.at[2])
+
+    wait(rows.at[s], sems.at[s])
 
     owner = lane_owner(4 * ROWS, jnp.where(s == 0, core, 1 - core))
     scale = HEAD_WIDTH**-0.5
@@ -541,8 +607,15 @@
                 grad_v[...] += more_v
         columns.append(jnp.concatenate(chunks, axis=0))
     grad_query = jnp.concatenate(columns, axis=1).astype(bf16)
-    query_b[...] += dot(inner_in[0].astype(f32).T[:32].astype(bf16), grad_query)
+    inner_t = inner_in[0].astype(f32).T
+    query_b[...] += dot(inner_t[:32].astype(bf16), grad_query)
     low = jnp.where(owner, dot_t(grad_query, q_out[...]), 0.0).astype(bf16)
+    grad_kv = jnp.concatenate([grad_k[...], grad_v[...]], axis=1).astype(bf16)
+    own_kv, far_kv = grad_kv[: 4 * ROWS], grad_kv[4 * ROWS :]
+    keyval_b[...] += dot(inner_t[32:64].astype(bf16), own_kv)
+    keyval_b[...] += dot(inner_far[0].astype(f32).T[32:64].astype(bf16), far_kv)
+    backs[0] = low + jnp.where(owner, dot_t(own_kv, kv_out[...]), 0.0).astype(bf16)
+    backs_far[0] = jnp.where(owner, dot_t(far_kv, kv_out[...]), 0.0).T[32:64].astype(bf16)
     for which in range(2):
 
         @pl.when(s == which)
@@ -551,11 +624,8 @@
                 here = slice(p * ROWS, (p + 1) * ROWS)
                 part = parts[which].at[p] if p < 3 else far_parts[which]
                 part[:, :2048] = dot_t(grad_query[here], ws[:, :256]).astype(bf16)
-                part[:, 2048:2176] = grad_k[here].astype(bf16)
-                part[:, 2176:2304] = grad_v[here].astype(bf16)
-                after = slice((p + 4) * ROWS, (p + 5) * ROWS)
-                part[:, 2304:2432] = grad_k[after].astype(bf16)
-                part[:, 2432:2560] = grad_v[after].astype(bf16)
+                part[:, 2048:2304] = own_kv[here]
+                part[:, 2304:2560] = far_kv[here]
                 part[:, 2560:] = low[here]
 
 
@@ -610,9 +680,9 @@
     return pltpu.SemaphoreType.DMA((n,))
 
 
-def sum_by_adapter(pieces, first, ids, count):
-    width = pieces[0].shape[-1]
-    block = max(w for w in range(128, 2305, 128) if width % w == 0)
+def sum_by_adapter(pieces, ids):
+    width, count = pieces[0].shape[-1], ADAPTER_COUNT
+    block = max(w for w in range(128, 3713, 128) if width % w == 0)
     return pl.pallas_call(
         sum_kernel,
         out_shape=jax.ShapeDtypeStruct((count, ADAPTER_RANK, width), bf16),
@@ -624,11 +694,11 @@
                 for p in pieces
             ],
             out_specs=pl.BlockSpec((count, ADAPTER_RANK, block), lambda i, at: (0, 0, i)),
-            scratch_shapes=[pltpu.VMEM((count + 1, ADAPTER_RANK, block), f32)],
+            scratch_shapes=[pltpu.VMEM((count, ADAPTER_RANK, block), f32)],
         ),
         compiler_params=pltpu.CompilerParams(vmem_limit_bytes=VMEM_LIMIT),
         name="sum_by_adapter",
-    )(jnp.concatenate([jnp.reshape(first, (1,)), ids]).astype(jnp.int32), *pieces)
+    )(ids, *pieces)
 
 
 def spread_out(kernel, at, pieces, widths, name):
@@ -698,8 +768,15 @@
     gain_one, shift_one = attention_norm_scale.astype(f32), attention_norm_bias.astype(f32)
     gain_two, shift_two = feedforward_norm_scale.astype(f32), feedforward_norm_bias.astype(f32)
 
-    cot_all = lax.all_gather(cotangent, ("core", "x"), axis=0, tiled=True)
-    cot_all = cot_all.reshape(2, 4, ROWS, MODEL_WIDTH)
+    def ride(inner, first):
+        wide = jnp.pad(inner, ((0, 0), (first, RIDE - 16 - first)))
+        return jnp.where(core == 0, wide, jnp.roll(wide, 16, axis=1))
+
+    mine = sequence_adapter[0, 0]
+    down_back = dot_t(cotangent, pick(down_adapter_output, mine)).astype(bf16)
+    cot_all = jnp.concatenate([cotangent, ride(down_back, 0)], axis=1)
+    cot_all = lax.all_gather(cot_all, ("core", "x"), axis=0, tiled=True)
+    cot_all = cot_all.reshape(2, 4, ROWS, MODEL_WIDTH + RIDE)
     attention_shard, feed_shard = call(
         pack_kernel,
         1,
@@ -716,12 +793,100 @@
         "pack",
     )
     attention_shard = turn(attention_shard)
+    column = gather_cross(attention_shard, False)
     input_rows = tokens.astype(f32)
     normed = layer_norm(input_rows, gain_one, shift_one).astype(bf16)
-    column = jnp.stack(gather_cross(attention_shard, False))
-    column, normed = lax.optimization_barrier((column, normed))
-    plane = gather_cross(column, True)
-    plane, normed_sides = lax.optimization_barrier((plane, gather_sides(normed)))
+
+    theirs = other_core(sequence_adapter)[0, 0]
+    low = jnp.where(core == 0, mine, theirs)
+    high = jnp.where(core == 0, theirs, mine)
+
+    stacks = (
+        query_adapter_input,
+        query_adapter_output,
+        keyvalue_adapter_input,
+        keyvalue_adapter_output,
+        output_adapter_input,
+        output_adapter_output,
+        up_adapter_input,
+        up_adapter_output,
+        down_adapter_input,
+        down_adapter_output,
+    )
+    column, normed, stacks, low, high = together((column, normed, stacks, low, high))
+    plane = gather_cross(jnp.stack(column), True)
+    normed_sides = gather_sides(normed)
+    (
+        query_adapter_input,
+        query_adapter_output,
+        keyvalue_adapter_input,
+        keyvalue_adapter_output,
+        output_adapter_input,
+        output_adapter_output,
+        up_adapter_input,
+        up_adapter_output,
+        down_adapter_input,
+        down_adapter_output,
+    ) = stacks
+
+    def ordered(stack):
+        return jnp.concatenate([pick(stack, low), pick(stack, high)], axis=0)
+
+    def ordered_t(stack):
+        return ordered(jnp.swapaxes(stack, 1, 2))
+
+    def padded(*pairs):
+        rest = jnp.zeros((RIDE - 32 * len(pairs), pairs[0].shape[1]), bf16)
+        return jnp.concatenate([*pairs, rest], axis=0)
+
+    small = jnp.concatenate(
+        [
+            ordered(query_adapter_output),
+            ordered_t(output_adapter_input),
+            ordered(up_adapter_output),
+            ordered_t(down_adapter_input),
+        ],
+        axis=1,
+    )
+    biases = jnp.concatenate(
+        [
+            query_projection_bias,
+            jnp.zeros((256,), bf16),
+            up_projection_bias,
+            jnp.zeros((1024,), bf16),
+        ]
+    )
+    small = turn(jnp.concatenate([small, biases[None], jnp.zeros((15, 2560), bf16)], axis=0))
+    q_in = padded(ordered_t(query_adapter_input), ordered_t(keyvalue_adapter_input))
+    u_in = padded(ordered_t(up_adapter_input))
+    kv_out_pair = ordered(keyvalue_adapter_output)
+    kv_out_both = padded(jnp.zeros_like(kv_out_pair), kv_out_pair)
+    o_out, d_out = padded(ordered(output_adapter_output)), padded(ordered(down_adapter_output))
+
+    kv_in, kv_out = pick(keyvalue_adapter_input, mine), pick(keyvalue_adapter_output, mine)
+    keyval_bias = jnp.concatenate(
+        [jnp.zeros((HEAD_WIDTH,), f32), value_projection_bias.astype(f32)]
+    )
+    place_block = jnp.stack([lax.rem(x + p, 4) for p in PLACES]) // 2
+    own = place_block[:, None] <= place_block[None, :]
+    bias = jnp.concatenate([own, jnp.broadcast_to(zh == 1, (4, 4))], axis=0)
+    bias = jnp.repeat(jnp.where(bias, 0.0, -1e30).astype(f32), ROWS, axis=1)
+
+    keyval_inner = dot(normed, kv_in).astype(bf16)
+    keyval_ride = ride(keyval_inner, 32)
+    q_bias, u_bias = small[32:33, :256].astype(f32), small[32:33, 512:1536].astype(f32)
+    small = padded(small[:32])
+    q_out, o_in, u_out, d_in = (
+        small[:, :256],
+        small[:, 256:512],
+        small[:, 512:1536],
+        small[:, 1536:],
+    )
+    prepared = (keyval_inner, keyval_ride, kv_in, kv_out, q_in, u_in, o_out, d_out)
+    prepared += (kv_out_both, q_out, o_in, u_out, d_in, bias)
+    plane, normed_sides, prepared = together((plane, normed_sides, prepared))
+    keyval_inner, keyval_ride, kv_in, kv_out, q_in, u_in, o_out, d_out = prepared[:8]
+    kv_out_both, q_out, o_in, u_out, d_in, bias = prepared[8:]
     normed_places = gather_rest(*normed_sides)
     (w,) = call(
         assemble_kernel,
@@ -732,76 +897,19 @@
         [pltpu.SemaphoreType.DMA],
         "assemble",
     )
-    feed_shard, w, cot_all = lax.optimization_barrier((feed_shard, w, cot_all))
+    feed_shard, w, cot_all = together((feed_shard, w, cot_all))
     feed = lax.all_gather(feed_shard, DP + ("zh",), axis=0, tiled=True)
     feed = feed.reshape(16, 2, ROWS, 2048)
 
-    mine = sequence_adapter[0, 0]
-    theirs = other_core(sequence_adapter)[0, 0]
-    low = jnp.where(core == 0, mine, theirs)
-    high = jnp.where(core == 0, theirs, mine)
-
-    def ordered(stack):
-        return jnp.concatenate([pick(stack, low), pick(stack, high)], axis=0)
-
-    def ordered_t(stack):
-        return ordered(jnp.swapaxes(stack, 1, 2))
-
-    def padded(*pairs):
-        rest = jnp.zeros((RIDE - 32 * len(pairs), pairs[0].shape[1]), bf16)
-        return jnp.concatenate([*pairs, rest], axis=0)
-
-    small = jnp.concatenate(
-        [
-            ordered(query_adapter_output),
-            ordered_t(output_adapter_input),
-            ordered(up_adapter_output),
-            ordered_t(down_adapter_input),
-        ],
-        axis=1,
-    )
-    biases = jnp.concatenate(
-        [
-            query_projection_bias,
-            jnp.zeros((256,), bf16),
-            up_projection_bias,
-            jnp.zeros((1024,), bf16),
-        ]
-    )
-    small = turn(jnp.concatenate([small, biases[None], jnp.zeros((15, 2560), bf16)], axis=0))
-    q_bias, u_bias = small[32:33, :256].astype(f32), small[32:33, 512:1536].astype(f32)
-    small = padded(small[:32])
-    q_out, o_in, u_out, d_in = (
-        small[:, :256],
-        small[:, 256:512],
-        small[:, 512:1536],
-        small[:, 1536:],
-    )
-    q_in = padded(ordered_t(query_adapter_input), ordered_t(keyvalue_adapter_input))
-    u_in = padded(ordered_t(up_adapter_input))
-    kv_out_pair = ordered(keyvalue_adapter_output)
-    kv_out_both = padded(jnp.zeros_like(kv_out_pair), kv_out_pair)
-    o_out, d_out = padded(ordered(output_adapter_output)), padded(ordered(down_adapter_output))
-
-    kv_in, kv_out = pick(keyvalue_adapter_input, mine), pick(keyvalue_adapter_output, mine)
-    keyval_inner = dot(normed, kv_in).astype(bf16)
-    keyval_bias = jnp.concatenate(
-        [jnp.zeros((HEAD_WIDTH,), f32), value_projection_bias.astype(f32)]
-    )
     keyval = (dot(normed, w[:, 256:512]) + keyval_bias + dot(keyval_inner, kv_out)).astype(bf16)
-    keyval = other_half(keyval)
+    keyval = other_half(jnp.concatenate([keyval, keyval_ride], axis=1))
     keyval = jnp.concatenate([keyval, other_core(keyval)], axis=0)
     keyval_places = (keyval, ring_x(keyval, 1), ring_x(keyval, -1), ring_x(keyval, 2))
-
-    place_block = jnp.stack([lax.rem(x + p, 4) for p in PLACES]) // 2
-    own = place_block[:, None] <= place_block[None, :]
-    bias = jnp.concatenate([own, jnp.broadcast_to(zh == 1, (4, 4))], axis=0)
-    bias = jnp.repeat(jnp.where(bias, 0.0, -1e30).astype(f32), ROWS, axis=1)
 
     group = (2, 4 * ROWS)
     row_scratch = pltpu.VMEM((2, 4 * ROWS, MODEL_WIDTH), bf16)
     w_scratch = pltpu.VMEM((MODEL_WIDTH, 768), bf16)
-    inner_one, query, keyval_all, log_total, attended, *out_parts = call(
+    inner_one, inner_far, query, keyval_all, log_total, attended, *out_parts = call(
         attention_kernel,
         2,
         at,
@@ -819,13 +927,14 @@
         ],
         [
             ((*group, RIDE), bf16, step_block((4 * ROWS, RIDE))),
+            ((*group, RIDE), bf16, step_block((4 * ROWS, RIDE))),
             ((*group, 256), bf16, step_block((4 * ROWS, 256))),
             ((2, 8, ROWS, 256), bf16, step_block((8, ROWS, 256))),
             ((2, 2, 4 * ROWS), f32, step_block((2, 4 * ROWS))),
             ((*group, 256), bf16, step_block((4 * ROWS, 256))),
             *part_outs(MODEL_WIDTH + RIDE),
         ],
-        [row_scratch, pltpu.VMEM((2, 4, ROWS, 256), bf16), w_scratch, dma(3)],
+        [row_scratch, pltpu.VMEM((2, 4, ROWS, 384), bf16), w_scratch, dma(4)],
         "attention",
         9000000000,
     )
@@ -863,7 +972,7 @@
         9500000000,
     )
     down_low = scatter_start(*down_parts)
-    down_low, act = lax.optimization_barrier((down_low, act))
+    down_low, act = together((down_low, act))
     down_moved = (ring_x(down_low[1], -1), ring_x(down_low[2], 1), ring_x(down_low[3], 2))
 
     up_b, down_a, *up_parts = call(
@@ -876,18 +985,25 @@
             (pre, step_block((2 * ROWS, 1024))),
             (act, step_block((2 * ROWS, 1024))),
             (inner_two, step_block((2 * ROWS, RIDE))),
-            (d_out, None),
             (d_in, None),
             (u_out, None),
         ],
         [((32, 1024), f32, None), ((32, 1024), f32, None), *part_outs(MODEL_WIDTH + RIDE, True)],
-        [place_scratch, feed_scratch, feed_scratch, dma(6)],
+        [
+            pltpu.VMEM((4, 2 * ROWS, MODEL_WIDTH + RIDE), bf16),
+            feed_scratch,
+            feed_scratch,
+            dma(6),
+        ],
         "feed_back",
         9500000000,
     )
-    up_parts, down_moved = lax.optimization_barrier((up_parts, down_moved))
+    up_parts, down_moved, up_b, down_a = together((up_parts, down_moved, up_b, down_a))
+    feed_set = row_slice(jnp.concatenate([up_b, down_a], axis=1), core, (1024, 1024))
+    up_far = scatter_far(*up_parts[2:])
+    up_far, feed_set = together((up_far, feed_set))
     down_sum = down_low[0] + sum(part.astype(f32) for part in down_moved)
-    up_sum = scatter_row(*up_parts)
+    up_sum = scatter_last(add_cores(*up_parts[:2]), *scatter_sides(up_far))
     up_back = up_sum[:, MODEL_WIDTH:].astype(bf16)
     grad_normed_two = up_sum[:, :MODEL_WIDTH] + dot(up_back, u_in)
     _, norm_two_back = jax.vjp(lambda v: layer_norm(v, gain_two, shift_two), middle)
@@ -902,32 +1018,33 @@
         + dot(down_inner, d_out)
     ).astype(bf16)
 
-    branch_all = lax.all_gather(grad_branch, ("core", "x"), axis=0, tiled=True)
-    branch_all = branch_all.reshape(2, 4, ROWS, MODEL_WIDTH)
+    branch_sides = gather_sides(grad_branch)
+    middle_slices = slices_of(
+        at,
+        [(up_back, normed_two), (output_inner, grad_branch), (down_inner, cotangent)],
+        "slices",
+    )
+    branch_sides, middle_slices = together((branch_sides, middle_slices))
+    branch_places = gather_rest(*branch_sides)
     feed_set = jnp.concatenate(
         [
-            row_slice(up_b, core),
-            row_slice(down_a, core),
-            scatter_sequence(
-                slices_of(
-                    at,
-                    [(up_back, normed_two), (output_inner, grad_branch), (down_inner, cotangent)],
-                    "slices",
-                )
-            ),
+            feed_set,
+            total(scatter_sequence(middle_slices)),
             jnp.full((16, RIDE), mine, jnp.int32).astype(bf16),
         ],
-        axis=-1,
-    )
-    feed_all = lax.all_gather(feed_set, DP + ("zh",), axis=0)
-    query_b, output_a, *query_parts = call(
+        axis=1,
+    )
+    feed_column, branch_places = together((gather_y(feed_set), branch_places))
+    feed_pieces = gather_z(jnp.stack(feed_column))
+    query_b, output_a, keyval_b, backs, backs_far, *query_parts = call(
         attention_back_kernel,
         2,
         at,
         [
-            (branch_all, ANY),
+            *flat(branch_places),
             (w, ANY),
             (inner_one, step_block((4 * ROWS, RIDE))),
+            (inner_far, step_block((4 * ROWS, RIDE))),
             (query, step_block((4 * ROWS, 256))),
             (keyval_all, step_block((8, ROWS, 256))),
             (log_total, step_block((2, 4 * ROWS))),
@@ -935,26 +1052,71 @@
             (o_out, None),
             (o_in, None),
             (q_out, None),
+            (kv_out_both, None),
             (bias, None),
         ],
-        [((32, 256), f32, None), ((32, 256), f32, None), *part_outs(2688)],
+        [
+            ((32, 256), f32, None),
+            ((32, 256), f32, None),
+            ((32, 256), f32, None),
+            ((*group, RIDE), bf16, step_block((4 * ROWS, RIDE))),
+            ((2, 32, 4 * ROWS), bf16, step_block((32, 4 * ROWS))),
+            *part_outs(2688),
+        ],
         [
             row_scratch,
             w_scratch,
             pltpu.VMEM((8 * ROWS, HEAD_WIDTH), f32),
             pltpu.VMEM((8 * ROWS, HEAD_WIDTH), f32),
-            dma(2),
+            dma(3),
         ],
         "attention_back",
         8000000000,
     )
-    query_sum = scatter_row(*query_parts)
+    query_b, output_a, keyval_b, backs, backs_far, query_parts, feed_pieces = together(
+        (query_b, output_a, keyval_b, backs, backs_far, query_parts, feed_pieces)
+    )
+    placed = row_slice(jnp.concatenate([query_b, output_a], axis=1), core, (256, 256))
+    query_far, backs_far, placed = together(
+        (scatter_far(*query_parts[2:]), other_half(backs_far), placed)
+    )
+    all_ids = jnp.concatenate([piece[:, 0, 5632] for piece in feed_pieces]).astype(jnp.int32)
+    feed_kept, feed_sent = halves_of(sum_by_adapter(feed_pieces, all_ids), core)
+    query_sides = scatter_sides(query_far)
+    query_near = add_cores(*query_parts[:2])
+    pack_shape = (4, ADAPTER_RANK, 1152)
+    late_mine, late_theirs = call(
+        late_kernel,
+        1,
+        at,
+        [
+            *flat(normed_places),
+            (backs, None),
+            (backs_far, None),
+            (keyval_b, None),
+        ],
+        [(pack_shape, bf16, None), (pack_shape, bf16, None)],
+        [row_scratch, dma(2)],
+        "late",
+    )
+    late_mine, late_theirs, query_near, query_sides, feed_kept, feed_sent = together(
+        (late_mine, late_theirs, query_near, query_sides, feed_kept, feed_sent)
+    )
+    late_pack = add_cores(late_mine, late_theirs).astype(bf16)
+    feed_half = add_cores(feed_kept, feed_sent).astype(bf16)
+    right, left = scatter_joined(query_near, *query_sides)
+    late_pack, right, left, feed_half = together((late_pack, right, left, feed_half))
+    feed_sum = lax.all_gather(feed_half, ("core", "x"), axis=0).reshape(2, 4, 4, 16, 5760)
+    query_moved = ring_x(right, 1), ring_x(left, -1)
+    late_set = jnp.concatenate([total(scatter_sequence(late_pack)), placed], axis=-1)
+    column, query_moved = together((gather_y(late_set), query_moved))
+    late_pieces = gather_z(jnp.stack(column))
+    query_sum = query_near[0] + sum(part.astype(f32) for part in query_moved)
     grad_keyval = (
         query_sum[:, 2048:2304] + other_half(query_sum[:, 2304:2560].astype(bf16)).astype(f32)
     ).astype(bf16)
     query_back = query_sum[:, 2560:].astype(bf16)
     keyval_back = dot_t(grad_keyval, kv_out).astype(bf16)
-    keyval_ride = jnp.pad(keyval_back, ((0, 0), (0, RIDE - 16)))
     grad_normed = (
         query_sum[:, :MODEL_WIDTH]
         + dot(query_back, q_in)
@@ -964,54 +1126,17 @@
     _, norm_one_back = jax.vjp(lambda v: layer_norm(v, gain_one, shift_one), input_rows)
     grad_tokens = (grad_middle + norm_one_back(grad_normed)[0]).astype(bf16)
 
-    late_set = jnp.concatenate(
-        [
-            scatter_sequence(
-                jnp.concatenate(
-                    [
-                        slices_of(
-                            at,
-                            [(query_back, normed), (keyval_ride, normed)],
-                            "late_slices",
-                        ),
-                        jnp.pad(
-                            rolled(
-                                tdot(keyval_inner, grad_keyval)
-                                .astype(bf16)
-                                .reshape(16, 4, 64)
-                                .transpose(1, 0, 2),
-                                x,
-                            ),
-                            ((0, 0), (0, 0), (0, 64)),
-                        ),
-                    ],
-                    axis=-1,
-                )
-            ),
-            row_slice(query_b, core),
-            row_slice(output_a, core),
-        ],
-        axis=-1,
-    )
-    column = jnp.stack(
-        [late_set, ring_y(late_set, -1), ring_y(late_set, 2), ring_y(late_set, 1)]
-    )
-    feed_all, column = lax.optimization_barrier((feed_all, column))
-    all_ids = feed_all[:, 0, 5632].astype(jnp.int32)
-    feed_sum = sum_by_adapter([feed_all], 4 * core, all_ids, 4)
-    feed_sum = lax.all_gather(feed_sum, ("core", "x"), axis=0).reshape(2, 4, 4, 16, 5760)
-    late_pieces = [column, ring_z(column, -1), ring_z(column, 2), ring_z(column, 1)]
-    plane_ids = all_ids.reshape(4, 2, 2, 2)
-    plane_ids = jnp.where(core == 0, plane_ids[:, :, 0], plane_ids[:, :, 1])
-    plane_ids = rolled(jnp.swapaxes(plane_ids, 1, 2).reshape(4, 4), y)
-    plane_ids = rolled(plane_ids.T, z)
-    late_sum = sum_by_adapter(late_pieces, 0, plane_ids.reshape(16), ADAPTER_COUNT)
-    kept = jnp.where(core == 0, late_sum[:4], late_sum[4:])
-    sent = jnp.where(core == 0, late_sum[4:], late_sum[:4])
-    own_half = (kept.astype(f32) + other_core(sent).astype(f32)).astype(bf16)
+    late_pieces, grad_tokens = together((late_pieces, grad_tokens))
+    kept, sent = halves_of(sum_by_adapter(late_pieces, all_ids), core)
+    own_half = add_cores(kept, sent).astype(bf16)
     other_part = other_core(own_half)
     near = ring_by_core(jnp.concatenate([own_half, other_part], axis=0))
     far = ring_x(own_half, 2)
+    feed_grads = spread_out(
+        feed_spread_kernel, at, [feed_sum], (1024, 1024, 256, 256, 256), "feed_spread"
+    )
+    near, far, feed_grads = together((near, far, feed_grads))
+    up_b, down_a, up_a, output_b, down_b = feed_grads
     query_a, keyval_a, keyval_b, query_b, output_a = spread_out(
         late_spread_kernel,
         at,
@@ -1019,10 +1144,7 @@
         (256, 256, 64, 256, 256),
         "late_spread",
     )
-    keyval_b = keyval_b.reshape(8, 16, 4, 128)[..., :64].reshape(8, 16, 256)
-    up_b, down_a, up_a, output_b, down_b = spread_out(
-        feed_spread_kernel, at, [feed_sum], (1024, 1024, 256, 256, 256), "feed_spread"
-    )
+    keyval_b = keyval_b.reshape(8, 16, 2, 2, 128).sum(axis=3).reshape(8, 16, 256)
 
     def side_in(a):
         return jnp.swapaxes(a, 1, 2)

time: 495 us -> 492 us (level)
  starting transfers between devices: 94.7 us -> 135 us
  waiting for transfers between devices: 163 us -> 132 us
  Pallas kernels: 133 us -> 125 us
    all_gather x4 -> x2, waiting for transfers between devices: 19.5 us -> 0.02 us  [the longest x1 0.02 us: shards(): cot_all = lax.all_gather(cot_all, ('core', 'x'), axis=0, tiled=True)]
    ppermute x28 -> x33, starting transfers between devices: 30.1 us -> 48.9 us  [other_core(): return lax.ppermute(a, 'core', [(0, 1), (1, 0)])]
    ppermute x1, waiting for transfers between devices: 13.7 us -> 2.57 us  [ring_by_core(): return lax.ppermute(a, ('core', 'x'), pairs)]
    pallas_call x8, Pallas kernels: 111 us -> 103 us  [call(): pl.pallas_call(kernel, out_shape=[jax.ShapeDtypeStruct(s, d) for s, d, _...]
    ppermute x3 -> x6, starting transfers between devices: 3.34 us -> 9.95 us  [ring_y(): return lax.ppermute(a, 'y', [(i, (i + step) % 4) for i in range(4)])]
    ppermute x33 -> x37, starting transfers between devices: 33.5 us -> 40 us  [ring_x(): return lax.ppermute(a, 'x', [(i, (i + step) % 4) for i in range(4)])]
    ppermute x33 -> x37, waiting for transfers between devices: 98.6 us -> 95.5 us  [ring_x(): return lax.ppermute(a, 'x', [(i, (i + step) % 4) for i in range(4)])]
    unnamed x173 -> x185, local copies, waits for them, and re-layouts: 11.9 us -> 12.4 us
  transfers between devices with their start and end apart: 83 -> 97, of which waited for: 41 -> 45; matrix products, arithmetic and copies ran while one was open for 13% -> 10% of each run, Pallas kernels for 20% -> 19%
where the time goes in v4:
time: 492 us; the launch traced here: 483 us
  starting transfers between devices  135 us (27%)
  waiting for transfers between devices  132 us (27%)
  Pallas kernels  125 us (25%)
  local copies, waits for them, and re-layouts  31.8 us (6%)
  other arithmetic  28.1 us (6%)
  between operations  17.8 us (4%)
  matrix products  12.6 us (3%)
    pallas_call x8, Pallas kernels, call(): pl.pallas_call(kernel, out_shape=[jax.ShapeDtypeStruct(s, d) for s, d, _...  103 us
    ppermute x37, waiting for transfers between devices, ring_x(): return lax.ppermute(a, 'x', [(i, (i + step) % 4) for i in range(4)])  95.5 us
    ppermute x33, starting transfers between devices, other_core(): return lax.ppermute(a, 'core', [(0, 1), (1, 0)])  48.9 us
    ppermute x37, starting transfers between devices, ring_x(): return lax.ppermute(a, 'x', [(i, (i + step) % 4) for i in range(4)])  40 us
    pallas_call x2, Pallas kernels, spread_out(): pl.pallas_call(functools.partial(kernel, widths), out_shape=[jax.ShapeDty...  14.2 us
    unnamed x185, local copies, waits for them, and re-layouts  12.4 us
    ppermute x33, waiting for transfers between devices, other_core(): return lax.ppermute(a, 'core', [(0, 1), (1, 0)])  11.7 us
    ppermute x2, starting transfers between devices, turn(): return lax.ppermute(a, ('core', 'zh'), [(0, 0), (1, 2), (2, 1), (3, 3)])  10.2 us
  transfers between devices with their start and end apart: 97, of which 45 were waited for; matrix products, arithmetic and copies ran while one was open for 10% of the time, Pallas kernels for 19%

profile of v4, /device:TPU:1, one launch (start us, length us, event | category | flops | bytes accessed | tf_op | source)
XLA Modules:
  0.0 482.6 jit_solution(16527395334894058489)
XLA Ops:
  16.4 5.5 %collective-permute-start = (bf16[128,768]{1,0:T(8,128)(2,1)}, bf16[128,768]{1,0:T(8,128)(2,1)S(1)}, u32[]{:S(2)}, u32[]{:S(2)}) collective-permute-start(bf16[128,768]{1,0:T(8,128)(2,1)} %get-tuple-element.180), channel_id=1, source_target_pairs={{0,0},{4,8},{8,4},{12,12},{1,1},{5,9},{9,5},{13,13},{2,2},{6,10},{... | collective-permute-start | bytes 589832 | tf_op jit(solution)/shard_map/ppermute | solution.py:57
  42.6 4.7 collective-permute-start.11
  64.5 9.7 %collective-permute-done.9.refs_2_ = bf16[128,2048]{1,0:T(8,128)(2,1)S(1)} collective-permute-done((bf16[128,2048]{1,0:T(8,128)(2,1)S(1)}, bf16[128,2048]{1,0:T(8,128)(2,1)S(1)}, u32[]{:S(2)}, u32[]{:S(2)}) %collective-permute-start.9) | collective-permute-done | bytes 524320 | tf_op jit(solution)/shard_map/ppermute | solution.py:37
  75.2 4.4 assemble.1.refs_14_.refs_10_
  94.0 4.1 collective-permute-done.22.refs_13_
  103.4 21.7 %attention.1 = (bf16[2,512,128]{2,1,0:T(8,128)(2,1)}, bf16[2,512,128]{2,1,0:T(8,128)(2,1)}, bf16[2,512,256]{2,1,0:T(8,128)(2,1)}, bf16[2,8,128,256]{3,2,1,0:T(8,...) custom-call(s32[5]{0:T(128)} %stack.83.at, ...), custom_call_target="tpu_custom_call" | custom-call | flops 8999999488 | bytes 23029760 | tf_op jit(solution)/shard_map/attention/pallas_call | solution.py:648
  132.1 5.9 %collective-permute-done.25 = bf16[64,2176]{1,0:T(8,128)(2,1)S(1)} collective-permute-done((bf16[64,2176]{1,0:T(8,128)(2,1)S(1)}, bf16[64,2176]{1,0:T(8,128)(2,1)S(1)}, u32[]{:S(2)}, u32[]{:S(2)}) %collective-permute-start.25) | collective-permute-done | bytes 278560 | tf_op jit(solution)/shard_map/ppermute | solution.py:37
  140.8 10.4 %collective-permute-done.28 = bf16[128,2176]{1,0:T(8,128)(2,1)S(1)} collective-permute-done((bf16[128,2176]{1,0:T(8,128)(2,1)S(1)}, bf16[128,2176]{1,0:T(8,128)(2,1)S(1)}, u32[]{:S(2)}, u32[]{:S(2)}) %collective-permute-start.28) | collective-permute-done | bytes 557088 | tf_op jit(solution)/shard_map/ppermute | solution.py:37
  160.2 6.1 %collective-permute-done.32.refs_4_ = bf16[128,2048]{1,0:T(8,128)(2,1)S(1)} collective-permute-done((bf16[128,2048]{1,0:T(8,128)(2,1)S(1)}, bf16[128,2048]{1,0:T(8,128)(2,1)S(1)}, u32[]{:S(2)}, u32[]{:S(2)}) %collective-permute-start.32) | collective-permute-done | bytes 524320 | tf_op jit(solution)/shard_map/ppermute | solution.py:37
  168.0 4.7 collective-permute-start.33
  182.3 21.1 %feed.1 = (bf16[4,256,128]{2,1,0:T(8,128)(2,1)}, f32[4,256,1024]{2,1,0:T(8,128)}, bf16[4,256,1024]{2,1,0:T(8,128)(2,1)}, bf16[3,128,2176]{2,1,0:T(8,128)(2,1)}, ...) custom-call(s32[5]{0:T(128)} %stack.83.at, bf16[128,2048]{1,0:T(8,128)(2,1)} %copy-done.13, ...), custom_call_target="tpu_custom_call" | custom-call | flops 9500000256 | bytes 39849984 | tf_op jit(solution)/shard_map/feed/pallas_call | solution.py:648
  212.7 20.3 %feed_back.1 = (f32[32,1024]{1,0:T(8,128)}, f32[32,1024]{1,0:T(8,128)}, bf16[3,128,2176]{2,1,0:T(8,128)(2,1)}, bf16[3,128,2176]{2,1,0:T(8,128)(2,1)}, bf16[128,2...) custom-call(s32[5]{0:T(128)} %stack.83.at, bf16[2,4,128,2176]{3,2,1,0:T(8,128)(2,1)} %bitcast.220, ...), custom_call_target="tpu_custom_call" | custom-call | flops 9500000256 | bytes 37486592 | tf_op jit(solution)/shard_map/feed_back/pallas_call | solution.py:648
  247.0 6.0 %collective-permute-done.46 = bf16[64,2176]{1,0:T(8,128)(2,1)S(1)} collective-permute-done((bf16[64,2176]{1,0:T(8,128)(2,1)S(1)}, bf16[64,2176]{1,0:T(8,128)(2,1)S(1)}, u32[]{:S(2)}, u32[]{:S(2)}) %collective-permute-start.46) | collective-permute-done | bytes 278560 | tf_op jit(solution)/shard_map/ppermute | solution.py:37
  256.5 9.9 %collective-permute-done.49 = bf16[128,2176]{1,0:T(8,128)(2,1)S(1)} collective-permute-done((bf16[128,2176]{1,0:T(8,128)(2,1)S(1)}, bf16[128,2176]{1,0:T(8,128)(2,1)S(1)}, u32[]{:S(2)}, u32[]{:S(2)}) %collective-permute-start.49) | collective-permute-done | bytes 557088 | tf_op jit(solution)/shard_map/ppermute | solution.py:37
  296.8 5.5 %collective-permute-start.59 = (bf16[128,2048]{1,0:T(8,128)(2,1)S(1)}, bf16[128,2048]{1,0:T(8,128)(2,1)S(1)}, u32[]{:S(2)}, u32[]{:S(2)}) collective-permute-start(bf16[128,2048]{1,0:T(8,128)(2,1)S(1)} %copy-done.52), channel_id=1, source_target_pairs={{0,8},{8,0},{1,9},{9,1},{2,10},{10,2},{3,11},{11,3},{4,12},{12,4},... | collective-permute-start | bytes 1572872 | tf_op jit(solution)/shard_map/ppermute | solution.py:49
  305.7 4.1 collective-permute-start.63
  320.5 24.0 %attention_back.1 = (f32[32,256]{1,0:T(8,128)}, f32[32,256]{1,0:T(8,128)}, f32[32,256]{1,0:T(8,128)}, bf16[2,512,128]{2,1,0:T(8,128)(2,1)}, bf16[2,32,512]{2,1,0...) custom-call(s32[5]{0:T(128)} %stack.83.at, ...), custom_call_target="tpu_custom_call" | custom-call | flops 8000000000 | bytes 22470656 | tf_op jit(solution)/shard_map/attention_back/pallas_call | solution.py:648
  344.6 4.5 collective-permute-done.66.refs_2_
  351.8 5.1 %sum_by_adapter.2 = bf16[8,16,5760]{2,1,0:T(8,128)(2,1)} custom-call(s32[16]{0:T(128)} %maximum_convert_fusion.ids, bf16[4,16,5760]{2,1,0:T(8,128)(2,1)} %copy-done.6, bf16[4,16,5760]{2,1,0:T(8,128)(2,1)} %copy-done.27, bf16[4,16,5760]{2,1,0:T(8,128)(2,1)} %copy-done.26, bf16[4,16,5760]{2,1,0:T(8,128)(2,1)} %copy-done.25), custom_call_target="tpu_custom_call" | custom-call | tf_op jit(solution)/shard_map/sum_by_adapter/pallas_call | solution.py:686
  368.7 5.5 %late.1 = (bf16[4,16,1152]{2,1,0:T(8,128)(2,1)}, bf16[4,16,1152]{2,1,0:T(8,128)(2,1)}) custom-call(s32[5]{0:T(128)} %stack.83.at, bf16[128,2048]{1,0:T(8,128)(2,1)} %copy-done.8, bf16[128,2048]{1,0:T(8,128)(2,1)} %copy-done.36, bf16[128,2048]{1,0:T(8,128)(2,1)} %copy-done.20, bf16[128,2048]{1,0:T(8,128)(2,1)} %copy-done.37, bf16[128,2048]{1,0:T(8,128)(2,1)} %copy-done.19, ...), custom_call_target="tpu_custom_call" | custom-call | bytes 5144576 | tf_op jit(solution)/shard_map/late/pallas_call | solution.py:648
  397.8 14.7 %collective-permute-done.82 = bf16[128,2688]{1,0:T(8,128)(2,1)S(1)} collective-permute-done((bf16[128,2688]{1,0:T(8,128)(2,1)}, bf16[128,2688]{1,0:T(8,128)(2,1)S(1)}, u32[]{:S(2)}, u32[]{:S(2)}) %collective-permute-start.82) | collective-permute-done | bytes 688160 | tf_op jit(solution)/shard_map/ppermute | solution.py:37
  434.4 6.0 %collective-permute-start.88 = (bf16[4,16,2176]{2,1,0:T(8,128)(2,1)S(1)}, bf16[4,16,2176]{2,1,0:T(8,128)(2,1)S(1)}, u32[]{:S(2)}, u32[]{:S(2)}) collective-permute-start(bf16[4,16,2176]{2,1,0:T(8,128)(2,1)S(1)} %broadcast_select_fusion.2), channel_id=1, source_target_pairs={{0,8},{8,0},{1,9},{9,1},{2,10},{10,2},{3,11},{11,3},{4,12},{12,4},... | collective-permute-start | bytes 835592 | tf_op jit(solution)/shard_map/ppermute | solution.py:49
  448.0 8.4 %feed_spread.1 = (f32[8,16,8192]{2,1,0:T(8,128)}, f32[8,16,8192]{2,1,0:T(8,128)}, f32[8,16,2048]{2,1,0:T(8,128)}, f32[8,16,2048]{2,1,0:T(8,128)}, f32[8,16,2048]{2,1,0:T(8,128)}) custom-call(s32[5]{0:T(128)} %stack.83.at, bf16[2,4,4,16,5760]{4,3,2,1,0:T(8,128)(2,1)} %bitcast.203), custom_call_target="tpu_custom_call" | custom-call | tf_op jit(solution)/shard_map/feed_spread/pallas_call | solution.py:708
  467.7 5.7 %late_spread.1 = (f32[8,16,2048]{2,1,0:T(8,128)}, f32[8,16,2048]{2,1,0:T(8,128)}, f32[8,16,512]{2,1,0:T(8,128)}, f32[8,16,2048]{2,1,0:T(8,128)}, f32[8,16,2048]{2,1,0:T(8,128)}) custom-call(s32[5]{0:T(128)} %stack.83.at, bf16[4,16,2176]{2,1,0:T(8,128)(2,1)} %copy-done.7, bf16[4,16,2176]{2,1,0:T(8,128)(2,1)} %copy-done.22, bf16[8,16,2176]{2,1,0:T(8,128)(2,1)} %copy-done.32, ...), custom_call_target="tpu_custom_call" | custom-call | tf_op jit(solution)/shard_map/late_spread/pallas_call | solution.py:708
  (525 shorter events, 246.6 us)
Async XLA Ops:
  7.2 72.5 %all-gather.5.cloned.1.call-start = ((), (), s32[]{:S(2)}) async-start(), calls=%async_computation | async-start | bytes 5013504 | tf_op jit(solution)/shard_map/all_gather | solution.py:778
  11.4 170.9 %all-gather.7.cloned.1.call-start = ((), (), s32[]{:S(2)}) async-start(), calls=%async_computation.1 | async-start | bytes 17301504 | tf_op jit(solution)/shard_map/all_gather | solution.py:901
  11.4 18.8 %collective-permute-start.4 = (s32[1,1]{1,0:T(1,128)}, s32[1,1]{1,0:T(1,128)}, u32[]{:S(2)}, u32[]{:S(2)}) collective-permute-start(s32[1,1]{1,0:T(1,128)} %param.43), channel_id=1, source_target_pairs={{0,8},{8,0},{1,9},{9,1},{2,10},{10,2},{3,11},{11,3},{4,12},{12,4},... | collective-permute-start | bytes 20 | tf_op jit(solution)/shard_map/ppermute | solution.py:49
  34.4 39.8 %collective-permute-start.7 = (bf16[4,128,768]{2,1,0:T(8,128)(2,1)S(1)}, bf16[4,128,768]{2,1,0:T(8,128)(2,1)}, u32[]{:S(2)}, u32[]{:S(2)}) collective-permute-start(bf16[4,128,768]{2,1,0:T(8,128)(2,1)S(1)} %pad_maximum_fusion.refs_0_), channel_id=1, source_target_pairs={{0,16},{8,40},{16,4},{24,56},{4,20},{12,44},{20,0},{28,60},{32,48}... | collective-permute-start | bytes 2359304 | tf_op jit(solution)/shard_map/ppermute | solution.py:78
  35.8 38.4 %collective-permute-start.6 = (bf16[4,128,768]{2,1,0:T(8,128)(2,1)S(1)}, bf16[4,128,768]{2,1,0:T(8,128)(2,1)}, u32[]{:S(2)}, u32[]{:S(2)}) collective-permute-start(bf16[4,128,768]{2,1,0:T(8,128)(2,1)S(1)} %pad_maximum_fusion.refs_0_), channel_id=1, source_target_pairs={{0,4},{8,72},{16,20},{24,88},{4,0},{12,76},{20,16},{28,92},{32,36}... | collective-permute-start | bytes 2359304 | tf_op jit(solution)/shard_map/ppermute | solution.py:78
  38.7 35.5 %collective-permute-start.5 = (bf16[4,128,768]{2,1,0:T(8,128)(2,1)S(1)}, bf16[4,128,768]{2,1,0:T(8,128)(2,1)}, u32[]{:S(2)}, u32[]{:S(2)}) collective-permute-start(bf16[4,128,768]{2,1,0:T(8,128)(2,1)S(1)} %pad_maximum_fusion.refs_0_), channel_id=1, source_target_pairs={{0,20},{8,104},{16,0},{24,120},{4,16},{12,108},{20,4},{28,124},{32... | collective-permute-start | bytes 2359304 | tf_op jit(solution)/shard_map/ppermute | solution.py:78
  42.6 18.9 %collective-permute-start.11 = (bf16[48,2560]{1,0:T(8,128)(2,1)S(1)}, bf16[48,2560]{1,0:T(8,128)(2,1)S(1)}, u32[]{:S(2)}, u32[]{:S(2)}) collective-permute-start(bf16[48,2560]{1,0:T(8,128)(2,1)S(1)} %maximum_maximum_fusion.3), channel_id=1, source_target_pairs={{0,0},{4,8},{8,4},{12,12},{1,1},{5,9},{9,5},{13,13},{2,2},{6,10},{... | collective-permute-start | bytes 737288 | tf_op jit(solution)/shard_map/ppermute | solution.py:57
  47.4 15.4 %collective-permute-start.10 = (bf16[128,2048]{1,0:T(8,128)(2,1)S(1)}, bf16[128,2048]{1,0:T(8,128)(2,1)S(1)}, u32[]{:S(2)}, u32[]{:S(2)}) collective-permute-start(bf16[128,2048]{1,0:T(8,128)(2,1)S(1)} %fusion.18.refs_0_), channel_id=1, source_target_pairs={{0,3},{1,0},{2,1},{3,2},{4,7},{5,4},{6,5},{7,6},{8,11},{9,8},{10,9... | collective-permute-start | bytes 1572872 | tf_op jit(solution)/shard_map/ppermute | solution.py:37
  79.7 368.3 %all-gather.9.cloned.1.call-start = ((), (), s32[]{:S(2)}) async-start(), calls=%async_computation.2 | async-start | bytes 6635520 | tf_op jit(solution)/shard_map/all_gather | solution.py:1109
  140.7 13.6 %collective-permute-start.26 = (bf16[128,2176]{1,0:T(8,128)(2,1)S(1)}, bf16[128,2176]{1,0:T(8,128)(2,1)S(1)}, u32[]{:S(2)}, u32[]{:S(2)}) collective-permute-start(bf16[128,2176]{1,0:T(8,128)(2,1)S(1)} %pad_maximum_fusion.5), channel_id=1, source_target_pairs={{0,1},{1,2},{2,3},{3,0},{4,5},{5,6},{6,7},{7,4},{8,9},{9,10},{10,1... | collective-permute-start | bytes 1671176 | tf_op jit(solution)/shard_map/ppermute | solution.py:37
  156.9 23.6 %collective-permute-start.29 = (bf16[128,2048]{1,0:T(8,128)(2,1)S(1)}, bf16[128,2048]{1,0:T(8,128)(2,1)S(1)}, u32[]{:S(2)}, u32[]{:S(2)}) collective-permute-start(bf16[128,2048]{1,0:T(8,128)(2,1)S(1)} %add_convert_fusion.6.refs_0_.refs_1_), channel_id=1, source_target_pairs={{0,8},{8,0},{1,9},{9,1},{2,10},{10,2},{3,11},{11,3},{4,12},{12,4},... | collective-permute-start | bytes 1572872 | tf_op jit(solution)/shard_map/ppermute | solution.py:49
  209.9 23.1 %collective-permute-start.40 = (bf16[128,2176]{1,0:T(8,128)(2,1)S(1)}, bf16[128,2176]{1,0:T(8,128)(2,1)S(1)}, u32[]{:S(2)}, u32[]{:S(2)}) collective-permute-start(bf16[128,2176]{1,0:T(8,128)(2,1)S(1)} %get-tuple-element.239), channel_id=1, source_target_pairs={{0,3},{1,0},{2,1},{3,2},{4,7},{5,4},{6,5},{7,6},{8,11},{9,8},{10,9... | collective-permute-start | bytes 1671176 | tf_op jit(solution)/shard_map/ppermute | solution.py:37
  211.0 22.0 %collective-permute-start.41 = (bf16[128,2176]{1,0:T(8,128)(2,1)S(1)}, bf16[128,2176]{1,0:T(8,128)(2,1)S(1)}, u32[]{:S(2)}, u32[]{:S(2)}) collective-permute-start(bf16[128,2176]{1,0:T(8,128)(2,1)S(1)} %get-tuple-element.240), channel_id=1, source_target_pairs={{0,1},{1,2},{2,3},{3,0},{4,5},{5,6},{6,7},{7,4},{8,9},{9,10},{10,1... | collective-permute-start | bytes 1671176 | tf_op jit(solution)/shard_map/ppermute | solution.py:37
  211.4 25.5 %collective-permute-start.42 = (bf16[128,2176]{1,0:T(8,128)(2,1)S(1)}, bf16[128,2176]{1,0:T(8,128)(2,1)S(1)}, u32[]{:S(2)}, u32[]{:S(2)}) collective-permute-start(bf16[128,2176]{1,0:T(8,128)(2,1)S(1)} %add_convert_fusion.3), channel_id=1, source_target_pairs={{0,2},{1,3},{2,0},{3,1},{4,6},{5,7},{6,4},{7,5},{8,10},{9,11},{10,... | collective-permute-start | bytes 1671176 | tf_op jit(solution)/shard_map/ppermute | solution.py:37
  253.2 13.2 %collective-permute-start.49 = (bf16[128,2176]{1,0:T(8,128)(2,1)S(1)}, bf16[128,2176]{1,0:T(8,128)(2,1)S(1)}, u32[]{:S(2)}, u32[]{:S(2)}) collective-permute-start(bf16[128,2176]{1,0:T(8,128)(2,1)S(1)} %pad_maximum_fusion.8), channel_id=1, source_target_pairs={{0,3},{1,0},{2,1},{3,2},{4,7},{5,4},{6,5},{7,6},{8,11},{9,8},{10,9... | collective-permute-start | bytes 1671176 | tf_op jit(solution)/shard_map/ppermute | solution.py:37
  255.8 13.8 %collective-permute-start.47 = (bf16[128,2176]{1,0:T(8,128)(2,1)S(1)}, bf16[128,2176]{1,0:T(8,128)(2,1)S(1)}, u32[]{:S(2)}, u32[]{:S(2)}) collective-permute-start(bf16[128,2176]{1,0:T(8,128)(2,1)S(1)} %pad_maximum_fusion.7), channel_id=1, source_target_pairs={{0,1},{1,2},{2,3},{3,0},{4,5},{5,6},{6,7},{7,4},{8,9},{9,10},{10,1... | collective-permute-start | bytes 1671176 | tf_op jit(solution)/shard_map/ppermute | solution.py:37
  296.8 18.0 %collective-permute-start.59 = (bf16[128,2048]{1,0:T(8,128)(2,1)S(1)}, bf16[128,2048]{1,0:T(8,128)(2,1)S(1)}, u32[]{:S(2)}, u32[]{:S(2)}) collective-permute-start(bf16[128,2048]{1,0:T(8,128)(2,1)S(1)} %copy-done.52), channel_id=1, source_target_pairs={{0,8},{8,0},{1,9},{9,1},{2,10},{10,2},{3,11},{11,3},{4,12},{12,4},... | collective-permute-start | bytes 1572872 | tf_op jit(solution)/shard_map/ppermute | solution.py:49
  315.6 28.9 %collective-permute-start.67 = (bf16[4,16,5760]{2,1,0:T(8,128)(2,1)S(1)}, bf16[4,16,5760]{2,1,0:T(8,128)(2,1)S(1)}, u32[]{:S(2)}, u32[]{:S(2)}) collective-permute-start(bf16[4,16,5760]{2,1,0:T(8,128)(2,1)S(1)} %pad_maximum_fusion.1.refs_0_), channel_id=1, source_target_pairs={{0,16},{16,4},{4,20},{20,0},{1,17},{17,5},{5,21},{21,1},{2,18},{18... | collective-permute-start | bytes 2211848 | tf_op jit(solution)/shard_map/ppermute | solution.py:45
  317.1 32.1 %collective-permute-start.66 = (bf16[4,16,5760]{2,1,0:T(8,128)(2,1)S(1)}, bf16[4,16,5760]{2,1,0:T(8,128)(2,1)S(1)}, u32[]{:S(2)}, u32[]{:S(2)}) collective-permute-start(bf16[4,16,5760]{2,1,0:T(8,128)(2,1)S(1)} %pad_maximum_fusion.1.refs_0_), channel_id=1, source_target_pairs={{0,4},{16,20},{4,0},{20,16},{1,5},{17,21},{5,1},{21,17},{2,6},{18,... | collective-permute-start | bytes 2211848 | tf_op jit(solution)/shard_map/ppermute | solution.py:45
  318.9 31.8 %collective-permute-start.65 = (bf16[4,16,5760]{2,1,0:T(8,128)(2,1)S(1)}, bf16[4,16,5760]{2,1,0:T(8,128)(2,1)S(1)}, u32[]{:S(2)}, u32[]{:S(2)}) collective-permute-start(bf16[4,16,5760]{2,1,0:T(8,128)(2,1)S(1)} %pad_maximum_fusion.1.refs_0_), channel_id=1, source_target_pairs={{0,20},{16,0},{4,16},{20,4},{1,21},{17,1},{5,17},{21,5},{2,22},{18... | collective-permute-start | bytes 2211848 | tf_op jit(solution)/shard_map/ppermute | solution.py:45
  360.3 13.9 %collective-permute-start.71 = (bf16[3,128,2688]{2,1,0:T(8,128)(2,1)}, bf16[3,128,2688]{2,1,0:T(8,128)(2,1)}, u32[]{:S(2)}, u32[]{:S(2)}) collective-permute-start(bf16[3,128,2688]{2,1,0:T(8,128)(2,1)} %get-tuple-element.301), channel_id=1, source_target_pairs={{0,8},{8,0},{1,9},{9,1},{2,10},{10,2},{3,11},{11,3},{4,12},{12,4},... | collective-permute-start | bytes 6193160 | tf_op jit(solution)/shard_map/ppermute | solution.py:49
  386.6 25.9 %collective-permute-start.82 = (bf16[128,2688]{1,0:T(8,128)(2,1)}, bf16[128,2688]{1,0:T(8,128)(2,1)S(1)}, u32[]{:S(2)}, u32[]{:S(2)}) collective-permute-start(bf16[128,2688]{1,0:T(8,128)(2,1)} %pad_maximum_fusion.2), channel_id=1, source_target_pairs={{0,1},{1,2},{2,3},{3,0},{4,5},{5,6},{6,7},{7,4},{8,9},{9,10},{10,1... | collective-permute-start | bytes 2064392 | tf_op jit(solution)/shard_map/ppermute | solution.py:37
  387.2 25.6 %collective-permute-start.83 = (bf16[128,2688]{1,0:T(8,128)(2,1)S(1)}, bf16[128,2688]{1,0:T(8,128)(2,1)S(1)}, u32[]{:S(2)}, u32[]{:S(2)}) collective-permute-start(bf16[128,2688]{1,0:T(8,128)(2,1)S(1)} %pad_maximum_fusion.3), channel_id=1, source_target_pairs={{0,3},{1,0},{2,1},{3,2},{4,7},{5,4},{6,5},{7,6},{8,11},{9,8},{10,9... | collective-permute-start | bytes 2064392 | tf_op jit(solution)/shard_map/ppermute | solution.py:37
  444.5 15.9 %collective-permute-start.90 = (bf16[8,16,2176]{2,1,0:T(8,128)(2,1)S(1)}, bf16[8,16,2176]{2,1,0:T(8,128)(2,1)S(1)}, u32[]{:S(2)}, u32[]{:S(2)}) collective-permute-start(bf16[8,16,2176]{2,1,0:T(8,128)(2,1)S(1)} %pad_maximum_fusion.9), channel_id=1, source_target_pairs={{0,1},{1,2},{2,3},{3,0},{8,11},{9,8},{10,9},{11,10},{4,5},{5,6},{6... | collective-permute-start | bytes 1671176 | tf_op jit(solution)/shard_map/ppermute | solution.py:152
  (162 other events, 1328.5 us)
Sparse Core Ops, SparseCore 0:
  11.5 36.8 all-gather.4
  79.8 101.0 all-gather.6
  384.0 47.0 all-gather.8

commit v5 on v4

--- a/solution.py
+++ b/solution.py
@@ -81,11 +81,12 @@
 
 
 def gather_sides(a):
-    return a, other_core(a), ring_x(a, 1), ring_x(a, -1)
-
-
-def gather_rest(a, near, left, right):
+    return a, ring_x(a, 1), ring_x(a, -1)
+
+
+def gather_rest(a, left, right, near=None):
     half = a.shape[0] // 2
+    near = other_core(a) if near is None else near
     top, bottom = ring_x(left[:half], 1), ring_x(right[half:], -1)
     return (
         (a, near),
@@ -96,7 +97,8 @@
 
 
 def gather_row(a):
-    return gather_rest(*gather_sides(a))
+    near = other_core(a)
+    return gather_rest(*gather_sides(a), near)
 
 
 def add_cores(mine, theirs):
@@ -141,10 +143,6 @@
 
 def gather_z(a):
     return [a, ring_z(a, -1), ring_z(a, 2), ring_z(a, 1)]
-
-
-def halves_of(sums, core):
-    return jnp.where(core == 0, sums[:4], sums[4:]), jnp.where(core == 0, sums[4:], sums[:4])
 
 
 def ring_by_core(a):
@@ -241,8 +239,8 @@
     core, x = at[0], at[1]
     for p in range(4):
         there = lax.rem(x + PLACES[p], 4)
-        copy(gathered.at[core, there], target_of(p, 0), sem_of(p))
-        copy(gathered.at[1 - core, there], target_of(p, 1), sem_of(p))
+        copy(gathered.at[core, there], target_of(p, 0), sem_of(p, 0))
+        copy(gathered.at[1 - core, there], target_of(p, 1), sem_of(p, 1))
 
 
 def assemble_kernel(at, *refs):
@@ -257,23 +255,87 @@
     wait(out, sem)
 
 
-def pack_kernel(at, query, keyval, output, up, down, attention_out, feed_out):
-    attention_out[:, :256] = query[...]
-    attention_out[:, 256:512] = keyval[...]
-    attention_out[:, 512:] = output[...].astype(f32).T.astype(bf16)
-    feed_out[:, :1024] = up[...]
-    feed_out[:, 1024:] = down[...].astype(f32).T.astype(bf16)
-
-
-def sum_kernel(ids, *refs):
-    pieces, (out, total) = refs[:-2], refs[-2:]
+def pack_kernel(at, *refs):
+    first = 0
+    for part in refs[:-2]:
+        refs[-1][:, first : first + part.shape[1]] = part[...]
+        first += part.shape[1]
+    refs[-1][:, first:] = refs[-2][...].astype(f32).T.astype(bf16)
+
+
+def norm_kernel(at, rows, gain, shift, out):
+    values = layer_norm(
+        rows[...].astype(f32), gain[...].astype(f32), shift[...].astype(f32)
+    )
+    out[...] = values.astype(bf16)
+
+
+def select_kernel(at, *refs):
+    pairs = [refs[2 * n : 2 * n + 2] for n in range(10)]
+    q_bias, u_bias = refs[20:22]
+    small, q_in, u_in, o_out, d_out, kv_out, bias = refs[22:]
+    for out, count in ((q_in, 4), (u_in, 2), (o_out, 2), (d_out, 2)):
+        out[16 * count :] = jnp.zeros((RIDE - 16 * count, MODEL_WIDTH), bf16)
+    kv_out[...] = jnp.zeros_like(kv_out)
+    for c in range(2):
+        here, after = slice(16 * c, 16 * c + 16), slice(32 + 16 * c, 48 + 16 * c)
+        q_in[here] = pairs[0][c][0]
+        q_in[after] = pairs[1][c][0]
+        u_in[here] = pairs[2][c][0]
+        o_out[here] = pairs[3][c][0]
+        d_out[here] = pairs[4][c][0]
+        kv_out[after] = pairs[5][c][0]
+        first = 0
+        for n in range(6, 10):
+            width = pairs[n][c].shape[2]
+            small[here, first : first + width] = pairs[n][c][0]
+            first += width
+    small[32:] = jnp.zeros((16, 2560), bf16)
+    small[32:33, :256] = q_bias[...]
+    small[32:33, 512:1536] = u_bias[...]
+    x, zh = at[2], at[3]
+
+    def block_of(place):
+        step = jnp.where(place == 0, 0, jnp.where(place == 1, 3, place - 1))
+        return ((x + step) & 3) >> 1
+
+    key = lax.broadcasted_iota(jnp.int32, (8, 4 * ROWS), 0)
+    query = lax.broadcasted_iota(jnp.int32, (8, 4 * ROWS), 1) >> 7
+    own = jnp.logical_and(key < 4, block_of(key) <= block_of(query))
+    other = jnp.logical_and(key >= 4, zh == 1)
+    bias[...] = jnp.where(jnp.logical_or(own, other), 0.0, -1e30)
+
+
+def turned_kernel(at, small, q_out, o_in, u_out, d_in, q_bias, u_bias):
+    first = 0
+    for out in (q_out, o_in, u_out, d_in):
+        width = out.shape[1]
+        out[:32] = small[:32, first : first + width]
+        out[32:] = jnp.zeros((RIDE - 32, width), bf16)
+        first += width
+    q_bias[...] = small[32:33, :256].astype(f32)
+    u_bias[...] = small[32:33, 512:1536].astype(f32)
+
+
+def own_keyval_kernel(at, rows, w, q_in, kv_out, kv_bias, out):
+    inner = dot_t(rows[...], q_in[...])
+    lane = lax.broadcasted_iota(jnp.int32, (ROWS, RIDE), 1)
+    inner = jnp.where(lane // ADAPTER_RANK == 2 + at[0], inner, 0.0).astype(bf16)
+    keyval = dot(rows[...], w[...]) + kv_bias[...] + dot(inner, kv_out[...])
+    out[:, :256] = keyval.astype(bf16)
+    out[:, 256:] = inner
+
+
+def sum_kernel(at, *refs):
+    pieces, (kept, sent, total) = refs[:-3], refs[-3:]
     total[...] = jnp.zeros_like(total)
-    row = 0
+    row = 1
     for piece in pieces:
         for k in range(piece.shape[0]):
-            total[ids[row]] += piece[k].astype(f32)
+            total[at[row]] += piece[k].astype(f32)
             row += 1
-    out[...] = total[...].astype(bf16)
+    kept[...] = total[pl.ds(4 * at[0], 4)].astype(bf16)
+    sent[...] = total[pl.ds(4 - 4 * at[0], 4)].astype(bf16)
 
 
 def slices_kernel(count, at, *refs):
@@ -357,11 +419,11 @@
 
 def attention_kernel(at, *refs):
     rows_in = split_pieces(refs[:10])
-    kv_in = refs[10:14]
-    w, q_in, q_out, kv_out, o_in, q_bias, kv_bias, bias = refs[14:22]
-    inner_out, inner_far, query_out, kv_all, lse_out, att_out = refs[22:28]
-    parts, far_parts = refs[28:30], refs[30:32]
-    rows, kvs, ws, sems = refs[32:]
+    kv_in = refs[10:15]
+    w, q_in, q_out, kv_out, o_in, q_bias, kv_bias, bias = refs[15:23]
+    inner_out, inner_far, query_out, kv_all, lse_out, att_out = refs[23:29]
+    parts, far_parts = refs[29:31], refs[31:33]
+    rows, kvs, ws, sems = refs[33:]
     s = pl.program_id(0)
     core = at[0]
 
@@ -369,9 +431,17 @@
     def _():
         copy(w, ws, sems.at[2])
         copy_rows(rows_in, rows, sems)
-        for p in range(4):
-            for q in range(2):
-                copy(kv_in[p].at[pl.ds(q * ROWS, ROWS)], kvs.at[q, p], sems.at[3])
+        pair, near, near_other, far, far_other = kv_in
+        first, second = pl.ds(0, ROWS), pl.ds(ROWS, ROWS)
+        side = jnp.where(core == 0, 1, 2)
+        copy(pair.at[first], kvs.at[0, 0], sems.at[3])
+        copy(pair.at[second], kvs.at[1, 0], sems.at[3])
+        copy(near.at[first], kvs.at[0, side], sems.at[3])
+        copy(near.at[second], kvs.at[1, side], sems.at[3])
+        copy(near_other.at[first], kvs.at[1, 3 - side], sems.at[3])
+        copy(near_other.at[second], kvs.at[0, 3 - side], sems.at[3])
+        copy(far, kvs.at[0, 3], sems.at[3])
+        copy(far_other, kvs.at[1, 3], sems.at[3])
         wait(ws, sems.at[2])
         wait(kvs, sems.at[3])
 
@@ -436,86 +506,64 @@
 
 def feed_kernel(at, *refs):
     rows_in = split_pieces(refs[:10])
-    feed, u_in, u_out, d_in, u_bias = refs[10:15]
-    inner_out, pre_out, act_out = refs[15:18]
-    parts, far_parts = refs[18:20], refs[20:22]
-    rows, up, down, sems = refs[22:]
+    cot, feed, u_in, u_out, d_in, u_bias = refs[10:16]
+    up_b, down_a = refs[16:18]
+    down_parts, down_far = refs[18:20], refs[20:22]
+    up_parts, up_far = refs[22:24], refs[24:26]
+    rows, grads, up, down, slopes, sems = refs[26:]
     p = pl.program_id(0)
     core = at[0]
 
     @pl.when(p == 0)
     def _():
-        copy(feed.at[:, core, :, pl.ds(0, 1024)], up, sems.at[4])
-        for k in range(4):
+        copy_place(rows_in[0], rows.at[0, pl.ds(0, ROWS)], rows.at[0, pl.ds(ROWS, ROWS)], sems.at[0])
+        copy(feed.at[:, core, :, pl.ds(0, 1024)], up, sems.at[8])
+        copy(feed.at[:, core, :, pl.ds(1024, 1024)], down, sems.at[9])
+        copy_row(
+            cot,
+            at,
+            lambda k, which: grads.at[k, pl.ds(which * ROWS, ROWS)],
+            lambda k, which: sems.at[4 + k],
+        )
+        for k in range(1, 4):
             copy_place(
                 rows_in[k], rows.at[k, pl.ds(0, ROWS)], rows.at[k, pl.ds(ROWS, ROWS)], sems.at[k]
             )
-        copy(feed.at[:, core, :, pl.ds(1024, 1024)], down, sems.at[5])
-        wait(up, sems.at[4])
+        up_b[...] = jnp.zeros_like(up_b)
+        down_a[...] = jnp.zeros_like(down_a)
+        wait(up, sems.at[8])
 
     wait(rows.at[p], sems.at[p])
     mask = place_mask(core)
     x = rows[p]
-    inner = jnp.where(mask, dot_t(x, u_in[...]), 0.0).astype(bf16)
-    inner_out[0] = inner
+    inner = jnp.where(mask, dot_t(x, u_in[...]), 0.0)
+    inner_t, inner = inner.T[:32].astype(bf16), inner.astype(bf16)
     pre = dot(x, up[...].reshape(MODEL_WIDTH, 1024)) + u_bias[...] + dot(inner, u_out[...])
-    pre_out[0] = pre
-    act = gelu_tanh(pre).astype(bf16)
-    act_out[0] = act
-
-    @pl.when(p == 0)
-    def _():
-        wait(down, sems.at[5])
-
-    low = jnp.where(mask, dot_t(act, d_in[...]), 0.0).astype(bf16)
-    out = dot_t(act, down[...].reshape(MODEL_WIDTH, 1024)).astype(bf16)
-    store_parts(p, parts, far_parts, out, low)
-
-
-def feed_back_kernel(at, *refs):
-    cot, feed, pre_in, act_in, inner_in, d_in, u_out = refs[:7]
-    up_b, down_a = refs[7:9]
-    parts, far_parts = refs[9:11], refs[11:13]
-    rows, up, down, sems = refs[13:]
-    p = pl.program_id(0)
-    core = at[0]
-
-    @pl.when(p == 0)
-    def _():
-        copy(feed.at[:, core, :, pl.ds(1024, 1024)], down, sems.at[5])
-        copy_row(
-            cot, at, lambda k, which: rows.at[k, pl.ds(which * ROWS, ROWS)], lambda k: sems.at[k]
-        )
-        copy(feed.at[:, core, :, pl.ds(0, 1024)], up, sems.at[4])
-        up_b[...] = jnp.zeros_like(up_b)
-        down_a[...] = jnp.zeros_like(down_a)
-        wait(down, sems.at[5])
-
-    wait(rows.at[p], sems.at[p])
-    mask = place_mask(core)
-    grad, back = rows[p, :, :MODEL_WIDTH], rows[p, :, MODEL_WIDTH:]
-    back_t = back.astype(f32).T[:32].astype(bf16)
-    act = act_in[0]
-    down_a[...] += dot(back_t, act)
-    grad_act = dot(grad, down[...].reshape(MODEL_WIDTH, 1024)) + dot(back, d_in[...])
-    pre = pre_in[0]
     k0 = math.sqrt(2.0 / math.pi)
     square = pre * pre
     bend = jnp.tanh(k0 * (pre + 0.044715 * square * pre))
-    slope = 0.5 * (1.0 + bend) + 0.5 * pre * (1.0 - bend * bend) * (
+    act = (0.5 * pre * (1.0 + bend)).astype(bf16)
+    slopes[...] = 0.5 * (1.0 + bend) + 0.5 * pre * (1.0 - bend * bend) * (
         k0 * (1.0 + 3.0 * 0.044715 * square)
     )
-    grad_pre = (grad_act * slope).astype(bf16)
-    inner_t = inner_in[0].astype(f32).T[:32].astype(bf16)
+
+    @pl.when(p == 0)
+    def _():
+        wait(down, sems.at[9])
+
+    low = jnp.where(mask, dot_t(act, d_in[...]), 0.0).astype(bf16)
+    out = dot_t(act, down[...].reshape(MODEL_WIDTH, 1024)).astype(bf16)
+    store_parts(p, down_parts, down_far, out, low)
+
+    wait(grads.at[p], sems.at[4 + p])
+    grad, back = grads[p, :, :MODEL_WIDTH], grads[p, :, MODEL_WIDTH:]
+    down_a[...] += dot(back.astype(f32).T[:32].astype(bf16), act)
+    grad_act = dot(grad, down[...].reshape(MODEL_WIDTH, 1024)) + dot(back, d_in[...])
+    grad_pre = (grad_act * slopes[...]).astype(bf16)
     up_b[...] += dot(inner_t, grad_pre)
     low = jnp.where(mask, dot_t(grad_pre, u_out[...]), 0.0).astype(bf16)
-
-    @pl.when(p == 0)
-    def _():
-        wait(up, sems.at[4])
-
     out = dot_t(grad_pre, up[...].reshape(MODEL_WIDTH, 1024)).astype(bf16)
-    store_parts(p, parts, far_parts, out, low)
+    store_parts(p, up_parts, up_far, out, low)
 
 
 def late_kernel(at, *refs):
@@ -552,19 +600,23 @@
 
 
 def attention_back_kernel(at, *refs):
-    rows_in = split_pieces(refs[:10])
-    w, inner_in, inner_far, query_in, kv_in, lse_in, att_in = refs[10:17]
-    o_out, o_in, q_out, kv_out, bias = refs[17:22]
-    query_b, output_a, keyval_b, backs, backs_far = refs[22:27]
-    parts, far_parts = refs[27:29], refs[29:31]
-    rows, ws, grad_k, grad_v, sems = refs[31:]
+    branch, w, inner_in, inner_far, query_in, kv_in, lse_in, att_in = refs[:8]
+    o_out, o_in, q_out, kv_out, bias = refs[8:13]
+    query_b, output_a, keyval_b, backs, backs_far = refs[13:18]
+    parts, far_parts = refs[18:20], refs[20:22]
+    rows, ws, grad_k, grad_v, sems = refs[22:]
     s = pl.program_id(0)
     core = at[0]
 
     @pl.when(s == 0)
     def _():
         copy(w, ws, sems.at[2])
-        copy_rows(rows_in, rows, sems)
+        copy_row(
+            branch,
+            at,
+            lambda p, which: rows.at[which, pl.ds(p * ROWS, ROWS)],
+            lambda p, which: sems.at[which],
+        )
         query_b[...] = jnp.zeros_like(query_b)
         output_a[...] = jnp.zeros_like(output_a)
         keyval_b[...] = jnp.zeros_like(keyval_b)
@@ -680,12 +732,13 @@
     return pltpu.SemaphoreType.DMA((n,))
 
 
-def sum_by_adapter(pieces, ids):
-    width, count = pieces[0].shape[-1], ADAPTER_COUNT
+def sum_by_adapter(pieces, core, ids):
+    width = pieces[0].shape[-1]
     block = max(w for w in range(128, 3713, 128) if width % w == 0)
+    half = (ADAPTER_COUNT // 2, ADAPTER_RANK)
     return pl.pallas_call(
         sum_kernel,
-        out_shape=jax.ShapeDtypeStruct((count, ADAPTER_RANK, width), bf16),
+        out_shape=[jax.ShapeDtypeStruct((*half, width), bf16)] * 2,
         grid_spec=pltpu.PrefetchScalarGridSpec(
             num_scalar_prefetch=1,
             grid=(width // block,),
@@ -693,12 +746,12 @@
                 pl.BlockSpec((p.shape[0], ADAPTER_RANK, block), lambda i, at: (0, 0, i))
                 for p in pieces
             ],
-            out_specs=pl.BlockSpec((count, ADAPTER_RANK, block), lambda i, at: (0, 0, i)),
-            scratch_shapes=[pltpu.VMEM((count, ADAPTER_RANK, block), f32)],
+            out_specs=[pl.BlockSpec((*half, block), lambda i, at: (0, 0, i))] * 2,
+            scratch_shapes=[pltpu.VMEM((ADAPTER_COUNT, ADAPTER_RANK, block), f32)],
         ),
         compiler_params=pltpu.CompilerParams(vmem_limit_bytes=VMEM_LIMIT),
         name="sum_by_adapter",
-    )(ids, *pieces)
+    )(jnp.concatenate([jnp.reshape(core, (1,)), ids]).astype(jnp.int32), *pieces)
 
 
 def spread_out(kernel, at, pieces, widths, name):
@@ -768,125 +821,84 @@
     gain_one, shift_one = attention_norm_scale.astype(f32), attention_norm_bias.astype(f32)
     gain_two, shift_two = feedforward_norm_scale.astype(f32), feedforward_norm_bias.astype(f32)
 
-    def ride(inner, first):
-        wide = jnp.pad(inner, ((0, 0), (first, RIDE - 16 - first)))
-        return jnp.where(core == 0, wide, jnp.roll(wide, 16, axis=1))
+    def pack(*parts):
+        width = sum(part.shape[1] for part in parts[:-1]) + parts[-1].shape[0]
+        ins = [(part, None) for part in parts]
+        return call(pack_kernel, 1, at, ins, [((ROWS, width), bf16, None)], [], "pack")[0]
 
     mine = sequence_adapter[0, 0]
+    theirs = other_core(sequence_adapter)[0, 0]
+    attention_shard = pack(query_projection, keyvalue_projection, attention_output_weight)
+    attention_shard, cotangent = together((attention_shard, cotangent))
     down_back = dot_t(cotangent, pick(down_adapter_output, mine)).astype(bf16)
-    cot_all = jnp.concatenate([cotangent, ride(down_back, 0)], axis=1)
+    down_back = jnp.pad(down_back, ((0, 0), (0, RIDE - 16)))
+    down_back = jnp.where(core == 0, down_back, jnp.roll(down_back, 16, axis=1))
+    cot_all = jnp.concatenate([cotangent, down_back], axis=1)
     cot_all = lax.all_gather(cot_all, ("core", "x"), axis=0, tiled=True)
     cot_all = cot_all.reshape(2, 4, ROWS, MODEL_WIDTH + RIDE)
-    attention_shard, feed_shard = call(
-        pack_kernel,
+
+    attention_shard = turn(attention_shard)
+    feed_shard = pack(up_projection_weight, down_projection_weight)
+    rows_shape = ((ROWS, MODEL_WIDTH), bf16, None)
+    normed = call(
+        norm_kernel,
         1,
         at,
-        [
-            (query_projection, None),
-            (keyvalue_projection, None),
-            (attention_output_weight, None),
-            (up_projection_weight, None),
-            (down_projection_weight, None),
-        ],
-        [((ROWS, 768), bf16, None), ((ROWS, 2048), bf16, None)],
+        [(tokens, None), (attention_norm_scale[None], None), (attention_norm_bias[None], None)],
+        [rows_shape],
         [],
-        "pack",
-    )
-    attention_shard = turn(attention_shard)
-    column = gather_cross(attention_shard, False)
-    input_rows = tokens.astype(f32)
-    normed = layer_norm(input_rows, gain_one, shift_one).astype(bf16)
-
-    theirs = other_core(sequence_adapter)[0, 0]
+        "norm",
+    )[0]
+    attention_shard, normed, feed_shard, mine, theirs = together(
+        (attention_shard, normed, feed_shard, mine, theirs)
+    )
+    column, mine, theirs = together((gather_cross(attention_shard, False), mine, theirs))
+    plane = gather_cross(jnp.stack(column), True)
+    normed_sides = gather_sides(normed)
+
     low = jnp.where(core == 0, mine, theirs)
     high = jnp.where(core == 0, theirs, mine)
-
     stacks = (
-        query_adapter_input,
+        jnp.swapaxes(query_adapter_input, 1, 2),
+        jnp.swapaxes(keyvalue_adapter_input, 1, 2),
+        jnp.swapaxes(up_adapter_input, 1, 2),
+        output_adapter_output,
+        down_adapter_output,
+        keyvalue_adapter_output,
         query_adapter_output,
-        keyvalue_adapter_input,
-        keyvalue_adapter_output,
-        output_adapter_input,
-        output_adapter_output,
-        up_adapter_input,
+        jnp.swapaxes(output_adapter_input, 1, 2),
         up_adapter_output,
-        down_adapter_input,
-        down_adapter_output,
-    )
-    column, normed, stacks, low, high = together((column, normed, stacks, low, high))
-    plane = gather_cross(jnp.stack(column), True)
-    normed_sides = gather_sides(normed)
-    (
-        query_adapter_input,
-        query_adapter_output,
-        keyvalue_adapter_input,
-        keyvalue_adapter_output,
-        output_adapter_input,
-        output_adapter_output,
-        up_adapter_input,
-        up_adapter_output,
-        down_adapter_input,
-        down_adapter_output,
-    ) = stacks
-
-    def ordered(stack):
-        return jnp.concatenate([pick(stack, low), pick(stack, high)], axis=0)
-
-    def ordered_t(stack):
-        return ordered(jnp.swapaxes(stack, 1, 2))
-
-    def padded(*pairs):
-        rest = jnp.zeros((RIDE - 32 * len(pairs), pairs[0].shape[1]), bf16)
-        return jnp.concatenate([*pairs, rest], axis=0)
-
-    small = jnp.concatenate(
+        jnp.swapaxes(down_adapter_input, 1, 2),
+    )
+    chosen = []
+    for stack in stacks:
+        block = (1, ADAPTER_RANK, stack.shape[2])
+        chosen.append((stack, pl.BlockSpec(block, lambda i, at: (at[0], 0, 0))))
+        chosen.append((stack, pl.BlockSpec(block, lambda i, at: (at[1], 0, 0))))
+    wide = ((RIDE, MODEL_WIDTH), bf16, None)
+    small, q_in, u_in, o_out, d_out, kv_out, bias = call(
+        select_kernel,
+        1,
+        jnp.stack([low, high, x, zh]).astype(jnp.int32),
+        [*chosen, (query_projection_bias[None], None), (up_projection_bias[None], None)],
         [
-            ordered(query_adapter_output),
-            ordered_t(output_adapter_input),
-            ordered(up_adapter_output),
-            ordered_t(down_adapter_input),
+            ((48, 2560), bf16, None),
+            wide,
+            wide,
+            wide,
+            wide,
+            ((RIDE, 256), bf16, None),
+            ((8, 4 * ROWS), f32, None),
         ],
-        axis=1,
-    )
-    biases = jnp.concatenate(
-        [
-            query_projection_bias,
-            jnp.zeros((256,), bf16),
-            up_projection_bias,
-            jnp.zeros((1024,), bf16),
-        ]
-    )
-    small = turn(jnp.concatenate([small, biases[None], jnp.zeros((15, 2560), bf16)], axis=0))
-    q_in = padded(ordered_t(query_adapter_input), ordered_t(keyvalue_adapter_input))
-    u_in = padded(ordered_t(up_adapter_input))
-    kv_out_pair = ordered(keyvalue_adapter_output)
-    kv_out_both = padded(jnp.zeros_like(kv_out_pair), kv_out_pair)
-    o_out, d_out = padded(ordered(output_adapter_output)), padded(ordered(down_adapter_output))
-
-    kv_in, kv_out = pick(keyvalue_adapter_input, mine), pick(keyvalue_adapter_output, mine)
+        [],
+        "select",
+    )
     keyval_bias = jnp.concatenate(
-        [jnp.zeros((HEAD_WIDTH,), f32), value_projection_bias.astype(f32)]
-    )
-    place_block = jnp.stack([lax.rem(x + p, 4) for p in PLACES]) // 2
-    own = place_block[:, None] <= place_block[None, :]
-    bias = jnp.concatenate([own, jnp.broadcast_to(zh == 1, (4, 4))], axis=0)
-    bias = jnp.repeat(jnp.where(bias, 0.0, -1e30).astype(f32), ROWS, axis=1)
-
-    keyval_inner = dot(normed, kv_in).astype(bf16)
-    keyval_ride = ride(keyval_inner, 32)
-    q_bias, u_bias = small[32:33, :256].astype(f32), small[32:33, 512:1536].astype(f32)
-    small = padded(small[:32])
-    q_out, o_in, u_out, d_in = (
-        small[:, :256],
-        small[:, 256:512],
-        small[:, 512:1536],
-        small[:, 1536:],
-    )
-    prepared = (keyval_inner, keyval_ride, kv_in, kv_out, q_in, u_in, o_out, d_out)
-    prepared += (kv_out_both, q_out, o_in, u_out, d_in, bias)
+        [jnp.zeros((1, HEAD_WIDTH), f32), value_projection_bias.astype(f32)[None]], axis=1
+    )
+    prepared = (q_in, u_in, o_out, d_out, kv_out, bias, keyval_bias, small)
     plane, normed_sides, prepared = together((plane, normed_sides, prepared))
-    keyval_inner, keyval_ride, kv_in, kv_out, q_in, u_in, o_out, d_out = prepared[:8]
-    kv_out_both, q_out, o_in, u_out, d_in, bias = prepared[8:]
+    q_in, u_in, o_out, d_out, kv_out, bias, keyval_bias, small = prepared
     normed_places = gather_rest(*normed_sides)
     (w,) = call(
         assemble_kernel,
@@ -901,10 +913,39 @@
     feed = lax.all_gather(feed_shard, DP + ("zh",), axis=0, tiled=True)
     feed = feed.reshape(16, 2, ROWS, 2048)
 
-    keyval = (dot(normed, w[:, 256:512]) + keyval_bias + dot(keyval_inner, kv_out)).astype(bf16)
-    keyval = other_half(jnp.concatenate([keyval, keyval_ride], axis=1))
+    w_keyval = pl.BlockSpec((MODEL_WIDTH, 256), lambda i, at: (0, 1))
+    keyval = call(
+        own_keyval_kernel,
+        1,
+        at,
+        [(normed, None), (w, w_keyval), (q_in, None), (kv_out, None), (keyval_bias, None)],
+        [((ROWS, 384), bf16, None)],
+        [],
+        "own_keyval",
+    )[0]
+    keyval = other_half(keyval)
+    keyval_far = ring_x(keyval, 2)
     keyval = jnp.concatenate([keyval, other_core(keyval)], axis=0)
-    keyval_places = (keyval, ring_x(keyval, 1), ring_x(keyval, -1), ring_x(keyval, 2))
+    keyval_near = ring_by_core(keyval)
+    keyval_pieces = (keyval, keyval_near, other_core(keyval_near))
+    keyval_pieces += (keyval_far, other_core(keyval_far))
+    q_out, o_in, u_out, d_in, q_bias, u_bias = call(
+        turned_kernel,
+        1,
+        at,
+        [(turn(small), None)],
+        [
+            ((RIDE, 256), bf16, None),
+            ((RIDE, 256), bf16, None),
+            ((RIDE, 1024), bf16, None),
+            ((RIDE, 1024), bf16, None),
+            ((1, 256), f32, None),
+            ((1, 1024), f32, None),
+        ],
+        [],
+        "turned",
+    )
+    input_rows = tokens.astype(f32)
 
     group = (2, 4 * ROWS)
     row_scratch = pltpu.VMEM((2, 4 * ROWS, MODEL_WIDTH), bf16)
@@ -915,14 +956,14 @@
         at,
         [
             *flat(normed_places),
-            *[(piece, ANY) for piece in keyval_places],
+            *[(piece, ANY) for piece in keyval_pieces],
             (w, ANY),
             (q_in, None),
             (q_out, None),
-            (kv_out_both, None),
+            (kv_out, None),
             (o_in, None),
             (q_bias, None),
-            (keyval_bias[None], None),
+            (keyval_bias, None),
             (bias, None),
         ],
         [
@@ -949,12 +990,13 @@
     normed_two = layer_norm(middle, gain_two, shift_two).astype(bf16)
     place_scratch = pltpu.VMEM((4, 2 * ROWS, MODEL_WIDTH), bf16)
     feed_scratch = pltpu.VMEM((16, ROWS, 1024), bf16)
-    inner_two, pre, act, *down_parts = call(
+    up_b, down_a, *feed_parts = call(
         feed_kernel,
         4,
         at,
         [
             *flat(gather_row(normed_two)),
+            (cot_all, ANY),
             (feed, ANY),
             (u_in, None),
             (u_out, None),
@@ -962,86 +1004,71 @@
             (u_bias, None),
         ],
         [
-            ((4, 2 * ROWS, RIDE), bf16, step_block((2 * ROWS, RIDE))),
-            ((4, 2 * ROWS, 1024), f32, step_block((2 * ROWS, 1024))),
-            ((4, 2 * ROWS, 1024), bf16, step_block((2 * ROWS, 1024))),
+            ((32, 1024), f32, None),
+            ((32, 1024), f32, None),
+            *part_outs(MODEL_WIDTH + RIDE, True),
             *part_outs(MODEL_WIDTH + RIDE, True),
         ],
-        [place_scratch, feed_scratch, feed_scratch, dma(6)],
-        "feed",
-        9500000000,
-    )
-    down_low = scatter_start(*down_parts)
-    down_low, act = together((down_low, act))
-    down_moved = (ring_x(down_low[1], -1), ring_x(down_low[2], 1), ring_x(down_low[3], 2))
-
-    up_b, down_a, *up_parts = call(
-        feed_back_kernel,
-        4,
-        at,
         [
-            (cot_all, ANY),
-            (feed, ANY),
-            (pre, step_block((2 * ROWS, 1024))),
-            (act, step_block((2 * ROWS, 1024))),
-            (inner_two, step_block((2 * ROWS, RIDE))),
-            (d_in, None),
-            (u_out, None),
-        ],
-        [((32, 1024), f32, None), ((32, 1024), f32, None), *part_outs(MODEL_WIDTH + RIDE, True)],
-        [
+            place_scratch,
             pltpu.VMEM((4, 2 * ROWS, MODEL_WIDTH + RIDE), bf16),
             feed_scratch,
             feed_scratch,
-            dma(6),
+            pltpu.VMEM((2 * ROWS, 1024), f32),
+            dma(10),
         ],
-        "feed_back",
-        9500000000,
-    )
-    up_parts, down_moved, up_b, down_a = together((up_parts, down_moved, up_b, down_a))
+        "feed",
+        19000000000,
+    )
+    down_parts, up_parts = feed_parts[:4], feed_parts[4:]
+    up_parts, down_parts, up_b, down_a = together((up_parts, down_parts, up_b, down_a))
+    up_far = scatter_far(*up_parts[2:])
+    up_far, up_b, down_a, down_parts = together((up_far, up_b, down_a, down_parts))
     feed_set = row_slice(jnp.concatenate([up_b, down_a], axis=1), core, (1024, 1024))
-    up_far = scatter_far(*up_parts[2:])
-    up_far, feed_set = together((up_far, feed_set))
-    down_sum = down_low[0] + sum(part.astype(f32) for part in down_moved)
-    up_sum = scatter_last(add_cores(*up_parts[:2]), *scatter_sides(up_far))
+    up_sides, up_near, feed_set = together(
+        (scatter_sides(up_far), add_cores(*up_parts[:2]), feed_set)
+    )
+    right, left = scatter_joined(up_near, *up_sides)
+    right, left, down_parts = together((right, left, down_parts))
+    up_moved = ring_x(right, 1), ring_x(left, -1)
+    down_far, down_near = scatter_far(*down_parts[2:]), add_cores(*down_parts[:2])
+    up_moved, down_far, down_near = together((up_moved, down_far, down_near))
+    up_sum = up_near[0] + sum(part.astype(f32) for part in up_moved)
     up_back = up_sum[:, MODEL_WIDTH:].astype(bf16)
     grad_normed_two = up_sum[:, :MODEL_WIDTH] + dot(up_back, u_in)
     _, norm_two_back = jax.vjp(lambda v: layer_norm(v, gain_two, shift_two), middle)
     grad_middle = cotangent.astype(f32) + norm_two_back(grad_normed_two)[0]
     grad_branch = grad_middle.astype(bf16)
 
-    down_inner = down_sum[:, MODEL_WIDTH:].astype(bf16)
-    layer_output = (
-        middle
-        + down_sum[:, :MODEL_WIDTH]
-        + down_projection_bias.astype(f32)
-        + dot(down_inner, d_out)
-    ).astype(bf16)
-
-    branch_sides = gather_sides(grad_branch)
+    branch_all = lax.all_gather(grad_branch, ("core", "x"), axis=0, tiled=True)
+    branch_all = branch_all.reshape(2, 4, ROWS, MODEL_WIDTH)
     middle_slices = slices_of(
         at,
-        [(up_back, normed_two), (output_inner, grad_branch), (down_inner, cotangent)],
+        [(up_back, normed_two), (output_inner, grad_branch)],
         "slices",
     )
-    branch_sides, middle_slices = together((branch_sides, middle_slices))
-    branch_places = gather_rest(*branch_sides)
     feed_set = jnp.concatenate(
         [
             feed_set,
             total(scatter_sequence(middle_slices)),
-            jnp.full((16, RIDE), mine, jnp.int32).astype(bf16),
+            jnp.full((16, 2 * RIDE), mine, jnp.int32).astype(bf16),
         ],
         axis=1,
     )
-    feed_column, branch_places = together((gather_y(feed_set), branch_places))
-    feed_pieces = gather_z(jnp.stack(feed_column))
+    down_sides = scatter_sides(down_far)
+    feed_column, branch_all, down_sides = together((gather_y(feed_set), branch_all, down_sides))
+    right, left = scatter_joined(down_near, *down_sides)
+    right, left, branch_all, feed_column = together(
+        (right, left, branch_all, jnp.stack(feed_column))
+    )
+    down_moved = ring_x(right, 1), ring_x(left, -1)
+    feed_pieces = gather_z(feed_column)
     query_b, output_a, keyval_b, backs, backs_far, *query_parts = call(
         attention_back_kernel,
         2,
         at,
         [
-            *flat(branch_places),
+            (branch_all, ANY),
             (w, ANY),
             (inner_one, step_block((4 * ROWS, RIDE))),
             (inner_far, step_block((4 * ROWS, RIDE))),
@@ -1052,7 +1079,7 @@
             (o_out, None),
             (o_in, None),
             (q_out, None),
-            (kv_out_both, None),
+            (kv_out, None),
             (bias, None),
         ],
         [
@@ -1073,15 +1100,22 @@
         "attention_back",
         8000000000,
     )
-    query_b, output_a, keyval_b, backs, backs_far, query_parts, feed_pieces = together(
-        (query_b, output_a, keyval_b, backs, backs_far, query_parts, feed_pieces)
+    query_b, output_a, keyval_b, backs, backs_far, query_parts, down_moved, feed_pieces = together(
+        (query_b, output_a, keyval_b, backs, backs_far, query_parts, down_moved, feed_pieces)
     )
     placed = row_slice(jnp.concatenate([query_b, output_a], axis=1), core, (256, 256))
-    query_far, backs_far, placed = together(
-        (scatter_far(*query_parts[2:]), other_half(backs_far), placed)
-    )
-    all_ids = jnp.concatenate([piece[:, 0, 5632] for piece in feed_pieces]).astype(jnp.int32)
-    feed_kept, feed_sent = halves_of(sum_by_adapter(feed_pieces, all_ids), core)
+    query_far, backs_far, placed, down_moved = together(
+        (scatter_far(*query_parts[2:]), other_half(backs_far), placed, down_moved)
+    )
+    down_sum = down_near[0] + sum(part.astype(f32) for part in down_moved)
+    down_inner = down_sum[:, MODEL_WIDTH:].astype(bf16)
+    layer_output = (
+        middle
+        + down_sum[:, :MODEL_WIDTH]
+        + down_projection_bias.astype(f32)
+        + dot(down_inner, d_out)
+    ).astype(bf16)
+    down_slices = slices_of(at, [(down_inner, cotangent)], "down_slices")
     query_sides = scatter_sides(query_far)
     query_near = add_cores(*query_parts[:2])
     pack_shape = (4, ADAPTER_RANK, 1152)
@@ -1099,49 +1133,53 @@
         [row_scratch, dma(2)],
         "late",
     )
-    late_mine, late_theirs, query_near, query_sides, feed_kept, feed_sent = together(
-        (late_mine, late_theirs, query_near, query_sides, feed_kept, feed_sent)
-    )
-    late_pack = add_cores(late_mine, late_theirs).astype(bf16)
+    late_mine, late_theirs, query_near, query_sides, down_slices = together(
+        (late_mine, late_theirs, query_near, query_sides, down_slices)
+    )
+    late_pack = jnp.concatenate(
+        [add_cores(late_mine, late_theirs).astype(bf16), down_slices], axis=-1
+    )
+    right, left = scatter_joined(query_near, *query_sides)
+    late_pack, right, left = together((late_pack, right, left))
+    query_moved = ring_x(right, 1), ring_x(left, -1)
+    late_parts, feed_pieces = together((scatter_sequence(late_pack), feed_pieces))
+    late_set = jnp.concatenate([total(late_parts), placed], axis=-1)
+    all_ids = jnp.concatenate([piece[:, 0, 5120] for piece in feed_pieces]).astype(jnp.int32)
+    feed_kept, feed_sent = sum_by_adapter(feed_pieces, core, all_ids)
+    column = gather_y(late_set)
     feed_half = add_cores(feed_kept, feed_sent).astype(bf16)
-    right, left = scatter_joined(query_near, *query_sides)
-    late_pack, right, left, feed_half = together((late_pack, right, left, feed_half))
-    feed_sum = lax.all_gather(feed_half, ("core", "x"), axis=0).reshape(2, 4, 4, 16, 5760)
-    query_moved = ring_x(right, 1), ring_x(left, -1)
-    late_set = jnp.concatenate([total(scatter_sequence(late_pack)), placed], axis=-1)
-    column, query_moved = together((gather_y(late_set), query_moved))
+    column, query_moved, feed_half = together((column, query_moved, feed_half))
+    feed_sum = lax.all_gather(feed_half, ("core", "x"), axis=0).reshape(2, 4, 4, 16, 5376)
     late_pieces = gather_z(jnp.stack(column))
     query_sum = query_near[0] + sum(part.astype(f32) for part in query_moved)
     grad_keyval = (
         query_sum[:, 2048:2304] + other_half(query_sum[:, 2304:2560].astype(bf16)).astype(f32)
     ).astype(bf16)
-    query_back = query_sum[:, 2560:].astype(bf16)
-    keyval_back = dot_t(grad_keyval, kv_out).astype(bf16)
+    keyval_back = dot_t(grad_keyval, kv_out)
+    keyval_back = jnp.where(jnp.arange(RIDE) // ADAPTER_RANK == 2 + core, keyval_back, 0.0)
+    back = (query_sum[:, 2560:] + keyval_back).astype(bf16)
     grad_normed = (
-        query_sum[:, :MODEL_WIDTH]
-        + dot(query_back, q_in)
-        + dot_t(grad_keyval, w[:, 256:512])
-        + dot_t(keyval_back, kv_in)
+        query_sum[:, :MODEL_WIDTH] + dot(back, q_in) + dot_t(grad_keyval, w[:, 256:512])
     )
     _, norm_one_back = jax.vjp(lambda v: layer_norm(v, gain_one, shift_one), input_rows)
     grad_tokens = (grad_middle + norm_one_back(grad_normed)[0]).astype(bf16)
 
     late_pieces, grad_tokens = together((late_pieces, grad_tokens))
-    kept, sent = halves_of(sum_by_adapter(late_pieces, all_ids), core)
+    kept, sent = sum_by_adapter(late_pieces, core, all_ids)
     own_half = add_cores(kept, sent).astype(bf16)
     other_part = other_core(own_half)
     near = ring_by_core(jnp.concatenate([own_half, other_part], axis=0))
     far = ring_x(own_half, 2)
     feed_grads = spread_out(
-        feed_spread_kernel, at, [feed_sum], (1024, 1024, 256, 256, 256), "feed_spread"
+        feed_spread_kernel, at, [feed_sum], (1024, 1024, 256, 256), "feed_spread"
     )
     near, far, feed_grads = together((near, far, feed_grads))
-    up_b, down_a, up_a, output_b, down_b = feed_grads
-    query_a, keyval_a, keyval_b, query_b, output_a = spread_out(
+    up_b, down_a, up_a, output_b = feed_grads
+    query_a, keyval_a, keyval_b, down_b, query_b, output_a = spread_out(
         late_spread_kernel,
         at,
         [own_half, other_part, near, other_core(near), far, other_core(far)],
-        (256, 256, 64, 256, 256),
+        (256, 256, 64, 256, 256, 256),
         "late_spread",
     )
     keyval_b = keyval_b.reshape(8, 16, 2, 2, 128).sum(axis=3).reshape(8, 16, 256)

time: 492 us -> 458 us (0.931)
  starting transfers between devices: 135 us -> 114 us
  waiting for transfers between devices: 132 us -> 114 us
  Pallas kernels: 125 us -> 139 us
  local copies, waits for them, and re-layouts: 31.8 us -> 20.6 us
  other arithmetic: 28.1 us -> 34.4 us
    ppermute x37 -> x32, waiting for transfers between devices: 95.5 us -> 54 us  [ring_x(): return lax.ppermute(a, 'x', [(i, (i + step) % 4) for i in range(4)])]
    all_gather x1 -> x2, waiting for transfers between devices: 0.01 us -> 16.5 us  [the longest x1 14.4 us: shards(): branch_all = lax.all_gather(grad_branch, ('core', 'x'), axis=0, tiled=True)]
    pallas_call x8 -> x13, Pallas kernels: 103 us -> 118 us  [call(): pl.pallas_call(kernel, out_shape=[jax.ShapeDtypeStruct(s, d) for s, d, _...]
    ppermute x33 -> x30, starting transfers between devices: 48.9 us -> 37 us  [other_core(): return lax.ppermute(a, 'core', [(0, 1), (1, 0)])]
    squeeze x10 -> x1, local copies, waits for them, and re-layouts: 7.37 us -> 0.02 us  [scatter_sequence(): slices[2]]
    ppermute x37 -> x32, starting transfers between devices: 40 us -> 33 us  [ring_x(): return lax.ppermute(a, 'x', [(i, (i + step) % 4) for i in range(4)])]
    unnamed x185 -> x177, local copies, waits for them, and re-layouts: 12.4 us -> 9.51 us
    ppermute x33 -> x30, waiting for transfers between devices: 11.7 us -> 9.72 us  [other_core(): return lax.ppermute(a, 'core', [(0, 1), (1, 0)])]
  transfers between devices with their start and end apart: 97 -> 91, of which waited for: 45 -> 34; matrix products, arithmetic and copies ran while one was open for 10% -> 10% of each run, Pallas kernels for 19% -> 20%
where the time goes in v5:
time: 458 us; the launch traced here: 449 us
  Pallas kernels  139 us (30%)
  starting transfers between devices  114 us (25%)
  waiting for transfers between devices  114 us (25%)
  other arithmetic  34.4 us (8%)
  local copies, waits for them, and re-layouts  20.6 us (4%)
  between operations  17.7 us (4%)
  matrix products  10.1 us (2%)
    pallas_call x13, Pallas kernels, call(): pl.pallas_call(kernel, out_shape=[jax.ShapeDtypeStruct(s, d) for s, d, _...  118 us
    ppermute x32, waiting for transfers between devices, ring_x(): return lax.ppermute(a, 'x', [(i, (i + step) % 4) for i in range(4)])  54 us
    ppermute x30, starting transfers between devices, other_core(): return lax.ppermute(a, 'core', [(0, 1), (1, 0)])  37 us
    ppermute x32, starting transfers between devices, ring_x(): return lax.ppermute(a, 'x', [(i, (i + step) % 4) for i in range(4)])  33 us
    all_gather x1, waiting for transfers between devices, shards(): branch_all = lax.all_gather(grad_branch, ('core', 'x'), axis=0, tiled=True)  14.4 us
    pallas_call x2, Pallas kernels, spread_out(): pl.pallas_call(functools.partial(kernel, widths), out_shape=[jax.ShapeDty...  14.2 us
    ppermute x2, starting transfers between devices, turn(): return lax.ppermute(a, ('core', 'zh'), [(0, 0), (1, 2), (2, 1), (3, 3)])  12.9 us
    ppermute x30, waiting for transfers between devices, other_core(): return lax.ppermute(a, 'core', [(0, 1), (1, 0)])  9.72 us
  transfers between devices with their start and end apart: 91, of which 34 were waited for; matrix products, arithmetic and copies ran while one was open for 10% of the time, Pallas kernels for 20%

profile of v5, /device:TPU:1, one launch (start us, length us, event | category | flops | bytes accessed | tf_op | source)
XLA Modules:
  0.0 449.0 jit_solution(7824230466693565109)
XLA Ops:
  13.5 6.9 %collective-permute-start = (bf16[128,768]{1,0:T(8,128)(2,1)S(1)}, bf16[128,768]{1,0:T(8,128)(2,1)S(1)}, u32[]{:S(2)}, u32[]{:S(2)}) collective-permute-start(bf16[128,768]{1,0:T(8,128)(2,1)S(1)} %copy-done.49), channel_id=1, source_target_pairs={{0,0},{4,8},{8,4},{12,12},{1,1},{5,9},{9,5},{13,13},{2,2},{6,10},{... | collective-permute-start | bytes 589832 | tf_op jit(solution)/shard_map/ppermute | solution.py:57
  30.7 5.1 %collective-permute-done.4 = bf16[128,768]{1,0:T(8,128)(2,1)S(1)} collective-permute-done((bf16[128,768]{1,0:T(8,128)(2,1)S(1)}, bf16[128,768]{1,0:T(8,128)(2,1)S(1)}, u32[]{:S(2)}, u32[]{:S(2)}) %collective-permute-start.4) | collective-permute-done | bytes 196640 | tf_op jit(solution)/shard_map/ppermute | solution.py:78
  51.0 7.6 %collective-permute-done.9.refs_4_ = bf16[128,2048]{1,0:T(8,128)(2,1)S(1)} collective-permute-done((bf16[128,2048]{1,0:T(8,128)(2,1)S(1)}, bf16[128,2048]{1,0:T(8,128)(2,1)S(1)}, u32[]{:S(2)}, u32[]{:S(2)}) %collective-permute-start.9) | collective-permute-done | bytes 524320 | tf_op jit(solution)/shard_map/ppermute | solution.py:37
  59.1 4.3 assemble.1.w.refs_15_.refs_1_
  65.5 6.0 %collective-permute-start.23 = (bf16[48,2560]{1,0:T(8,128)(2,1)S(1)}, bf16[48,2560]{1,0:T(8,128)(2,1)S(1)}, u32[]{:S(2)}, u32[]{:S(2)}) collective-permute-start(bf16[48,2560]{1,0:T(8,128)(2,1)S(1)} %copy-done.79), channel_id=1, source_target_pairs={{0,0},{4,8},{8,4},{12,12},{1,1},{5,9},{9,5},{13,13},{2,2},{6,10},{... | collective-permute-start | bytes 737288 | tf_op jit(solution)/shard_map/ppermute | solution.py:57
  76.2 4.8 %collective-permute-done.17 = bf16[128,384]{1,0:T(8,128)(2,1)S(1)} collective-permute-done((bf16[128,384]{1,0:T(8,128)(2,1)}, bf16[128,384]{1,0:T(8,128)(2,1)S(1)}, u32[]{:S(2)}, u32[]{:S(2)}) %collective-permute-start.17) | collective-permute-done | bytes 98336 | tf_op jit(solution)/shard_map/ppermute | solution.py:53
  85.1 4.7 %collective-permute-done.19.refs_11_ = bf16[256,384]{1,0:T(8,128)(2,1)S(1)} collective-permute-done((bf16[256,384]{1,0:T(8,128)(2,1)S(1)}, bf16[256,384]{1,0:T(8,128)(2,1)S(1)}, u32[]{:S(2)}, u32[]{:S(2)}) %collective-permute-start.19) | collective-permute-done | bytes 196640 | tf_op jit(solution)/shard_map/ppermute | solution.py:150
  96.9 21.7 %attention.1 = (bf16[2,512,128]{2,1,0:T(8,128)(2,1)}, bf16[2,512,128]{2,1,0:T(8,128)(2,1)}, bf16[2,512,256]{2,1,0:T(8,128)(2,1)}, bf16[2,8,128,256]{3,2,1,0:T(8,...) custom-call(s32[5]{0:T(128)} %stack.79.at, ...), custom_call_target="tpu_custom_call" | custom-call | flops 8999999488 | bytes 23029760 | tf_op jit(solution)/shard_map/attention/pallas_call | solution.py:700
  125.4 6.2 %collective-permute-done.26 = bf16[64,2176]{1,0:T(8,128)(2,1)S(1)} collective-permute-done((bf16[64,2176]{1,0:T(8,128)(2,1)S(1)}, bf16[64,2176]{1,0:T(8,128)(2,1)S(1)}, u32[]{:S(2)}, u32[]{:S(2)}) %collective-permute-start.26) | collective-permute-done | bytes 278560 | tf_op jit(solution)/shard_map/ppermute | solution.py:37
  134.4 10.7 %collective-permute-done.29 = bf16[128,2176]{1,0:T(8,128)(2,1)S(1)} collective-permute-done((bf16[128,2176]{1,0:T(8,128)(2,1)S(1)}, bf16[128,2176]{1,0:T(8,128)(2,1)S(1)}, u32[]{:S(2)}, u32[]{:S(2)}) %collective-permute-start.29) | collective-permute-done | bytes 557088 | tf_op jit(solution)/shard_map/ppermute | solution.py:37
  154.2 6.5 %collective-permute-done.33.refs_4_ = bf16[128,2048]{1,0:T(8,128)(2,1)S(1)} collective-permute-done((bf16[128,2048]{1,0:T(8,128)(2,1)S(1)}, bf16[128,2048]{1,0:T(8,128)(2,1)S(1)}, u32[]{:S(2)}, u32[]{:S(2)}) %collective-permute-start.33) | collective-permute-done | bytes 524320 | tf_op jit(solution)/shard_map/ppermute | solution.py:37
  162.9 3.8 collective-permute-start.34
  166.7 3.8 collective-permute-start.38
  175.7 39.2 %feed.1 = (f32[32,1024]{1,0:T(8,128)}, f32[32,1024]{1,0:T(8,128)}, bf16[3,128,2176]{2,1,0:T(8,128)(2,1)}, bf16[3,128,2176]{2,1,0:T(8,128)(2,1)}, bf16[128,2176]{...) custom-call(s32[5]{0:T(128)} %stack.79.at, ...), custom_call_target="tpu_custom_call" | custom-call | flops 19000000512 | bytes 44568576 | tf_op jit(solution)/shard_map/feed/pallas_call | solution.py:700
  221.0 6.2 %collective-permute-done.41 = bf16[64,2176]{1,0:T(8,128)(2,1)S(1)} collective-permute-done((bf16[64,2176]{1,0:T(8,128)(2,1)S(1)}, bf16[64,2176]{1,0:T(8,128)(2,1)S(1)}, u32[]{:S(2)}, u32[]{:S(2)}) %collective-permute-start.41) | collective-permute-done | bytes 278560 | tf_op jit(solution)/shard_map/ppermute | solution.py:37
  237.5 8.7 %collective-permute-done.44 = bf16[128,2176]{1,0:T(8,128)(2,1)S(1)} collective-permute-done((bf16[128,2176]{1,0:T(8,128)(2,1)S(1)}, bf16[128,2176]{1,0:T(8,128)(2,1)S(1)}, u32[]{:S(2)}, u32[]{:S(2)}) %collective-permute-start.44) | collective-permute-done | bytes 557088 | tf_op jit(solution)/shard_map/ppermute | solution.py:37
  274.4 14.4 %all-gather.10.cloned.1.call-done = bf16[1024,2048]{1,0:T(8,128)(2,1)} async-done(((bf16[128,2048]{1,0:T(8,128)(2,1)}), bf16[1024,2048]{1,0:T(8,128)(2,1)}) %all-gather.10.cloned.1.call-update) | async-done | bytes 4194320 | tf_op jit(solution)/shard_map/all_gather | solution.py:1043
  298.9 24.5 %attention_back.1 = (f32[32,256]{1,0:T(8,128)}, f32[32,256]{1,0:T(8,128)}, f32[32,256]{1,0:T(8,128)}, bf16[2,512,128]{2,1,0:T(8,128)(2,1)}, bf16[2,32,512]{2,1,0...) custom-call(s32[5]{0:T(128)} %stack.79.at, ...), custom_call_target="tpu_custom_call" | custom-call | flops 8000000000 | bytes 22470656 | tf_op jit(solution)/shard_map/attention_back/pallas_call | solution.py:700
  339.8 5.4 %late.1 = (bf16[4,16,1152]{2,1,0:T(8,128)(2,1)}, bf16[4,16,1152]{2,1,0:T(8,128)(2,1)}) custom-call(s32[5]{0:T(128)} %stack.79.at, bf16[128,2048]{1,0:T(8,128)(2,1)} %norm.1.rows.refs_0_, bf16[128,2048]{1,0:T(8,128)(2,1)} %copy-done.33, bf16[128,2048]{1,0:T(8,128)(2,1)} %copy-done.24, bf16[128,2048]{1,0:T(8,128)(2,1)} %copy-done.31, ...), custom_call_target="tpu_custom_call" | custom-call | bytes 5144576 | tf_op jit(solution)/shard_map/late/pallas_call | solution.py:700
  361.8 3.7 sum_by_adapter.2
  395.4 5.1 %collective-permute-done.78.refs_2_ = bf16[4,16,2688]{2,1,0:T(8,128)(2,1)} collective-permute-done((bf16[4,16,2688]{2,1,0:T(8,128)(2,1)S(1)}, bf16[4,16,2688]{2,1,0:T(8,128)(2,1)}, u32[]{:S(2)}, u32[]{:S(2)}) %collective-permute-start.78) | collective-permute-done | bytes 344096 | tf_op jit(solution)/shard_map/ppermute | solution.py:45
  413.0 8.1 %feed_spread.1 = (f32[8,16,8192]{2,1,0:T(8,128)}, f32[8,16,8192]{2,1,0:T(8,128)}, f32[8,16,2048]{2,1,0:T(8,128)}, f32[8,16,2048]{2,1,0:T(8,128)}) custom-call(s32[5]{0:T(128)} %stack.79.at, bf16[2,4,4,16,5376]{4,3,2,1,0:T(8,128)(2,1)} %bitcast.134), custom_call_target="tpu_custom_call" | custom-call | tf_op jit(solution)/shard_map/feed_spread/pallas_call | solution.py:761
  423.8 5.9 %collective-permute-start.85 = (bf16[8,16,2688]{2,1,0:T(8,128)(2,1)S(1)}, bf16[8,16,2688]{2,1,0:T(8,128)(2,1)S(1)}, u32[]{:S(2)}, u32[]{:S(2)}) collective-permute-start(bf16[8,16,2688]{2,1,0:T(8,128)(2,1)S(1)} %collective-permute-done.83.refs_2_), channel_id=1, source_target_pairs={{0,8},{8,0},{1,9},{9,1},{2,10},{10,2},{3,11},{11,3},{4,12},{12,4},... | collective-permute-start | bytes 2064392 | tf_op jit(solution)/shard_map/ppermute | solution.py:49
  433.7 6.1 %late_spread.1 = (f32[8,16,2048]{2,1,0:T(8,128)}, f32[8,16,2048]{2,1,0:T(8,128)}, f32[8,16,512]{2,1,0:T(8,128)}, f32[8,16,2048]{2,1,0:T(8,128)}, f32[8,16,2048]{2,1,0:T(8,128)}, /*index=5*/f32[8,16,2048]{2,1,0:T(8,128)}) custom-call(s32[5]{0:T(128)} %stack.79.at, bf16[4,16,2688]{2,1,0:T(8,128)(2,1)} %copy-done.9, bf16[4,16,2688]{2,1,0:T(8,128)(2,1)} %copy-done.18, ...), custom_call_target="tpu_custom_call" | custom-call | tf_op jit(solution)/shard_map/late_spread/pallas_call | solution.py:761
  (474 shorter events, 212.0 us)
Async XLA Ops:
  7.2 56.3 %all-gather.6.cloned.1.call-start = ((), (), s32[]{:S(2)}) async-start(), calls=%async_computation | async-start | bytes 5013504 | tf_op jit(solution)/shard_map/all_gather | solution.py:837
  13.4 161.7 %all-gather.8.cloned.1.call-start = ((), (), s32[]{:S(2)}) async-start(), calls=%async_computation.1 | async-start | bytes 17301504 | tf_op jit(solution)/shard_map/all_gather | solution.py:913
  36.5 22.6 %collective-permute-start.7 = (bf16[4,128,768]{2,1,0:T(8,128)(2,1)S(1)}, bf16[4,128,768]{2,1,0:T(8,128)(2,1)}, u32[]{:S(2)}, u32[]{:S(2)}) collective-permute-start(bf16[4,128,768]{2,1,0:T(8,128)(2,1)S(1)} %pad_maximum_fusion.refs_0_), channel_id=1, source_target_pairs={{0,16},{8,40},{16,4},{24,56},{4,20},{12,44},{20,0},{28,60},{32,48}... | collective-permute-start | bytes 2359304 | tf_op jit(solution)/shard_map/ppermute | solution.py:78
  37.8 21.3 %collective-permute-start.6 = (bf16[4,128,768]{2,1,0:T(8,128)(2,1)S(1)}, bf16[4,128,768]{2,1,0:T(8,128)(2,1)}, u32[]{:S(2)}, u32[]{:S(2)}) collective-permute-start(bf16[4,128,768]{2,1,0:T(8,128)(2,1)S(1)} %pad_maximum_fusion.refs_0_), channel_id=1, source_target_pairs={{0,4},{8,72},{16,20},{24,88},{4,0},{12,76},{20,16},{28,92},{32,36}... | collective-permute-start | bytes 2359304 | tf_op jit(solution)/shard_map/ppermute | solution.py:78
  40.4 18.6 %collective-permute-start.5 = (bf16[4,128,768]{2,1,0:T(8,128)(2,1)S(1)}, bf16[4,128,768]{2,1,0:T(8,128)(2,1)}, u32[]{:S(2)}, u32[]{:S(2)}) collective-permute-start(bf16[4,128,768]{2,1,0:T(8,128)(2,1)S(1)} %pad_maximum_fusion.refs_0_), channel_id=1, source_target_pairs={{0,20},{8,104},{16,0},{24,120},{4,16},{12,108},{20,4},{28,124},{32... | collective-permute-start | bytes 2359304 | tf_op jit(solution)/shard_map/ppermute | solution.py:78
  41.5 17.1 %collective-permute-start.9 = (bf16[128,2048]{1,0:T(8,128)(2,1)S(1)}, bf16[128,2048]{1,0:T(8,128)(2,1)S(1)}, u32[]{:S(2)}, u32[]{:S(2)}) collective-permute-start(bf16[128,2048]{1,0:T(8,128)(2,1)S(1)} %copy-done.6), channel_id=1, source_target_pairs={{0,3},{1,0},{2,1},{3,2},{4,7},{5,4},{6,5},{7,6},{8,11},{9,8},{10,9... | collective-permute-start | bytes 1572872 | tf_op jit(solution)/shard_map/ppermute | solution.py:37
  44.0 15.1 %collective-permute-start.8 = (bf16[128,2048]{1,0:T(8,128)(2,1)S(1)}, bf16[128,2048]{1,0:T(8,128)(2,1)S(1)}, u32[]{:S(2)}, u32[]{:S(2)}) collective-permute-start(bf16[128,2048]{1,0:T(8,128)(2,1)S(1)} %copy-done.6), channel_id=1, source_target_pairs={{0,1},{1,2},{2,3},{3,0},{4,5},{5,6},{6,7},{7,4},{8,9},{9,10},{10,1... | collective-permute-start | bytes 1572872 | tf_op jit(solution)/shard_map/ppermute | solution.py:37
  63.5 225.3 %all-gather.10.cloned.1.call-start = ((), (), s32[]{:S(2)}) async-start(), calls=%async_computation.2 | async-start | bytes 4718592 | tf_op jit(solution)/shard_map/all_gather | solution.py:1043
  75.4 20.3 %collective-permute-start.11 = (bf16[128,2048]{1,0:T(8,128)(2,1)S(1)}, bf16[128,2048]{1,0:T(8,128)(2,1)S(1)}, u32[]{:S(2)}, u32[]{:S(2)}) collective-permute-start(bf16[128,2048]{1,0:T(8,128)(2,1)S(1)} %collective-permute-done.8.refs_2_), channel_id=1, source_target_pairs={{0,8},{8,0},{1,9},{9,1},{2,10},{10,2},{3,11},{11,3},{4,12},{12,4},... | collective-permute-start | bytes 1572872 | tf_op jit(solution)/shard_map/ppermute | solution.py:49
  75.5 20.1 %collective-permute-start.12 = (bf16[128,2048]{1,0:T(8,128)(2,1)S(1)}, bf16[128,2048]{1,0:T(8,128)(2,1)S(1)}, u32[]{:S(2)}, u32[]{:S(2)}) collective-permute-start(bf16[128,2048]{1,0:T(8,128)(2,1)S(1)} %collective-permute-done.9.refs_4_), channel_id=1, source_target_pairs={{0,8},{8,0},{1,9},{9,1},{2,10},{10,2},{3,11},{11,3},{4,12},{12,4},... | collective-permute-start | bytes 1572872 | tf_op jit(solution)/shard_map/ppermute | solution.py:49
  76.0 19.7 %collective-permute-start.10 = (bf16[128,2048]{1,0:T(8,128)(2,1)S(1)}, bf16[128,2048]{1,0:T(8,128)(2,1)S(1)}, u32[]{:S(2)}, u32[]{:S(2)}) collective-permute-start(bf16[128,2048]{1,0:T(8,128)(2,1)S(1)} %copy-done.7), channel_id=1, source_target_pairs={{0,8},{8,0},{1,9},{9,1},{2,10},{10,2},{3,11},{11,3},{4,12},{12,4},... | collective-permute-start | bytes 1572872 | tf_op jit(solution)/shard_map/ppermute | solution.py:49
  151.2 22.7 %collective-permute-start.30 = (bf16[128,2048]{1,0:T(8,128)(2,1)S(1)}, bf16[128,2048]{1,0:T(8,128)(2,1)S(1)}, u32[]{:S(2)}, u32[]{:S(2)}) collective-permute-start(bf16[128,2048]{1,0:T(8,128)(2,1)S(1)} %add_convert_fusion.6.refs_0_.refs_1_), channel_id=1, source_target_pairs={{0,8},{8,0},{1,9},{9,1},{2,10},{10,2},{3,11},{11,3},{4,12},{12,4},... | collective-permute-start | bytes 1572872 | tf_op jit(solution)/shard_map/ppermute | solution.py:49
  231.3 14.9 %collective-permute-start.44 = (bf16[128,2176]{1,0:T(8,128)(2,1)S(1)}, bf16[128,2176]{1,0:T(8,128)(2,1)S(1)}, u32[]{:S(2)}, u32[]{:S(2)}) collective-permute-start(bf16[128,2176]{1,0:T(8,128)(2,1)S(1)} %pad_maximum_fusion.8), channel_id=1, source_target_pairs={{0,1},{1,2},{2,3},{3,0},{4,5},{5,6},{6,7},{7,4},{8,9},{9,10},{10,1... | collective-permute-start | bytes 1671176 | tf_op jit(solution)/shard_map/ppermute | solution.py:37
  249.4 163.7 %all-gather.12.cloned.1.call-start = ((), (), s32[]{:S(2)}) async-start(), calls=%async_computation.3 | async-start | bytes 6193152 | tf_op jit(solution)/shard_map/all_gather | solution.py:1152
  291.2 32.2 %collective-permute-start.60 = (bf16[4,16,5376]{2,1,0:T(8,128)(2,1)S(1)}, bf16[4,16,5376]{2,1,0:T(8,128)(2,1)S(1)}, u32[]{:S(2)}, u32[]{:S(2)}) collective-permute-start(bf16[4,16,5376]{2,1,0:T(8,128)(2,1)S(1)} %pad_maximum_fusion.1.refs_0_), channel_id=1, source_target_pairs={{0,16},{16,4},{4,20},{20,0},{1,17},{17,5},{5,21},{21,1},{2,18},{18... | collective-permute-start | bytes 2064392 | tf_op jit(solution)/shard_map/ppermute | solution.py:45
  293.5 32.3 %collective-permute-start.59 = (bf16[4,16,5376]{2,1,0:T(8,128)(2,1)S(1)}, bf16[4,16,5376]{2,1,0:T(8,128)(2,1)S(1)}, u32[]{:S(2)}, u32[]{:S(2)}) collective-permute-start(bf16[4,16,5376]{2,1,0:T(8,128)(2,1)S(1)} %pad_maximum_fusion.1.refs_0_), channel_id=1, source_target_pairs={{0,4},{16,20},{4,0},{20,16},{1,5},{17,21},{5,1},{21,17},{2,6},{18,... | collective-permute-start | bytes 2064392 | tf_op jit(solution)/shard_map/ppermute | solution.py:45
  295.7 30.1 %collective-permute-start.58 = (bf16[4,16,5376]{2,1,0:T(8,128)(2,1)S(1)}, bf16[4,16,5376]{2,1,0:T(8,128)(2,1)S(1)}, u32[]{:S(2)}, u32[]{:S(2)}) collective-permute-start(bf16[4,16,5376]{2,1,0:T(8,128)(2,1)S(1)} %pad_maximum_fusion.1.refs_0_), channel_id=1, source_target_pairs={{0,20},{16,0},{4,16},{20,4},{1,21},{17,1},{5,17},{21,5},{2,22},{18... | collective-permute-start | bytes 2064392 | tf_op jit(solution)/shard_map/ppermute | solution.py:45
  296.0 27.3 %collective-permute-start.56 = (bf16[128,2176]{1,0:T(8,128)(2,1)S(1)}, bf16[128,2176]{1,0:T(8,128)(2,1)S(1)}, u32[]{:S(2)}, u32[]{:S(2)}) collective-permute-start(bf16[128,2176]{1,0:T(8,128)(2,1)S(1)} %pad_maximum_fusion.10), channel_id=1, source_target_pairs={{0,1},{1,2},{2,3},{3,0},{4,5},{5,6},{6,7},{7,4},{8,9},{9,10},{10,1... | collective-permute-start | bytes 1671176 | tf_op jit(solution)/shard_map/ppermute | solution.py:37
  296.3 27.1 %collective-permute-start.57 = (bf16[128,2176]{1,0:T(8,128)(2,1)S(1)}, bf16[128,2176]{1,0:T(8,128)(2,1)S(1)}, u32[]{:S(2)}, u32[]{:S(2)}) collective-permute-start(bf16[128,2176]{1,0:T(8,128)(2,1)S(1)} %pad_maximum_fusion.11), channel_id=1, source_target_pairs={{0,3},{1,0},{2,1},{3,2},{4,7},{5,4},{6,5},{7,6},{8,11},{9,8},{10,9... | collective-permute-start | bytes 1671176 | tf_op jit(solution)/shard_map/ppermute | solution.py:37
  330.1 15.1 %collective-permute-start.64 = (bf16[3,128,2688]{2,1,0:T(8,128)(2,1)}, bf16[3,128,2688]{2,1,0:T(8,128)(2,1)}, u32[]{:S(2)}, u32[]{:S(2)}) collective-permute-start(bf16[3,128,2688]{2,1,0:T(8,128)(2,1)} %get-tuple-element.328), channel_id=1, source_target_pairs={{0,8},{8,0},{1,9},{9,1},{2,10},{10,2},{3,11},{11,3},{4,12},{12,4},... | collective-permute-start | bytes 6193160 | tf_op jit(solution)/shard_map/ppermute | solution.py:49
  356.4 20.7 %collective-permute-start.74 = (bf16[128,2688]{1,0:T(8,128)(2,1)}, bf16[128,2688]{1,0:T(8,128)(2,1)}, u32[]{:S(2)}, u32[]{:S(2)}) collective-permute-start(bf16[128,2688]{1,0:T(8,128)(2,1)} %pad_maximum_fusion.2), channel_id=1, source_target_pairs={{0,1},{1,2},{2,3},{3,0},{4,5},{5,6},{6,7},{7,4},{8,9},{9,10},{10,1... | collective-permute-start | bytes 2064392 | tf_op jit(solution)/shard_map/ppermute | solution.py:37
  357.1 20.0 %collective-permute-start.75 = (bf16[128,2688]{1,0:T(8,128)(2,1)}, bf16[128,2688]{1,0:T(8,128)(2,1)}, u32[]{:S(2)}, u32[]{:S(2)}) collective-permute-start(bf16[128,2688]{1,0:T(8,128)(2,1)} %pad_maximum_fusion.3), channel_id=1, source_target_pairs={{0,3},{1,0},{2,1},{3,2},{4,7},{5,4},{6,5},{7,6},{8,11},{9,8},{10,9... | collective-permute-start | bytes 2064392 | tf_op jit(solution)/shard_map/ppermute | solution.py:37
  383.4 17.1 %collective-permute-start.78 = (bf16[4,16,2688]{2,1,0:T(8,128)(2,1)S(1)}, bf16[4,16,2688]{2,1,0:T(8,128)(2,1)}, u32[]{:S(2)}, u32[]{:S(2)}) collective-permute-start(bf16[4,16,2688]{2,1,0:T(8,128)(2,1)S(1)} %pad_maximum_fusion.12.refs_0_), channel_id=1, source_target_pairs={{0,4},{16,20},{4,0},{20,16},{1,5},{17,21},{5,1},{21,17},{2,6},{18,... | collective-permute-start | bytes 1032200 | tf_op jit(solution)/shard_map/ppermute | solution.py:45
  385.4 15.2 %collective-permute-start.77 = (bf16[4,16,2688]{2,1,0:T(8,128)(2,1)S(1)}, bf16[4,16,2688]{2,1,0:T(8,128)(2,1)}, u32[]{:S(2)}, u32[]{:S(2)}) collective-permute-start(bf16[4,16,2688]{2,1,0:T(8,128)(2,1)S(1)} %pad_maximum_fusion.12.refs_0_), channel_id=1, source_target_pairs={{0,20},{16,0},{4,16},{20,4},{1,21},{17,1},{5,17},{21,5},{2,22},{18... | collective-permute-start | bytes 1032200 | tf_op jit(solution)/shard_map/ppermute | solution.py:45
  (154 other events, 1245.5 us)
Sparse Core Ops, SparseCore 0:
  13.5 39.1 all-gather.5
  63.6 108.7 all-gather.7
  249.5 39.1 all-gather.9
  377.2 35.7 all-gather.11

commit v6 on v5

--- a/solution.py
+++ b/solution.py
@@ -359,7 +359,16 @@
     first = 0
     for out, width in zip(outs, widths):
         if width < 128:
-            out[...] = scratch[x, :, :, first : first + 128].astype(f32)
+            part = scratch[x, :, :, first : first + 128].astype(f32)
+
+            @pl.when(jnp.logical_and(c == 0, x % 2 == 0))
+            def _(out=out, part=part):
+                out[...] = part
+
+            @pl.when(jnp.logical_and(c == 0, x % 2 == 1))
+            def _(out=out, part=part):
+                out[...] += part
+
             first += 128
         else:
             here = pl.ds(pl.multiple_of(first + c * width, 128), width)
@@ -507,10 +516,11 @@
 def feed_kernel(at, *refs):
     rows_in = split_pieces(refs[:10])
     cot, feed, u_in, u_out, d_in, u_bias = refs[10:16]
-    up_b, down_a = refs[16:18]
-    down_parts, down_far = refs[18:20], refs[20:22]
-    up_parts, up_far = refs[22:24], refs[24:26]
-    rows, grads, up, down, slopes, sems = refs[26:]
+    placed = refs[16]
+    up_b, down_a = placed.at[:, pl.ds(0, 1024)], placed.at[:, pl.ds(1024, 1024)]
+    down_parts, down_far = refs[17:19], refs[19:21]
+    up_parts, up_far = refs[21:23], refs[23:25]
+    rows, grads, up, down, slopes, sems = refs[25:]
     p = pl.program_id(0)
     core = at[0]
 
@@ -529,8 +539,7 @@
             copy_place(
                 rows_in[k], rows.at[k, pl.ds(0, ROWS)], rows.at[k, pl.ds(ROWS, ROWS)], sems.at[k]
             )
-        up_b[...] = jnp.zeros_like(up_b)
-        down_a[...] = jnp.zeros_like(down_a)
+        placed[...] = jnp.zeros_like(placed)
         wait(up, sems.at[8])
 
     wait(rows.at[p], sems.at[p])
@@ -568,10 +577,20 @@
 
 def late_kernel(at, *refs):
     rows_in = split_pieces(refs[:10])
-    backs, backs_far, keyval_b = refs[10:13]
-    outs, (rows, sems) = refs[13:15], refs[15:]
+    backs, backs_far, keyval_b, cotangent = refs[10:14]
+    down_parts = refs[14:18]
+    outs, (rows, sems) = refs[18:20], refs[20:]
     core, x = at[0], at[1]
     copy_rows(rows_in, rows, sems)
+    inner = sum(part[...].astype(f32) for part in down_parts).T
+    inner = (inner[:16] + inner[16:32]).astype(bf16)
+    down_b = dot(inner, cotangent[...]).astype(bf16)
+    for to in range(4):
+        place = lax.rem(to + 4 - x, 4)
+        for c in range(2):
+            begin = (c * 4 + to) * 256
+            lanes = slice(1152 + c * 256, 1152 + (c + 1) * 256)
+            outs[0][place, :, lanes] = down_b[:, begin : begin + 256]
     product = jnp.zeros((64, MODEL_WIDTH), f32)
     for s in range(2):
         wait(rows.at[s], sems.at[s])
@@ -602,9 +621,10 @@
 def attention_back_kernel(at, *refs):
     branch, w, inner_in, inner_far, query_in, kv_in, lse_in, att_in = refs[:8]
     o_out, o_in, q_out, kv_out, bias = refs[8:13]
-    query_b, output_a, keyval_b, backs, backs_far = refs[13:18]
-    parts, far_parts = refs[18:20], refs[20:22]
-    rows, ws, grad_k, grad_v, sems = refs[22:]
+    placed, keyval_b, backs, backs_far = refs[13:17]
+    query_b, output_a = placed.at[:, pl.ds(0, 256)], placed.at[:, pl.ds(256, 256)]
+    parts, far_parts = refs[17:19], refs[19:21]
+    rows, ws, grad_k, grad_v, sems = refs[21:]
     s = pl.program_id(0)
     core = at[0]
 
@@ -617,8 +637,7 @@
             lambda p, which: rows.at[which, pl.ds(p * ROWS, ROWS)],
             lambda p, which: sems.at[which],
         )
-        query_b[...] = jnp.zeros_like(query_b)
-        output_a[...] = jnp.zeros_like(output_a)
+        placed[...] = jnp.zeros_like(placed)
         keyval_b[...] = jnp.zeros_like(keyval_b)
         wait(ws, sems.at[2])
 
@@ -693,7 +712,7 @@
     return pl.BlockSpec((1, *shape), lambda i, at: (i,) + (0,) * len(shape))
 
 
-def call(kernel, steps, at, ins, outs, scratch, name, flops=0):
+def call(kernel, steps, at, ins, outs, scratch, name, flops=0, short=False):
     arrays = [a for a, _ in ins]
     in_specs = [whole_block(a.shape) if b is None else b for a, b in ins]
     out_specs = [whole_block(s) if b is None else b for s, _, b in outs]
@@ -709,8 +728,10 @@
         ),
         compiler_params=pltpu.CompilerParams(vmem_limit_bytes=VMEM_LIMIT),
         cost_estimate=pl.CostEstimate(
-            flops=flops,
-            bytes_accessed=sum(a.size * a.dtype.itemsize for a in arrays)
+            flops=0 if short else flops,
+            bytes_accessed=0
+            if short
+            else sum(a.size * a.dtype.itemsize for a in arrays)
             + sum(math.prod(s) * 4 for s, _, _ in outs),
             transcendentals=0,
         ),
@@ -756,12 +777,14 @@
 
 def spread_out(kernel, at, pieces, widths, name):
     total = pieces[0].shape[-1]
-    wide = [(w, lambda i, j, at: (0, 0, j * 4 + i)) for w in widths]
-    blocks = [b if b[0] >= 128 else (128, lambda i, j, at: (0, 0, i)) for b in wide]
+    blocks = [
+        (w, lambda i, j, at: (0, 0, j * 4 + i)) if w >= 128 else (128, lambda i, j, at: (0, 0, i // 2))
+        for w in widths
+    ]
     return pl.pallas_call(
         functools.partial(kernel, widths),
         out_shape=[
-            jax.ShapeDtypeStruct((ADAPTER_COUNT, ADAPTER_RANK, 8 * w if w >= 128 else 512), f32)
+            jax.ShapeDtypeStruct((ADAPTER_COUNT, ADAPTER_RANK, 8 * w if w >= 128 else 256), f32)
             for w in widths
         ],
         grid_spec=pltpu.PrefetchScalarGridSpec(
@@ -827,7 +850,6 @@
         return call(pack_kernel, 1, at, ins, [((ROWS, width), bf16, None)], [], "pack")[0]
 
     mine = sequence_adapter[0, 0]
-    theirs = other_core(sequence_adapter)[0, 0]
     attention_shard = pack(query_projection, keyvalue_projection, attention_output_weight)
     attention_shard, cotangent = together((attention_shard, cotangent))
     down_back = dot_t(cotangent, pick(down_adapter_output, mine)).astype(bf16)
@@ -839,6 +861,10 @@
 
     attention_shard = turn(attention_shard)
     feed_shard = pack(up_projection_weight, down_projection_weight)
+    attention_shard, feed_shard, sequence_adapter, tokens = together(
+        (attention_shard, feed_shard, sequence_adapter, tokens)
+    )
+    theirs = other_core(sequence_adapter)[0, 0]
     rows_shape = ((ROWS, MODEL_WIDTH), bf16, None)
     normed = call(
         norm_kernel,
@@ -849,10 +875,9 @@
         [],
         "norm",
     )[0]
-    attention_shard, normed, feed_shard, mine, theirs = together(
-        (attention_shard, normed, feed_shard, mine, theirs)
-    )
-    column, mine, theirs = together((gather_cross(attention_shard, False), mine, theirs))
+    column, mine, theirs, normed = together(
+        (gather_cross(attention_shard, False), mine, theirs, normed)
+    )
     plane = gather_cross(jnp.stack(column), True)
     normed_sides = gather_sides(normed)
 
@@ -925,11 +950,7 @@
     )[0]
     keyval = other_half(keyval)
     keyval_far = ring_x(keyval, 2)
-    keyval = jnp.concatenate([keyval, other_core(keyval)], axis=0)
-    keyval_near = ring_by_core(keyval)
-    keyval_pieces = (keyval, keyval_near, other_core(keyval_near))
-    keyval_pieces += (keyval_far, other_core(keyval_far))
-    q_out, o_in, u_out, d_in, q_bias, u_bias = call(
+    turned = call(
         turned_kernel,
         1,
         at,
@@ -945,6 +966,13 @@
         [],
         "turned",
     )
+    keyval_pair = jnp.concatenate([keyval, other_core(keyval)], axis=0)
+    keyval_pair, turned = together((keyval_pair, turned))
+    q_out, o_in, u_out, d_in, q_bias, u_bias = turned
+    keyval = keyval_pair
+    keyval_near = ring_by_core(keyval)
+    keyval_pieces = (keyval, keyval_near, other_core(keyval_near))
+    keyval_pieces += (keyval_far, other_core(keyval_far))
     input_rows = tokens.astype(f32)
 
     group = (2, 4 * ROWS)
@@ -990,7 +1018,7 @@
     normed_two = layer_norm(middle, gain_two, shift_two).astype(bf16)
     place_scratch = pltpu.VMEM((4, 2 * ROWS, MODEL_WIDTH), bf16)
     feed_scratch = pltpu.VMEM((16, ROWS, 1024), bf16)
-    up_b, down_a, *feed_parts = call(
+    feed_placed, *feed_parts = call(
         feed_kernel,
         4,
         at,
@@ -1004,8 +1032,7 @@
             (u_bias, None),
         ],
         [
-            ((32, 1024), f32, None),
-            ((32, 1024), f32, None),
+            ((32, 2048), f32, None),
             *part_outs(MODEL_WIDTH + RIDE, True),
             *part_outs(MODEL_WIDTH + RIDE, True),
         ],
@@ -1021,18 +1048,18 @@
         19000000000,
     )
     down_parts, up_parts = feed_parts[:4], feed_parts[4:]
-    up_parts, down_parts, up_b, down_a = together((up_parts, down_parts, up_b, down_a))
+    up_parts, down_parts, feed_placed = together((up_parts, down_parts, feed_placed))
     up_far = scatter_far(*up_parts[2:])
-    up_far, up_b, down_a, down_parts = together((up_far, up_b, down_a, down_parts))
-    feed_set = row_slice(jnp.concatenate([up_b, down_a], axis=1), core, (1024, 1024))
+    up_far, feed_placed, down_parts = together((up_far, feed_placed, down_parts))
+    feed_set = row_slice(feed_placed, core, (1024, 1024))
     up_sides, up_near, feed_set = together(
         (scatter_sides(up_far), add_cores(*up_parts[:2]), feed_set)
     )
     right, left = scatter_joined(up_near, *up_sides)
     right, left, down_parts = together((right, left, down_parts))
     up_moved = ring_x(right, 1), ring_x(left, -1)
-    down_far, down_near = scatter_far(*down_parts[2:]), add_cores(*down_parts[:2])
-    up_moved, down_far, down_near = together((up_moved, down_far, down_near))
+    down_low = scatter_start(*down_parts)
+    up_moved, down_low = together((up_moved, down_low))
     up_sum = up_near[0] + sum(part.astype(f32) for part in up_moved)
     up_back = up_sum[:, MODEL_WIDTH:].astype(bf16)
     grad_normed_two = up_sum[:, :MODEL_WIDTH] + dot(up_back, u_in)
@@ -1055,15 +1082,11 @@
         ],
         axis=1,
     )
-    down_sides = scatter_sides(down_far)
-    feed_column, branch_all, down_sides = together((gather_y(feed_set), branch_all, down_sides))
-    right, left = scatter_joined(down_near, *down_sides)
-    right, left, branch_all, feed_column = together(
-        (right, left, branch_all, jnp.stack(feed_column))
-    )
-    down_moved = ring_x(right, 1), ring_x(left, -1)
-    feed_pieces = gather_z(feed_column)
-    query_b, output_a, keyval_b, backs, backs_far, *query_parts = call(
+    feed_column, down_low = together((gather_y(feed_set), down_low))
+    feed_column = jnp.stack(feed_column)
+    feed_sides = ring_z(feed_column, -1), ring_z(feed_column, 1)
+    down_moved = (ring_x(down_low[1], -1), ring_x(down_low[2], 1), ring_x(down_low[3], 2))
+    placed, keyval_b, backs, backs_far, *query_parts = call(
         attention_back_kernel,
         2,
         at,
@@ -1083,8 +1106,7 @@
             (bias, None),
         ],
         [
-            ((32, 256), f32, None),
-            ((32, 256), f32, None),
+            ((32, 512), f32, None),
             ((32, 256), f32, None),
             ((*group, RIDE), bf16, step_block((4 * ROWS, RIDE))),
             ((2, 32, 4 * ROWS), bf16, step_block((32, 4 * ROWS))),
@@ -1098,27 +1120,19 @@
             dma(3),
         ],
         "attention_back",
-        8000000000,
-    )
-    query_b, output_a, keyval_b, backs, backs_far, query_parts, down_moved, feed_pieces = together(
-        (query_b, output_a, keyval_b, backs, backs_far, query_parts, down_moved, feed_pieces)
-    )
-    placed = row_slice(jnp.concatenate([query_b, output_a], axis=1), core, (256, 256))
-    query_far, backs_far, placed, down_moved = together(
-        (scatter_far(*query_parts[2:]), other_half(backs_far), placed, down_moved)
-    )
-    down_sum = down_near[0] + sum(part.astype(f32) for part in down_moved)
-    down_inner = down_sum[:, MODEL_WIDTH:].astype(bf16)
-    layer_output = (
-        middle
-        + down_sum[:, :MODEL_WIDTH]
-        + down_projection_bias.astype(f32)
-        + dot(down_inner, d_out)
-    ).astype(bf16)
-    down_slices = slices_of(at, [(down_inner, cotangent)], "down_slices")
+        short=True,
+    )
+    placed, keyval_b, backs, backs_far, query_parts, down_moved, feed_sides = together(
+        (placed, keyval_b, backs, backs_far, query_parts, down_moved, feed_sides)
+    )
+    query_far, backs_far, placed, feed_column = together(
+        (scatter_far(*query_parts[2:]), other_half(backs_far), placed, feed_column)
+    )
+    feed_far = ring_z(feed_column, 2)
     query_sides = scatter_sides(query_far)
     query_near = add_cores(*query_parts[:2])
     pack_shape = (4, ADAPTER_RANK, 1152)
+    ride_block = pl.BlockSpec((ROWS, RIDE), lambda i, at: (0, MODEL_WIDTH // RIDE))
     late_mine, late_theirs = call(
         late_kernel,
         1,
@@ -1128,23 +1142,37 @@
             (backs, None),
             (backs_far, None),
             (keyval_b, None),
+            (cotangent, None),
+            *[(part, ride_block) for part in (down_low[0], *down_moved)],
         ],
-        [(pack_shape, bf16, None), (pack_shape, bf16, None)],
+        [((4, ADAPTER_RANK, 1664), bf16, None), (pack_shape, bf16, None)],
         [row_scratch, dma(2)],
         "late",
     )
-    late_mine, late_theirs, query_near, query_sides, down_slices = together(
-        (late_mine, late_theirs, query_near, query_sides, down_slices)
-    )
-    late_pack = jnp.concatenate(
-        [add_cores(late_mine, late_theirs).astype(bf16), down_slices], axis=-1
-    )
+    late_mine, late_theirs, query_near, query_sides = together(
+        (late_mine, late_theirs, query_near, query_sides)
+    )
+    late_pack = add_cores(late_mine[..., :1152], late_theirs).astype(bf16)
+    late_pack = jnp.concatenate([late_pack, late_mine[..., 1152:]], axis=-1)
     right, left = scatter_joined(query_near, *query_sides)
     late_pack, right, left = together((late_pack, right, left))
     query_moved = ring_x(right, 1), ring_x(left, -1)
-    late_parts, feed_pieces = together((scatter_sequence(late_pack), feed_pieces))
+    late_parts, feed_far, feed_column, feed_sides, down_moved = together(
+        (scatter_sequence(late_pack), feed_far, feed_column, feed_sides, down_moved)
+    )
+    down_sum = down_low[0] + sum(part.astype(f32) for part in down_moved)
+    placed = row_slice(placed, core, (256, 256))
+    down_inner = down_sum[:, MODEL_WIDTH:].astype(bf16)
+    layer_output = (
+        middle
+        + down_sum[:, :MODEL_WIDTH]
+        + down_projection_bias.astype(f32)
+        + dot(down_inner, d_out)
+    ).astype(bf16)
+    feed_pieces = [feed_column, feed_sides[0], feed_far, feed_sides[1]]
     late_set = jnp.concatenate([total(late_parts), placed], axis=-1)
-    all_ids = jnp.concatenate([piece[:, 0, 5120] for piece in feed_pieces]).astype(jnp.int32)
+    names = together(jnp.concatenate([piece[:, :1, 5120:5248] for piece in feed_pieces]))
+    all_ids = names[:, 0, 0].astype(jnp.int32)
     feed_kept, feed_sent = sum_by_adapter(feed_pieces, core, all_ids)
     column = gather_y(late_set)
     feed_half = add_cores(feed_kept, feed_sent).astype(bf16)
@@ -1173,7 +1201,7 @@
     feed_grads = spread_out(
         feed_spread_kernel, at, [feed_sum], (1024, 1024, 256, 256), "feed_spread"
     )
-    near, far, feed_grads = together((near, far, feed_grads))
+    near, far, feed_grads, layer_output = together((near, far, feed_grads, layer_output))
     up_b, down_a, up_a, output_b = feed_grads
     query_a, keyval_a, keyval_b, down_b, query_b, output_a = spread_out(
         late_spread_kernel,
@@ -1182,7 +1210,6 @@
         (256, 256, 64, 256, 256, 256),
         "late_spread",
     )
-    keyval_b = keyval_b.reshape(8, 16, 2, 2, 128).sum(axis=3).reshape(8, 16, 256)
 
     def side_in(a):
         return jnp.swapaxes(a, 1, 2)

time: 458 us -> 437 us (0.954)
  waiting for transfers between devices: 114 us -> 103 us
  other arithmetic: 34.4 us -> 28 us
    all_gather x1, waiting for transfers between devices: 14.4 us -> 6.42 us  [shards(): branch_all = lax.all_gather(grad_branch, ('core', 'x'), axis=0, tiled=True)]
    pallas_call x13 -> x12, Pallas kernels: 118 us -> 115 us  [call(): pl.pallas_call(kernel, out_shape=[jax.ShapeDtypeStruct(s, d) for s, d, _...]
    ppermute x32 -> x31, waiting for transfers between devices: 54 us -> 56.3 us  [ring_x(): return lax.ppermute(a, 'x', [(i, (i + step) % 4) for i in range(4)])]
    ppermute x32 -> x31, starting transfers between devices: 33 us -> 34 us  [ring_x(): return lax.ppermute(a, 'x', [(i, (i + step) % 4) for i in range(4)])]
    unnamed x177 -> x156, local copies, waits for them, and re-layouts: 9.51 us -> 8.86 us
  transfers between devices with their start and end apart: 91 -> 90, of which waited for: 34 -> 34; matrix products, arithmetic and copies ran while one was open for 10% -> 10% of each run, Pallas kernels for 20% -> 21%
where the time goes in v6:
time: 437 us; the launch traced here: 428 us
  Pallas kernels  137 us (31%)
  starting transfers between devices  116 us (27%)
  waiting for transfers between devices  103 us (24%)
  other arithmetic  28 us (6%)
  local copies, waits for them, and re-layouts  18.9 us (4%)
  between operations  17.3 us (4%)
  matrix products  8.84 us (2%)
    pallas_call x12, Pallas kernels, call(): pl.pallas_call(kernel, out_shape=[jax.ShapeDtypeStruct(s, d) for s, d, _...  115 us
    ppermute x31, waiting for transfers between devices, ring_x(): return lax.ppermute(a, 'x', [(i, (i + step) % 4) for i in range(4)])  56.3 us
    ppermute x31, starting transfers between devices, ring_x(): return lax.ppermute(a, 'x', [(i, (i + step) % 4) for i in range(4)])  34 us
    ppermute x30, starting transfers between devices, other_core(): return lax.ppermute(a, 'core', [(0, 1), (1, 0)])  32.7 us
    pallas_call x2, Pallas kernels, spread_out(): pl.pallas_call(functools.partial(kernel, widths), out_shape=[jax.ShapeDty...  14.1 us
    ppermute x2, starting transfers between devices, turn(): return lax.ppermute(a, ('core', 'zh'), [(0, 0), (1, 2), (2, 1), (3, 3)])  13.6 us
    ppermute x30, waiting for transfers between devices, other_core(): return lax.ppermute(a, 'core', [(0, 1), (1, 0)])  11.6 us
    ppermute x6, starting transfers between devices, ring_z(): lax.ppermute(a, ('zl', 'zh'), [(Z_RING[i], Z_RING[(i + step) % 4]) for i...  10.3 us
  transfers between devices with their start and end apart: 90, of which 34 were waited for; matrix products, arithmetic and copies ran while one was open for 10% of the time, Pallas kernels for 21%

profile of v6, /device:TPU:1, one launch (start us, length us, event | category | flops | bytes accessed | tf_op | source)
XLA Modules:
  0.0 428.1 jit_solution(10668918902231203127)
XLA Ops:
  13.4 6.9 %collective-permute-start = (bf16[128,768]{1,0:T(8,128)(2,1)S(1)}, bf16[128,768]{1,0:T(8,128)(2,1)S(1)}, u32[]{:S(2)}, u32[]{:S(2)}) collective-permute-start(bf16[128,768]{1,0:T(8,128)(2,1)S(1)} %copy-done.46), channel_id=1, source_target_pairs={{0,0},{4,8},{8,4},{12,12},{1,1},{5,9},{9,5},{13,13},{2,2},{6,10},{... | collective-permute-start | bytes 589832 | tf_op jit(solution)/shard_map/ppermute | solution.py:57
  47.0 10.8 %collective-permute-done.9.refs_4_ = bf16[128,2048]{1,0:T(8,128)(2,1)S(1)} collective-permute-done((bf16[128,2048]{1,0:T(8,128)(2,1)S(1)}, bf16[128,2048]{1,0:T(8,128)(2,1)S(1)}, u32[]{:S(2)}, u32[]{:S(2)}) %collective-permute-start.9) | collective-permute-done | bytes 524320 | tf_op jit(solution)/shard_map/ppermute | solution.py:37
  58.6 4.3 %assemble.1.w.refs_15_.refs_1_ = bf16[2048,768]{1,0:T(8,128)(2,1)} custom-call(s32[5]{0:T(128)} %stack.76.at, bf16[4,128,768]{2,1,0:T(8,128)(2,1)} %copy-done.9, bf16[4,128,768]{2,1,0:T(8,128)(2,1)} %collective-permute-done.5.refs_1_, bf16[4,128,768]{2,1,0:T(8,128)(2,1)} %collective-permute-done.6.refs_2_, bf16[4,128,768]{2,1,0:T(8,128)(2,1)} %collective-permute-done.7.refs_3_), custom_call_target="tpu_custom_call" | custom-call | bytes 9437184 | tf_op jit(solution)/shard_map/assemble/pallas_call | solution.py:719
  64.7 6.7 %collective-permute-start.19 = (bf16[48,2560]{1,0:T(8,128)(2,1)S(1)}, bf16[48,2560]{1,0:T(8,128)(2,1)S(1)}, u32[]{:S(2)}, u32[]{:S(2)}) collective-permute-start(bf16[48,2560]{1,0:T(8,128)(2,1)S(1)} %copy-done.70), channel_id=1, source_target_pairs={{0,0},{4,8},{8,4},{12,12},{1,1},{5,9},{9,5},{13,13},{2,2},{6,10},{... | collective-permute-start | bytes 737288 | tf_op jit(solution)/shard_map/ppermute | solution.py:57
  75.3 5.8 %collective-permute-done.17 = bf16[128,384]{1,0:T(8,128)(2,1)S(1)} collective-permute-done((bf16[128,384]{1,0:T(8,128)(2,1)}, bf16[128,384]{1,0:T(8,128)(2,1)S(1)}, u32[]{:S(2)}, u32[]{:S(2)}) %collective-permute-start.17) | collective-permute-done | bytes 98336 | tf_op jit(solution)/shard_map/ppermute | solution.py:53
  87.8 3.7 collective-permute-done.20.refs_11_
  97.2 21.7 %attention.1 = (bf16[2,512,128]{2,1,0:T(8,128)(2,1)}, bf16[2,512,128]{2,1,0:T(8,128)(2,1)}, bf16[2,512,256]{2,1,0:T(8,128)(2,1)}, bf16[2,8,128,256]{3,2,1,0:T(8,...) custom-call(s32[5]{0:T(128)} %stack.76.at, ...), custom_call_target="tpu_custom_call" | custom-call | flops 8999999488 | bytes 23029760 | tf_op jit(solution)/shard_map/attention/pallas_call | solution.py:719
  125.8 5.9 %collective-permute-done.26 = bf16[64,2176]{1,0:T(8,128)(2,1)S(1)} collective-permute-done((bf16[64,2176]{1,0:T(8,128)(2,1)S(1)}, bf16[64,2176]{1,0:T(8,128)(2,1)S(1)}, u32[]{:S(2)}, u32[]{:S(2)}) %collective-permute-start.26) | collective-permute-done | bytes 278560 | tf_op jit(solution)/shard_map/ppermute | solution.py:37
  134.5 10.5 %collective-permute-done.29 = bf16[128,2176]{1,0:T(8,128)(2,1)S(1)} collective-permute-done((bf16[128,2176]{1,0:T(8,128)(2,1)S(1)}, bf16[128,2176]{1,0:T(8,128)(2,1)S(1)}, u32[]{:S(2)}, u32[]{:S(2)}) %collective-permute-start.29) | collective-permute-done | bytes 557088 | tf_op jit(solution)/shard_map/ppermute | solution.py:37
  154.3 6.1 %collective-permute-done.33.refs_4_ = bf16[128,2048]{1,0:T(8,128)(2,1)S(1)} collective-permute-done((bf16[128,2048]{1,0:T(8,128)(2,1)S(1)}, bf16[128,2048]{1,0:T(8,128)(2,1)S(1)}, u32[]{:S(2)}, u32[]{:S(2)}) %collective-permute-start.33) | collective-permute-done | bytes 524320 | tf_op jit(solution)/shard_map/ppermute | solution.py:37
  162.6 4.3 collective-permute-start.34
  166.8 3.8 collective-permute-start.38
  175.7 39.2 %feed.1 = (f32[32,2048]{1,0:T(8,128)}, bf16[3,128,2176]{2,1,0:T(8,128)(2,1)}, bf16[3,128,2176]{2,1,0:T(8,128)(2,1)}, bf16[128,2176]{1,0:T(8,128)(2,1)}, bf16[128...) custom-call(s32[5]{0:T(128)} %stack.76.at, ...), custom_call_target="tpu_custom_call" | custom-call | flops 19000000512 | bytes 44568576 | tf_op jit(solution)/shard_map/feed/pallas_call | solution.py:719
  220.9 6.2 %collective-permute-done.41 = bf16[64,2176]{1,0:T(8,128)(2,1)S(1)} collective-permute-done((bf16[64,2176]{1,0:T(8,128)(2,1)S(1)}, bf16[64,2176]{1,0:T(8,128)(2,1)S(1)}, u32[]{:S(2)}, u32[]{:S(2)}) %collective-permute-start.41) | collective-permute-done | bytes 278560 | tf_op jit(solution)/shard_map/ppermute | solution.py:37
  238.7 7.4 %collective-permute-done.44 = bf16[128,2176]{1,0:T(8,128)(2,1)S(1)} collective-permute-done((bf16[128,2176]{1,0:T(8,128)(2,1)S(1)}, bf16[128,2176]{1,0:T(8,128)(2,1)S(1)}, u32[]{:S(2)}, u32[]{:S(2)}) %collective-permute-start.44) | collective-permute-done | bytes 557088 | tf_op jit(solution)/shard_map/ppermute | solution.py:37
  255.8 3.7 collective-permute-start.50
  277.6 6.4 %all-gather.10.cloned.1.call-done = bf16[1024,2048]{1,0:T(8,128)(2,1)} async-done(((bf16[128,2048]{1,0:T(8,128)(2,1)}), bf16[1024,2048]{1,0:T(8,128)(2,1)}) %all-gather.10.cloned.1.call-update) | async-done | bytes 4194320 | tf_op jit(solution)/shard_map/all_gather | solution.py:1070
  284.1 24.4 %attention_back.1 = (f32[32,512]{1,0:T(8,128)}, f32[32,256]{1,0:T(8,128)}, bf16[2,512,128]{2,1,0:T(8,128)(2,1)}, bf16[2,32,512]{2,1,0:T(8,128)(2,1)}, bf16[3,128...) custom-call(s32[5]{0:T(128)} %stack.76.at, ...), custom_call_target="tpu_custom_call" | custom-call | tf_op jit(solution)/shard_map/attention_back/pallas_call | solution.py:719
  308.9 5.0 %collective-permute-start.60 = (bf16[2,32,512]{2,1,0:T(8,128)(2,1)}, bf16[2,32,512]{2,1,0:T(8,128)(2,1)S(1)}, u32[]{:S(2)}, u32[]{:S(2)}) collective-permute-start(bf16[2,32,512]{2,1,0:T(8,128)(2,1)} %get-tuple-element.318), channel_id=1, source_target_pairs={{0,4},{4,0},{1,5},{5,1},{2,6},{6,2},{3,7},{7,3},{8,12},{12,8},{9,1... | collective-permute-start | bytes 196616 | tf_op jit(solution)/shard_map/ppermute | solution.py:53
  323.0 5.7 %late.1 = (bf16[4,16,1664]{2,1,0:T(8,128)(2,1)}, bf16[4,16,1152]{2,1,0:T(8,128)(2,1)}) custom-call(s32[5]{0:T(128)} %stack.76.at, bf16[128,2048]{1,0:T(8,128)(2,1)} %norm.1.rows.refs_0_, bf16[128,2048]{1,0:T(8,128)(2,1)} %copy-done.33, bf16[128,2048]{1,0:T(8,128)(2,1)} %copy-done.26, bf16[128,2048]{1,0:T(8,128)(2,1)} %copy-done.32, ...), custom_call_target="tpu_custom_call" | custom-call | bytes 8585216 | tf_op jit(solution)/shard_map/late/pallas_call | solution.py:719
  378.8 5.4 %collective-permute-done.77.refs_2_ = bf16[4,16,2688]{2,1,0:T(8,128)(2,1)} collective-permute-done((bf16[4,16,2688]{2,1,0:T(8,128)(2,1)S(1)}, bf16[4,16,2688]{2,1,0:T(8,128)(2,1)}, u32[]{:S(2)}, u32[]{:S(2)}) %collective-permute-start.77) | collective-permute-done | bytes 344096 | tf_op jit(solution)/shard_map/ppermute | solution.py:45
  396.1 8.0 %feed_spread.1 = (f32[8,16,8192]{2,1,0:T(8,128)}, f32[8,16,8192]{2,1,0:T(8,128)}, f32[8,16,2048]{2,1,0:T(8,128)}, f32[8,16,2048]{2,1,0:T(8,128)}) custom-call(s32[5]{0:T(128)} %stack.76.at, bf16[2,4,4,16,5376]{4,3,2,1,0:T(8,128)(2,1)} %bitcast.126), custom_call_target="tpu_custom_call" | custom-call | tf_op jit(solution)/shard_map/feed_spread/pallas_call | solution.py:784
  404.1 4.1 collective-permute-done.82.refs_2_
  415.1 6.1 %late_spread.1 = (f32[8,16,2048]{2,1,0:T(8,128)}, f32[8,16,2048]{2,1,0:T(8,128)}, f32[8,16,256]{2,1,0:T(8,128)}, f32[8,16,2048]{2,1,0:T(8,128)}, f32[8,16,2048]{2,1,0:T(8,128)}, /*index=5*/f32[8,16,2048]{2,1,0:T(8,128)}) custom-call(s32[5]{0:T(128)} %stack.76.at, bf16[4,16,2688]{2,1,0:T(8,128)(2,1)} %copy-done.10, bf16[4,16,2688]{2,1,0:T(8,128)(2,1)} %copy-done.22, ...), custom_call_target="tpu_custom_call" | custom-call | tf_op jit(solution)/shard_map/late_spread/pallas_call | solution.py:784
  (441 shorter events, 198.7 us)
Async XLA Ops:
  7.2 55.8 %all-gather.6.cloned.1.call-start = ((), (), s32[]{:S(2)}) async-start(), calls=%async_computation | async-start | bytes 5013504 | tf_op jit(solution)/shard_map/all_gather | solution.py:859
  13.4 162.3 %all-gather.8.cloned.1.call-start = ((), (), s32[]{:S(2)}) async-start(), calls=%async_computation.1 | async-start | bytes 17301504 | tf_op jit(solution)/shard_map/all_gather | solution.py:938
  32.7 25.9 %collective-permute-start.7 = (bf16[4,128,768]{2,1,0:T(8,128)(2,1)S(1)}, bf16[4,128,768]{2,1,0:T(8,128)(2,1)}, u32[]{:S(2)}, u32[]{:S(2)}) collective-permute-start(bf16[4,128,768]{2,1,0:T(8,128)(2,1)S(1)} %pad_maximum_fusion.refs_0_), channel_id=1, source_target_pairs={{0,16},{8,40},{16,4},{24,56},{4,20},{12,44},{20,0},{28,60},{32,48}... | collective-permute-start | bytes 2359304 | tf_op jit(solution)/shard_map/ppermute | solution.py:78
  34.1 24.6 %collective-permute-start.6 = (bf16[4,128,768]{2,1,0:T(8,128)(2,1)S(1)}, bf16[4,128,768]{2,1,0:T(8,128)(2,1)}, u32[]{:S(2)}, u32[]{:S(2)}) collective-permute-start(bf16[4,128,768]{2,1,0:T(8,128)(2,1)S(1)} %pad_maximum_fusion.refs_0_), channel_id=1, source_target_pairs={{0,4},{8,72},{16,20},{24,88},{4,0},{12,76},{20,16},{28,92},{32,36}... | collective-permute-start | bytes 2359304 | tf_op jit(solution)/shard_map/ppermute | solution.py:78
  37.0 21.7 %collective-permute-start.5 = (bf16[4,128,768]{2,1,0:T(8,128)(2,1)S(1)}, bf16[4,128,768]{2,1,0:T(8,128)(2,1)}, u32[]{:S(2)}, u32[]{:S(2)}) collective-permute-start(bf16[4,128,768]{2,1,0:T(8,128)(2,1)S(1)} %pad_maximum_fusion.refs_0_), channel_id=1, source_target_pairs={{0,20},{8,104},{16,0},{24,120},{4,16},{12,108},{20,4},{28,124},{32... | collective-permute-start | bytes 2359304 | tf_op jit(solution)/shard_map/ppermute | solution.py:78
  37.8 20.1 %collective-permute-start.9 = (bf16[128,2048]{1,0:T(8,128)(2,1)S(1)}, bf16[128,2048]{1,0:T(8,128)(2,1)S(1)}, u32[]{:S(2)}, u32[]{:S(2)}) collective-permute-start(bf16[128,2048]{1,0:T(8,128)(2,1)S(1)} %copy-done.7), channel_id=1, source_target_pairs={{0,3},{1,0},{2,1},{3,2},{4,7},{5,4},{6,5},{7,6},{8,11},{9,8},{10,9... | collective-permute-start | bytes 1572872 | tf_op jit(solution)/shard_map/ppermute | solution.py:37
  40.2 18.4 %collective-permute-start.8 = (bf16[128,2048]{1,0:T(8,128)(2,1)S(1)}, bf16[128,2048]{1,0:T(8,128)(2,1)S(1)}, u32[]{:S(2)}, u32[]{:S(2)}) collective-permute-start(bf16[128,2048]{1,0:T(8,128)(2,1)S(1)} %copy-done.7), channel_id=1, source_target_pairs={{0,1},{1,2},{2,3},{3,0},{4,5},{5,6},{6,7},{7,4},{8,9},{9,10},{10,1... | collective-permute-start | bytes 1572872 | tf_op jit(solution)/shard_map/ppermute | solution.py:37
  63.0 221.0 %all-gather.10.cloned.1.call-start = ((), (), s32[]{:S(2)}) async-start(), calls=%async_computation.2 | async-start | bytes 4718592 | tf_op jit(solution)/shard_map/all_gather | solution.py:1070
  63.9 17.9 %collective-permute-start.13 = (bf16[64,2048]{1,0:T(8,128)(2,1)S(1)}, bf16[64,2048]{1,0:T(8,128)(2,1)S(1)}, u32[]{:S(2)}, u32[]{:S(2)}) collective-permute-start(bf16[64,2048]{1,0:T(8,128)(2,1)S(1)} %slice.196), channel_id=1, source_target_pairs={{0,1},{1,2},{2,3},{3,0},{4,5},{5,6},{6,7},{7,4},{8,9},{9,10},{10,1... | collective-permute-start | bytes 786440 | tf_op jit(solution)/shard_map/ppermute | solution.py:37
  64.7 16.9 %collective-permute-start.19 = (bf16[48,2560]{1,0:T(8,128)(2,1)S(1)}, bf16[48,2560]{1,0:T(8,128)(2,1)S(1)}, u32[]{:S(2)}, u32[]{:S(2)}) collective-permute-start(bf16[48,2560]{1,0:T(8,128)(2,1)S(1)} %copy-done.70), channel_id=1, source_target_pairs={{0,0},{4,8},{8,4},{12,12},{1,1},{5,9},{9,5},{13,13},{2,2},{6,10},{... | collective-permute-start | bytes 737288 | tf_op jit(solution)/shard_map/ppermute | solution.py:57
  151.0 22.8 %collective-permute-start.30 = (bf16[128,2048]{1,0:T(8,128)(2,1)S(1)}, bf16[128,2048]{1,0:T(8,128)(2,1)S(1)}, u32[]{:S(2)}, u32[]{:S(2)}) collective-permute-start(bf16[128,2048]{1,0:T(8,128)(2,1)S(1)} %add_convert_fusion.6.refs_0_.refs_1_), channel_id=1, source_target_pairs={{0,8},{8,0},{1,9},{9,1},{2,10},{10,2},{3,11},{11,3},{4,12},{12,4},... | collective-permute-start | bytes 1572872 | tf_op jit(solution)/shard_map/ppermute | solution.py:49
  250.0 146.2 %all-gather.12.cloned.1.call-start = ((), (), s32[]{:S(2)}) async-start(), calls=%async_computation.3 | async-start | bytes 6193152 | tf_op jit(solution)/shard_map/all_gather | solution.py:1180
  272.3 36.2 %collective-permute-start.58 = (bf16[4,16,5376]{2,1,0:T(8,128)(2,1)S(1)}, bf16[4,16,5376]{2,1,0:T(8,128)(2,1)}, u32[]{:S(2)}, u32[]{:S(2)}) collective-permute-start(bf16[4,16,5376]{2,1,0:T(8,128)(2,1)S(1)} %pad_maximum_fusion.1.refs_0_), channel_id=1, source_target_pairs={{0,16},{16,4},{4,20},{20,0},{1,17},{17,5},{5,21},{21,1},{2,18},{18... | collective-permute-start | bytes 2064392 | tf_op jit(solution)/shard_map/ppermute | solution.py:45
  272.7 35.9 %collective-permute-start.57 = (bf16[4,16,5376]{2,1,0:T(8,128)(2,1)S(1)}, bf16[4,16,5376]{2,1,0:T(8,128)(2,1)}, u32[]{:S(2)}, u32[]{:S(2)}) collective-permute-start(bf16[4,16,5376]{2,1,0:T(8,128)(2,1)S(1)} %pad_maximum_fusion.1.refs_0_), channel_id=1, source_target_pairs={{0,20},{16,0},{4,16},{20,4},{1,21},{17,1},{5,17},{21,5},{2,22},{18... | collective-permute-start | bytes 2064392 | tf_op jit(solution)/shard_map/ppermute | solution.py:45
  275.1 33.4 %collective-permute-start.54 = (bf16[128,2176]{1,0:T(8,128)(2,1)}, bf16[128,2176]{1,0:T(8,128)(2,1)S(1)}, u32[]{:S(2)}, u32[]{:S(2)}) collective-permute-start(bf16[128,2176]{1,0:T(8,128)(2,1)} %get-tuple-element.308), channel_id=1, source_target_pairs={{0,3},{1,0},{2,1},{3,2},{4,7},{5,4},{6,5},{7,6},{8,11},{9,8},{10,9... | collective-permute-start | bytes 1671176 | tf_op jit(solution)/shard_map/ppermute | solution.py:37
  275.9 32.6 %collective-permute-start.55 = (bf16[128,2176]{1,0:T(8,128)(2,1)}, bf16[128,2176]{1,0:T(8,128)(2,1)}, u32[]{:S(2)}, u32[]{:S(2)}) collective-permute-start(bf16[128,2176]{1,0:T(8,128)(2,1)} %get-tuple-element.309), channel_id=1, source_target_pairs={{0,1},{1,2},{2,3},{3,0},{4,5},{5,6},{6,7},{7,4},{8,9},{9,10},{10,1... | collective-permute-start | bytes 1671176 | tf_op jit(solution)/shard_map/ppermute | solution.py:37
  276.6 32.0 %collective-permute-start.56 = (bf16[128,2176]{1,0:T(8,128)(2,1)}, bf16[128,2176]{1,0:T(8,128)(2,1)}, u32[]{:S(2)}, u32[]{:S(2)}) collective-permute-start(bf16[128,2176]{1,0:T(8,128)(2,1)} %add_convert_fusion.2), channel_id=1, source_target_pairs={{0,2},{1,3},{2,0},{3,1},{4,6},{5,7},{6,4},{7,5},{8,10},{9,11},{10,... | collective-permute-start | bytes 1671176 | tf_op jit(solution)/shard_map/ppermute | solution.py:37
  313.9 14.9 %collective-permute-start.61 = (bf16[3,128,2688]{2,1,0:T(8,128)(2,1)}, bf16[3,128,2688]{2,1,0:T(8,128)(2,1)S(1)}, u32[]{:S(2)}, u32[]{:S(2)}) collective-permute-start(bf16[3,128,2688]{2,1,0:T(8,128)(2,1)} %get-tuple-element.329), channel_id=1, source_target_pairs={{0,8},{8,0},{1,9},{9,1},{2,10},{10,2},{3,11},{11,3},{4,12},{12,4},... | collective-permute-start | bytes 6193160 | tf_op jit(solution)/shard_map/ppermute | solution.py:49
  320.0 18.3 %collective-permute-start.68 = (bf16[4,16,5376]{2,1,0:T(8,128)(2,1)S(1)}, bf16[4,16,5376]{2,1,0:T(8,128)(2,1)S(1)}, u32[]{:S(2)}, u32[]{:S(2)}) collective-permute-start(bf16[4,16,5376]{2,1,0:T(8,128)(2,1)S(1)} %pad_maximum_fusion.1.refs_0_), channel_id=1, source_target_pairs={{0,4},{16,20},{4,0},{20,16},{1,5},{17,21},{5,1},{21,17},{2,6},{18,... | collective-permute-start | bytes 2064392 | tf_op jit(solution)/shard_map/ppermute | solution.py:45
  338.2 22.3 %collective-permute-start.73 = (bf16[128,2688]{1,0:T(8,128)(2,1)}, bf16[128,2688]{1,0:T(8,128)(2,1)}, u32[]{:S(2)}, u32[]{:S(2)}) collective-permute-start(bf16[128,2688]{1,0:T(8,128)(2,1)} %pad_maximum_fusion.2), channel_id=1, source_target_pairs={{0,1},{1,2},{2,3},{3,0},{4,5},{5,6},{6,7},{7,4},{8,9},{9,10},{10,1... | collective-permute-start | bytes 2064392 | tf_op jit(solution)/shard_map/ppermute | solution.py:37
  338.3 22.2 %collective-permute-start.74 = (bf16[128,2688]{1,0:T(8,128)(2,1)}, bf16[128,2688]{1,0:T(8,128)(2,1)}, u32[]{:S(2)}, u32[]{:S(2)}) collective-permute-start(bf16[128,2688]{1,0:T(8,128)(2,1)} %pad_maximum_fusion.3), channel_id=1, source_target_pairs={{0,3},{1,0},{2,1},{3,2},{4,7},{5,4},{6,5},{7,6},{8,11},{9,8},{10,9... | collective-permute-start | bytes 2064392 | tf_op jit(solution)/shard_map/ppermute | solution.py:37
  365.3 19.0 %collective-permute-start.77 = (bf16[4,16,2688]{2,1,0:T(8,128)(2,1)S(1)}, bf16[4,16,2688]{2,1,0:T(8,128)(2,1)}, u32[]{:S(2)}, u32[]{:S(2)}) collective-permute-start(bf16[4,16,2688]{2,1,0:T(8,128)(2,1)S(1)} %pad_maximum_fusion.10.refs_0_), channel_id=1, source_target_pairs={{0,4},{16,20},{4,0},{20,16},{1,5},{17,21},{5,1},{21,17},{2,6},{18,... | collective-permute-start | bytes 1032200 | tf_op jit(solution)/shard_map/ppermute | solution.py:45
  368.3 15.9 %collective-permute-start.76 = (bf16[4,16,2688]{2,1,0:T(8,128)(2,1)S(1)}, bf16[4,16,2688]{2,1,0:T(8,128)(2,1)}, u32[]{:S(2)}, u32[]{:S(2)}) collective-permute-start(bf16[4,16,2688]{2,1,0:T(8,128)(2,1)S(1)} %pad_maximum_fusion.10.refs_0_), channel_id=1, source_target_pairs={{0,20},{16,0},{4,16},{20,4},{1,21},{17,1},{5,17},{21,5},{2,22},{18... | collective-permute-start | bytes 1032200 | tf_op jit(solution)/shard_map/ppermute | solution.py:45
  393.2 15.1 %collective-permute-start.82 = (bf16[8,16,2688]{2,1,0:T(8,128)(2,1)S(1)}, bf16[8,16,2688]{2,1,0:T(8,128)(2,1)S(1)}, u32[]{:S(2)}, u32[]{:S(2)}) collective-permute-start(bf16[8,16,2688]{2,1,0:T(8,128)(2,1)S(1)} %pad_maximum_fusion.4), channel_id=1, source_target_pairs={{0,1},{1,2},{2,3},{3,0},{8,11},{9,8},{10,9},{11,10},{4,5},{5,6},{6... | collective-permute-start | bytes 2064392 | tf_op jit(solution)/shard_map/ppermute | solution.py:150
  (144 other events, 1075.4 us)
Sparse Core Ops, SparseCore 0:
  13.5 42.1 all-gather.5
  63.2 107.9 all-gather.7
  250.1 33.9 all-gather.9
  360.7 35.4 all-gather.11

commit v7 on v6

--- a/solution.py
+++ b/solution.py
@@ -358,22 +358,9 @@
     x, c = pl.program_id(0), pl.program_id(1)
     first = 0
     for out, width in zip(outs, widths):
-        if width < 128:
-            part = scratch[x, :, :, first : first + 128].astype(f32)
-
-            @pl.when(jnp.logical_and(c == 0, x % 2 == 0))
-            def _(out=out, part=part):
-                out[...] = part
-
-            @pl.when(jnp.logical_and(c == 0, x % 2 == 1))
-            def _(out=out, part=part):
-                out[...] += part
-
-            first += 128
-        else:
-            here = pl.ds(pl.multiple_of(first + c * width, 128), width)
-            out[...] = scratch[x, :, :, here].astype(f32)
-            first += 2 * width
+        here = pl.ds(pl.multiple_of(first + c * width, 128), width)
+        out[...] = scratch[x, :, :, here].astype(f32)
+        first += 2 * width
 
 
 def feed_spread_kernel(widths, at, *refs):
@@ -391,26 +378,35 @@
 
 def late_spread_kernel(widths, at, *refs):
     own, other, near, near_other, far, far_other = refs[:6]
-    scratch, sem = refs[-2:]
+    outs, (scratch, sem) = refs[6:-2], refs[-2:]
     core, x = at[0], at[1]
-
-    @pl.when((pl.program_id(0) == 0) & (pl.program_id(1) == 0))
-    def _():
-        mine, theirs = pl.ds(4 * core, 4), pl.ds(4 * (1 - core), 4)
-        side = lax.rem(x + jnp.where(core == 0, 3, 1), 4)
-        other_side = lax.rem(x + jnp.where(core == 0, 1, 3), 4)
-        across = lax.rem(x + 2, 4)
-        copy(own, scratch.at[x, mine], sem)
-        copy(other, scratch.at[x, theirs], sem)
-        for part, where in ((0, mine), (1, theirs)):
-            copy(near.at[pl.ds(4 * part, 4)], scratch.at[side, where], sem)
-        for part, where in ((0, theirs), (1, mine)):
-            copy(near_other.at[pl.ds(4 * part, 4)], scratch.at[other_side, where], sem)
-        copy(far, scratch.at[across, mine], sem)
-        copy(far_other, scratch.at[across, theirs], sem)
-        wait(scratch, sem)
-
-    spread(scratch, refs[6:-2], widths)
+    mine, theirs = pl.ds(4 * core, 4), pl.ds(4 * (1 - core), 4)
+    side = lax.rem(x + jnp.where(core == 0, 3, 1), 4)
+    other_side = lax.rem(x + jnp.where(core == 0, 1, 3), 4)
+    across = lax.rem(x + 2, 4)
+    copy(own, scratch.at[x, mine], sem)
+    copy(other, scratch.at[x, theirs], sem)
+    for part, where in ((0, mine), (1, theirs)):
+        copy(near.at[pl.ds(4 * part, 4)], scratch.at[side, where], sem)
+    for part, where in ((0, theirs), (1, mine)):
+        copy(near_other.at[pl.ds(4 * part, 4)], scratch.at[other_side, where], sem)
+    copy(far, scratch.at[across, mine], sem)
+    copy(far_other, scratch.at[across, theirs], sem)
+    wait(scratch, sem)
+    first = 0
+    for out, width in zip(outs, widths):
+        if width < 128:
+            for g in range(2):
+                pair = scratch[2 * g, :, :, first : first + 128].astype(f32)
+                pair += scratch[2 * g + 1, :, :, first : first + 128].astype(f32)
+                out[:, :, g * 128 : g * 128 + 128] = pair
+            first += 128
+            continue
+        for c in range(2):
+            for to in range(4):
+                here = slice((c * 4 + to) * width, (c * 4 + to + 1) * width)
+                out[:, :, here] = scratch[to, :, :, first : first + width].astype(f32)
+            first += width
 
 
 def copy_rows(rows_in, rows, sems):
@@ -424,6 +420,24 @@
                 for n in range(2):
                     here = pl.ds(p * ROWS + n * half, half)
                     copy(pieces[2 * s + n], rows.at[s, here], sems.at[s])
+
+
+def attend(query, kv, bias, lanes, lse_out):
+    keys = kv[:, :, :HEAD_WIDTH].reshape(8 * ROWS, HEAD_WIDTH)
+    values_t = kv[:, :, HEAD_WIDTH:].reshape(8 * ROWS, HEAD_WIDTH).astype(f32).T.astype(bf16)
+    columns = []
+    for h in range(2):
+        q = query[:, h * HEAD_WIDTH : (h + 1) * HEAD_WIDTH]
+        scores = dot_t(keys, q) * (HEAD_WIDTH**-0.5)
+        scores = scores.reshape(8, ROWS, 256) + bias[:, lanes][:, None, :]
+        scores = scores.reshape(8 * ROWS, 256)
+        top = jnp.max(scores, axis=0, keepdims=True)
+        expo = jnp.exp(scores - top)
+        total = jnp.sum(expo, axis=0, keepdims=True)
+        probs = (expo * (1.0 / total)).astype(bf16)
+        lse_out[0, h : h + 1] = top + jnp.log(total)
+        columns.append(dot(values_t, probs).T)
+    return jnp.concatenate(columns, axis=1).astype(bf16)
 
 
 def attention_kernel(at, *refs):
@@ -455,7 +469,6 @@
         wait(kvs, sems.at[3])
 
     wait(rows.at[s], sems.at[s])
-
     owner = lane_owner(4 * ROWS, jnp.where(s == 0, core, 1 - core))
     x = rows[s]
     inner = jnp.where(owner, dot_t(x, q_in[...]), 0.0).astype(bf16)
@@ -466,36 +479,35 @@
     inner_far[0] = kvs[s, :, :, 256:].reshape(4 * ROWS, RIDE)
     kv = jnp.concatenate([kv_own.reshape(4, ROWS, 256), kvs[s, :, :, :256]], axis=0)
     kv_all[0] = kv
-    keys = kv[:, :, :HEAD_WIDTH].reshape(8 * ROWS, HEAD_WIDTH)
-    values_t = kv[:, :, HEAD_WIDTH:].reshape(8 * ROWS, HEAD_WIDTH).astype(f32).T.astype(bf16)
-    columns = []
-    for h in range(2):
-        chunks = []
-        for c in range(2):
-            lanes = slice(c * 256, c * 256 + 256)
-            q = query[lanes, h * HEAD_WIDTH : (h + 1) * HEAD_WIDTH]
-            scores = dot_t(keys, q) * (HEAD_WIDTH**-0.5)
-            scores = scores.reshape(8, ROWS, 256) + bias[:, lanes][:, None, :]
-            scores = scores.reshape(8 * ROWS, 256)
-            top = jnp.max(scores, axis=0, keepdims=True)
-            expo = jnp.exp(scores - top)
-            total = jnp.sum(expo, axis=0, keepdims=True)
-            probs = (expo * (1.0 / total)).astype(bf16)
-            lse_out[0, h : h + 1, lanes] = top + jnp.log(total)
-            chunks.append(dot(values_t, probs).T)
-        columns.append(jnp.concatenate(chunks, axis=0))
-    attended = jnp.concatenate(columns, axis=1).astype(bf16)
+    attended = attend(query[2 * ROWS :], kv, bias, slice(2 * ROWS, 4 * ROWS), lse_out)
+    att_out[0] = attended
+    low = jnp.where(owner[2 * ROWS :], dot_t(attended, o_in[...]), 0.0).astype(bf16)
+    out = dot_t(attended, ws[:, 512:]).astype(bf16)
+    for which in range(2):
+
+        @pl.when(s == which)
+        def _(which=which):
+            for n, part in enumerate((parts[which], far_parts[which])):
+                here = slice(n * ROWS, (n + 1) * ROWS)
+                part[:, :MODEL_WIDTH] = out[here]
+                part[:, MODEL_WIDTH:] = low[here]
+
+
+def attention_rest_kernel(at, query_in, kv_in, w, o_in, bias, lse_out, att_out, mine, theirs):
+    s = pl.program_id(0)
+    owner = lane_owner(2 * ROWS, jnp.where(s == 0, at[0], 1 - at[0]))
+    attended = attend(query_in[0, : 2 * ROWS], kv_in[0], bias, slice(0, 2 * ROWS), lse_out)
     att_out[0] = attended
     low = jnp.where(owner, dot_t(attended, o_in[...]), 0.0).astype(bf16)
-    for which in range(2):
+    out = dot_t(attended, w[...]).astype(bf16)
+    for which, part in enumerate((mine, theirs)):
 
         @pl.when(s == which)
-        def _(which=which):
-            for p in range(4):
-                here = slice(p * ROWS, (p + 1) * ROWS)
-                part = parts[which].at[p] if p < 3 else far_parts[which]
-                part[:, :MODEL_WIDTH] = dot_t(attended[here], ws[:, 512:]).astype(bf16)
-                part[:, MODEL_WIDTH:] = low[here]
+        def _(part=part):
+            for n in range(2):
+                here = slice(n * ROWS, (n + 1) * ROWS)
+                part[n, :, :MODEL_WIDTH] = out[here]
+                part[n, :, MODEL_WIDTH:] = low[here]
 
 
 def store_parts(p, parts, far_parts, out, low):
@@ -619,12 +631,13 @@
 
 
 def attention_back_kernel(at, *refs):
-    branch, w, inner_in, inner_far, query_in, kv_in, lse_in, att_in = refs[:8]
-    o_out, o_in, q_out, kv_out, bias = refs[8:13]
-    placed, keyval_b, backs, backs_far = refs[13:17]
+    branch, w, inner_in, inner_far, query_in, kv_in = refs[:6]
+    lse_in, att_in = refs[6:8], refs[8:10]
+    o_out, o_in, q_out, kv_out, bias = refs[10:15]
+    placed, keyval_b, backs, backs_far = refs[15:19]
     query_b, output_a = placed.at[:, pl.ds(0, 256)], placed.at[:, pl.ds(256, 256)]
-    parts, far_parts = refs[17:19], refs[19:21]
-    rows, ws, grad_k, grad_v, sems = refs[21:]
+    parts, far_parts = refs[19:21], refs[21:23]
+    rows, ws, grad_k, grad_v, sems = refs[23:]
     s = pl.program_id(0)
     core = at[0]
 
@@ -647,7 +660,9 @@
     scale = HEAD_WIDTH**-0.5
     x = rows[s]
     back = jnp.where(owner, dot_t(x, o_out[...]), 0.0)
-    output_a[...] += dot(back.T[:32].astype(bf16), att_in[0])
+    output_a[...] += dot(
+        back.T[:32].astype(bf16), jnp.concatenate([att_in[0][0], att_in[1][0]], axis=0)
+    )
     grad_att = (dot(x, ws[:, 512:]) + dot(back.astype(bf16), o_in[...])).astype(bf16)
     query = query_in[0]
     kv = kv_in[0]
@@ -663,7 +678,7 @@
             q, g = query[lanes, head], grad_att[lanes, head]
             scores = dot_t(keys, q) * scale
             scores = scores.reshape(8, ROWS, 256) + bias[:, lanes][:, None, :]
-            probs = jnp.exp(scores.reshape(8 * ROWS, 256) - lse_in[0, h : h + 1, lanes])
+            probs = jnp.exp(scores.reshape(8 * ROWS, 256) - lse_in[c][0, h : h + 1])
             grad_probs = dot_t(values, g)
             delta = jnp.sum(probs * grad_probs, axis=0, keepdims=True)
             grad_scores = (probs * (grad_probs - delta)).astype(bf16)
@@ -775,27 +790,25 @@
     )(jnp.concatenate([jnp.reshape(core, (1,)), ids]).astype(jnp.int32), *pieces)
 
 
-def spread_out(kernel, at, pieces, widths, name):
+def spread_out(kernel, at, pieces, widths, name, steps=True):
     total = pieces[0].shape[-1]
-    blocks = [
-        (w, lambda i, j, at: (0, 0, j * 4 + i)) if w >= 128 else (128, lambda i, j, at: (0, 0, i // 2))
-        for w in widths
-    ]
+    full = [8 * w if w >= 128 else 256 for w in widths]
+    rows = (ADAPTER_COUNT, ADAPTER_RANK)
+    if steps:
+        grid = (4, 2)
+        out_specs = [pl.BlockSpec((*rows, w), lambda i, j, at: (0, 0, j * 4 + i)) for w in widths]
+    else:
+        grid = (1,)
+        out_specs = [pl.BlockSpec((*rows, w), lambda i, at: (0, 0, 0)) for w in full]
     return pl.pallas_call(
         functools.partial(kernel, widths),
-        out_shape=[
-            jax.ShapeDtypeStruct((ADAPTER_COUNT, ADAPTER_RANK, 8 * w if w >= 128 else 256), f32)
-            for w in widths
-        ],
+        out_shape=[jax.ShapeDtypeStruct((*rows, w), f32) for w in full],
         grid_spec=pltpu.PrefetchScalarGridSpec(
             num_scalar_prefetch=1,
-            grid=(4, 2),
+            grid=grid,
             in_specs=[ANY] * len(pieces),
-            out_specs=[pl.BlockSpec((ADAPTER_COUNT, ADAPTER_RANK, w), m) for w, m in blocks],
-            scratch_shapes=[
-                pltpu.VMEM((4, ADAPTER_COUNT, ADAPTER_RANK, total), bf16),
-                pltpu.SemaphoreType.DMA,
-            ],
+            out_specs=out_specs,
+            scratch_shapes=[pltpu.VMEM((4, *rows, total), bf16), pltpu.SemaphoreType.DMA],
         ),
         compiler_params=pltpu.CompilerParams(vmem_limit_bytes=VMEM_LIMIT),
         name=name,
@@ -922,7 +935,9 @@
         [jnp.zeros((1, HEAD_WIDTH), f32), value_projection_bias.astype(f32)[None]], axis=1
     )
     prepared = (q_in, u_in, o_out, d_out, kv_out, bias, keyval_bias, small)
-    plane, normed_sides, prepared = together((plane, normed_sides, prepared))
+    plane, normed_sides, prepared, feed_shard, cot_all = together(
+        (plane, normed_sides, prepared, feed_shard, cot_all)
+    )
     q_in, u_in, o_out, d_out, kv_out, bias, keyval_bias, small = prepared
     normed_places = gather_rest(*normed_sides)
     (w,) = call(
@@ -934,10 +949,10 @@
         [pltpu.SemaphoreType.DMA],
         "assemble",
     )
-    feed_shard, w, cot_all = together((feed_shard, w, cot_all))
     feed = lax.all_gather(feed_shard, DP + ("zh",), axis=0, tiled=True)
     feed = feed.reshape(16, 2, ROWS, 2048)
 
+    w, keyval_bias = together((w, keyval_bias))
     w_keyval = pl.BlockSpec((MODEL_WIDTH, 256), lambda i, at: (0, 1))
     keyval = call(
         own_keyval_kernel,
@@ -978,7 +993,7 @@
     group = (2, 4 * ROWS)
     row_scratch = pltpu.VMEM((2, 4 * ROWS, MODEL_WIDTH), bf16)
     w_scratch = pltpu.VMEM((MODEL_WIDTH, 768), bf16)
-    inner_one, inner_far, query, keyval_all, log_total, attended, *out_parts = call(
+    inner_one, inner_far, query, keyval_all, lse_high, att_high, *out_parts = call(
         attention_kernel,
         2,
         at,
@@ -999,15 +1014,43 @@
             ((*group, RIDE), bf16, step_block((4 * ROWS, RIDE))),
             ((*group, 256), bf16, step_block((4 * ROWS, 256))),
             ((2, 8, ROWS, 256), bf16, step_block((8, ROWS, 256))),
-            ((2, 2, 4 * ROWS), f32, step_block((2, 4 * ROWS))),
-            ((*group, 256), bf16, step_block((4 * ROWS, 256))),
-            *part_outs(MODEL_WIDTH + RIDE),
+            ((2, 2, 2 * ROWS), f32, step_block((2, 2 * ROWS))),
+            ((2, 2 * ROWS, 256), bf16, step_block((2 * ROWS, 256))),
+            *[((ROWS, MODEL_WIDTH + RIDE), bf16, None)] * 4,
         ],
         [row_scratch, pltpu.VMEM((2, 4, ROWS, 384), bf16), w_scratch, dma(4)],
         "attention",
         9000000000,
     )
-    out_sum = scatter_row(*out_parts)
+    out_far, query = together((scatter_far(*out_parts[2:]), query))
+    out_sides = scatter_sides(out_far)
+    out_right = add_cores(*out_parts[:2])
+    lse_low, att_low, out_mine, out_theirs = call(
+        attention_rest_kernel,
+        2,
+        at,
+        [
+            (query, step_block((4 * ROWS, 256))),
+            (keyval_all, step_block((8, ROWS, 256))),
+            (w, pl.BlockSpec((MODEL_WIDTH, 256), lambda i, at: (0, 2))),
+            (o_in, None),
+            (bias, None),
+        ],
+        [
+            ((2, 2, 2 * ROWS), f32, step_block((2, 2 * ROWS))),
+            ((2, 2 * ROWS, 256), bf16, step_block((2 * ROWS, 256))),
+            ((2, ROWS, MODEL_WIDTH + RIDE), bf16, None),
+            ((2, ROWS, MODEL_WIDTH + RIDE), bf16, None),
+        ],
+        [],
+        "attention_rest",
+        short=True,
+    )
+    out_mine, out_theirs, out_sides, out_right = together(
+        (out_mine, out_theirs, out_sides, out_right)
+    )
+    out_near = add_cores(out_mine, out_theirs)
+    out_sum = scatter_last(jnp.concatenate([out_near, out_right[None]]), *out_sides)
     output_inner = out_sum[:, MODEL_WIDTH:].astype(bf16)
     middle = (
         input_rows
@@ -1097,8 +1140,10 @@
             (inner_far, step_block((4 * ROWS, RIDE))),
             (query, step_block((4 * ROWS, 256))),
             (keyval_all, step_block((8, ROWS, 256))),
-            (log_total, step_block((2, 4 * ROWS))),
-            (attended, step_block((4 * ROWS, 256))),
+            (lse_low, step_block((2, 2 * ROWS))),
+            (lse_high, step_block((2, 2 * ROWS))),
+            (att_low, step_block((2 * ROWS, 256))),
+            (att_high, step_block((2 * ROWS, 256))),
             (o_out, None),
             (o_in, None),
             (q_out, None),
@@ -1209,6 +1254,7 @@
         [own_half, other_part, near, other_core(near), far, other_core(far)],
         (256, 256, 64, 256, 256, 256),
         "late_spread",
+        False,
     )
 
     def side_in(a):

time: 437 us -> 438 us (level)
  starting transfers between devices: 116 us -> 111 us
    ppermute x30 -> x31, starting transfers between devices: 32.7 us -> 28.7 us  [other_core(): return lax.ppermute(a, 'core', [(0, 1), (1, 0)])]
    pallas_call x12 -> x13, Pallas kernels: 115 us -> 119 us  [call(): pl.pallas_call(kernel, out_shape=[jax.ShapeDtypeStruct(s, d) for s, d, _...]
    ppermute x30 -> x31, waiting for transfers between devices: 11.6 us -> 14.7 us  [other_core(): return lax.ppermute(a, 'core', [(0, 1), (1, 0)])]
  transfers between devices with their start and end apart: 90 -> 91, of which waited for: 34 -> 37; matrix products, arithmetic and copies ran while one was open for 10% -> 10% of each run, Pallas kernels for 21% -> 21%
where the time goes in v7:
time: 438 us; the launch traced here: 429 us
  Pallas kernels  139 us (32%)
  starting transfers between devices  111 us (25%)
  waiting for transfers between devices  106 us (24%)
  other arithmetic  27.9 us (6%)
  local copies, waits for them, and re-layouts  19.3 us (4%)
  between operations  17.5 us (4%)
  matrix products  8.84 us (2%)
    pallas_call x13, Pallas kernels, call(): pl.pallas_call(kernel, out_shape=[jax.ShapeDtypeStruct(s, d) for s, d, _...  119 us
    ppermute x31, waiting for transfers between devices, ring_x(): return lax.ppermute(a, 'x', [(i, (i + step) % 4) for i in range(4)])  56.8 us
    ppermute x31, starting transfers between devices, ring_x(): return lax.ppermute(a, 'x', [(i, (i + step) % 4) for i in range(4)])  33.7 us
    ppermute x31, starting transfers between devices, other_core(): return lax.ppermute(a, 'core', [(0, 1), (1, 0)])  28.7 us
    ppermute x31, waiting for transfers between devices, other_core(): return lax.ppermute(a, 'core', [(0, 1), (1, 0)])  14.7 us
    ppermute x2, starting transfers between devices, turn(): return lax.ppermute(a, ('core', 'zh'), [(0, 0), (1, 2), (2, 1), (3, 3)])  13.3 us
    pallas_call x2, Pallas kernels, spread_out(): pl.pallas_call(functools.partial(kernel, widths), out_shape=[jax.ShapeDty...  12.8 us
    ppermute x6, starting transfers between devices, ring_y(): return lax.ppermute(a, 'y', [(i, (i + step) % 4) for i in range(4)])  10.5 us
  transfers between devices with their start and end apart: 91, of which 37 were waited for; matrix products, arithmetic and copies ran while one was open for 10% of the time, Pallas kernels for 21%

profile of v7, /device:TPU:1, one launch (start us, length us, event | category | flops | bytes accessed | tf_op | source)
XLA Modules:
  0.0 429.4 jit_solution(14317949302514574662)
XLA Ops:
  13.4 6.9 %collective-permute-start = (bf16[128,768]{1,0:T(8,128)(2,1)S(1)}, bf16[128,768]{1,0:T(8,128)(2,1)S(1)}, u32[]{:S(2)}, u32[]{:S(2)}) collective-permute-start(bf16[128,768]{1,0:T(8,128)(2,1)S(1)} %copy-done.47), channel_id=1, source_target_pairs={{0,0},{4,8},{8,4},{12,12},{1,1},{5,9},{9,5},{13,13},{2,2},{6,10},{... | collective-permute-start | bytes 589832 | tf_op jit(solution)/shard_map/ppermute | solution.py:57
  47.2 10.6 %collective-permute-done.9.refs_4_ = bf16[128,2048]{1,0:T(8,128)(2,1)S(1)} collective-permute-done((bf16[128,2048]{1,0:T(8,128)(2,1)S(1)}, bf16[128,2048]{1,0:T(8,128)(2,1)S(1)}, u32[]{:S(2)}, u32[]{:S(2)}) %collective-permute-start.9) | collective-permute-done | bytes 524320 | tf_op jit(solution)/shard_map/ppermute | solution.py:37
  59.5 6.4 %collective-permute-start.19 = (bf16[48,2560]{1,0:T(8,128)(2,1)}, bf16[48,2560]{1,0:T(8,128)(2,1)S(1)}, u32[]{:S(2)}, u32[]{:S(2)}) collective-permute-start(bf16[48,2560]{1,0:T(8,128)(2,1)} %get-tuple-element.244), channel_id=1, source_target_pairs={{0,0},{4,8},{8,4},{12,12},{1,1},{5,9},{9,5},{13,13},{2,2},{6,10},{... | collective-permute-start | bytes 737288 | tf_op jit(solution)/shard_map/ppermute | solution.py:57
  65.9 4.3 %assemble.1.w.refs_15_.refs_1_ = bf16[2048,768]{1,0:T(8,128)(2,1)} custom-call(s32[5]{0:T(128)} %stack.76.at, bf16[4,128,768]{2,1,0:T(8,128)(2,1)} %copy-done.9, bf16[4,128,768]{2,1,0:T(8,128)(2,1)} %collective-permute-done.5.refs_1_, bf16[4,128,768]{2,1,0:T(8,128)(2,1)} %collective-permute-done.6.refs_2_, bf16[4,128,768]{2,1,0:T(8,128)(2,1)} %collective-permute-done.7.refs_3_), custom_call_target="tpu_custom_call" | custom-call | bytes 9437184 | tf_op jit(solution)/shard_map/assemble/pallas_call | solution.py:734
  70.2 3.6 own_keyval.1
  74.7 5.3 %collective-permute-done.17 = bf16[128,384]{1,0:T(8,128)(2,1)S(1)} collective-permute-done((bf16[128,384]{1,0:T(8,128)(2,1)}, bf16[128,384]{1,0:T(8,128)(2,1)S(1)}, u32[]{:S(2)}, u32[]{:S(2)}) %collective-permute-start.17) | collective-permute-done | bytes 98336 | tf_op jit(solution)/shard_map/ppermute | solution.py:53
  90.0 3.7 collective-permute-done.20.refs_11_
  99.0 16.6 %attention.1 = (bf16[2,512,128]{2,1,0:T(8,128)(2,1)}, bf16[2,512,128]{2,1,0:T(8,128)(2,1)}, bf16[2,512,256]{2,1,0:T(8,128)(2,1)}, bf16[2,8,128,256]{3,2,1,0:T(8,...) custom-call(s32[5]{0:T(128)} %stack.76.at, ...), custom_call_target="tpu_custom_call" | custom-call | flops 8999999488 | bytes 18044928 | tf_op jit(solution)/shard_map/attention/pallas_call | solution.py:734
  120.8 8.4 %attention_rest.1 = (f32[2,2,256]{2,1,0:T(2,128)}, bf16[2,256,256]{2,1,0:T(8,128)(2,1)}, bf16[2,128,2176]{2,1,0:T(8,128)(2,1)}, bf16[2,128,2176]{2,1,0:T(8,128)(2,1)}) custom-call(s32[5]{0:T(128)} %stack.76.at, bf16[2,512,256]{2,1,0:T(8,128)(2,1)} %get-tuple-element.259.query_in.refs_4_, bf16[2,8,128,256]{3,2,1,0:T(8,128)(2,1)} %get-tuple-element.260.kv_in.refs_5_, ...), custom_call_target="tpu_custom_call" | custom-call | tf_op jit(solution)/shard_map/attention_rest/pallas_call | solution.py:734
  134.7 11.2 %collective-permute-done.29 = bf16[128,2176]{1,0:T(8,128)(2,1)S(1)} collective-permute-done((bf16[128,2176]{1,0:T(8,128)(2,1)S(1)}, bf16[128,2176]{1,0:T(8,128)(2,1)S(1)}, u32[]{:S(2)}, u32[]{:S(2)}) %collective-permute-start.29) | collective-permute-done | bytes 557088 | tf_op jit(solution)/shard_map/ppermute | solution.py:37
  152.8 9.0 %collective-permute-done.34.refs_4_ = bf16[128,2048]{1,0:T(8,128)(2,1)S(1)} collective-permute-done((bf16[128,2048]{1,0:T(8,128)(2,1)S(1)}, bf16[128,2048]{1,0:T(8,128)(2,1)S(1)}, u32[]{:S(2)}, u32[]{:S(2)}) %collective-permute-start.34) | collective-permute-done | bytes 524320 | tf_op jit(solution)/shard_map/ppermute | solution.py:37
  176.8 39.2 %feed.1 = (f32[32,2048]{1,0:T(8,128)}, bf16[3,128,2176]{2,1,0:T(8,128)(2,1)}, bf16[3,128,2176]{2,1,0:T(8,128)(2,1)}, bf16[128,2176]{1,0:T(8,128)(2,1)}, bf16[128...) custom-call(s32[5]{0:T(128)} %stack.76.at, ...), custom_call_target="tpu_custom_call" | custom-call | flops 19000000512 | bytes 44568576 | tf_op jit(solution)/shard_map/feed/pallas_call | solution.py:734
  222.0 6.2 %collective-permute-done.42 = bf16[64,2176]{1,0:T(8,128)(2,1)S(1)} collective-permute-done((bf16[64,2176]{1,0:T(8,128)(2,1)S(1)}, bf16[64,2176]{1,0:T(8,128)(2,1)S(1)}, u32[]{:S(2)}, u32[]{:S(2)}) %collective-permute-start.42) | collective-permute-done | bytes 278560 | tf_op jit(solution)/shard_map/ppermute | solution.py:37
  240.4 7.4 %collective-permute-done.45 = bf16[128,2176]{1,0:T(8,128)(2,1)S(1)} collective-permute-done((bf16[128,2176]{1,0:T(8,128)(2,1)S(1)}, bf16[128,2176]{1,0:T(8,128)(2,1)S(1)}, u32[]{:S(2)}, u32[]{:S(2)}) %collective-permute-start.45) | collective-permute-done | bytes 557088 | tf_op jit(solution)/shard_map/ppermute | solution.py:37
  257.6 3.7 collective-permute-start.51
  279.2 8.4 %all-gather.10.cloned.1.call-done = bf16[1024,2048]{1,0:T(8,128)(2,1)} async-done(((bf16[128,2048]{1,0:T(8,128)(2,1)}), bf16[1024,2048]{1,0:T(8,128)(2,1)}) %all-gather.10.cloned.1.call-update) | async-done | bytes 4194320 | tf_op jit(solution)/shard_map/all_gather | solution.py:1113
  287.6 24.5 %attention_back.1 = (f32[32,512]{1,0:T(8,128)}, f32[32,256]{1,0:T(8,128)}, bf16[2,512,128]{2,1,0:T(8,128)(2,1)}, bf16[2,32,512]{2,1,0:T(8,128)(2,1)}, bf16[3,128...) custom-call(s32[5]{0:T(128)} %stack.76.at, ...), custom_call_target="tpu_custom_call" | custom-call | tf_op jit(solution)/shard_map/attention_back/pallas_call | solution.py:734
  312.5 4.2 collective-permute-start.61
  325.8 5.7 %late.1 = (bf16[4,16,1664]{2,1,0:T(8,128)(2,1)}, bf16[4,16,1152]{2,1,0:T(8,128)(2,1)}) custom-call(s32[5]{0:T(128)} %stack.76.at, bf16[128,2048]{1,0:T(8,128)(2,1)} %norm.1.rows.refs_0_, bf16[128,2048]{1,0:T(8,128)(2,1)} %copy-done.35, bf16[128,2048]{1,0:T(8,128)(2,1)} %copy-done.25, bf16[128,2048]{1,0:T(8,128)(2,1)} %copy-done.33, ...), custom_call_target="tpu_custom_call" | custom-call | bytes 8585216 | tf_op jit(solution)/shard_map/late/pallas_call | solution.py:734
  347.6 3.7 sum_by_adapter.2
  381.5 5.3 %collective-permute-done.78.refs_2_ = bf16[4,16,2688]{2,1,0:T(8,128)(2,1)} collective-permute-done((bf16[4,16,2688]{2,1,0:T(8,128)(2,1)S(1)}, bf16[4,16,2688]{2,1,0:T(8,128)(2,1)}, u32[]{:S(2)}, u32[]{:S(2)}) %collective-permute-start.78) | collective-permute-done | bytes 344096 | tf_op jit(solution)/shard_map/ppermute | solution.py:45
  399.0 8.0 %feed_spread.1 = (f32[8,16,8192]{2,1,0:T(8,128)}, f32[8,16,8192]{2,1,0:T(8,128)}, f32[8,16,2048]{2,1,0:T(8,128)}, f32[8,16,2048]{2,1,0:T(8,128)}) custom-call(s32[5]{0:T(128)} %stack.76.at, bf16[2,4,4,16,5376]{4,3,2,1,0:T(8,128)(2,1)} %bitcast.127), custom_call_target="tpu_custom_call" | custom-call | tf_op jit(solution)/shard_map/feed_spread/pallas_call | solution.py:803
  407.0 4.1 collective-permute-done.83.refs_2_
  417.7 4.8 %late_spread.1 = (f32[8,16,2048]{2,1,0:T(8,128)}, f32[8,16,2048]{2,1,0:T(8,128)}, f32[8,16,256]{2,1,0:T(8,128)}, f32[8,16,2048]{2,1,0:T(8,128)}, f32[8,16,2048]{2,1,0:T(8,128)}, /*index=5*/f32[8,16,2048]{2,1,0:T(8,128)}) custom-call(s32[5]{0:T(128)} %stack.76.at, bf16[4,16,2688]{2,1,0:T(8,128)(2,1)} %copy-done.10, bf16[4,16,2688]{2,1,0:T(8,128)(2,1)} %copy-done.21, ...), custom_call_target="tpu_custom_call" | custom-call | tf_op jit(solution)/shard_map/late_spread/pallas_call | solution.py:803
  (447 shorter events, 200.8 us)
Async XLA Ops:
  7.2 51.5 %all-gather.6.cloned.1.call-start = ((), (), s32[]{:S(2)}) async-start(), calls=%async_computation | async-start | bytes 5013504 | tf_op jit(solution)/shard_map/all_gather | solution.py:872
  13.4 163.4 %all-gather.8.cloned.1.call-start = ((), (), s32[]{:S(2)}) async-start(), calls=%async_computation.1 | async-start | bytes 17301504 | tf_op jit(solution)/shard_map/all_gather | solution.py:952
  32.7 25.9 %collective-permute-start.7 = (bf16[4,128,768]{2,1,0:T(8,128)(2,1)S(1)}, bf16[4,128,768]{2,1,0:T(8,128)(2,1)}, u32[]{:S(2)}, u32[]{:S(2)}) collective-permute-start(bf16[4,128,768]{2,1,0:T(8,128)(2,1)S(1)} %pad_maximum_fusion.refs_0_), channel_id=1, source_target_pairs={{0,16},{8,40},{16,4},{24,56},{4,20},{12,44},{20,0},{28,60},{32,48}... | collective-permute-start | bytes 2359304 | tf_op jit(solution)/shard_map/ppermute | solution.py:78
  34.1 24.6 %collective-permute-start.6 = (bf16[4,128,768]{2,1,0:T(8,128)(2,1)S(1)}, bf16[4,128,768]{2,1,0:T(8,128)(2,1)}, u32[]{:S(2)}, u32[]{:S(2)}) collective-permute-start(bf16[4,128,768]{2,1,0:T(8,128)(2,1)S(1)} %pad_maximum_fusion.refs_0_), channel_id=1, source_target_pairs={{0,4},{8,72},{16,20},{24,88},{4,0},{12,76},{20,16},{28,92},{32,36}... | collective-permute-start | bytes 2359304 | tf_op jit(solution)/shard_map/ppermute | solution.py:78
  37.0 21.7 %collective-permute-start.5 = (bf16[4,128,768]{2,1,0:T(8,128)(2,1)S(1)}, bf16[4,128,768]{2,1,0:T(8,128)(2,1)}, u32[]{:S(2)}, u32[]{:S(2)}) collective-permute-start(bf16[4,128,768]{2,1,0:T(8,128)(2,1)S(1)} %pad_maximum_fusion.refs_0_), channel_id=1, source_target_pairs={{0,20},{8,104},{16,0},{24,120},{4,16},{12,108},{20,4},{28,124},{32... | collective-permute-start | bytes 2359304 | tf_op jit(solution)/shard_map/ppermute | solution.py:78
  37.8 20.1 %collective-permute-start.9 = (bf16[128,2048]{1,0:T(8,128)(2,1)S(1)}, bf16[128,2048]{1,0:T(8,128)(2,1)S(1)}, u32[]{:S(2)}, u32[]{:S(2)}) collective-permute-start(bf16[128,2048]{1,0:T(8,128)(2,1)S(1)} %copy-done.7), channel_id=1, source_target_pairs={{0,3},{1,0},{2,1},{3,2},{4,7},{5,4},{6,5},{7,6},{8,11},{9,8},{10,9... | collective-permute-start | bytes 1572872 | tf_op jit(solution)/shard_map/ppermute | solution.py:37
  40.2 18.4 %collective-permute-start.8 = (bf16[128,2048]{1,0:T(8,128)(2,1)S(1)}, bf16[128,2048]{1,0:T(8,128)(2,1)S(1)}, u32[]{:S(2)}, u32[]{:S(2)}) collective-permute-start(bf16[128,2048]{1,0:T(8,128)(2,1)S(1)} %copy-done.7), channel_id=1, source_target_pairs={{0,1},{1,2},{2,3},{3,0},{4,5},{5,6},{6,7},{7,4},{8,9},{9,10},{10,1... | collective-permute-start | bytes 1572872 | tf_op jit(solution)/shard_map/ppermute | solution.py:37
  58.7 228.9 %all-gather.10.cloned.1.call-start = ((), (), s32[]{:S(2)}) async-start(), calls=%async_computation.2 | async-start | bytes 4718592 | tf_op jit(solution)/shard_map/all_gather | solution.py:1113
  58.8 27.0 %collective-permute-start.14 = (bf16[64,2048]{1,0:T(8,128)(2,1)S(1)}, bf16[64,2048]{1,0:T(8,128)(2,1)S(1)}, u32[]{:S(2)}, u32[]{:S(2)}) collective-permute-start(bf16[64,2048]{1,0:T(8,128)(2,1)S(1)} %slice.198), channel_id=1, source_target_pairs={{0,3},{1,0},{2,1},{3,2},{4,7},{5,4},{6,5},{7,6},{8,11},{9,8},{10,9... | collective-permute-start | bytes 786440 | tf_op jit(solution)/shard_map/ppermute | solution.py:37
  59.5 26.1 %collective-permute-start.19 = (bf16[48,2560]{1,0:T(8,128)(2,1)}, bf16[48,2560]{1,0:T(8,128)(2,1)S(1)}, u32[]{:S(2)}, u32[]{:S(2)}) collective-permute-start(bf16[48,2560]{1,0:T(8,128)(2,1)} %get-tuple-element.244), channel_id=1, source_target_pairs={{0,0},{4,8},{8,4},{12,12},{1,1},{5,9},{9,5},{13,13},{2,2},{6,10},{... | collective-permute-start | bytes 737288 | tf_op jit(solution)/shard_map/ppermute | solution.py:57
  130.4 15.5 %collective-permute-start.29 = (bf16[128,2176]{1,0:T(8,128)(2,1)S(1)}, bf16[128,2176]{1,0:T(8,128)(2,1)S(1)}, u32[]{:S(2)}, u32[]{:S(2)}) collective-permute-start(bf16[128,2176]{1,0:T(8,128)(2,1)S(1)} %pad_maximum_fusion.6), channel_id=1, source_target_pairs={{0,1},{1,2},{2,3},{3,0},{4,5},{5,6},{6,7},{7,4},{8,9},{9,10},{10,1... | collective-permute-start | bytes 1671176 | tf_op jit(solution)/shard_map/ppermute | solution.py:37
  151.3 23.6 %collective-permute-start.31 = (bf16[128,2048]{1,0:T(8,128)(2,1)S(1)}, bf16[128,2048]{1,0:T(8,128)(2,1)S(1)}, u32[]{:S(2)}, u32[]{:S(2)}) collective-permute-start(bf16[128,2048]{1,0:T(8,128)(2,1)S(1)} %add_convert_fusion.6.refs_0_.refs_1_), channel_id=1, source_target_pairs={{0,8},{8,0},{1,9},{9,1},{2,10},{10,2},{3,11},{11,3},{4,12},{12,4},... | collective-permute-start | bytes 1572872 | tf_op jit(solution)/shard_map/ppermute | solution.py:49
  251.7 147.3 %all-gather.12.cloned.1.call-start = ((), (), s32[]{:S(2)}) async-start(), calls=%async_computation.3 | async-start | bytes 6193152 | tf_op jit(solution)/shard_map/all_gather | solution.py:1225
  273.7 38.4 %collective-permute-start.59 = (bf16[4,16,5376]{2,1,0:T(8,128)(2,1)S(1)}, bf16[4,16,5376]{2,1,0:T(8,128)(2,1)}, u32[]{:S(2)}, u32[]{:S(2)}) collective-permute-start(bf16[4,16,5376]{2,1,0:T(8,128)(2,1)S(1)} %pad_maximum_fusion.1.refs_0_), channel_id=1, source_target_pairs={{0,16},{16,4},{4,20},{20,0},{1,17},{17,5},{5,21},{21,1},{2,18},{18... | collective-permute-start | bytes 2064392 | tf_op jit(solution)/shard_map/ppermute | solution.py:45
  274.8 37.3 %collective-permute-start.58 = (bf16[4,16,5376]{2,1,0:T(8,128)(2,1)S(1)}, bf16[4,16,5376]{2,1,0:T(8,128)(2,1)}, u32[]{:S(2)}, u32[]{:S(2)}) collective-permute-start(bf16[4,16,5376]{2,1,0:T(8,128)(2,1)S(1)} %pad_maximum_fusion.1.refs_0_), channel_id=1, source_target_pairs={{0,20},{16,0},{4,16},{20,4},{1,21},{17,1},{5,17},{21,5},{2,22},{18... | collective-permute-start | bytes 2064392 | tf_op jit(solution)/shard_map/ppermute | solution.py:45
  276.7 35.4 %collective-permute-start.55 = (bf16[128,2176]{1,0:T(8,128)(2,1)}, bf16[128,2176]{1,0:T(8,128)(2,1)S(1)}, u32[]{:S(2)}, u32[]{:S(2)}) collective-permute-start(bf16[128,2176]{1,0:T(8,128)(2,1)} %get-tuple-element.332), channel_id=1, source_target_pairs={{0,3},{1,0},{2,1},{3,2},{4,7},{5,4},{6,5},{7,6},{8,11},{9,8},{10,9... | collective-permute-start | bytes 1671176 | tf_op jit(solution)/shard_map/ppermute | solution.py:37
  277.4 34.6 %collective-permute-start.56 = (bf16[128,2176]{1,0:T(8,128)(2,1)}, bf16[128,2176]{1,0:T(8,128)(2,1)}, u32[]{:S(2)}, u32[]{:S(2)}) collective-permute-start(bf16[128,2176]{1,0:T(8,128)(2,1)} %get-tuple-element.333), channel_id=1, source_target_pairs={{0,1},{1,2},{2,3},{3,0},{4,5},{5,6},{6,7},{7,4},{8,9},{9,10},{10,1... | collective-permute-start | bytes 1671176 | tf_op jit(solution)/shard_map/ppermute | solution.py:37
  278.1 33.9 %collective-permute-start.57 = (bf16[128,2176]{1,0:T(8,128)(2,1)}, bf16[128,2176]{1,0:T(8,128)(2,1)}, u32[]{:S(2)}, u32[]{:S(2)}) collective-permute-start(bf16[128,2176]{1,0:T(8,128)(2,1)} %add_convert_fusion.2), channel_id=1, source_target_pairs={{0,2},{1,3},{2,0},{3,1},{4,6},{5,7},{6,4},{7,5},{8,10},{9,11},{10,... | collective-permute-start | bytes 1671176 | tf_op jit(solution)/shard_map/ppermute | solution.py:37
  322.8 18.3 %collective-permute-start.69 = (bf16[4,16,5376]{2,1,0:T(8,128)(2,1)S(1)}, bf16[4,16,5376]{2,1,0:T(8,128)(2,1)S(1)}, u32[]{:S(2)}, u32[]{:S(2)}) collective-permute-start(bf16[4,16,5376]{2,1,0:T(8,128)(2,1)S(1)} %pad_maximum_fusion.1.refs_0_), channel_id=1, source_target_pairs={{0,4},{16,20},{4,0},{20,16},{1,5},{17,21},{5,1},{21,17},{2,6},{18,... | collective-permute-start | bytes 2064392 | tf_op jit(solution)/shard_map/ppermute | solution.py:45
  341.0 22.1 %collective-permute-start.74 = (bf16[128,2688]{1,0:T(8,128)(2,1)}, bf16[128,2688]{1,0:T(8,128)(2,1)}, u32[]{:S(2)}, u32[]{:S(2)}) collective-permute-start(bf16[128,2688]{1,0:T(8,128)(2,1)} %pad_maximum_fusion.2), channel_id=1, source_target_pairs={{0,1},{1,2},{2,3},{3,0},{4,5},{5,6},{6,7},{7,4},{8,9},{9,10},{10,1... | collective-permute-start | bytes 2064392 | tf_op jit(solution)/shard_map/ppermute | solution.py:37
  341.1 22.0 %collective-permute-start.75 = (bf16[128,2688]{1,0:T(8,128)(2,1)}, bf16[128,2688]{1,0:T(8,128)(2,1)}, u32[]{:S(2)}, u32[]{:S(2)}) collective-permute-start(bf16[128,2688]{1,0:T(8,128)(2,1)} %pad_maximum_fusion.3), channel_id=1, source_target_pairs={{0,3},{1,0},{2,1},{3,2},{4,7},{5,4},{6,5},{7,6},{8,11},{9,8},{10,9... | collective-permute-start | bytes 2064392 | tf_op jit(solution)/shard_map/ppermute | solution.py:37
  368.5 18.3 %collective-permute-start.78 = (bf16[4,16,2688]{2,1,0:T(8,128)(2,1)S(1)}, bf16[4,16,2688]{2,1,0:T(8,128)(2,1)}, u32[]{:S(2)}, u32[]{:S(2)}) collective-permute-start(bf16[4,16,2688]{2,1,0:T(8,128)(2,1)S(1)} %pad_maximum_fusion.10.refs_0_), channel_id=1, source_target_pairs={{0,4},{16,20},{4,0},{20,16},{1,5},{17,21},{5,1},{21,17},{2,6},{18,... | collective-permute-start | bytes 1032200 | tf_op jit(solution)/shard_map/ppermute | solution.py:45
  370.9 15.9 %collective-permute-start.77 = (bf16[4,16,2688]{2,1,0:T(8,128)(2,1)S(1)}, bf16[4,16,2688]{2,1,0:T(8,128)(2,1)}, u32[]{:S(2)}, u32[]{:S(2)}) collective-permute-start(bf16[4,16,2688]{2,1,0:T(8,128)(2,1)S(1)} %pad_maximum_fusion.10.refs_0_), channel_id=1, source_target_pairs={{0,20},{16,0},{4,16},{20,4},{1,21},{17,1},{5,17},{21,5},{2,22},{18... | collective-permute-start | bytes 1032200 | tf_op jit(solution)/shard_map/ppermute | solution.py:45
  395.9 15.2 %collective-permute-start.83 = (bf16[8,16,2688]{2,1,0:T(8,128)(2,1)S(1)}, bf16[8,16,2688]{2,1,0:T(8,128)(2,1)S(1)}, u32[]{:S(2)}, u32[]{:S(2)}) collective-permute-start(bf16[8,16,2688]{2,1,0:T(8,128)(2,1)S(1)} %pad_maximum_fusion.4), channel_id=1, source_target_pairs={{0,1},{1,2},{2,3},{3,0},{8,11},{9,8},{10,9},{11,10},{4,5},{5,6},{6... | collective-permute-start | bytes 2064392 | tf_op jit(solution)/shard_map/ppermute | solution.py:150
  (145 other events, 1054.3 us)
Sparse Core Ops, SparseCore 0:
  13.5 42.1 all-gather.5
  58.8 106.9 all-gather.7
  251.8 35.7 all-gather.9
  363.3 35.6 all-gather.11
